TPU v7x, 32 devices: a whole 2x2x4 slice. The times are simulated.
32 devices in a mesh: dp: 4 (over z), fsdp: 8 (over y, x, core).
Axes of the slice: x: 2, y: 2, z: 4, core: 2. Of those that a mesh axis runs over, the one named last changes fastest.
Arguments:
- tokens: bfloat16 [36864, 768], P(('dp', 'fsdp')), may hold values from -6 to 6
- input_weight: bfloat16 [768, 2304], P(('dp', 'fsdp')), may hold values from -0.21875 to 0.21875
- query_bias: bfloat16 [768], P(('dp', 'fsdp')), may hold values from -3 to 3
- value_bias: bfloat16 [768], P(('dp', 'fsdp')), may hold values from -2 to 2
- output_weight: bfloat16 [768, 768], P(('dp', 'fsdp')), may hold values from -0.875 to 0.875
- output_bias: bfloat16 [768], P(('dp', 'fsdp')), may hold values from -2 to 2
- first_gain: bfloat16 [768], P(('dp', 'fsdp')), may hold values from 0.5 to 1.5
- first_shift: bfloat16 [768], P(('dp', 'fsdp')), may hold values from -2 to 2
- up_weight: bfloat16 [768, 3072], P(('dp', 'fsdp')), may hold values from -0.21875 to 0.21875
- up_bias: bfloat16 [3072], P(('dp', 'fsdp')), may hold values from -2 to 2
- down_weight: bfloat16 [3072, 768], P(('dp', 'fsdp')), may hold values from -0.109375 to 0.109375
- down_bias: bfloat16 [768], P(('dp', 'fsdp')), may hold values from -2 to 2
- second_gain: bfloat16 [768], P(('dp', 'fsdp')), may hold values from 0.5 to 1.5
- second_shift: bfloat16 [768], P(('dp', 'fsdp')), may hold values from -2 to 2
- retriever_weight: bfloat16 [768, 128], P(('dp', 'fsdp')), may hold values from -0.21875 to 0.21875
- document_table: bfloat16 [8192, 128], P(('dp', 'fsdp')), may hold values from -0.5 to 0.5
- document_index: int32 [128], P(('dp', 'fsdp')), may hold values from 0 to 8191
- output_grad: bfloat16 [36864, 768], P(('dp', 'fsdp')), may hold values from -6 to 6
- score_grad: float32 [128], P(('dp', 'fsdp')), may hold values from -6 to 6
Outputs:
- output: bfloat16 [36864, 768], P(('dp', 'fsdp'))
- retrieval_scores: float32 [128], P(('dp', 'fsdp'))
- tokens_gradient: bfloat16 [36864, 768], P(('dp', 'fsdp'))
- input_weight_gradient: float32 [768, 2304], P(('dp', 'fsdp'))
- query_bias_gradient: float32 [768], P(('dp', 'fsdp'))
- value_bias_gradient: float32 [768], P(('dp', 'fsdp'))
- output_weight_gradient: float32 [768, 768], P(('dp', 'fsdp'))
- output_bias_gradient: float32 [768], P(('dp', 'fsdp'))
- first_gain_gradient: float32 [768], P(('dp', 'fsdp'))
- first_shift_gradient: float32 [768], P(('dp', 'fsdp'))
- up_weight_gradient: float32 [768, 3072], P(('dp', 'fsdp'))
- up_bias_gradient: float32 [3072], P(('dp', 'fsdp'))
- down_weight_gradient: float32 [3072, 768], P(('dp', 'fsdp'))
- down_bias_gradient: float32 [768], P(('dp', 'fsdp'))
- second_gain_gradient: float32 [768], P(('dp', 'fsdp'))
- second_shift_gradient: float32 [768], P(('dp', 'fsdp'))
- retriever_gradient: float32 [768, 128], P(('dp', 'fsdp'))
- table_gradient: float32 [8192, 128], P(('dp', 'fsdp'))
All inputs are finite; a program needn't handle non-finite values.
Results may differ from a plain program's by a relative error of at most 0.014.
Values may be sent and summed in bfloat16 or wider, within the bound.
No kernel may reach another device: no remote copies, remote signals or barrier semaphores. Data moves between devices by JAX's collectives and lax.ppermute only.
A program may use at most 192 MiB of HBM per device.

v0:
```python
from functools import partial

import jax
import jax.numpy as jnp
from jax import lax
from jax.sharding import PartitionSpec as P

HEAD_DIM = 64


epsilon = 1e-12


def normalize(hidden, norm_gain, norm_shift):
    average = jnp.mean(hidden, axis=-1, keepdims=True)
    centered = hidden - average
    variance = jnp.mean(centered * centered, axis=-1, keepdims=True)
    return centered * lax.rsqrt(variance + epsilon) * norm_gain + norm_shift


def normalize_back(back_out, hidden, norm_gain):
    average = jnp.mean(hidden, axis=-1, keepdims=True)
    centered = hidden - average
    variance = jnp.mean(centered * centered, axis=-1, keepdims=True)
    inverse = lax.rsqrt(variance + epsilon)
    normed = centered * inverse
    back_gain = jnp.sum(back_out * normed, axis=0)
    back_shift = jnp.sum(back_out, axis=0)
    scaled = back_out * norm_gain.astype(jnp.float32)
    back_hidden = inverse * (
        scaled
        - jnp.mean(scaled, axis=-1, keepdims=True)
        - normed * jnp.mean(scaled * normed, axis=-1, keepdims=True)
    )
    return (back_hidden, back_gain, back_shift)


def to_heads(matrix, sequences, head_count):
    row_count, model_width = matrix.shape
    shaped = matrix.reshape(
        sequences, row_count // sequences, head_count, model_width // head_count
    )
    return shaped.transpose(2, 0, 1, 3)


def from_heads(stacked):
    head_count, sequences, token_count, head_size = stacked.shape
    return stacked.transpose(1, 2, 0, 3).reshape(sequences * token_count, head_count * head_size)


def layer_forward(tokens, weights, sequences):
    (
        input_weight,
        query_bias,
        value_bias,
        output_weight,
        output_bias,
        first_gain,
        first_shift,
        up_weight,
        up_bias,
        down_weight,
        down_bias,
        second_gain,
        second_shift,
        retriever_weight,
    ) = weights
    model_width = tokens.shape[1]
    head_count = model_width // HEAD_DIM
    head_scale = HEAD_DIM ** (-0.5)
    mixed = jnp.dot(tokens, input_weight, preferred_element_type=jnp.float32)
    queries = (mixed[:, :model_width] + query_bias).astype(jnp.bfloat16)
    keys_all = mixed[:, model_width : 2 * model_width].astype(jnp.bfloat16)
    values = (mixed[:, 2 * model_width :] + value_bias).astype(jnp.bfloat16)
    query_heads = to_heads(queries, sequences, head_count)
    key_heads = to_heads(keys_all, sequences, head_count)
    value_heads = to_heads(values, sequences, head_count)

    def layer_one_head(operands):
        queries_one, keys_one, values_one = operands
        scores = (
            jnp.einsum("gqe,gke->gqk", queries_one, keys_one, preferred_element_type=jnp.float32)
            * head_scale
        )
        row_peak = jnp.max(scores, axis=-1, keepdims=True)
        raised = jnp.exp(scores - row_peak)
        row_total = jnp.sum(raised, axis=-1, keepdims=True)
        soft_weights = (raised / row_total).astype(jnp.bfloat16)
        context = jnp.einsum(
            "gqk,gke->gqe", soft_weights, values_one, preferred_element_type=jnp.float32
        )
        return (context, row_peak[..., 0] + jnp.log(row_total[..., 0]))

    context_heads, log_totals = lax.map(layer_one_head, (query_heads, key_heads, value_heads))
    context = from_heads(context_heads).astype(jnp.bfloat16)
    attended = jnp.dot(context, output_weight, preferred_element_type=jnp.float32) + output_bias
    hidden_one = tokens.astype(jnp.float32) + attended
    first_out = normalize(hidden_one, first_gain, first_shift).astype(jnp.bfloat16)
    inner_sum = jnp.dot(first_out, up_weight, preferred_element_type=jnp.float32) + up_bias
    active = jax.nn.gelu(inner_sum, approximate=False).astype(jnp.bfloat16)
    feed_out = jnp.dot(active, down_weight, preferred_element_type=jnp.float32) + down_bias
    hidden_two = first_out.astype(jnp.float32) + feed_out
    final_out = normalize(hidden_two, second_gain, second_shift).astype(jnp.bfloat16)
    return (
        query_heads,
        key_heads,
        value_heads,
        log_totals,
        context,
        hidden_one,
        first_out,
        inner_sum,
        active,
        hidden_two,
        final_out,
    )


def attention_back(
    query_heads, key_heads, value_heads, log_totals, back_context, sequences, head_count
):
    head_scale = HEAD_DIM ** (-0.5)
    back_heads = to_heads(back_context, sequences, head_count)

    def attention_one_head(operands):
        queries_one, keys_one, values_one, log_one, back_one = operands
        scores = (
            jnp.einsum("gqe,gke->gqk", queries_one, keys_one, preferred_element_type=jnp.float32)
            * head_scale
        )
        soft = jnp.exp(scores - log_one[..., None])
        soft_low = soft.astype(jnp.bfloat16)
        back_values = jnp.einsum(
            "gqk,gqe->gke", soft_low, back_one, preferred_element_type=jnp.float32
        )
        back_soft = jnp.einsum(
            "gqe,gke->gqk", back_one, values_one, preferred_element_type=jnp.float32
        )
        back_scores = soft * (back_soft - jnp.sum(soft * back_soft, axis=-1, keepdims=True))
        back_scores = back_scores.astype(jnp.bfloat16)
        back_queries = (
            jnp.einsum("gqk,gke->gqe", back_scores, keys_one, preferred_element_type=jnp.float32)
            * head_scale
        )
        back_keys = (
            jnp.einsum("gqk,gqe->gke", back_scores, queries_one, preferred_element_type=jnp.float32)
            * head_scale
        )
        return (
            back_queries.astype(jnp.bfloat16),
            back_keys.astype(jnp.bfloat16),
            back_values.astype(jnp.bfloat16),
        )

    return lax.map(
        attention_one_head, (query_heads, key_heads, value_heads, log_totals, back_heads)
    )


def local(
    tokens,
    input_weight,
    query_bias,
    value_bias,
    output_weight,
    output_bias,
    first_gain,
    first_shift,
    up_weight,
    up_bias,
    down_weight,
    down_bias,
    second_gain,
    second_shift,
    retriever_weight,
    document_table,
    document_index,
    output_grad,
    score_grad,
):
    sequences = document_index.shape[0]
    token_count = tokens.shape[0] // sequences
    model_width = tokens.shape[1]
    head_count = model_width // HEAD_DIM
    gathered = (
        lax.all_gather(input_weight, ("dp", "fsdp"), axis=0, tiled=True),
        lax.all_gather(query_bias, ("dp", "fsdp"), axis=0, tiled=True),
        lax.all_gather(value_bias, ("dp", "fsdp"), axis=0, tiled=True),
        lax.all_gather(output_weight, ("dp", "fsdp"), axis=0, tiled=True),
        lax.all_gather(output_bias, ("dp", "fsdp"), axis=0, tiled=True),
        lax.all_gather(first_gain, ("dp", "fsdp"), axis=0, tiled=True),
        lax.all_gather(first_shift, ("dp", "fsdp"), axis=0, tiled=True),
        lax.all_gather(up_weight, ("dp", "fsdp"), axis=0, tiled=True),
        lax.all_gather(up_bias, ("dp", "fsdp"), axis=0, tiled=True),
        lax.all_gather(down_weight, ("dp", "fsdp"), axis=0, tiled=True),
        lax.all_gather(down_bias, ("dp", "fsdp"), axis=0, tiled=True),
        lax.all_gather(second_gain, ("dp", "fsdp"), axis=0, tiled=True),
        lax.all_gather(second_shift, ("dp", "fsdp"), axis=0, tiled=True),
        lax.all_gather(retriever_weight, ("dp", "fsdp"), axis=0, tiled=True),
        lax.all_gather(document_table, ("dp", "fsdp"), axis=0, tiled=True),
    )
    weights = tuple(gathered[:14])
    table_full = gathered[14]
    kept_state = layer_forward(tokens, weights, sequences)
    final_out = kept_state[10]
    leading = final_out.reshape(sequences, token_count, model_width)[:, 0]
    projected = jnp.dot(leading, weights[13], preferred_element_type=jnp.float32).astype(
        jnp.bfloat16
    )
    table_rows = table_full.shape[0]
    picker = (document_index[:, None] == jnp.arange(table_rows, dtype=jnp.int32)[None, :]).astype(
        jnp.bfloat16
    )
    chosen = jnp.dot(picker, table_full, preferred_element_type=jnp.float32)
    scores = jnp.sum(projected.astype(jnp.float32) * chosen, axis=-1)
    back_projected = (score_grad[:, None] * chosen).astype(jnp.bfloat16)
    table_term = jnp.dot(
        picker.astype(jnp.float32).T,
        score_grad[:, None] * projected.astype(jnp.float32),
        precision=lax.Precision.HIGHEST,
    )
    weights = tuple(
        (
            lax.all_gather(input_weight, ("dp", "fsdp"), axis=0, tiled=True),
            lax.all_gather(query_bias, ("dp", "fsdp"), axis=0, tiled=True),
            lax.all_gather(value_bias, ("dp", "fsdp"), axis=0, tiled=True),
            lax.all_gather(output_weight, ("dp", "fsdp"), axis=0, tiled=True),
            lax.all_gather(output_bias, ("dp", "fsdp"), axis=0, tiled=True),
            lax.all_gather(first_gain, ("dp", "fsdp"), axis=0, tiled=True),
            lax.all_gather(first_shift, ("dp", "fsdp"), axis=0, tiled=True),
            lax.all_gather(up_weight, ("dp", "fsdp"), axis=0, tiled=True),
            lax.all_gather(up_bias, ("dp", "fsdp"), axis=0, tiled=True),
            lax.all_gather(down_weight, ("dp", "fsdp"), axis=0, tiled=True),
            lax.all_gather(down_bias, ("dp", "fsdp"), axis=0, tiled=True),
            lax.all_gather(second_gain, ("dp", "fsdp"), axis=0, tiled=True),
            lax.all_gather(second_shift, ("dp", "fsdp"), axis=0, tiled=True),
            lax.all_gather(retriever_weight, ("dp", "fsdp"), axis=0, tiled=True),
        )
    )
    kept_state = layer_forward(tokens, weights, sequences)
    (
        query_heads,
        key_heads,
        value_heads,
        log_totals,
        context,
        hidden_one,
        first_out,
        inner_sum,
        active,
        hidden_two,
        final_kept,
    ) = kept_state
    input_full = weights[0]
    output_full = weights[3]
    first_gain_full = weights[5]
    up_full = weights[7]
    down_full = weights[9]
    second_gain_full = weights[11]
    retriever_full = weights[13]
    retriever_back = jnp.dot(leading.T, back_projected, preferred_element_type=jnp.float32)
    back_leading = jnp.dot(back_projected, retriever_full.T, preferred_element_type=jnp.float32)
    back_final = output_grad.astype(jnp.float32).reshape(sequences, token_count, model_width)
    back_final = back_final.at[:, 0].add(back_leading).reshape(sequences * token_count, model_width)
    back_two, second_gain_back, second_shift_back = normalize_back(
        back_final, hidden_two, second_gain_full
    )
    back_feed = back_two.astype(jnp.bfloat16)
    down_back = jnp.dot(active.T, back_feed, preferred_element_type=jnp.float32)
    down_bias_back = jnp.sum(back_feed.astype(jnp.float32), axis=0)
    back_active = jnp.dot(back_feed, down_full.T, preferred_element_type=jnp.float32)
    gelu_pull = jax.vjp(partial(jax.nn.gelu, approximate=False), inner_sum)[1]
    back_inner = gelu_pull(back_active)[0].astype(jnp.bfloat16)
    up_back = jnp.dot(first_out.T, back_inner, preferred_element_type=jnp.float32)
    up_bias_back = jnp.sum(back_inner.astype(jnp.float32), axis=0)
    back_first = back_two + jnp.dot(back_inner, up_full.T, preferred_element_type=jnp.float32)
    back_one, first_gain_back, first_shift_back = normalize_back(
        back_first, hidden_one, first_gain_full
    )
    back_attend = back_one.astype(jnp.bfloat16)
    output_back = jnp.dot(context.T, back_attend, preferred_element_type=jnp.float32)
    output_bias_back = jnp.sum(back_attend.astype(jnp.float32), axis=0)
    back_context = jnp.dot(back_attend, output_full.T, preferred_element_type=jnp.float32).astype(
        jnp.bfloat16
    )
    back_queries, back_keys, back_values = attention_back(
        query_heads, key_heads, value_heads, log_totals, back_context, sequences, head_count
    )
    back_mixed = jnp.concatenate(
        (from_heads(back_queries), from_heads(back_keys), from_heads(back_values)), axis=1
    )
    input_back = jnp.dot(tokens.T, back_mixed, preferred_element_type=jnp.float32)
    query_bias_back = jnp.sum(back_mixed[:, :model_width].astype(jnp.float32), axis=0)
    value_bias_back = jnp.sum(back_mixed[:, 2 * model_width :].astype(jnp.float32), axis=0)
    tokens_back = (
        back_one + jnp.dot(back_mixed, input_full.T, preferred_element_type=jnp.float32)
    ).astype(jnp.bfloat16)
    owned = (
        lax.psum_scatter(input_back, ("dp", "fsdp"), scatter_dimension=0, tiled=True),
        lax.psum_scatter(query_bias_back, ("dp", "fsdp"), scatter_dimension=0, tiled=True),
        lax.psum_scatter(value_bias_back, ("dp", "fsdp"), scatter_dimension=0, tiled=True),
        lax.psum_scatter(output_back, ("dp", "fsdp"), scatter_dimension=0, tiled=True),
        lax.psum_scatter(output_bias_back, ("dp", "fsdp"), scatter_dimension=0, tiled=True),
        lax.psum_scatter(first_gain_back, ("dp", "fsdp"), scatter_dimension=0, tiled=True),
        lax.psum_scatter(first_shift_back, ("dp", "fsdp"), scatter_dimension=0, tiled=True),
        lax.psum_scatter(up_back, ("dp", "fsdp"), scatter_dimension=0, tiled=True),
        lax.psum_scatter(up_bias_back, ("dp", "fsdp"), scatter_dimension=0, tiled=True),
        lax.psum_scatter(down_back, ("dp", "fsdp"), scatter_dimension=0, tiled=True),
        lax.psum_scatter(down_bias_back, ("dp", "fsdp"), scatter_dimension=0, tiled=True),
        lax.psum_scatter(second_gain_back, ("dp", "fsdp"), scatter_dimension=0, tiled=True),
        lax.psum_scatter(second_shift_back, ("dp", "fsdp"), scatter_dimension=0, tiled=True),
        lax.psum_scatter(retriever_back, ("dp", "fsdp"), scatter_dimension=0, tiled=True),
        lax.psum_scatter(table_term, ("dp", "fsdp"), scatter_dimension=0, tiled=True),
    )
    table_gradient = owned[14]
    return (
        final_out,
        scores,
        tokens_back,
        owned[0],
        owned[1],
        owned[2],
        owned[3],
        owned[4],
        owned[5],
        owned[6],
        owned[7],
        owned[8],
        owned[9],
        owned[10],
        owned[11],
        owned[12],
        owned[13],
        table_gradient,
    )


def solution(mesh):
    in_specs = (
        P(("dp", "fsdp"), None),
        P(("dp", "fsdp"), None),
        P(("dp", "fsdp")),
        P(("dp", "fsdp")),
        P(("dp", "fsdp"), None),
        P(("dp", "fsdp")),
        P(("dp", "fsdp")),
        P(("dp", "fsdp")),
        P(("dp", "fsdp"), None),
        P(("dp", "fsdp")),
        P(("dp", "fsdp"), None),
        P(("dp", "fsdp")),
        P(("dp", "fsdp")),
        P(("dp", "fsdp")),
        P(("dp", "fsdp"), None),
        P(("dp", "fsdp"), None),
        P(("dp", "fsdp")),
        P(("dp", "fsdp"), None),
        P(("dp", "fsdp")),
    )
    out_specs = (
        P(("dp", "fsdp"), None),
        P(("dp", "fsdp")),
        P(("dp", "fsdp"), None),
        P(("dp", "fsdp"), None),
        P(("dp", "fsdp")),
        P(("dp", "fsdp")),
        P(("dp", "fsdp"), None),
        P(("dp", "fsdp")),
        P(("dp", "fsdp")),
        P(("dp", "fsdp")),
        P(("dp", "fsdp"), None),
        P(("dp", "fsdp")),
        P(("dp", "fsdp"), None),
        P(("dp", "fsdp")),
        P(("dp", "fsdp")),
        P(("dp", "fsdp")),
        P(("dp", "fsdp"), None),
        P(("dp", "fsdp"), None),
    )
    return jax.shard_map(local, mesh=mesh, in_specs=in_specs, out_specs=out_specs, check_vma=False)
```

profile of v0, /device:TPU:0, one launch (start us, length us, event | category | flops | bytes accessed | tf_op | source)
XLA Modules:
  0.0 1211.5 jit_solution(10632448965899696666)
XLA Ops:
  22.9 43.0 %all-reduce.20 = (bf16[3072]{0:T(1024)(128)(2,1)}, bf16[768]{0:T(1024)(128)(2,1)}, bf16[768]{0:T(1024)(128)(2,1)}, bf16[768]{0:T(1024)(128)(2,1)}, bf16[768]{0:T...) all-reduce(bf16[3072]{0:T(1024)(128)(2,1)S(1)} %dynamic-update-slic, ...), channel_id=1, replica_groups=mesh['dp'=4,'fsdp'=8] {'dp','fsdp'}, use_global_device_ids=true, to_apply=%add.5 | all-reduce | flops 9216 | bytes 36864
  75.6 44.5 %all_gather.71 = bf16[768,128]{1,0:T(8,128)(2,1)} all-gather(bf16[24,128]{1,0:T(8,128)(2,1)} %param.41), channel_id=1, replica_groups=mesh['dp'=4,'fsdp'=8] {'dp','fsdp'}, dimensions={0}, use_global_device_ids=true | all-gather | bytes 202752 | tf_op jit(solution)/shard_map/all_gather | solution.py:199
  126.6 5.7 all-gather.6.cloned.1.call-done
  132.3 6.9 fusion.205
  145.2 4.6 reshape.219
  151.7 3.9 copy.85
  155.6 4.6 reshape.221
  162.1 2.7 copy.84
  164.9 3.2 reshape.220
  172.0 51.3 %while.37 = (s32[]{:T(128)}, bf16[12,4,288,64]{2,3,1,0:T(8,128)(2,1)}, bf16[12,4,288,64]{2,3,1,0:T(8,128)(2,1)}, bf16[12,4,288,64]{2,3,1,0:T(8,128)(2,1)S(1)}, bf16[12,4,288,64]{2,3,1,0:T(8,128)(2,1)}, /*index=5*/s32[]{:T(128)}) while((s32[]{:T(128)}, bf16[12,4,288,64]{2,3,1,0:T(8,128)(2,1)}, bf16[12,4,288,64]{2,3,1,0:T(8,128)(2,1)}, ...), condition=%wide.region_3.4_spmd, body=%wide.region_0.3_spmd.sunk | while | flops 129726144 | bytes 1390149 | solution.py:94
  173.6 2.8 fusion.266
  223.3 4.9 copy.89
  228.3 4.8 convert_element_type.162
  233.1 4.8 fusion.202
  242.6 53.2 %while.38 = (s32[]{:T(128)}, bf16[12,4,288,64]{2,3,1,0:T(8,128)(2,1)}, f32[12,4,288]{2,1,0:T(4,128)}, bf16[12,4,288,64]{2,3,1,0:T(8,128)(2,1)}, bf16[12,4,288,64...) while((s32[]{:T(128)}, bf16[12,4,288,64]{2,3,1,0:T(8,128)(2,1)}, ...), condition=%wide.region_12.13_spmd, body=%wide.region_9.12_spmd.sunk | while | flops 87919488 | bytes 5005389 | solution.py:94
  295.8 5.7 copy.94
  301.5 4.6 convert_element_type.178
  306.2 4.2 fusion.200
  313.7 41.0 %fusion.87.clone.5.clone.4 = bf16[1152,3072]{1,0:T(8,128)(2,1)} fusion(bf16[768,3072]{1,0:T(8,128)(2,1)} %all-gather.10.cloned.1.call-done, f32[3072]{0:T(1024)} %convert_element_type.168, f32[1152,768]{1,0:T(8,128)S(1)} %copy-done.10, f32[768]{0:T(1024)S(1)} %copy-done.37, f32[768]{0:T(1024)S(1)} %copy-done.24, ...), kind=kOutput, calls=%fused_computation.78.clone.clone.clone.clone.clone.clone.clone.clone.clone.1 | convolution fusion | flops 5673811968 | bytes 15363072 | tf_op jit(solution)/shard_map/dot_general | solution.py:99
  354.8 12.0 fusion.203
  366.9 38.7 %multiply_convert_fusion.1 = (bf16[1152,3072]{1,0:T(8,128)(2,1)S(1)}, f32[1152,3072]{1,0:T(8,128)}, f32[1152,3072]{1,0:T(8,128)}) fusion(f32[3072]{0:T(1024)S(1)} %copy-done.32, bf16[768,3072]{1,0:T(8,128)(2,1)S(1)} %copy-done.44, f32[1152,768]{1,0:T(8,128)S(1)} %copy-done.3, f32[1152]{0:T(1024)S(1)} %copy-done.19, f32[1152]{0:T(1024)S(1)} %copy-done.14, ...), kind=kOutput, calls=%fused_computation.82 | convolution fusion | flops 5673811968 | bytes 43674624 | tf_op jit(solution)/shard_map/dot_general | solution.py:99
  405.6 6.4 fusion.201
  415.8 4.2 convert_reduce_fusion.3
  420.0 21.1 %convert_reduce_fusion = (f32[3072]{0:T(1024)}, bf16[1152,3072]{1,0:T(8,128)(2,1)}) fusion(f32[1152,3072]{1,0:T(8,128)} %get-tuple-element.310, f32[1152,3072]{1,0:T(8,128)} %get-tuple-element.320, bf16[3072,768]{1,0:T(8,128)(2,1)} %all-gather.12.cloned.1.call-done, f32[1152,768]{1,0:T(8,128)} %get-tuple-element.306), kind=kOutput, calls=%fused_computation.80 | convolution fusion | flops 5493322752 | bytes 43659264 | tf_op jit(solution)/shard_map/dot_general | solution.py:271
  441.2 14.3 %multiply_reduce_fusion.3 = (f32[768]{0:T(1024)}, f32[1152]{0:T(1024)S(1)}, f32[1152]{0:T(1024)S(1)}, f32[768]{0:T(1024)}, f32[1152,768]{1,0:T(8,128)}) fusion(f32[1152,768]{1,0:T(8,128)S(1)} %copy-done.3, f32[1152]{0:T(1024)S(1)} %copy-done.19, f32[1152]{0:T(1024)S(1)} %copy-done.14, f32[768]{0:T(1024)} %convert_element_type.164, ...), kind=kOutput, calls=%fused_computation.166 | convolution fusion | flops 5444661248 | bytes 22440960 | tf_op jit(solution)/shard_map/dot_general | solution.py:276
  459.2 4.0 convert_reduce_fusion.4
  465.0 3.1 fusion.157
  468.2 5.2 convolution_convert_fusion.1
  473.3 3.9 copy.98
  477.2 5.6 reshape.227
  484.5 5.8 fusion.150
  490.4 121.2 %while.39 = (s32[]{:T(128)}, bf16[12,4,288,64]{2,3,1,0:T(8,128)(2,1)}, bf16[12,4,288,64]{2,3,1,0:T(8,128)(2,1)}, bf16[12,4,288,64]{2,3,1,0:T(8,128)(2,1)}, bf16[...) while((s32[]{:T(128)}, ...), condition=%wide.region_23.24_spmd, body=%wide.region_21.23_spmd.sunk | while | flops 215358336 | bytes 12143213 | solution.py:155
  611.6 4.9 copy.103
  616.5 4.6 reshape.228
  621.2 4.9 copy.104
  626.1 4.7 reshape.229
  630.7 4.9 copy.105
  635.7 4.7 reshape.230
  645.5 6.9 convolution_bitcast_fusion.2
  652.3 8.1 copy.113
  660.5 11.9 fusion.160
  672.5 12.2 %fusion.204 = f32[768,3072]{1,0:T(8,128)} fusion(bf16[1152,3072]{1,0:T(8,128)(2,1)} %get-tuple-element.331, f32[1152,768]{1,0:T(8,128)S(1)} %copy-done.3, f32[1152]{0:T(1024)S(1)} %copy-done.19, f32[1152]{0:T(1024)S(1)} %copy-done.14, f32[768]{0:T(1024)} %convert_element_type.165, f32[768]{0:T(1024)} %convert_element_type.164), kind=kOutput, calls=%fused_computation.263 | convolution fusion | flops 5440241664 | bytes 20069376 | tf_op jit(solution)/shard_map/dot_general | solution.py:274
  689.1 40.0 %all-reduce.19 = (f32[768]{0:T(1024)S(1)}, f32[768]{0:T(1024)S(1)}, f32[768]{0:T(1024)S(1)}, f32[768]{0:T(1024)S(1)}, f32[768]{0:T(1024)S(1)}, /*index=5*/f32[30...) all-reduce(f32[768]{0:T(1024)S(1)} %reduce_sum.251, ...), channel_id=3, replica_groups=mesh['dp'=4,'fsdp'=8] {'dp','fsdp'}, use_global_device_ids=true, to_apply=%region_26.27.clone | all-reduce | flops 9216 | bytes 73728
  734.4 10.1 fusion.139
  744.5 55.5 %reduce-scatter.17.cloned.1.call-done = f32[256,128]{1,0:T(8,128)} async-done(((f32[8192,128]{1,0:T(8,128)}), f32[256,128]{1,0:T(8,128)}) %reduce-scatter.17.cloned.1.call-update) | async-done | bytes 131088 | tf_op jit(solution)/shard_map/reduce_scatter | solution.py:313
  800.1 121.3 %reduce-scatter.19.cloned.1.call-done = f32[24,2304]{1,0:T(8,128)} async-done(((f32[768,2304]{1,0:T(8,128)}), f32[24,2304]{1,0:T(8,128)}) %reduce-scatter.19.cloned.1.call-update) | async-done | bytes 221200
  921.3 142.2 %reduce-scatter.15.cloned.1.call-done = f32[96,768]{1,0:T(8,128)} async-done(((f32[3072,768]{1,0:T(8,128)}), f32[96,768]{1,0:T(8,128)}) %reduce-scatter.15.cloned.1.call-update) | async-done | bytes 294928 | tf_op jit(solution)/shard_map/reduce_scatter | solution.py:308
  1063.5 141.2 %reduce-scatter.13.cloned.1.call-done = f32[24,3072]{1,0:T(8,128)} async-done(((f32[768,3072]{1,0:T(8,128)}), f32[24,3072]{1,0:T(8,128)}) %reduce-scatter.13.cloned.1.call-update) | async-done | bytes 294928 | tf_op jit(solution)/shard_map/reduce_scatter | solution.py:306
  (382 shorter events, 301.5 us)
Async XLA Ops:
  7.2 6.7 copy-start.46
  7.2 6.9 copy-start.47
  7.2 7.1 copy-start.48
  7.2 114.1 %all-gather.14.cloned.1.call-start = ((), (), s32[]{:S(2)}) async-start(), calls=%async_computation.10 | async-start | bytes 2162688 | tf_op jit(solution)/shard_map/all_gather | solution.py:200
  8.0 124.3 %all-gather.6.cloned.1.call-start = ((), (), s32[]{:S(2)}) async-start(), calls=%async_computation.6 | async-start | bytes 3649536 | tf_op jit(solution)/shard_map/all_gather | solution.py:186
  8.7 224.4 %all-gather.8.cloned.1.call-start = ((), (), s32[]{:S(2)}) async-start(), calls=%async_computation.7 | async-start | bytes 1216512 | tf_op jit(solution)/shard_map/all_gather | solution.py:189
  9.4 304.0 %all-gather.10.cloned.1.call-start = ((), (), s32[]{:S(2)}) async-start(), calls=%async_computation.8 | async-start | bytes 4866048 | tf_op jit(solution)/shard_map/all_gather | solution.py:193
  10.0 344.7 %all-gather.12.cloned.1.call-start = ((), (), s32[]{:S(2)}) async-start(), calls=%async_computation.9 | async-start | bytes 4866048 | tf_op jit(solution)/shard_map/all_gather | solution.py:195
  10.6 733.9 %reduce-scatter.21.cloned.1.call-start = ((), (), s32[]{:S(2)}) async-start(), calls=%async_computation.16 | async-start | bytes 405504
  14.3 6.9 copy-start.34
  14.6 6.6 copy-start.35
  15.4 4.4 copy-start.36
  75.6 63.6 %copy-start.15 = (f32[768]{0:T(1024)}, f32[768]{0:T(1024)S(1)}, u32[]{:S(2)}) copy-start(f32[768]{0:T(1024)S(1)} %convert_element_type.171) | copy-start | bytes 9220
  124.7 14.5 %copy-start = (f32[4,288,768]{2,1,0:T(8,128)}, f32[4,288,768]{2,1,0:T(8,128)S(1)}, u32[]{:S(2)}) copy-start(f32[4,288,768]{2,1,0:T(8,128)S(1)} %scatter-add.4) | copy-start | bytes 10616836
  223.3 9.8 copy-start.40
  237.9 75.5 %copy-start.20 = (f32[1152]{0:T(1024)}, f32[1152]{0:T(1024)S(1)}, u32[]{:S(2)}) copy-start(f32[1152]{0:T(1024)S(1)} %broadcast_multiply_fusion.6) | copy-start | bytes 13828
  295.8 10.4 copy-start.4
  310.4 3.3 copy-start.10
  310.4 3.3 copy-start.24
  310.4 3.3 copy-start.37
  354.7 12.1 copy-start.3
  354.7 12.1 copy-start.14
  354.7 12.1 copy-start.19
  354.8 12.1 copy-start.25
  354.8 12.1 copy-start.32
  354.8 12.1 copy-start.38
  354.8 12.1 copy-start.44
  354.8 50.8 %slice-start = ((s8[4718592]{0:T(1024)(128)(4,1)}), s8[4194304]{0:T(1024)(128)(4,1)S(1)}, s32[]{:S(2)}) async-start(s8[4718592]{0:T(1024)(128)(4,1)} %bitcast.241), calls=%async_computation.17 | async-start | bytes 8388608
  366.8 38.7 %copy-start.39 = (f32[768]{0:T(1024)S(1)}, f32[768]{0:T(1024)}, u32[]{:S(2)}) copy-start(f32[768]{0:T(1024)} %convert_element_type.170) | copy-start | bytes 9220
  366.9 38.7 %slice-start.1 = ((s8[4718592]{0:T(1024)(128)(4,1)}), s8[524288]{0:T(1024)(128)(4,1)S(1)}, s32[]{:S(2)}) async-start(s8[4718592]{0:T(1024)(128)(4,1)} %bitcast.241), calls=%async_computation.18 | async-start | bytes 1048576
  405.6 6.4 copy-start.49
  441.2 16.9 %copy-start.22 = (f32[4,128]{1,0:T(4,128)S(1)}, f32[4,128]{1,0:T(4,128)}, u32[]{:S(2)}) copy-start(f32[4,128]{1,0:T(4,128)} %copy-done.21) | copy-start | bytes 6148
  441.2 16.9 %copy-start.43 = (f32[4]{0:T(128)S(1)}, f32[4]{0:T(128)}, u32[]{:S(2)}) copy-start(f32[4]{0:T(128)} %param.45) | copy-start | bytes 52
  459.1 285.4 %reduce-scatter.11.cloned.1.call-start = ((), (), s32[]{:S(2)}) async-start(), calls=%async_computation.11 | async-start | bytes 2433024 | tf_op jit(solution)/shard_map/reduce_scatter | solution.py:302
  459.2 5.8 copy-start.11
  468.1 332.0 %reduce-scatter.17.cloned.1.call-start = ((), (), s32[]{:S(2)}) async-start(), calls=%async_computation.14 | async-start | bytes 4325376 | tf_op jit(solution)/shard_map/reduce_scatter | solution.py:313
  490.4 431.0 %reduce-scatter.19.cloned.1.call-start = ((), (), s32[]{:S(2)}) async-start(), calls=%async_computation.15 | async-start | bytes 7299072
  640.3 2.5 copy-start.7
  642.3 3.2 copy-start.45
  660.4 403.0 %reduce-scatter.15.cloned.1.call-start = ((), (), s32[]{:S(2)}) async-start(), calls=%async_computation.13 | async-start | bytes 9732096 | tf_op jit(solution)/shard_map/reduce_scatter | solution.py:308
  672.4 532.3 %reduce-scatter.13.cloned.1.call-start = ((), (), s32[]{:S(2)}) async-start(), calls=%async_computation.12 | async-start | bytes 9732096 | tf_op jit(solution)/shard_map/reduce_scatter | solution.py:306
  684.7 4.3 copy-start.23
  684.8 4.3 copy-start.29
  684.8 4.3 copy-start.30
  684.8 4.3 copy-start.31
  684.8 4.3 copy-start.33
  684.8 4.3 copy-start.41
  684.8 4.3 copy-start.42
  (15 other events, 25.8 us)
Sparse Core Ops, SparseCore 0:
  10.9 59.2 all-gather.13
  73.1 59.1 all-gather.5
  135.2 52.7 all-gather.7
  190.8 62.5 all-gather.9
  256.1 62.4 all-gather.11
  459.3 93.0 reduce-scatter.20
  559.1 98.1 reduce-scatter.10
  660.2 139.8 reduce-scatter.16
  806.3 114.9 reduce-scatter.18
  928.6 134.7 reduce-scatter.14
  1070.0 134.6 reduce-scatter.12
where the time goes:
time: 1220 us; the launch traced here: 1210 us
  waiting for transfers between devices  469 us (38%)
  matrix products  401 us (33%)
  local copies, waits for them, and re-layouts  151 us (12%)
  blocking collectives  128 us (10%)
  other arithmetic  47 us (4%)
  between operations  14.9 us (1%)
    reduce_scatter x1, waiting for transfers between devices, local(): lax.psum_scatter(down_back, ('dp', 'fsdp'), scatter_dimension=0, tiled=True)  142 us
    reduce_scatter x1, waiting for transfers between devices, local(): lax.psum_scatter(up_back, ('dp', 'fsdp'), scatter_dimension=0, tiled=True)  141 us
    unnamed x13, waiting for transfers between devices  124 us
    unnamed x2, blocking collectives  83 us
    dot_general x2, matrix products, layer_forward(): jnp.dot(first_out, up_weight, preferred_element_type=jnp.float32) + up_bias  79.7 us
    dot_general x24, matrix products, layer_one_head(): jnp.einsum('gqk,gke->gqe', soft_weights, values_one, preferred_element_ty...  57 us
    reduce_scatter x1, waiting for transfers between devices, local(): lax.psum_scatter(table_term, ('dp', 'fsdp'), scatter_dimension=0, tiled=T...  55.5 us
    all_gather x1, blocking collectives, local(): lax.all_gather(retriever_weight, ('dp', 'fsdp'), axis=0, tiled=True)  44.5 us
  transfers between devices with their start and end apart: 11, of which 5 were waited for; matrix products, arithmetic and copies ran while one was open for 40% of the time, Pallas kernels for 0%

commit v1 on v0

v1 whole, which is shorter than its diff:
```python
import functools
import math
import jax
import jax.numpy as jnp
from jax import lax
from jax.experimental import pallas as pl
from jax.experimental.pallas import tpu as pltpu
from jax.sharding import PartitionSpec as P

HEAD_DIM = 64
EPS = 1e-12
VMEM = 56 * 2**20
bf16, f32 = jnp.bfloat16, jnp.float32
ERFC_P = 0.33
ERFC_Q = (-0.1359291, 0.46268956, -0.35544136, 0.41254396, 0.04500932, 0.20192425, 0.18283717, 0.18636611)


def dot(a, b, ca=1, cb=0):
    return lax.dot_general(a, b, (((ca,), (cb,)), ((), ())), preferred_element_type=f32)


def rows_spec(rows, cols):
    return pl.BlockSpec((rows, cols), lambda i: (i, 0))


def full_spec(shape):
    return pl.BlockSpec(shape, lambda *_: (0,) * len(shape))


def head_mask(rows, cols, h):
    lane = lax.broadcasted_iota(jnp.int32, (rows, cols), 1)
    return (lane >= h * HEAD_DIM) & (lane < (h + 1) * HEAD_DIM)


def run(body, name, grid, ins, in_specs, outs, out_specs, scratch=(), flops=0, moved=0, vmem=VMEM):
    return pl.pallas_call(
        body,
        name=name,
        grid=grid,
        in_specs=in_specs,
        out_specs=out_specs,
        out_shape=outs,
        scratch_shapes=list(scratch),
        cost_estimate=pl.CostEstimate(flops=int(flops), bytes_accessed=int(moved), transcendentals=0),
        compiler_params=pltpu.CompilerParams(vmem_limit_bytes=vmem),
    )(*ins)


def sds(shape, dtype):
    return jax.ShapeDtypeStruct(shape, dtype)


def attend_body(x_ref, w_ref, qb_ref, vb_ref, qkv_ref, soft_ref, ctx_ref):
    length = x_ref.shape[0]
    gc = ctx_ref.shape[1]
    mixed = dot(x_ref[...], w_ref[...])
    q = (mixed[:, :gc] + qb_ref[...]).astype(bf16)
    k = mixed[:, gc : 2 * gc].astype(bf16)
    v = (mixed[:, 2 * gc :] + vb_ref[...]).astype(bf16)
    qkv_ref[:, :gc] = q
    qkv_ref[:, gc : 2 * gc] = k
    qkv_ref[:, 2 * gc :] = v
    qs = q * bf16(HEAD_DIM ** -0.5)
    zero = jnp.zeros((), bf16)
    total = jnp.zeros((length, gc), f32)
    for h in range(gc // HEAD_DIM):
        mask = head_mask(length, gc, h)
        s = dot(jnp.where(mask, qs, zero), k, 1, 1)
        peak = jnp.max(s, axis=-1, keepdims=True)
        e = jnp.exp(s - peak)
        norm = 1.0 / jnp.sum(e, axis=-1, keepdims=True)
        p = (e * norm).astype(bf16)
        soft_ref[h] = p
        total += dot(p, jnp.where(mask, v, zero))
    ctx_ref[...] = total.astype(bf16)


def attend(x, w, qb, vb, seqs):
    T, D = x.shape
    gc = w.shape[1] // 3
    hg = gc // HEAD_DIM
    L = T // seqs
    return run(
        attend_body, "attend", (seqs,), (x, w, qb, vb),
        [rows_spec(L, D), full_spec(w.shape), full_spec(qb.shape), full_spec(vb.shape)],
        [sds((T, 3 * gc), bf16), sds((hg, T, L), bf16), sds((T, gc), bf16)],
        [rows_spec(L, 3 * gc), pl.BlockSpec((hg, L, L), lambda i: (0, i, 0)), rows_spec(L, gc)],
        flops=2 * T * D * 3 * gc + 16 * T * L * gc, moved=2 * (T * D + w.size + 4 * T * gc + hg * T * L),
    )


def erfc_parts(u):
    e = jnp.exp(u * u * -0.5)
    t = 1.0 / (1.0 + (ERFC_P * math.sqrt(0.5)) * jnp.abs(u))
    q = jnp.full_like(t, 0.5 * ERFC_Q[0])
    for c in ERFC_Q[1:]:
        q = q * t + 0.5 * c
    return q * t * e, e


def norm_rows(h):
    mean = jnp.mean(h, axis=-1, keepdims=True)
    c = h - mean
    var = jnp.mean(c * c, axis=-1, keepdims=True)
    inv = lax.rsqrt(var + EPS)
    return c * inv, inv


def norm_rows_back(cot, n, inv, gain):
    scaled = cot * gain
    return inv * (scaled - jnp.mean(scaled, axis=-1, keepdims=True) - n * jnp.mean(scaled * n, axis=-1, keepdims=True))


def up_body(ngroups, step, *refs):
    ctx_refs = refs[:ngroups]
    x_ref, wo_ref, ob_ref, g_ref, s_ref, wu_ref, ub_ref = refs[ngroups : ngroups + 7]
    n_ref, inv_ref, first_ref, act_ref, slope_ref = refs[ngroups + 7 :]
    gc = ctx_refs[0].shape[1]
    hidden = x_ref[...].astype(f32) + ob_ref[...]
    for g, c in enumerate(ctx_refs):
        hidden += dot(c[...], wo_ref[g * gc : (g + 1) * gc, :])
    n, inv = norm_rows(hidden)
    n_ref[...] = n
    inv_ref[...] = inv
    first = (n * g_ref[...] + s_ref[...]).astype(bf16)
    first_ref[...] = first
    ff = wu_ref.shape[1]
    for at in range(0, ff, step):
        cols = slice(at, at + step)
        u = dot(first, wu_ref[:, cols]) + ub_ref[:, cols]
        tail, e = erfc_parts(u)
        phi = jnp.where(u < 0, tail, 1.0 - tail)
        act_ref[:, cols] = (u * phi).astype(bf16)
        slope_ref[:, cols] = (phi + u * e * (1.0 / math.sqrt(2 * math.pi))).astype(bf16)


def up(ctxs, x, wo, ob, g, s, wu, ub, rows, step=512):
    T, D = x.shape
    F = wu.shape[1]
    return run(
        functools.partial(up_body, len(ctxs), step), "up", (T // rows,), (*ctxs, x, wo, ob, g, s, wu, ub),
        [rows_spec(rows, c.shape[1]) for c in ctxs] + [rows_spec(rows, D)] + [full_spec(a.shape) for a in (wo, ob, g, s, wu, ub)],
        [sds((T, D), f32), sds((T, 1), f32), sds((T, D), bf16), sds((T, F), bf16), sds((T, F), bf16)],
        [rows_spec(rows, D), rows_spec(rows, 1), rows_spec(rows, D), rows_spec(rows, F), rows_spec(rows, F)],
        flops=2 * T * D * (D + F), moved=T * D * 10 + 4 * T * F + 2 * (wo.size + wu.size),
    )


def add_rows(ref, value):
    @pl.when(pl.program_id(0) == 0)
    def _():
        ref[...] = jnp.zeros_like(ref)
    ref[...] += jnp.sum(value, axis=0, keepdims=True)


def down_body(step, first_ref, act_ref, slope_ref, w_ref, b_ref, g_ref, s_ref, og_ref, lead_ref,
              out_ref, two_ref, feed_ref, inner_ref, gg_ref, gs_ref, gb_ref, gub_ref):
    rows = first_ref.shape[0]
    hidden = first_ref[...].astype(f32) + b_ref[...] + dot(act_ref[...], w_ref[...])
    n, inv = norm_rows(hidden)
    out_ref[...] = (n * g_ref[...] + s_ref[...]).astype(bf16)
    row = lax.broadcasted_iota(jnp.int32, (rows, 1), 0)
    cot = og_ref[...].astype(f32) + jnp.where(row == 0, lead_ref[0], 0.0)
    add_rows(gg_ref, cot * n)
    add_rows(gs_ref, cot)
    two = norm_rows_back(cot, n, inv, g_ref[...])
    two_ref[...] = two
    feed = two.astype(bf16)
    feed_ref[...] = feed
    add_rows(gb_ref, feed.astype(f32))
    ff = w_ref.shape[0]
    for at in range(0, ff, step):
        cols = slice(at, at + step)
        inner = (dot(feed, w_ref[cols, :], 1, 1) * slope_ref[:, cols].astype(f32)).astype(bf16)
        inner_ref[:, cols] = inner
        @pl.when(pl.program_id(0) == 0)
        def _():
            gub_ref[:, cols] = jnp.zeros((1, step), f32)
        gub_ref[:, cols] += jnp.sum(inner.astype(f32), axis=0, keepdims=True)


def down(first, act, slope, w, b, g, s, og, lead, seqs, step=512):
    T, D = first.shape
    F = act.shape[1]
    L = T // seqs
    return run(
        functools.partial(down_body, step), "down", (seqs,), (first, act, slope, w, b, g, s, og, lead),
        [rows_spec(L, D), rows_spec(L, F), rows_spec(L, F)] + [full_spec((F, D))] + [full_spec(a.shape) for a in (b, g, s)]
        + [rows_spec(L, D), pl.BlockSpec((1, 1, D), lambda i: (i, 0, 0))],
        [sds((T, D), bf16), sds((T, D), f32), sds((T, D), bf16), sds((T, F), bf16),
         sds((1, D), f32), sds((1, D), f32), sds((1, D), f32), sds((1, F), f32)],
        [rows_spec(L, D), rows_spec(L, D), rows_spec(L, D), rows_spec(L, F)] + [full_spec((1, D))] * 3 + [full_spec((1, F))],
        flops=4 * T * D * F, moved=6 * T * F + 12 * T * D + 2 * w.size,
    )


def mid_body(two_ref, inner_ref, wu_ref, n_ref, inv_ref, g_ref, wo_ref,
             one_ref, att_ref, bctx_ref, gg_ref, gs_ref, gob_ref):
    cot = two_ref[...] + dot(inner_ref[...], wu_ref[...], 1, 1)
    n = n_ref[...]
    add_rows(gg_ref, cot * n)
    add_rows(gs_ref, cot)
    one = norm_rows_back(cot, n, inv_ref[...], g_ref[...])
    one_ref[...] = one
    att = one.astype(bf16)
    att_ref[...] = att
    add_rows(gob_ref, att.astype(f32))
    bctx_ref[...] = dot(att, wo_ref[...], 1, 1).astype(bf16)


def mid(two, inner, wu, n, inv, g, wo, rows):
    T, D = two.shape
    F = inner.shape[1]
    return run(
        mid_body, "mid", (T // rows,), (two, inner, wu, n, inv, g, wo),
        [rows_spec(rows, D), rows_spec(rows, F), full_spec(wu.shape), rows_spec(rows, D), rows_spec(rows, 1), full_spec(g.shape), full_spec(wo.shape)],
        [sds((T, D), f32), sds((T, D), bf16), sds((T, D), bf16)] + [sds((1, D), f32)] * 3,
        [rows_spec(rows, D)] * 3 + [full_spec((1, D))] * 3,
        flops=2 * T * D * (F + D), moved=2 * T * F + 16 * T * D + 2 * wu.size,
    )


def attend_back_body(qkv_ref, soft_ref, ctx_ref, bctx_ref, out_ref, gq_ref, gv_ref):
    length, gc = ctx_ref.shape
    q = qkv_ref[:, :gc]
    k = qkv_ref[:, gc : 2 * gc]
    v = qkv_ref[:, 2 * gc :]
    do = bctx_ref[...]
    prod = do.astype(f32) * ctx_ref[...].astype(f32)
    zero = jnp.zeros((), bf16)
    dq = jnp.zeros((length, gc), f32)
    dk = jnp.zeros((length, gc), f32)
    dv = jnp.zeros((length, gc), f32)
    for h in range(gc // HEAD_DIM):
        mask = head_mask(length, gc, h)
        p = soft_ref[h]
        do_h = jnp.where(mask, do, zero)
        dp = dot(do_h, v, 1, 1)
        delta = jnp.sum(jnp.where(mask, prod, 0.0), axis=-1, keepdims=True)
        ds = (p.astype(f32) * (dp - delta)).astype(bf16)
        dv += dot(p, do_h, 0, 0)
        dq += dot(ds, jnp.where(mask, k, zero))
        dk += dot(ds, jnp.where(mask, q, zero), 0, 0)
    scale = HEAD_DIM ** -0.5
    dq = (dq * scale).astype(bf16)
    dv = dv.astype(bf16)
    out_ref[:, :gc] = dq
    out_ref[:, gc : 2 * gc] = (dk * scale).astype(bf16)
    out_ref[:, 2 * gc :] = dv
    add_rows(gq_ref, dq.astype(f32))
    add_rows(gv_ref, dv.astype(f32))


def attend_back(qkv, soft, ctx, bctx, g, seqs):
    T, gc = ctx.shape
    hg = gc // HEAD_DIM
    L = T // seqs
    return run(
        attend_back_body, "attend_back", (seqs,), (qkv, soft, ctx, bctx),
        [rows_spec(L, 3 * gc), pl.BlockSpec((hg, L, L), lambda i: (0, i, 0)), rows_spec(L, gc), pl.BlockSpec((L, gc), lambda i: (i, g))],
        [sds((T, 3 * gc), bf16), sds((1, gc), f32), sds((1, gc), f32)],
        [rows_spec(L, 3 * gc), full_spec((1, gc)), full_spec((1, gc))],
        flops=32 * T * L * gc, moved=2 * (8 * T * gc + hg * T * L),
    )


def tokens_back_body(ngroups, one_ref, *refs):
    total = one_ref[...]
    for g in range(ngroups):
        total += dot(refs[g][...], refs[ngroups + g][...], 1, 1)
    refs[-1][...] = total.astype(bf16)


def tokens_back(one, mixed, ws, rows):
    T, D = one.shape
    n = len(mixed)
    return run(
        functools.partial(tokens_back_body, n), "tokens_back", (T // rows,), (one, *mixed, *ws),
        [rows_spec(rows, D)] + [rows_spec(rows, m.shape[1]) for m in mixed] + [full_spec(w.shape) for w in ws],
        sds((T, D), bf16), rows_spec(rows, D),
        flops=2 * T * D * sum(m.shape[1] for m in mixed), moved=T * D * 12,
    )


def after(x, *deps):
    return lax.optimization_barrier((x,) + deps)[0]


ANY = pl.BlockSpec(memory_space=pl.ANY)
SMEM = pl.BlockSpec(memory_space=pltpu.SMEM)
WHOLE = pl.BlockSpec(memory_space=pltpu.VMEM)
LANES = 128


def plain(body, name, ins, in_specs, outs, out_specs, scratch=(), moved=0, flops=0):
    return pl.pallas_call(
        body, name=name, in_specs=in_specs, out_specs=out_specs, out_shape=outs, scratch_shapes=list(scratch),
        cost_estimate=pl.CostEstimate(flops=int(flops), bytes_accessed=int(moved), transcendentals=0),
        compiler_params=pltpu.CompilerParams(vmem_limit_bytes=VMEM),
    )(*ins)


def cut_points(widths):
    cuts, at = [], 0
    for w in widths:
        cuts.append((at, at + w))
        at += w
    return cuts


def pack_body(D, gc, w_ref, o_ref, r_ref, v_ref, head_ref, rest_ref, held):
    G = D // gc
    rows, nvec = w_ref.shape[0], v_ref.shape[0]
    held[...] = jnp.zeros_like(held)
    held[0:nvec, 0:rows] = v_ref[...].astype(f32)
    turned = held[...].T
    for m in range(3):
        head_ref[:, m * gc : (m + 1) * gc] = w_ref[:, m * D : m * D + gc]
    head_ref[:, 3 * gc :] = turned[:rows, :].astype(bf16)
    at = 0
    for g in range(1, G):
        for m in range(3):
            rest_ref[:, at : at + gc] = w_ref[:, m * D + g * gc : m * D + (g + 1) * gc]
            at += gc
    rest_ref[:, at : at + D] = o_ref[...]
    rest_ref[:, at + D :] = r_ref[...]


def pack(w, o, r, v, gc):
    rows, D = o.shape
    head = 3 * gc + LANES
    rest = 3 * D - 3 * gc + D + r.shape[1]
    return plain(
        functools.partial(pack_body, D, gc), "pack", (w, o, r, v), [WHOLE] * 4,
        [sds((rows, head), bf16), sds((rows, rest), bf16)], [WHOLE] * 2,
        scratch=[pltpu.VMEM((LANES, LANES), f32)], moved=4 * rows * (head + rest),
    )


def stack_body(*refs):
    for k, ref in enumerate(refs[:-1]):
        refs[-1][k] = ref[...]


def stack(blocks):
    n = len(blocks)
    return plain(
        stack_body, "stack", blocks, [WHOLE] * n, sds((n,) + blocks[0].shape, bf16), WHOLE, moved=4 * n * blocks[0].size
    )


def pairs(n, flip):
    return [(i, i ^ flip) for i in range(n)]


def spread_dp(block, Z):
    return stack([block] + [lax.ppermute(block, "dp", pairs(Z, k)) for k in range(1, Z)])


def spread_fsdp(along, N):
    chips = [along] + [lax.ppermute(along, "fsdp", pairs(N, 2 * m)) for m in range(1, N // 2)]
    pieces = []
    for piece in chips:
        pieces += [piece, lax.ppermute(piece, "fsdp", pairs(N, 1))]
    return pieces


def place_body(N, cuts, turned, me_ref, *refs):
    pieces = refs[:N]
    outs = refs[N : N + len(cuts)]
    vec_ref = refs[N + len(cuts)] if turned else None
    held = refs[N + len(cuts) + turned : N + 2 * len(cuts) + turned]
    flat = refs[-3] if turned else None
    in_sem, out_sem = refs[-2:]
    Z = pieces[0].shape[0]
    copies = []
    for j in range(N):
        for k in range(Z):
            for c, (lo, hi) in enumerate(cuts):
                copies.append(
                    pltpu.make_async_copy(
                        pieces[j].at[k, :, lo:hi], held[c].at[me_ref[0] ^ k, me_ref[1] ^ j], in_sem.at[len(copies)]
                    )
                )
    for copy in copies:
        copy.start()
    for copy in copies:
        copy.wait()
    last = [pltpu.make_async_copy(held[c], outs[c], out_sem.at[c]) for c in range(len(cuts))]
    for copy in last:
        copy.start()
    if turned:
        for z in range(Z):
            for f in range(N):
                flat[z, f] = held[-1][z, f].astype(f32)
        vec_ref[...] = flat[...].reshape(vec_ref.shape[1], LANES).T[: vec_ref.shape[0]]
    for copy in last:
        copy.wait()


def place(me, pieces, widths, turned=0):
    N = len(pieces)
    Z, rows, _ = pieces[0].shape
    cuts = cut_points(widths)
    if turned and rows % 8:
        outs = place(me, pieces, widths)
        return outs + [outs[-1][:, :turned].T.astype(f32)]
    shapes = [(Z, N, rows, w) for w in widths]
    outs = plain(
        functools.partial(place_body, N, cuts, 1 if turned else 0), "place", (me, *pieces), [SMEM] + [ANY] * N,
        [sds(s, bf16) for s in shapes] + ([sds((turned, Z * N * rows), f32)] if turned else []),
        [ANY] * len(cuts) + ([WHOLE] if turned else []),
        scratch=[pltpu.VMEM(s, bf16) for s in shapes] + ([pltpu.VMEM(shapes[-1], f32)] if turned else [])
        + [pltpu.SemaphoreType.DMA((Z * N * len(cuts),)), pltpu.SemaphoreType.DMA((len(cuts),))],
        moved=4 * Z * N * rows * cuts[-1][1],
    )
    return [o.reshape(Z * N * rows, o.shape[3]) for o in outs[: len(cuts)]] + list(outs[len(cuts) :])


def grads_body(N, counts, nvec, has_retr, me_ref, *refs):
    at = 0
    outs, held = refs[-1 - N - (nvec > 0) : -1 - (nvec > 0)], refs[-1 - (nvec > 0)]
    Z, _, rows, _ = held.shape
    D = Z * N * rows
    col = 0
    for n in counts:
        y = refs[at + n][...]
        parts = [dot(r[...], y, 0, 0) for r in refs[at : at + n]]
        part = parts[0] if n == 1 else jnp.concatenate(parts, axis=0)
        w = part.shape[1]
        held[:, :, :, col : col + w] = part.reshape(Z, N, rows, w)
        at += n + 1
        col += w
    if has_retr:
        w = refs[at].shape[1]
        held[:, :, :, col : col + w] = refs[at][...].reshape(Z, N, rows, w)
        at += 1
        col += w
    if nvec:
        turn = refs[-1]
        turn[...] = jnp.zeros_like(turn)
        row = 0
        for r in refs[at : at + nvec]:
            turn[row : row + r.shape[0], :] = r[...]
            row += r.shape[0]
        held[:, :, :, col:] = turn[...].T.reshape(Z, N, rows, LANES)
    for j in range(N):
        for z in range(Z):
            outs[j][z] = held[z, me_ref[1] ^ j].astype(bf16)


def grads(me, Z, N, name, products, retr=None, vectors=(), tile=None):
    counts = [len(xs) for xs, _ in products]
    D = sum(x.shape[1] for x in products[0][0])
    rows = D // (Z * N)
    width = sum(y.shape[1] for _, y in products) + (0 if retr is None else retr.shape[1]) + (LANES if vectors else 0)
    if rows % 8:
        cols = [jnp.concatenate([dot(x, y, 0, 0) for x in xs], axis=0) for xs, y in products]
        cols += [] if retr is None else [retr]
        if vectors:
            turned = jnp.concatenate(vectors, axis=0).T
            cols += [turned, jnp.zeros((D, LANES - turned.shape[1]), f32)]
        whole = jnp.concatenate(cols, axis=1).astype(bf16).reshape(Z, N, rows, width)
        return [lax.dynamic_index_in_dim(whole, me[1] ^ j, 1, keepdims=False) for j in range(N)]
    ins = [a for xs, y in products for a in (*xs, y)] + ([] if retr is None else [retr]) + list(vectors)
    T = products[0][1].shape[0]
    if tile is None:
        tile, specs, grid = width, [full_spec(a.shape) for a in ins], (1,)
    else:
        specs, grid = [full_spec(ins[0].shape), pl.BlockSpec((T, tile), lambda i: (0, i))], (width // tile,)
    return run(
        functools.partial(grads_body, N, counts, len(vectors), retr is not None), name, grid, (me, *ins), [SMEM] + specs,
        [sds((Z, rows, width), bf16)] * N, [pl.BlockSpec((Z, rows, tile), lambda i: (0, 0, i))] * N,
        scratch=[pltpu.VMEM((Z, N, rows, tile), f32)] + ([pltpu.VMEM((LANES, D), f32)] if vectors else []),
        flops=2 * T * D * width, moved=2 * T * (D + width) + 2 * D * width,
    )


def grad_rows_body(x_ref, y_ref, o_ref):
    o_ref[...] = dot(x_ref[...], y_ref[...], 0, 0).astype(bf16)


def grad_rows(x, y, name, tile):
    T, M = x.shape
    D = y.shape[1]
    return run(
        grad_rows_body, name, (M // tile,), (x, y), [pl.BlockSpec((T, tile), lambda i: (0, i)), full_spec(y.shape)],
        sds((M, D), bf16), rows_spec(tile, D), flops=2 * T * M * D, moved=2 * (T * M + T * D + M * D),
    )


def pair_body(R, *refs):
    for m in range(R):
        refs[2 * R + m][...] = (refs[m][...].astype(f32) + refs[R + m][...].astype(f32)).astype(bf16)


def pair_sum(parts, Z, N):
    R = N // 2
    _, rows, width = parts[0].shape
    ins = [parts[2 * m] for m in range(R)]
    ins += [lax.ppermute(parts[2 * m + 1], "fsdp", pairs(N, 1)) for m in range(R)]
    block = pl.BlockSpec((1, rows, width), lambda i: (i, 0, 0))
    return run(
        functools.partial(pair_body, R), "pair_sum", (Z,), ins, [block] * (2 * R),
        [sds((Z, rows, width), bf16)] * R, [block] * R, moved=6 * R * Z * rows * width,
    )


def chips_body(n, me_ref, *refs):
    ins, outs = refs[:n], refs[n:]
    for k in range(len(outs)):
        z = me_ref[0] ^ k
        total = ins[0][z].astype(f32)
        for r in ins[1:]:
            total += r[z].astype(f32)
        outs[k][...] = total.astype(outs[k].dtype)


def chips_sum(me, sums, Z, N):
    R = N // 2
    _, rows, width = sums[0].shape
    got = [lax.ppermute(sums[m], "fsdp", pairs(N, 2 * m)) for m in range(1, R)]
    return plain(
        functools.partial(chips_body, R), "chips_sum", (me, sums[0], *got), [SMEM] + [WHOLE] * R,
        [sds((rows, width), f32)] + [sds((rows, width), bf16)] * (Z - 1), [WHOLE] * Z,
        moved=2 * (R + 1) * Z * rows * width,
    )


def last_body(n, cuts, turned, *refs):
    ins, outs = refs[:n], refs[n : n + len(cuts)]
    for c, (out, (lo, hi)) in enumerate(zip(outs, cuts)):
        total = ins[0][:, lo:hi].astype(f32)
        for r in ins[1:]:
            total += r[:, lo:hi].astype(f32)
        if turned and c == len(cuts) - 1:
            turn = refs[-1]
            rows = total.shape[0]
            turn[...] = jnp.zeros_like(turn)
            turn[0:rows, :] = total
            out[...] = turn[...].T[: out.shape[0], : out.shape[1]]
        else:
            out[...] = total


def last_sum(outs, Z, widths, turned=0):
    rows = outs[0].shape[0]
    got = [lax.ppermute(outs[k], "dp", pairs(Z, k)) for k in range(1, Z)]
    cuts = cut_points(widths)
    shapes = [(rows, w) for w in widths]
    if turned:
        shapes[-1] = (turned, rows)
    return plain(
        functools.partial(last_body, Z, cuts, turned), "last_sum", (outs[0], *got), [WHOLE] * Z,
        [sds(s, f32) for s in shapes], [WHOLE] * len(cuts), moved=2 * (Z + 2) * rows * cuts[-1][1],
        scratch=[pltpu.VMEM((LANES, LANES), f32)] if turned else [],
    )


def local(
    Z, N, tokens, input_weight, query_bias, value_bias, output_weight, output_bias, first_gain, first_shift,
    up_weight, up_bias, down_weight, down_bias, second_gain, second_shift, retriever_weight, document_table,
    document_index, output_grad, score_grad,
):
    both = ("dp", "fsdp")
    T, D = tokens.shape
    rows = input_weight.shape[0]
    F = up_weight.shape[1]
    Rw = retriever_weight.shape[1]
    seqs = document_index.shape[0]
    L = T // seqs
    gc = 4 * HEAD_DIM
    G = D // gc
    Q = F // D
    me = jnp.stack([lax.axis_index("dp"), lax.axis_index("fsdp")]).astype(jnp.int32)

    trows, drows = document_table.shape[0], down_weight.shape[0]
    folds = -(-trows // drows)
    folded = jnp.pad(document_table, ((0, folds * drows - trows), (0, 0)))
    wd = lax.all_gather(
        jnp.concatenate([down_weight] + [folded[i * drows : (i + 1) * drows] for i in range(folds)], axis=1),
        both, axis=0, tiled=True,
    )

    vectors = jnp.concatenate(
        [query_bias, value_bias, output_bias, first_gain, first_shift, down_bias, second_gain, second_shift, up_bias]
    ).reshape(8 + Q, rows)
    head, rest = pack(input_weight, output_weight, retriever_weight, vectors, gc)
    head = spread_dp(head, Z)
    rest = spread_dp(after(rest, head), Z)
    wu = spread_dp(after(up_weight, rest), Z)
    head = spread_fsdp(head, N)
    rest = spread_fsdp(after(rest, *head), N)
    wu = spread_fsdp(after(wu, *rest), N)
    win = [None] * G
    win[0], _, vec = place(me, head, [3 * gc, LANES], turned=16)
    vec, tok = lax.optimization_barrier((vec, tokens))
    qb, vb, ob, fg, fs, db, sg, ss = (vec[i : i + 1] for i in range(8))
    ub = vec[8 : 8 + Q].reshape(Q, Z * N, rows).transpose(1, 0, 2).reshape(1, F)

    qkv, soft, ctx = [None] * G, [None] * G, [None] * G

    def attend_group(g):
        cols = slice(g * gc, (g + 1) * gc)
        qkv[g], soft[g], ctx[g] = attend(tokens, win[g], qb[:, cols], vb[:, cols], seqs)

    attend_group(0)
    rest = [after(p, ctx[0]) for p in rest]
    *win[1:], wo, wr = place(me, rest, [3 * gc] * (G - 1) + [D, Rw])
    for g in range(1, G):
        attend_group(g)
    (wu,) = place(me, [after(p, ctx[G - 1]) for p in wu], [F])
    n, inv, first, act, slope = up(ctx, tokens, wo, ob, fg, fs, wu, ub, L)

    owner, within = document_index // trows, document_index % trows
    at_row, at_col = owner * drows + within % drows, D + Rw * (within // drows)
    chosen = jnp.concatenate([lax.dynamic_slice(wd, (at_row[s], at_col[s]), (1, Rw)) for s in range(seqs)], axis=0)
    back_projected = (score_grad[:, None] * chosen.astype(f32)).astype(bf16)
    lead = dot(back_projected, wr, 1, 1)
    final, two, feed, inner, gsg, gss, gdb, gub = down(
        first, act, slope, wd, db, sg, ss, output_grad, lead.reshape(seqs, 1, D), seqs
    )
    leading = final.reshape(seqs, L, D)[:, 0]
    projected = dot(leading, wr).astype(bf16).astype(f32)
    scores = jnp.sum(projected * chosen.astype(f32), axis=-1)
    retriever_back = dot(leading, back_projected, 0, 0)

    term = jnp.concatenate(
        [score_grad[:, None] * projected, jnp.broadcast_to(document_index[:, None].astype(f32), (seqs, LANES))], axis=1
    )
    term = jnp.pad(term, ((0, 32 - seqs), (0, 0)))
    term = lax.all_gather(term, both, axis=0, tiled=True).reshape(Z * N, 32, -1)[:, :seqs].reshape(Z * N * seqs, -1)
    ids = term[:, Rw].astype(jnp.int32) - (me[0] * N + me[1]) * trows
    picker = (jnp.arange(trows, dtype=jnp.int32)[:, None] == ids[None, :]).astype(f32)
    table_back = jnp.dot(picker, term[:, :Rw], precision=lax.Precision.HIGHEST)

    down_back = grad_rows(act, feed, "down_grad", D)
    inner, down_back = lax.optimization_barrier((inner, down_back))
    down_back = lax.psum_scatter(down_back, both, scatter_dimension=0, tiled=True).astype(f32)
    up_parts = grads(me, Z, N, "up_grad", [([first], inner)], tile=D)
    two, *up_parts = lax.optimization_barrier((two, *up_parts))
    one, att, bctx, gfg, gfs, gob = mid(two, inner, wu, n, inv, fg, wo, L)
    up_sums = pair_sum(up_parts, Z, N)
    mixed, gq, gv = [None] * G, [None] * G, [None] * G
    for g in range(G - 1):
        mixed[g], gq[g], gv[g] = attend_back(qkv[g], soft[g], ctx[g], bctx, g, seqs)
    gub = gub.reshape(Z * N, Q, rows).transpose(1, 0, 2).reshape(Q, D)
    parts = grads(
        me, Z, N, "mix_grad", [(ctx, att)] + [([tokens], mixed[g]) for g in range(G - 1)],
        retr=retriever_back, vectors=[gob, gfg, gfs, gdb, gsg, gss, gub],
    )
    bctx, *parts = lax.optimization_barrier((bctx, *parts))
    up_sums = chips_sum(me, up_sums, Z, N)
    mix_sums = pair_sum(parts, Z, N)
    g = G - 1
    mixed[g], gq[g], gv[g] = attend_back(qkv[g], soft[g], ctx[g], bctx, g, seqs)
    parts = grads(
        me, Z, N, "in_grad", [([tokens], mixed[g])],
        vectors=[jnp.concatenate(gq, axis=1), jnp.concatenate(gv, axis=1)],
    )
    one, *parts = lax.optimization_barrier((one, *parts))
    in_sums = pair_sum(parts, Z, N)
    back_tokens = tokens_back(one, mixed, win, L)
    (up_back,) = last_sum(up_sums, Z, [F])
    mix_sums = chips_sum(me, mix_sums, Z, N)
    in_sums = chips_sum(me, in_sums, Z, N)
    output_back, *pieces, retriever_back, small_one = last_sum(mix_sums, Z, [D] + [3 * gc] * (G - 1) + [Rw, LANES], turned=16)
    last, small_two = last_sum(in_sums, Z, [3 * gc, LANES], turned=8)
    pieces += [last]
    input_back = jnp.concatenate([p[:, m * gc : (m + 1) * gc] for m in range(3) for p in pieces], axis=1)
    ob_back, fg_back, fs_back, db_back, sg_back, ss_back = (small_one[i] for i in range(6))
    ub_back = small_one[6 : 6 + Q].reshape(-1)
    return (
        final, scores, back_tokens, input_back, small_two[0], small_two[1], output_back, ob_back, fg_back, fs_back,
        up_back, ub_back, down_back, db_back, sg_back, ss_back, retriever_back, table_back,
    )


def solution(mesh):
    both = ("dp", "fsdp")
    mat, vec = P(both, None), P(both)
    in_specs = (mat, mat, vec, vec, mat, vec, vec, vec, mat, vec, mat, vec, vec, vec, mat, mat, vec, mat, vec)
    out_specs = (mat, vec, mat, mat, vec, vec, mat, vec, vec, vec, mat, vec, mat, vec, vec, vec, mat, mat)
    body = functools.partial(local, mesh.shape["dp"], mesh.shape["fsdp"])
    return jax.shard_map(body, mesh=mesh, in_specs=in_specs, out_specs=out_specs, check_vma=False)
```

time: 1220 us -> 479 us (0.39)
  matrix products: 401 us -> 2.85 us
  waiting for transfers between devices: 469 us -> 107 us
  Pallas kernels: 0 us -> 226 us
  blocking collectives: 128 us -> 0 us
  local copies, waits for them, and re-layouts: 151 us -> 39 us
  starting transfers between devices: 0.44 us -> 60.8 us
  other arithmetic: 47 us -> 7.78 us
  between operations: 14.9 us -> 30.2 us
    dot_general x116 -> x4, matrix products: 381 us -> 2.85 us  [the longest x3 1.98 us: dot(): lax.dot_general(a, b, (((ca,), (cb,)), ((), ())), preferred_element_type=...]
    reduce_scatter x4 -> x1, waiting for transfers between devices: 339 us -> 0.01 us  [local(): lax.psum_scatter(down_back, both, scatter_dimension=0, tiled=True)]
    pallas_call x0 -> x30, Pallas kernels: none -> 226 us  [the longest x17 191 us: run(): pl.pallas_call(body, name=name, grid=grid, in_specs=in_specs, out_specs=o...]
    unnamed x13 -> x3, waiting for transfers between devices: 124 us -> 0.05 us
    ppermute x0 -> x60, waiting for transfers between devices: none -> 107 us  [the longest x9 31.9 us: chips_sum(): got = [lax.ppermute(sums[m], 'fsdp', pairs(N, 2 * m)) for m in range(1, R)]]
    unnamed x2 -> x0, blocking collectives: 83 us -> none
    ppermute x0 -> x60, starting transfers between devices: none -> 60.7 us  [the longest x9 18.9 us: last_sum(): got = [lax.ppermute(outs[k], 'dp', pairs(Z, k)) for k in range(1, Z)]]
    all_gather x1 -> x0, blocking collectives: 44.5 us -> none  [local(): lax.all_gather(retriever_weight, ('dp', 'fsdp'), axis=0, tiled=True)]
  transfers between devices with their start and end apart: 11 -> 63, of which waited for: 5 -> 21; matrix products, arithmetic and copies ran while one was open for 40% -> 6% of each run, Pallas kernels for 0% -> 41%
where the time goes in v1:
time: 479 us; the launch traced here: 473 us
  Pallas kernels  226 us (47%)
  waiting for transfers between devices  107 us (22%)
  starting transfers between devices  60.8 us (13%)
  local copies, waits for them, and re-layouts  39 us (8%)
  between operations  30.2 us (6%)
  other arithmetic  7.78 us (2%)
    pallas_call x17, Pallas kernels, run(): pl.pallas_call(body, name=name, grid=grid, in_specs=in_specs, out_specs=o...  191 us
    pallas_call x13, Pallas kernels, plain(): pl.pallas_call(body, name=name, in_specs=in_specs, out_specs=out_specs, o...  35 us
    ppermute x9, waiting for transfers between devices, chips_sum(): got = [lax.ppermute(sums[m], 'fsdp', pairs(N, 2 * m)) for m in range(1, R)]  31.9 us
    ppermute x9, waiting for transfers between devices, spread_fsdp(): lax.ppermute(along, 'fsdp', pairs(N, 2 * m))  30.5 us
    ppermute x9, waiting for transfers between devices, spread_dp(): lax.ppermute(block, 'dp', pairs(Z, k))  22.5 us
    ppermute x9, waiting for transfers between devices, last_sum(): got = [lax.ppermute(outs[k], 'dp', pairs(Z, k)) for k in range(1, Z)]  21.6 us
    ppermute x9, starting transfers between devices, last_sum(): got = [lax.ppermute(outs[k], 'dp', pairs(Z, k)) for k in range(1, Z)]  18.9 us
    unnamed x146, local copies, waits for them, and re-layouts  16.3 us
  transfers between devices with their start and end apart: 63, of which 21 were waited for; matrix products, arithmetic and copies ran while one was open for 6% of the time, Pallas kernels for 41%

profile of v1, /device:TPU:0, one launch (start us, length us, event | category | flops | bytes accessed | tf_op | source)
XLA Modules:
  0.0 473.3 jit_solution(9358906332023703715)
XLA Ops:
  9.7 6.1 %concatenate.21 = bf16[288]{0:T(512)(128)(2,1)S(1)} concatenate(bf16[24]{0:T(256)(128)(2,1)} %param.21, bf16[24]{0:T(256)(128)(2,1)} %param.22, bf16[24]{0:T(256)(128)(2,1)} %param.24, bf16[24]{0:T(256)(128)(2,1)} %param.25, bf16[24]{0:T(256)(128)(2,1)} %param.26, bf16[24]{0:T(256)(128)(2,1)} %param.30, bf16[24]{0:T(256)(128)(2,1)} %param.31, bf16[24]{0:T(256)(128)(2,1)} %param.32, ...), dimensions={0} | concatenate | bytes 1152 | tf_op jit(solution)/shard_map/concatenate | solution.py:585
  18.1 3.0 collective-permute-start
  21.2 2.6 collective-permute-start.1
  23.8 4.8 %collective-permute-done.1.refs_2_ = bf16[24,896]{1,0:T(8,128)(2,1)S(1)} collective-permute-done((bf16[24,896]{1,0:T(8,128)(2,1)}, bf16[24,896]{1,0:T(8,128)(2,1)S(1)}, u32[]{:S(2)}, u32[]{:S(2)}) %collective-permute-start.1) | collective-permute-done | bytes 43040 | tf_op jit(solution)/shard_map/ppermute | solution.py:357
  36.3 2.5 collective-permute-start.11
  43.4 2.5 collective-permute-start.12
  45.9 7.7 %collective-permute-done.12.refs_3_ = bf16[24,2432]{1,0:T(8,128)(2,1)S(1)} collective-permute-done((bf16[24,2432]{1,0:T(8,128)(2,1)}, bf16[24,2432]{1,0:T(8,128)(2,1)S(1)}, u32[]{:S(2)}, u32[]{:S(2)}) %collective-permute-start.12) | collective-permute-done | bytes 116768 | tf_op jit(solution)/shard_map/ppermute | solution.py:357
  59.7 4.3 collective-permute-start.20
  64.1 6.4 %collective-permute-done.20.refs_1_ = bf16[24,3072]{1,0:T(8,128)(2,1)} collective-permute-done((bf16[24,3072]{1,0:T(8,128)(2,1)}, bf16[24,3072]{1,0:T(8,128)(2,1)}, u32[]{:S(2)}, u32[]{:S(2)}) %collective-permute-start.20) | collective-permute-done | bytes 147488 | tf_op jit(solution)/shard_map/ppermute | solution.py:357
  70.5 2.6 collective-permute-done.14.refs_2_
  74.2 16.8 %collective-permute-done.18.refs_6_ = bf16[4,24,2432]{2,1,0:T(8,128)(2,1)S(1)} collective-permute-done((bf16[4,24,2432]{2,1,0:T(8,128)(2,1)}, bf16[4,24,2432]{2,1,0:T(8,128)(2,1)S(1)}, u32[]{:S(2)}, u32[]{:S(2)}) %collective-permute-start.18) | collective-permute-done | bytes 466976 | tf_op jit(solution)/shard_map/ppermute | solution.py:361
  114.8 4.3 place.3
  120.5 10.3 %attend.3 = (bf16[1152,768]{1,0:T(8,128)(2,1)}, bf16[4,1152,288]{2,1,0:T(8,128)(2,1)}, bf16[1152,256]{1,0:T(8,128)(2,1)}) custom-call(bf16[1152,768]{1,0:T(8,128)(2,1)} %refs_0_.2, bf16[768,768]{1,0:T(8,128)(2,1)} %bitcast.50, f32[1,256]{1,0:T(1,128)} %get-tuple-element.336.qb_ref, f32[1,256]{1,0:T(1,128)} %get-tuple-element.335.vb_ref), custom_call_target="tpu_custom_call" | custom-call | flops 2717908992 | bytes 7962624 | tf_op jit(solution)/shard_map/attend/pallas_call | solution.py:36
  131.4 8.5 %collective-permute-done.26.refs_4_ = bf16[4,24,3072]{2,1,0:T(8,128)(2,1)S(1)} collective-permute-done((bf16[4,24,3072]{2,1,0:T(8,128)(2,1)}, bf16[4,24,3072]{2,1,0:T(8,128)(2,1)S(1)}, u32[]{:S(2)}, u32[]{:S(2)}) %collective-permute-start.26) | collective-permute-done | bytes 589856 | tf_op jit(solution)/shard_map/ppermute | solution.py:361
  144.8 5.9 %place.4 = (bf16[4,8,24,768]{3,2,1,0:T(8,128)(2,1)}, bf16[4,8,24,768]{3,2,1,0:T(8,128)(2,1)}, bf16[4,8,24,768]{3,2,1,0:T(8,128)(2,1)}, bf16[4,8,24,128]{3,2,1,0:T(8,128)(2,1)}) custom-call(s32[2]{0:T(128)} %pad_add_fusion.me_ref, bf16[4,24,2432]{2,1,0:T(8,128)(2,1)} %stack.16.refs_0_, bf16[4,24,2432]{2,1,0:T(8,128)(2,1)} %copy-done.23, ...), custom_call_target="tpu_custom_call" | custom-call | bytes 7471104 | tf_op jit(solution)/shard_map/place/pallas_call | solution.py:296
  150.7 10.1 %attend.5 = (bf16[1152,768]{1,0:T(8,128)(2,1)}, bf16[4,1152,288]{2,1,0:T(8,128)(2,1)}, bf16[1152,256]{1,0:T(8,128)(2,1)}) custom-call(bf16[1152,768]{1,0:T(8,128)(2,1)} %refs_0_.2, bf16[768,768]{1,0:T(8,128)(2,1)} %bitcast.54, f32[1,256]{1,0:T(1,128)} %get-tuple-element.332.qb_ref, f32[1,256]{1,0:T(1,128)} %get-tuple-element.331.vb_ref), custom_call_target="tpu_custom_call" | custom-call | flops 2717908992 | bytes 7962624 | tf_op jit(solution)/shard_map/attend/pallas_call | solution.py:36
  160.9 10.1 %attend.4 = (bf16[1152,768]{1,0:T(8,128)(2,1)}, bf16[4,1152,288]{2,1,0:T(8,128)(2,1)}, bf16[1152,256]{1,0:T(8,128)(2,1)}) custom-call(bf16[1152,768]{1,0:T(8,128)(2,1)} %refs_0_.2, bf16[768,768]{1,0:T(8,128)(2,1)} %bitcast.52, f32[1,256]{1,0:T(1,128)} %get-tuple-element.334.qb_ref, f32[1,256]{1,0:T(1,128)} %get-tuple-element.333.vb_ref), custom_call_target="tpu_custom_call" | custom-call | flops 2717908992 | bytes 7962624 | tf_op jit(solution)/shard_map/attend/pallas_call | solution.py:36
  172.1 5.5 %place.5 = bf16[4,8,24,3072]{3,2,1,0:T(8,128)(2,1)} custom-call(s32[2]{0:T(128)} %pad_add_fusion.me_ref, bf16[4,24,3072]{2,1,0:T(8,128)(2,1)} %stack.17.refs_0_, bf16[4,24,3072]{2,1,0:T(8,128)(2,1)} %copy-done.7, bf16[4,24,3072]{2,1,0:T(8,128)(2,1)} %copy-done.5, bf16[4,24,3072]{2,1,0:T(8,128)(2,1)} %collective-permute-done.25.refs_3_, ...), custom_call_target="tpu_custom_call" | custom-call | bytes 9437184 | tf_op jit(solution)/shard_map/place/pallas_call | solution.py:296
  177.6 27.8 %up.1 = (f32[1152,768]{1,0:T(8,128)}, f32[1152,1]{1,0:T(8,128)}, bf16[1152,768]{1,0:T(8,128)(2,1)}, bf16[1152,3072]{1,0:T(8,128)(2,1)}, bf16[1152,3072]{1,0:T(8,128)(2,1)}) custom-call(bf16[1152,256]{1,0:T(8,128)(2,1)} %get-tuple-element.172.refs_0_.ctx_ref, bf16[1152,256]{1,0:T(8,128)(2,1)} %get-tuple-element.185.refs_1_.ctx_ref, ...), custom_call_target="tpu_custom_call" | custom-call | flops 6794772480 | bytes 28901376 | tf_op jit(solution)/shard_map/up/pallas_call | solution.py:36
  207.0 30.0 %down.1 = (bf16[1152,768]{1,0:T(8,128)(2,1)}, f32[1152,768]{1,0:T(8,128)}, bf16[1152,768]{1,0:T(8,128)(2,1)}, bf16[1152,3072]{1,0:T(8,128)(2,1)}, f32[1,768]{1,0...) custom-call(bf16[1152,768]{1,0:T(8,128)(2,1)} %get-tuple-element.199.first_ref.refs_0_, ...), custom_call_target="tpu_custom_call" | custom-call | flops 10871635968 | bytes 38928384 | tf_op jit(solution)/shard_map/down/pallas_call | solution.py:36
  239.4 10.3 %down_grad.1 = bf16[3072,768]{1,0:T(8,128)(2,1)} custom-call(bf16[1152,3072]{1,0:T(8,128)(2,1)} %get-tuple-element.200.act_ref.x_ref, bf16[1152,768]{1,0:T(8,128)(2,1)} %get-tuple-element.206.y_ref), custom_call_target="tpu_custom_call" | custom-call | flops 5435817984 | bytes 13565952 | tf_op jit(solution)/shard_map/down_grad/pallas_call | solution.py:36
  249.7 10.6 %up_grad.1 = (bf16[4,24,3072]{2,1,0:T(8,128)(2,1)}, bf16[4,24,3072]{2,1,0:T(8,128)(2,1)}, bf16[4,24,3072]{2,1,0:T(8,128)(2,1)}, bf16[4,24,3072]{2,1,0:T(8,128)(2...) custom-call(s32[2]{0:T(128)} %pad_add_fusion.me_ref, ...), custom_call_target="tpu_custom_call" | custom-call | flops 5435817984 | bytes 13565952 | tf_op jit(solution)/shard_map/up_grad/pallas_call | solution.py:36
  263.3 18.6 %mid.1 = (f32[1152,768]{1,0:T(8,128)}, bf16[1152,768]{1,0:T(8,128)(2,1)}, bf16[1152,768]{1,0:T(8,128)(2,1)}, f32[1,768]{1,0:T(1,128)}, f32[1,768]{1,0:T(1,128)}, /*index=5*/f32[1,768]{1,0:T(1,128)}) custom-call(f32[1152,768]{1,0:T(8,128)} %get-tuple-element.216.two_ref, bf16[1152,3072]{1,0:T(8,128)(2,1)} %get-tuple-element.207.refs_1_.inner_ref, ...), custom_call_target="tpu_custom_call" | custom-call | flops 6794772480 | bytes 25952256 | tf_op jit(solution)/shard_map/mid/pallas_call | solution.py:36
  281.9 8.6 %attend_back.4 = (bf16[1152,768]{1,0:T(8,128)(2,1)}, f32[1,256]{1,0:T(1,128)}, f32[1,256]{1,0:T(1,128)}) custom-call(bf16[1152,768]{1,0:T(8,128)(2,1)} %get-tuple-element.227.qkv_ref, bf16[4,1152,288]{2,1,0:T(8,128)(2,1)} %get-tuple-element.228.soft_ref, bf16[1152,256]{1,0:T(8,128)(2,1)} %get-tuple-element.185.refs_1_.ctx_ref, ...), custom_call_target="tpu_custom_call" | custom-call | flops 2717908992 | bytes 7372800 | tf_op jit(solution)/shard_map/attend_back/pallas_call | solution.py:36
  290.6 8.8 %attend_back.3 = (bf16[1152,768]{1,0:T(8,128)(2,1)}, f32[1,256]{1,0:T(1,128)}, f32[1,256]{1,0:T(1,128)}) custom-call(bf16[1152,768]{1,0:T(8,128)(2,1)} %get-tuple-element.224.qkv_ref, bf16[4,1152,288]{2,1,0:T(8,128)(2,1)} %get-tuple-element.225.soft_ref, bf16[1152,256]{1,0:T(8,128)(2,1)} %get-tuple-element.172.refs_0_.ctx_ref, ...), custom_call_target="tpu_custom_call" | custom-call | flops 2717908992 | bytes 7372800 | tf_op jit(solution)/shard_map/attend_back/pallas_call | solution.py:36
  299.3 11.1 %mix_grad.1 = (bf16[4,24,2560]{2,1,0:T(8,128)(2,1)}, bf16[4,24,2560]{2,1,0:T(8,128)(2,1)}, bf16[4,24,2560]{2,1,0:T(8,128)(2,1)}, bf16[4,24,2560]{2,1,0:T(8,128)(...) custom-call(s32[2]{0:T(128)} %pad_add_fusion.me_ref, ...), custom_call_target="tpu_custom_call" | custom-call | flops 4529848320 | bytes 11599872 | tf_op jit(solution)/shard_map/mix_grad/pallas_call | solution.py:36
  311.5 8.7 %attend_back.5 = (bf16[1152,768]{1,0:T(8,128)(2,1)}, f32[1,256]{1,0:T(1,128)}, f32[1,256]{1,0:T(1,128)}) custom-call(bf16[1152,768]{1,0:T(8,128)(2,1)} %get-tuple-element.220.qkv_ref, bf16[4,1152,288]{2,1,0:T(8,128)(2,1)} %get-tuple-element.221.soft_ref, bf16[1152,256]{1,0:T(8,128)(2,1)} %get-tuple-element.187.refs_2_.ctx_ref, ...), custom_call_target="tpu_custom_call" | custom-call | flops 2717908992 | bytes 7372800 | tf_op jit(solution)/shard_map/attend_back/pallas_call | solution.py:36
  322.7 5.0 %in_grad.1 = (bf16[4,24,896]{2,1,0:T(8,128)(2,1)}, bf16[4,24,896]{2,1,0:T(8,128)(2,1)}, bf16[4,24,896]{2,1,0:T(8,128)(2,1)}, bf16[4,24,896]{2,1,0:T(8,128)(2,1)}...) custom-call(s32[2]{0:T(128)} %pad_add_fusion.me_ref, ...), custom_call_target="tpu_custom_call" | custom-call | flops 1585446912 | bytes 5210112 | tf_op jit(solution)/shard_map/in_grad/pallas_call | solution.py:36
  329.9 4.2 pair_sum.3
  337.6 3.3 pair_sum.4
  344.4 9.4 %collective-permute-done.44.refs_1_ = bf16[4,24,896]{2,1,0:T(8,128)(2,1)S(1)} collective-permute-done((bf16[4,24,896]{2,1,0:T(8,128)(2,1)}, bf16[4,24,896]{2,1,0:T(8,128)(2,1)S(1)}, u32[]{:S(2)}, u32[]{:S(2)}) %collective-permute-start.44) | collective-permute-done | bytes 172064 | tf_op jit(solution)/shard_map/ppermute | solution.py:522
  353.7 2.4 collective-permute-done.45.refs_2_
  356.2 4.2 collective-permute-done.46.refs_3_
  362.9 8.1 %collective-permute-start.47 = (bf16[24,896]{1,0:T(8,128)(2,1)}, bf16[24,896]{1,0:T(8,128)(2,1)S(1)}, u32[]{:S(2)}, u32[]{:S(2)}) collective-permute-start(bf16[24,896]{1,0:T(8,128)(2,1)} %get-tuple-element.293), channel_id=1, source_target_pairs={{0,8},{8,0},{16,24},{24,16},{1,9},{9,1},{17,25},{25,17},{2,10},{10... | collective-permute-start | bytes 129032 | tf_op jit(solution)/shard_map/ppermute | solution.py:548
  371.5 5.1 %collective-permute-done.47.refs_1_ = bf16[24,896]{1,0:T(8,128)(2,1)S(1)} collective-permute-done((bf16[24,896]{1,0:T(8,128)(2,1)}, bf16[24,896]{1,0:T(8,128)(2,1)S(1)}, u32[]{:S(2)}, u32[]{:S(2)}) %collective-permute-start.47) | collective-permute-done | bytes 43040 | tf_op jit(solution)/shard_map/ppermute | solution.py:548
  376.5 5.1 %collective-permute-done.48.refs_2_ = bf16[24,896]{1,0:T(8,128)(2,1)S(1)} collective-permute-done((bf16[24,896]{1,0:T(8,128)(2,1)}, bf16[24,896]{1,0:T(8,128)(2,1)S(1)}, u32[]{:S(2)}, u32[]{:S(2)}) %collective-permute-start.48) | collective-permute-done | bytes 43040 | tf_op jit(solution)/shard_map/ppermute | solution.py:548
  381.7 2.1 collective-permute-start.49
  383.8 4.6 collective-permute-done.49.refs_3_
  390.4 9.1 %tokens_back.1 = bf16[1152,768]{1,0:T(8,128)(2,1)} custom-call(f32[1152,768]{1,0:T(8,128)} %get-tuple-element.261.one_ref, bf16[1152,768]{1,0:T(8,128)(2,1)} %get-tuple-element.226.refs_5_.refs_0_, bf16[1152,768]{1,0:T(8,128)(2,1)} %get-tuple-element.229.refs_7_.refs_1_, bf16[1152,768]{1,0:T(8,128)(2,1)} %get-tuple-element.246.refs_1_.refs_2_, ...), custom_call_target="tpu_custom_call" | custom-call | flops 4076863488 | bytes 10616832 | tf_op jit(solution)/shard_map/tokens_back/pallas_call | solution.py:36
  401.9 2.4 chips_sum.3
  404.3 2.7 collective-permute-start.38
  411.6 4.5 pair_sum.5
  428.0 4.7 collective-permute-done.54.refs_1_
  432.7 11.3 %collective-permute-done.55.refs_2_ = bf16[4,24,3072]{2,1,0:T(8,128)(2,1)S(1)} collective-permute-done((bf16[4,24,3072]{2,1,0:T(8,128)(2,1)}, bf16[4,24,3072]{2,1,0:T(8,128)(2,1)S(1)}, u32[]{:S(2)}, u32[]{:S(2)}) %collective-permute-start.55) | collective-permute-done | bytes 589856 | tf_op jit(solution)/shard_map/ppermute | solution.py:522
  445.1 2.6 chips_sum.5
  447.7 2.7 collective-permute-start.58
  453.5 2.1 collective-permute-done.57.refs_1_
  455.6 4.8 %collective-permute-done.58.refs_2_ = bf16[24,3072]{1,0:T(8,128)(2,1)S(1)} collective-permute-done((bf16[24,3072]{1,0:T(8,128)(2,1)}, bf16[24,3072]{1,0:T(8,128)(2,1)S(1)}, u32[]{:S(2)}, u32[]{:S(2)}) %collective-permute-start.58) | collective-permute-done | bytes 147488 | tf_op jit(solution)/shard_map/ppermute | solution.py:548
  (295 shorter events, 94.5 us)
Async XLA Ops:
  7.2 198.2 %all-gather.3.cloned.1.call-start = ((), (), s32[]{:S(2)}) async-start(), calls=%async_computation.1 | async-start | bytes 7299072 | tf_op jit(solution)/shard_map/all_gather | solution.py:580
  9.7 453.3 %all-gather.5.cloned.1.call-start = ((), (), s32[]{:S(2)}) async-start(), calls=%async_computation.3 | async-start | bytes 1081344 | tf_op jit(solution)/shard_map/all_gather | solution.py:632
  40.7 15.5 %collective-permute-start.3 = (bf16[4,24,896]{2,1,0:T(8,128)(2,1)}, bf16[4,24,896]{2,1,0:T(8,128)(2,1)S(1)}, u32[]{:S(2)}, u32[]{:S(2)}) collective-permute-start(bf16[4,24,896]{2,1,0:T(8,128)(2,1)} %stack.15.refs_0_), channel_id=1, source_target_pairs={{0,1},{1,0},{2,3},{3,2},{4,5},{5,4},{6,7},{7,6},{8,9},{9,8},{10,11... | collective-permute-start | bytes 516104 | tf_op jit(solution)/shard_map/ppermute | solution.py:364
  40.7 15.4 %collective-permute-start.5 = (bf16[4,24,896]{2,1,0:T(8,128)(2,1)S(1)}, bf16[4,24,896]{2,1,0:T(8,128)(2,1)S(1)}, u32[]{:S(2)}, u32[]{:S(2)}) collective-permute-start(bf16[4,24,896]{2,1,0:T(8,128)(2,1)S(1)} %collective-permute-done.4.refs_2_), channel_id=1, source_target_pairs={{0,1},{1,0},{2,3},{3,2},{4,5},{5,4},{6,7},{7,6},{8,9},{9,8},{10,11... | collective-permute-start | bytes 516104 | tf_op jit(solution)/shard_map/ppermute | solution.py:364
  42.7 13.5 %collective-permute-start.7 = (bf16[4,24,896]{2,1,0:T(8,128)(2,1)S(1)}, bf16[4,24,896]{2,1,0:T(8,128)(2,1)S(1)}, u32[]{:S(2)}, u32[]{:S(2)}) collective-permute-start(bf16[4,24,896]{2,1,0:T(8,128)(2,1)S(1)} %collective-permute-done.6.refs_4_), channel_id=1, source_target_pairs={{0,1},{1,0},{2,3},{3,2},{4,5},{5,4},{6,7},{7,6},{8,9},{9,8},{10,11... | collective-permute-start | bytes 516104 | tf_op jit(solution)/shard_map/ppermute | solution.py:364
  42.7 13.5 %collective-permute-start.9 = (bf16[4,24,896]{2,1,0:T(8,128)(2,1)S(1)}, bf16[4,24,896]{2,1,0:T(8,128)(2,1)S(1)}, u32[]{:S(2)}, u32[]{:S(2)}) collective-permute-start(bf16[4,24,896]{2,1,0:T(8,128)(2,1)S(1)} %collective-permute-done.8.refs_6_), channel_id=1, source_target_pairs={{0,1},{1,0},{2,3},{3,2},{4,5},{5,4},{6,7},{7,6},{8,9},{9,8},{10,11... | collective-permute-start | bytes 516104 | tf_op jit(solution)/shard_map/ppermute | solution.py:364
  43.4 10.1 %collective-permute-start.12 = (bf16[24,2432]{1,0:T(8,128)(2,1)}, bf16[24,2432]{1,0:T(8,128)(2,1)S(1)}, u32[]{:S(2)}, u32[]{:S(2)}) collective-permute-start(bf16[24,2432]{1,0:T(8,128)(2,1)} %get-tuple-element.174.refs_0_), channel_id=1, source_target_pairs={{0,24},{8,16},{16,8},{24,0},{1,25},{9,17},{17,9},{25,1},{2,26},{10... | collective-permute-start | bytes 350216 | tf_op jit(solution)/shard_map/ppermute | solution.py:357
  56.2 17.0 %collective-permute-start.14 = (bf16[4,24,2432]{2,1,0:T(8,128)(2,1)}, bf16[4,24,2432]{2,1,0:T(8,128)(2,1)S(1)}, u32[]{:S(2)}, u32[]{:S(2)}) collective-permute-start(bf16[4,24,2432]{2,1,0:T(8,128)(2,1)} %stack.16.refs_0_), channel_id=1, source_target_pairs={{0,2},{1,3},{2,0},{3,1},{4,6},{5,7},{6,4},{7,5},{8,10},{9,11},{10,... | collective-permute-start | bytes 1400840 | tf_op jit(solution)/shard_map/ppermute | solution.py:361
  57.4 16.8 %collective-permute-start.16 = (bf16[4,24,2432]{2,1,0:T(8,128)(2,1)}, bf16[4,24,2432]{2,1,0:T(8,128)(2,1)S(1)}, u32[]{:S(2)}, u32[]{:S(2)}) collective-permute-start(bf16[4,24,2432]{2,1,0:T(8,128)(2,1)} %stack.16.refs_0_), channel_id=1, source_target_pairs={{0,4},{1,5},{2,6},{3,7},{4,0},{5,1},{6,2},{7,3},{8,12},{9,13},{10,... | collective-permute-start | bytes 1400840 | tf_op jit(solution)/shard_map/ppermute | solution.py:361
  59.0 32.0 %collective-permute-start.18 = (bf16[4,24,2432]{2,1,0:T(8,128)(2,1)}, bf16[4,24,2432]{2,1,0:T(8,128)(2,1)S(1)}, u32[]{:S(2)}, u32[]{:S(2)}) collective-permute-start(bf16[4,24,2432]{2,1,0:T(8,128)(2,1)} %stack.16.refs_0_), channel_id=1, source_target_pairs={{0,6},{1,7},{2,4},{3,5},{4,2},{5,3},{6,0},{7,1},{8,14},{9,15},{10,... | collective-permute-start | bytes 1400840 | tf_op jit(solution)/shard_map/ppermute | solution.py:361
  59.7 10.8 %collective-permute-start.20 = (bf16[24,3072]{1,0:T(8,128)(2,1)}, bf16[24,3072]{1,0:T(8,128)(2,1)}, u32[]{:S(2)}, u32[]{:S(2)}) collective-permute-start(bf16[24,3072]{1,0:T(8,128)(2,1)} %refs_0_.1), channel_id=1, source_target_pairs={{0,8},{8,0},{16,24},{24,16},{1,9},{9,1},{17,25},{25,17},{2,10},{10... | collective-permute-start | bytes 442376 | tf_op jit(solution)/shard_map/ppermute | solution.py:357
  64.1 26.9 %collective-permute-start.21 = (bf16[24,3072]{1,0:T(8,128)(2,1)}, bf16[24,3072]{1,0:T(8,128)(2,1)S(1)}, u32[]{:S(2)}, u32[]{:S(2)}) collective-permute-start(bf16[24,3072]{1,0:T(8,128)(2,1)} %refs_0_.1), channel_id=1, source_target_pairs={{0,16},{8,24},{16,0},{24,8},{1,17},{9,25},{17,1},{25,9},{2,18},{10... | collective-permute-start | bytes 442376 | tf_op jit(solution)/shard_map/ppermute | solution.py:357
  70.5 39.4 %collective-permute-start.13 = (bf16[4,24,2432]{2,1,0:T(8,128)(2,1)}, bf16[4,24,2432]{2,1,0:T(8,128)(2,1)S(1)}, u32[]{:S(2)}, u32[]{:S(2)}) collective-permute-start(bf16[4,24,2432]{2,1,0:T(8,128)(2,1)} %stack.16.refs_0_), channel_id=1, source_target_pairs={{0,1},{1,0},{2,3},{3,2},{4,5},{5,4},{6,7},{7,6},{8,9},{9,8},{10,11... | collective-permute-start | bytes 1400840 | tf_op jit(solution)/shard_map/ppermute | solution.py:364
  73.2 36.8 %collective-permute-start.15 = (bf16[4,24,2432]{2,1,0:T(8,128)(2,1)S(1)}, bf16[4,24,2432]{2,1,0:T(8,128)(2,1)S(1)}, u32[]{:S(2)}, u32[]{:S(2)}) collective-permute-start(bf16[4,24,2432]{2,1,0:T(8,128)(2,1)S(1)} %collective-permute-done.14.refs_2_), channel_id=1, source_target_pairs={{0,1},{1,0},{2,3},{3,2},{4,5},{5,4},{6,7},{7,6},{8,9},{9,8},{10,11... | collective-permute-start | bytes 1400840 | tf_op jit(solution)/shard_map/ppermute | solution.py:364
  74.2 35.8 %collective-permute-start.17 = (bf16[4,24,2432]{2,1,0:T(8,128)(2,1)S(1)}, bf16[4,24,2432]{2,1,0:T(8,128)(2,1)S(1)}, u32[]{:S(2)}, u32[]{:S(2)}) collective-permute-start(bf16[4,24,2432]{2,1,0:T(8,128)(2,1)S(1)} %collective-permute-done.16.refs_4_), channel_id=1, source_target_pairs={{0,1},{1,0},{2,3},{3,2},{4,5},{5,4},{6,7},{7,6},{8,9},{9,8},{10,11... | collective-permute-start | bytes 1400840 | tf_op jit(solution)/shard_map/ppermute | solution.py:364
  91.0 19.0 %collective-permute-start.19 = (bf16[4,24,2432]{2,1,0:T(8,128)(2,1)S(1)}, bf16[4,24,2432]{2,1,0:T(8,128)(2,1)S(1)}, u32[]{:S(2)}, u32[]{:S(2)}) collective-permute-start(bf16[4,24,2432]{2,1,0:T(8,128)(2,1)S(1)} %collective-permute-done.18.refs_6_), channel_id=1, source_target_pairs={{0,1},{1,0},{2,3},{3,2},{4,5},{5,4},{6,7},{7,6},{8,9},{9,8},{10,11... | collective-permute-start | bytes 1400840 | tf_op jit(solution)/shard_map/ppermute | solution.py:364
  91.0 16.9 %collective-permute-start.22 = (bf16[24,3072]{1,0:T(8,128)(2,1)}, bf16[24,3072]{1,0:T(8,128)(2,1)}, u32[]{:S(2)}, u32[]{:S(2)}) collective-permute-start(bf16[24,3072]{1,0:T(8,128)(2,1)} %refs_0_.1), channel_id=1, source_target_pairs={{0,24},{8,16},{16,8},{24,0},{1,25},{9,17},{17,9},{25,1},{2,26},{10... | collective-permute-start | bytes 442376 | tf_op jit(solution)/shard_map/ppermute | solution.py:357
  110.7 20.1 %collective-permute-start.28 = (bf16[4,24,3072]{2,1,0:T(8,128)(2,1)}, bf16[4,24,3072]{2,1,0:T(8,128)(2,1)S(1)}, u32[]{:S(2)}, u32[]{:S(2)}) collective-permute-start(bf16[4,24,3072]{2,1,0:T(8,128)(2,1)} %stack.17.refs_0_), channel_id=1, source_target_pairs={{0,6},{1,7},{2,4},{3,5},{4,2},{5,3},{6,0},{7,1},{8,14},{9,15},{10,... | collective-permute-start | bytes 1769480 | tf_op jit(solution)/shard_map/ppermute | solution.py:361
  111.6 28.2 %collective-permute-start.26 = (bf16[4,24,3072]{2,1,0:T(8,128)(2,1)}, bf16[4,24,3072]{2,1,0:T(8,128)(2,1)S(1)}, u32[]{:S(2)}, u32[]{:S(2)}) collective-permute-start(bf16[4,24,3072]{2,1,0:T(8,128)(2,1)} %stack.17.refs_0_), channel_id=1, source_target_pairs={{0,4},{1,5},{2,6},{3,7},{4,0},{5,1},{6,2},{7,3},{8,12},{9,13},{10,... | collective-permute-start | bytes 1769480 | tf_op jit(solution)/shard_map/ppermute | solution.py:361
  112.6 27.3 %collective-permute-start.24 = (bf16[4,24,3072]{2,1,0:T(8,128)(2,1)}, bf16[4,24,3072]{2,1,0:T(8,128)(2,1)S(1)}, u32[]{:S(2)}, u32[]{:S(2)}) collective-permute-start(bf16[4,24,3072]{2,1,0:T(8,128)(2,1)} %stack.17.refs_0_), channel_id=1, source_target_pairs={{0,2},{1,3},{2,0},{3,1},{4,6},{5,7},{6,4},{7,5},{8,10},{9,11},{10,... | collective-permute-start | bytes 1769480 | tf_op jit(solution)/shard_map/ppermute | solution.py:361
  130.8 40.2 %collective-permute-start.23 = (bf16[4,24,3072]{2,1,0:T(8,128)(2,1)S(1)}, bf16[4,24,3072]{2,1,0:T(8,128)(2,1)S(1)}, u32[]{:S(2)}, u32[]{:S(2)}) collective-permute-start(bf16[4,24,3072]{2,1,0:T(8,128)(2,1)S(1)} %copy-done), channel_id=1, source_target_pairs={{0,1},{1,0},{2,3},{3,2},{4,5},{5,4},{6,7},{7,6},{8,9},{9,8},{10,11... | collective-permute-start | bytes 1769480 | tf_op jit(solution)/shard_map/ppermute | solution.py:364
  130.9 40.2 %collective-permute-start.29 = (bf16[4,24,3072]{2,1,0:T(8,128)(2,1)S(1)}, bf16[4,24,3072]{2,1,0:T(8,128)(2,1)S(1)}, u32[]{:S(2)}, u32[]{:S(2)}) collective-permute-start(bf16[4,24,3072]{2,1,0:T(8,128)(2,1)S(1)} %collective-permute-done.28.refs_6_), channel_id=1, source_target_pairs={{0,1},{1,0},{2,3},{3,2},{4,5},{5,4},{6,7},{7,6},{8,9},{9,8},{10,11... | collective-permute-start | bytes 1769480 | tf_op jit(solution)/shard_map/ppermute | solution.py:364
  139.9 31.2 %collective-permute-start.27 = (bf16[4,24,3072]{2,1,0:T(8,128)(2,1)S(1)}, bf16[4,24,3072]{2,1,0:T(8,128)(2,1)}, u32[]{:S(2)}, u32[]{:S(2)}) collective-permute-start(bf16[4,24,3072]{2,1,0:T(8,128)(2,1)S(1)} %collective-permute-done.26.refs_4_), channel_id=1, source_target_pairs={{0,1},{1,0},{2,3},{3,2},{4,5},{5,4},{6,7},{7,6},{8,9},{9,8},{10,11... | collective-permute-start | bytes 1769480 | tf_op jit(solution)/shard_map/ppermute | solution.py:364
  139.9 31.2 %collective-permute-start.25 = (bf16[4,24,3072]{2,1,0:T(8,128)(2,1)S(1)}, bf16[4,24,3072]{2,1,0:T(8,128)(2,1)}, u32[]{:S(2)}, u32[]{:S(2)}) collective-permute-start(bf16[4,24,3072]{2,1,0:T(8,128)(2,1)S(1)} %collective-permute-done.24.refs_2_), channel_id=1, source_target_pairs={{0,1},{1,0},{2,3},{3,2},{4,5},{5,4},{6,7},{7,6},{8,9},{9,8},{10,11... | collective-permute-start | bytes 1769480 | tf_op jit(solution)/shard_map/ppermute | solution.py:364
  239.3 225.6 %reduce-scatter.2.cloned.1.call-start = ((), (), s32[]{:S(2)}) async-start(), calls=%async_computation.2 | async-start | bytes 4866048 | tf_op jit(solution)/shard_map/reduce_scatter | solution.py:639
  310.4 17.4 %collective-permute-start.30 = (bf16[4,24,2560]{2,1,0:T(8,128)(2,1)}, bf16[4,24,2560]{2,1,0:T(8,128)(2,1)S(1)}, u32[]{:S(2)}, u32[]{:S(2)}) collective-permute-start(bf16[4,24,2560]{2,1,0:T(8,128)(2,1)} %get-tuple-element.266), channel_id=1, source_target_pairs={{0,1},{1,0},{2,3},{3,2},{4,5},{5,4},{6,7},{7,6},{8,9},{9,8},{10,11... | collective-permute-start | bytes 1474568 | tf_op jit(solution)/shard_map/ppermute | solution.py:501
  310.6 17.5 %collective-permute-start.31 = (bf16[4,24,2560]{2,1,0:T(8,128)(2,1)}, bf16[4,24,2560]{2,1,0:T(8,128)(2,1)S(1)}, u32[]{:S(2)}, u32[]{:S(2)}) collective-permute-start(bf16[4,24,2560]{2,1,0:T(8,128)(2,1)} %get-tuple-element.267), channel_id=1, source_target_pairs={{0,1},{1,0},{2,3},{3,2},{4,5},{5,4},{6,7},{7,6},{8,9},{9,8},{10,11... | collective-permute-start | bytes 1474568 | tf_op jit(solution)/shard_map/ppermute | solution.py:501
  311.0 17.4 %collective-permute-start.32 = (bf16[4,24,2560]{2,1,0:T(8,128)(2,1)}, bf16[4,24,2560]{2,1,0:T(8,128)(2,1)S(1)}, u32[]{:S(2)}, u32[]{:S(2)}) collective-permute-start(bf16[4,24,2560]{2,1,0:T(8,128)(2,1)} %get-tuple-element.268), channel_id=1, source_target_pairs={{0,1},{1,0},{2,3},{3,2},{4,5},{5,4},{6,7},{7,6},{8,9},{9,8},{10,11... | collective-permute-start | bytes 1474568 | tf_op jit(solution)/shard_map/ppermute | solution.py:501
  311.1 17.5 %collective-permute-start.33 = (bf16[4,24,2560]{2,1,0:T(8,128)(2,1)}, bf16[4,24,2560]{2,1,0:T(8,128)(2,1)S(1)}, u32[]{:S(2)}, u32[]{:S(2)}) collective-permute-start(bf16[4,24,2560]{2,1,0:T(8,128)(2,1)} %get-tuple-element.269), channel_id=1, source_target_pairs={{0,1},{1,0},{2,3},{3,2},{4,5},{5,4},{6,7},{7,6},{8,9},{9,8},{10,11... | collective-permute-start | bytes 1474568 | tf_op jit(solution)/shard_map/ppermute | solution.py:501
  334.2 55.6 %collective-permute-start.34 = (bf16[4,24,2560]{2,1,0:T(8,128)(2,1)}, bf16[4,24,2560]{2,1,0:T(8,128)(2,1)S(1)}, u32[]{:S(2)}, u32[]{:S(2)}) collective-permute-start(bf16[4,24,2560]{2,1,0:T(8,128)(2,1)} %get-tuple-element.271), channel_id=1, source_target_pairs={{0,2},{1,3},{2,0},{3,1},{4,6},{5,7},{6,4},{7,5},{8,10},{9,11},{10,... | collective-permute-start | bytes 1474568 | tf_op jit(solution)/shard_map/ppermute | solution.py:522
  334.9 54.9 %collective-permute-start.35 = (bf16[4,24,2560]{2,1,0:T(8,128)(2,1)}, bf16[4,24,2560]{2,1,0:T(8,128)(2,1)S(1)}, u32[]{:S(2)}, u32[]{:S(2)}) collective-permute-start(bf16[4,24,2560]{2,1,0:T(8,128)(2,1)} %get-tuple-element.272), channel_id=1, source_target_pairs={{0,4},{1,5},{2,6},{3,7},{4,0},{5,1},{6,2},{7,3},{8,12},{9,13},{10,... | collective-permute-start | bytes 1474568 | tf_op jit(solution)/shard_map/ppermute | solution.py:522
  340.8 12.9 %collective-permute-start.44 = (bf16[4,24,896]{2,1,0:T(8,128)(2,1)}, bf16[4,24,896]{2,1,0:T(8,128)(2,1)S(1)}, u32[]{:S(2)}, u32[]{:S(2)}) collective-permute-start(bf16[4,24,896]{2,1,0:T(8,128)(2,1)} %get-tuple-element.289), channel_id=1, source_target_pairs={{0,2},{1,3},{2,0},{3,1},{4,6},{5,7},{6,4},{7,5},{8,10},{9,11},{10,... | collective-permute-start | bytes 516104 | tf_op jit(solution)/shard_map/ppermute | solution.py:522
  341.9 14.3 %collective-permute-start.45 = (bf16[4,24,896]{2,1,0:T(8,128)(2,1)}, bf16[4,24,896]{2,1,0:T(8,128)(2,1)S(1)}, u32[]{:S(2)}, u32[]{:S(2)}) collective-permute-start(bf16[4,24,896]{2,1,0:T(8,128)(2,1)} %get-tuple-element.290), channel_id=1, source_target_pairs={{0,4},{1,5},{2,6},{3,7},{4,0},{5,1},{6,2},{7,3},{8,12},{9,13},{10,... | collective-permute-start | bytes 516104 | tf_op jit(solution)/shard_map/ppermute | solution.py:522
  343.0 17.3 %collective-permute-start.46 = (bf16[4,24,896]{2,1,0:T(8,128)(2,1)}, bf16[4,24,896]{2,1,0:T(8,128)(2,1)S(1)}, u32[]{:S(2)}, u32[]{:S(2)}) collective-permute-start(bf16[4,24,896]{2,1,0:T(8,128)(2,1)} %get-tuple-element.291), channel_id=1, source_target_pairs={{0,6},{1,7},{2,4},{3,5},{4,2},{5,3},{6,0},{7,1},{8,14},{9,15},{10,... | collective-permute-start | bytes 516104 | tf_op jit(solution)/shard_map/ppermute | solution.py:522
  362.9 13.6 %collective-permute-start.47 = (bf16[24,896]{1,0:T(8,128)(2,1)}, bf16[24,896]{1,0:T(8,128)(2,1)S(1)}, u32[]{:S(2)}, u32[]{:S(2)}) collective-permute-start(bf16[24,896]{1,0:T(8,128)(2,1)} %get-tuple-element.293), channel_id=1, source_target_pairs={{0,8},{8,0},{16,24},{24,16},{1,9},{9,1},{17,25},{25,17},{2,10},{10... | collective-permute-start | bytes 129032 | tf_op jit(solution)/shard_map/ppermute | solution.py:548
  371.0 33.3 %collective-permute-start.50 = (bf16[4,24,3072]{2,1,0:T(8,128)(2,1)}, bf16[4,24,3072]{2,1,0:T(8,128)(2,1)S(1)}, u32[]{:S(2)}, u32[]{:S(2)}) collective-permute-start(bf16[4,24,3072]{2,1,0:T(8,128)(2,1)} %get-tuple-element.304), channel_id=1, source_target_pairs={{0,1},{1,0},{2,3},{3,2},{4,5},{5,4},{6,7},{7,6},{8,9},{9,8},{10,11... | collective-permute-start | bytes 1769480 | tf_op jit(solution)/shard_map/ppermute | solution.py:501
  371.0 36.0 %collective-permute-start.51 = (bf16[4,24,3072]{2,1,0:T(8,128)(2,1)}, bf16[4,24,3072]{2,1,0:T(8,128)(2,1)S(1)}, u32[]{:S(2)}, u32[]{:S(2)}) collective-permute-start(bf16[4,24,3072]{2,1,0:T(8,128)(2,1)} %get-tuple-element.305), channel_id=1, source_target_pairs={{0,1},{1,0},{2,3},{3,2},{4,5},{5,4},{6,7},{7,6},{8,9},{9,8},{10,11... | collective-permute-start | bytes 1769480 | tf_op jit(solution)/shard_map/ppermute | solution.py:501
  388.4 12.8 %collective-permute-start.36 = (bf16[4,24,2560]{2,1,0:T(8,128)(2,1)}, bf16[4,24,2560]{2,1,0:T(8,128)(2,1)S(1)}, u32[]{:S(2)}, u32[]{:S(2)}) collective-permute-start(bf16[4,24,2560]{2,1,0:T(8,128)(2,1)} %get-tuple-element.273), channel_id=1, source_target_pairs={{0,6},{1,7},{2,4},{3,5},{4,2},{5,3},{6,0},{7,1},{8,14},{9,15},{10,... | collective-permute-start | bytes 1474568 | tf_op jit(solution)/shard_map/ppermute | solution.py:522
  389.8 20.2 %collective-permute-start.52 = (bf16[4,24,3072]{2,1,0:T(8,128)(2,1)}, bf16[4,24,3072]{2,1,0:T(8,128)(2,1)S(1)}, u32[]{:S(2)}, u32[]{:S(2)}) collective-permute-start(bf16[4,24,3072]{2,1,0:T(8,128)(2,1)} %get-tuple-element.306), channel_id=1, source_target_pairs={{0,1},{1,0},{2,3},{3,2},{4,5},{5,4},{6,7},{7,6},{8,9},{9,8},{10,11... | collective-permute-start | bytes 1769480 | tf_op jit(solution)/shard_map/ppermute | solution.py:501
  389.8 20.2 %collective-permute-start.53 = (bf16[4,24,3072]{2,1,0:T(8,128)(2,1)S(1)}, bf16[4,24,3072]{2,1,0:T(8,128)(2,1)S(1)}, u32[]{:S(2)}, u32[]{:S(2)}) collective-permute-start(bf16[4,24,3072]{2,1,0:T(8,128)(2,1)S(1)} %copy-done.67), channel_id=1, source_target_pairs={{0,1},{1,0},{2,3},{3,2},{4,5},{5,4},{6,7},{7,6},{8,9},{9,8},{10,11... | collective-permute-start | bytes 1769480 | tf_op jit(solution)/shard_map/ppermute | solution.py:501
  404.3 13.9 %collective-permute-start.37 = (bf16[24,2560]{1,0:T(8,128)(2,1)}, bf16[24,2560]{1,0:T(8,128)(2,1)S(1)}, u32[]{:S(2)}, u32[]{:S(2)}) collective-permute-start(bf16[24,2560]{1,0:T(8,128)(2,1)} %get-tuple-element.275), channel_id=1, source_target_pairs={{0,8},{8,0},{16,24},{24,16},{1,9},{9,1},{17,25},{25,17},{2,10},{10... | collective-permute-start | bytes 368648 | tf_op jit(solution)/shard_map/ppermute | solution.py:548
  404.3 15.4 %collective-permute-start.38 = (bf16[24,2560]{1,0:T(8,128)(2,1)}, bf16[24,2560]{1,0:T(8,128)(2,1)S(1)}, u32[]{:S(2)}, u32[]{:S(2)}) collective-permute-start(bf16[24,2560]{1,0:T(8,128)(2,1)} %get-tuple-element.276), channel_id=1, source_target_pairs={{0,16},{8,24},{16,0},{24,8},{1,17},{9,25},{17,1},{25,9},{2,18},{10... | collective-permute-start | bytes 368648 | tf_op jit(solution)/shard_map/ppermute | solution.py:548
  407.0 12.7 %collective-permute-start.39 = (bf16[24,2560]{1,0:T(8,128)(2,1)}, bf16[24,2560]{1,0:T(8,128)(2,1)S(1)}, u32[]{:S(2)}, u32[]{:S(2)}) collective-permute-start(bf16[24,2560]{1,0:T(8,128)(2,1)} %get-tuple-element.277), channel_id=1, source_target_pairs={{0,24},{8,16},{16,8},{24,0},{1,25},{9,17},{17,9},{25,1},{2,26},{10... | collective-permute-start | bytes 368648 | tf_op jit(solution)/shard_map/ppermute | solution.py:548
  416.1 16.5 %collective-permute-start.54 = (bf16[4,24,3072]{2,1,0:T(8,128)(2,1)}, bf16[4,24,3072]{2,1,0:T(8,128)(2,1)S(1)}, u32[]{:S(2)}, u32[]{:S(2)}) collective-permute-start(bf16[4,24,3072]{2,1,0:T(8,128)(2,1)} %get-tuple-element.309), channel_id=1, source_target_pairs={{0,2},{1,3},{2,0},{3,1},{4,6},{5,7},{6,4},{7,5},{8,10},{9,11},{10,... | collective-permute-start | bytes 1769480 | tf_op jit(solution)/shard_map/ppermute | solution.py:522
  416.8 27.1 %collective-permute-start.55 = (bf16[4,24,3072]{2,1,0:T(8,128)(2,1)}, bf16[4,24,3072]{2,1,0:T(8,128)(2,1)S(1)}, u32[]{:S(2)}, u32[]{:S(2)}) collective-permute-start(bf16[4,24,3072]{2,1,0:T(8,128)(2,1)} %get-tuple-element.310), channel_id=1, source_target_pairs={{0,4},{1,5},{2,6},{3,7},{4,0},{5,1},{6,2},{7,3},{8,12},{9,13},{10,... | collective-permute-start | bytes 1769480 | tf_op jit(solution)/shard_map/ppermute | solution.py:522
  418.3 25.7 %collective-permute-start.56 = (bf16[4,24,3072]{2,1,0:T(8,128)(2,1)}, bf16[4,24,3072]{2,1,0:T(8,128)(2,1)S(1)}, u32[]{:S(2)}, u32[]{:S(2)}) collective-permute-start(bf16[4,24,3072]{2,1,0:T(8,128)(2,1)} %get-tuple-element.311), channel_id=1, source_target_pairs={{0,6},{1,7},{2,4},{3,5},{4,2},{5,3},{6,0},{7,1},{8,14},{9,15},{10,... | collective-permute-start | bytes 1769480 | tf_op jit(solution)/shard_map/ppermute | solution.py:522
  447.7 12.6 %collective-permute-start.58 = (bf16[24,3072]{1,0:T(8,128)(2,1)}, bf16[24,3072]{1,0:T(8,128)(2,1)S(1)}, u32[]{:S(2)}, u32[]{:S(2)}) collective-permute-start(bf16[24,3072]{1,0:T(8,128)(2,1)} %get-tuple-element.314), channel_id=1, source_target_pairs={{0,16},{8,24},{16,0},{24,8},{1,17},{9,25},{17,1},{25,9},{2,18},{10... | collective-permute-start | bytes 442376 | tf_op jit(solution)/shard_map/ppermute | solution.py:548
  450.4 9.9 %collective-permute-start.59 = (bf16[24,3072]{1,0:T(8,128)(2,1)}, bf16[24,3072]{1,0:T(8,128)(2,1)S(1)}, u32[]{:S(2)}, u32[]{:S(2)}) collective-permute-start(bf16[24,3072]{1,0:T(8,128)(2,1)} %get-tuple-element.315), channel_id=1, source_target_pairs={{0,24},{8,16},{16,8},{24,0},{1,25},{9,17},{17,9},{25,1},{2,26},{10... | collective-permute-start | bytes 442376 | tf_op jit(solution)/shard_map/ppermute | solution.py:548
  (84 other events, 1062.0 us)
Sparse Core Ops, SparseCore 0:
  11.5 98.1 all-gather.2
  239.5 55.1 all-gather.4
  300.2 125.7 reduce-scatter.1

commit v2 on v1

v2 whole, which is shorter than its diff:
```python
import functools
import math
import jax
import jax.numpy as jnp
from jax import lax
from jax.experimental import pallas as pl
from jax.experimental.pallas import tpu as pltpu
from jax.sharding import PartitionSpec as P

HEAD_DIM = 64
EPS = 1e-12
QB, VB, OB, FG, FS, DB, SG, SS, UB = range(9)
bf16, f32 = jnp.bfloat16, jnp.float32
ERFC_P = 0.33
ERFC_Q = (-0.1359291, 0.46268956, -0.35544136, 0.41254396, 0.04500932, 0.20192425, 0.18283717, 0.18636611)


def dot(a, b, ca=1, cb=0):
    return lax.dot_general(a, b, (((ca,), (cb,)), ((), ())), preferred_element_type=f32)


def rows_spec(rows, cols):
    return pl.BlockSpec((rows, cols), lambda i: (i, 0))


def full_spec(shape):
    return pl.BlockSpec(shape, lambda *_: (0,) * len(shape))


def head_mask(rows, cols, h):
    lane = lax.broadcasted_iota(jnp.int32, (rows, cols), 1)
    return (lane >= h * HEAD_DIM) & (lane < (h + 1) * HEAD_DIM)


def run(body, name, grid, ins, in_specs, outs, out_specs, scratch=(), flops=0, moved=0, vmem=60, alias=None):
    return pl.pallas_call(
        body,
        name=name,
        grid=grid,
        in_specs=in_specs,
        out_specs=out_specs,
        out_shape=outs,
        scratch_shapes=list(scratch),
        cost_estimate=estimate(flops, moved),
        input_output_aliases=alias or {},
        compiler_params=pltpu.CompilerParams(vmem_limit_bytes=vmem * 2**20),
    )(*ins)


def estimate(flops, moved):
    return pl.CostEstimate(flops=int(flops), bytes_accessed=int(moved), transcendentals=0)


def sds(shape, dtype):
    return jax.ShapeDtypeStruct(shape, dtype)


def attend_body(x_ref, w_ref, v_ref, qkv_ref, soft_ref, ctx_ref):
    length = x_ref.shape[0]
    gc = ctx_ref.shape[1]
    mixed = dot(x_ref[...], w_ref[...])
    q = (mixed[:, :gc] + v_ref[QB : QB + 1, :]).astype(bf16)
    k = mixed[:, gc : 2 * gc].astype(bf16)
    v = (mixed[:, 2 * gc :] + v_ref[VB : VB + 1, :]).astype(bf16)
    qkv_ref[:, :gc] = q
    qkv_ref[:, gc : 2 * gc] = k
    qkv_ref[:, 2 * gc :] = v
    qs = q * bf16(HEAD_DIM ** -0.5)
    zero = jnp.zeros((), bf16)
    total = jnp.zeros((length, gc), f32)
    for h in range(gc // HEAD_DIM):
        mask = head_mask(length, gc, h)
        s = dot(jnp.where(mask, qs, zero), k, 1, 1)
        peak = jnp.max(s, axis=-1, keepdims=True)
        e = jnp.exp(s - peak)
        norm = 1.0 / jnp.sum(e, axis=-1, keepdims=True)
        p = (e * norm).astype(bf16)
        soft_ref[h] = p
        total += dot(p, jnp.where(mask, v, zero))
    ctx_ref[...] = total.astype(bf16)


def attend(x, w, vec, g, seqs):
    T, D = x.shape
    gc = w.shape[1] // 3
    hg = gc // HEAD_DIM
    L = T // seqs
    return run(
        attend_body, "attend", (seqs,), (x, w, vec),
        [rows_spec(L, D), full_spec(w.shape), pl.BlockSpec((vec.shape[0], gc), lambda i: (0, g))],
        [sds((T, 3 * gc), bf16), sds((hg, T, L), bf16), sds((T, gc), bf16)],
        [rows_spec(L, 3 * gc), pl.BlockSpec((hg, L, L), lambda i: (0, i, 0)), rows_spec(L, gc)],
        flops=2 * T * D * 3 * gc + 16 * T * L * gc, moved=2 * (T * D + w.size + 4 * T * gc + hg * T * L),
    )


def erfc_parts(u):
    e = jnp.exp(u * u * -0.5)
    t = 1.0 / (1.0 + (ERFC_P * math.sqrt(0.5)) * jnp.abs(u))
    q = jnp.full_like(t, 0.5 * ERFC_Q[0])
    for c in ERFC_Q[1:]:
        q = q * t + 0.5 * c
    return q * t * e, e


def norm_rows(h):
    mean = jnp.mean(h, axis=-1, keepdims=True)
    c = h - mean
    var = jnp.mean(c * c, axis=-1, keepdims=True)
    inv = lax.rsqrt(var + EPS)
    return c * inv, inv


def norm_rows_back(cot, n, inv, gain):
    scaled = cot * gain
    return inv * (scaled - jnp.mean(scaled, axis=-1, keepdims=True) - n * jnp.mean(scaled * n, axis=-1, keepdims=True))


def up_body(ngroups, step, *refs):
    ctx_refs = refs[:ngroups]
    x_ref, wo_ref, v_ref, wu_ref, ub_ref = refs[ngroups : ngroups + 5]
    n_ref, inv_ref, first_ref, act_ref, slope_ref = refs[ngroups + 5 :]
    gc = ctx_refs[0].shape[1]
    hidden = x_ref[...].astype(f32) + v_ref[OB : OB + 1, :]
    for g, c in enumerate(ctx_refs):
        hidden += dot(c[...], wo_ref[g * gc : (g + 1) * gc, :])
    n, inv = norm_rows(hidden)
    n_ref[...] = n
    inv_ref[...] = inv
    first = (n * v_ref[FG : FG + 1, :] + v_ref[FS : FS + 1, :]).astype(bf16)
    first_ref[...] = first
    ff = wu_ref.shape[1]
    for at in range(0, ff, step):
        cols = slice(at, at + step)
        u = dot(first, wu_ref[:, cols]) + ub_ref[:, cols]
        tail, e = erfc_parts(u)
        phi = jnp.where(u < 0, tail, 1.0 - tail)
        act_ref[:, cols] = (u * phi).astype(bf16)
        slope_ref[:, cols] = (phi + u * e * (1.0 / math.sqrt(2 * math.pi))).astype(bf16)


def up(ctxs, x, wo, vec, wu, ub, rows, step=512):
    T, D = x.shape
    F = ub.shape[1]
    return run(
        functools.partial(up_body, len(ctxs), step), "up", (T // rows,), (*ctxs, x, wo, vec, wu, ub),
        [rows_spec(rows, c.shape[1]) for c in ctxs] + [rows_spec(rows, D)] + [full_spec(wo.shape), full_spec(vec.shape), full_spec((D, F)), full_spec(ub.shape)],
        [sds((T, D), f32), sds((T, 1), f32), sds((T, D), bf16), sds((T, F), bf16), sds((T, F), bf16)],
        [rows_spec(rows, D), rows_spec(rows, 1), rows_spec(rows, D), rows_spec(rows, F), rows_spec(rows, F)],
        flops=2 * T * D * (D + F), moved=T * D * 10 + 4 * T * F + 2 * (wo.size + wu.size),
    )


def add_rows(ref, value):
    @pl.when(pl.program_id(0) == 0)
    def _():
        ref[...] = jnp.zeros_like(ref)
    ref[...] += jnp.sum(value, axis=0, keepdims=True)


def down_body(step, first_ref, act_ref, slope_ref, w_ref, v_ref, og_ref, lead_ref,
              out_ref, top_ref, two_ref, feed_ref, inner_ref, gg_ref, gs_ref, gb_ref, gub_ref):
    rows = first_ref.shape[0]
    gain = v_ref[SG : SG + 1, :]
    hidden = first_ref[...].astype(f32) + v_ref[DB : DB + 1, :] + dot(act_ref[...], w_ref[...])
    n, inv = norm_rows(hidden)
    out = (n * gain + v_ref[SS : SS + 1, :]).astype(bf16)
    out_ref[...] = out
    top_ref[0] = out[0:16, :].astype(f32)[0:1, :]
    row = lax.broadcasted_iota(jnp.int32, (rows, 1), 0)
    cot = og_ref[...].astype(f32) + jnp.where(row == 0, lead_ref[0], 0.0)
    add_rows(gg_ref, cot * n)
    add_rows(gs_ref, cot)
    two = norm_rows_back(cot, n, inv, gain)
    two_ref[...] = two
    feed = two.astype(bf16)
    feed_ref[...] = feed
    add_rows(gb_ref, feed.astype(f32))
    ff = w_ref.shape[0]
    for at in range(0, ff, step):
        cols = slice(at, at + step)
        inner = (dot(feed, w_ref[cols, :], 1, 1) * slope_ref[:, cols].astype(f32)).astype(bf16)
        inner_ref[:, cols] = inner
        @pl.when(pl.program_id(0) == 0)
        def _():
            gub_ref[:, cols] = jnp.zeros((1, step), f32)
        gub_ref[:, cols] += jnp.sum(inner.astype(f32), axis=0, keepdims=True)


def down(first, act, slope, w, vec, og, lead, seqs, step=512):
    T, D = first.shape
    F = act.shape[1]
    L = T // seqs
    return run(
        functools.partial(down_body, step), "down", (seqs,), (first, act, slope, w, vec, og, lead),
        [rows_spec(L, D), rows_spec(L, F), rows_spec(L, F)] + [full_spec((F, D)), full_spec(vec.shape)]
        + [rows_spec(L, D), pl.BlockSpec((1, 1, D), lambda i: (i, 0, 0))],
        [sds((T, D), bf16), sds((seqs, 1, D), f32), sds((T, D), f32), sds((T, D), bf16), sds((T, F), bf16),
         sds((1, D), f32), sds((1, D), f32), sds((1, D), f32), sds((1, F), f32)],
        [rows_spec(L, D), pl.BlockSpec((1, 1, D), lambda i: (i, 0, 0)), rows_spec(L, D), rows_spec(L, D), rows_spec(L, F)] + [full_spec((1, D))] * 3 + [full_spec((1, F))],
        flops=4 * T * D * F, moved=6 * T * F + 12 * T * D + 2 * w.size,
    )


def mid_body(two_ref, inner_ref, wu_ref, n_ref, inv_ref, v_ref, wo_ref,
             one_ref, att_ref, bctx_ref, gg_ref, gs_ref, gob_ref):
    cot = two_ref[...] + dot(inner_ref[...], wu_ref[...], 1, 1)
    n = n_ref[...]
    add_rows(gg_ref, cot * n)
    add_rows(gs_ref, cot)
    one = norm_rows_back(cot, n, inv_ref[...], v_ref[FG : FG + 1, :])
    one_ref[...] = one
    att = one.astype(bf16)
    att_ref[...] = att
    add_rows(gob_ref, att.astype(f32))
    bctx_ref[...] = dot(att, wo_ref[...], 1, 1).astype(bf16)


def mid(two, inner, wu, n, inv, vec, wo, rows):
    T, D = two.shape
    F = inner.shape[1]
    return run(
        mid_body, "mid", (T // rows,), (two, inner, wu, n, inv, vec, wo),
        [rows_spec(rows, D), rows_spec(rows, F), full_spec((D, F)), rows_spec(rows, D), rows_spec(rows, 1), full_spec(vec.shape), full_spec(wo.shape)],
        [sds((T, D), f32), sds((T, D), bf16), sds((T, D), bf16)] + [sds((1, D), f32)] * 3,
        [rows_spec(rows, D)] * 3 + [full_spec((1, D))] * 3,
        flops=2 * T * D * (F + D), moved=2 * T * F + 16 * T * D + 2 * wu.size,
    )


def attend_back_body(qkv_ref, soft_ref, ctx_ref, bctx_ref, out_ref, gq_ref, gv_ref):
    length, gc = ctx_ref.shape
    q = qkv_ref[:, :gc]
    k = qkv_ref[:, gc : 2 * gc]
    v = qkv_ref[:, 2 * gc :]
    do = bctx_ref[...]
    prod = do.astype(f32) * ctx_ref[...].astype(f32)
    zero = jnp.zeros((), bf16)
    dq = jnp.zeros((length, gc), f32)
    dk = jnp.zeros((length, gc), f32)
    dv = jnp.zeros((length, gc), f32)
    for h in range(gc // HEAD_DIM):
        mask = head_mask(length, gc, h)
        p = soft_ref[h]
        do_h = jnp.where(mask, do, zero)
        dp = dot(do_h, v, 1, 1)
        delta = jnp.sum(jnp.where(mask, prod, 0.0), axis=-1, keepdims=True)
        ds = (p.astype(f32) * (dp - delta)).astype(bf16)
        dv += dot(p, do_h, 0, 0)
        dq += dot(ds, jnp.where(mask, k, zero))
        dk += dot(ds, jnp.where(mask, q, zero), 0, 0)
    scale = HEAD_DIM ** -0.5
    dq = (dq * scale).astype(bf16)
    dv = dv.astype(bf16)
    out_ref[:, :gc] = dq
    out_ref[:, gc : 2 * gc] = (dk * scale).astype(bf16)
    out_ref[:, 2 * gc :] = dv
    add_rows(gq_ref, dq.astype(f32))
    add_rows(gv_ref, dv.astype(f32))


def attend_back(qkv, soft, ctx, bctx, g, seqs):
    T, gc = ctx.shape
    hg = gc // HEAD_DIM
    L = T // seqs
    return run(
        attend_back_body, "attend_back", (seqs,), (qkv, soft, ctx, bctx),
        [rows_spec(L, 3 * gc), pl.BlockSpec((hg, L, L), lambda i: (0, i, 0)), rows_spec(L, gc), pl.BlockSpec((L, gc), lambda i: (i, g))],
        [sds((T, 3 * gc), bf16), sds((1, gc), f32), sds((1, gc), f32)],
        [rows_spec(L, 3 * gc), full_spec((1, gc)), full_spec((1, gc))],
        flops=32 * T * L * gc, moved=2 * (8 * T * gc + hg * T * L),
    )


def tokens_back_body(ngroups, one_ref, *refs):
    total = one_ref[...]
    for g in range(ngroups):
        total += dot(refs[g][...], refs[ngroups + g][...], 1, 1)
    refs[-1][...] = total.astype(bf16)


def tokens_back(one, mixed, ws, rows):
    T, D = one.shape
    n = len(mixed)
    return run(
        functools.partial(tokens_back_body, n), "tokens_back", (T // rows,), (one, *mixed, *ws),
        [rows_spec(rows, D)] + [rows_spec(rows, m.shape[1]) for m in mixed] + [full_spec(w.shape) for w in ws],
        sds((T, D), bf16), rows_spec(rows, D),
        flops=2 * T * D * sum(m.shape[1] for m in mixed), moved=T * D * 12,
    )


def after(x, *deps):
    return lax.optimization_barrier((x,) + deps)[0]


ANY = pl.BlockSpec(memory_space=pl.ANY)
SMEM = pl.BlockSpec(memory_space=pltpu.SMEM)
LANES = 128


def once(body, name, ins, in_specs, outs, scratch=(), moved=0, flops=0, vmem=60):
    specs = [full_spec(a.shape) if spec is None else spec for a, spec in zip(ins, in_specs)]
    return run(body, name, (1,), ins, specs, outs, [full_spec(o.shape) for o in outs], scratch, flops, moved, vmem)


def cut_points(widths):
    cuts, at = [], 0
    for w in widths:
        cuts.append((at, at + w))
        at += w
    return cuts


def pack_body(D, gc, nvec, *refs):
    w_ref, o_ref, r_ref, u_ref, t_ref = refs[:5]
    head_ref, rest_ref, up_ref, held = refs[5 + nvec :]
    G = D // gc
    rows = w_ref.shape[0]
    held[...] = jnp.zeros_like(held)
    row = 0
    for v_ref in refs[5 : 5 + nvec]:
        v = v_ref[...].astype(f32)
        for at in range(0, v.shape[1], rows):
            held[row : row + 1, 0:rows] = v[:, at : at + rows]
            row += 1
    turned = held[...].T
    for m in range(3):
        head_ref[:, m * gc : (m + 1) * gc] = w_ref[:, m * D : m * D + gc]
    head_ref[:, 3 * gc :] = turned[:rows, :].astype(bf16)
    at = 0
    for g in range(1, G):
        for m in range(3):
            rest_ref[:, at : at + gc] = w_ref[:, m * D + g * gc : m * D + (g + 1) * gc]
            at += gc
    rest_ref[:, at : at + D] = o_ref[...]
    rest_ref[:, at + D :] = r_ref[...]
    trows, width = t_ref.shape
    at = u_ref.shape[1]
    up_ref[:, :at] = u_ref[...]
    for lo in range(0, trows, rows):
        n = min(rows, trows - lo)
        up_ref[:n, at : at + width] = t_ref[lo : lo + n, :]
        if n < rows:
            up_ref[n:, at : at + width] = jnp.zeros((rows - n, width), bf16)
        at += width


def pack(w, o, r, u, t, vectors, gc):
    rows, D = o.shape
    head = 3 * gc + LANES
    rest = 3 * D - 3 * gc + D + r.shape[1]
    ups = u.shape[1] + -(-t.shape[0] // rows) * t.shape[1]
    return once(
        functools.partial(pack_body, D, gc, len(vectors)), "pack", (w, o, r, u, t, *vectors), [None] * (5 + len(vectors)),
        [sds((rows, head), bf16), sds((rows, rest), bf16), sds((rows, ups), bf16)],
        scratch=[pltpu.VMEM((LANES, LANES), f32)], moved=4 * rows * (head + rest + ups),
    )


def pairs(n, flip):
    return [(i, i ^ flip) for i in range(n)]


def along_dp(block, Z):
    return [block] + [lax.ppermute(block, "dp", pairs(Z, k)) for k in range(1, Z)]


def between_chips(blocks, N):
    return lax.all_to_all(blocks, "fsdp", 0, 0, axis_index_groups=[list(range(c, N, 2)) for c in range(2)], tiled=True)


def other_core(blocks, N):
    return lax.ppermute(blocks, "fsdp", pairs(N, 1))


def repeat_body(*refs):
    out = refs[-1]
    for r in range(out.shape[0]):
        for k, ref in enumerate(refs[:-1]):
            out[r, k] = ref[...]


def repeat(blocks, R):
    n = len(blocks)
    return once(
        repeat_body, "repeat", blocks, [None] * n, [sds((R, n) + blocks[0].shape, bf16)], moved=2 * (R + 1) * n * blocks[0].size
    )[0]


def place_body(n, cuts, turned, me_ref, *refs):
    pieces = refs[:n]
    outs = refs[n : n + len(cuts)]
    vec_ref = refs[n + len(cuts)] if turned else None
    held = refs[n + len(cuts) + turned : n + 2 * len(cuts) + turned]
    flat = refs[-3] if turned else None
    in_sem, out_sem = refs[-2:]
    Z = held[0].shape[0]
    copies = []
    for k in range(Z):
        for other in range(2):
            piece = pieces[other].at[:, k] if n == 2 else pieces[other * Z + k]
            for c, (lo, hi) in enumerate(cuts):
                copy = pltpu.make_async_copy(
                    piece.at[:, :, lo:hi], held[c].at[me_ref[0] ^ k, :, me_ref[2] ^ other], in_sem.at[len(copies)]
                )
                copies.append((copy, k))
    for copy, _ in copies:
        copy.start()
    last = []
    for k in range(Z):
        for copy, slot in copies:
            if slot == k:
                copy.wait()
        for c in range(len(cuts)):
            z = me_ref[0] ^ k
            last.append(pltpu.make_async_copy(held[c].at[z], outs[c].at[z], out_sem.at[k * len(cuts) + c]))
            last[-1].start()
    if turned:
        for z in range(Z):
            for r in range(held[-1].shape[1]):
                for c in range(2):
                    flat[z, r, c] = held[-1][z, r, c].astype(f32)
        vec_ref[...] = flat[...].reshape(vec_ref.shape[1], LANES).T[: vec_ref.shape[0]]
    for copy in last:
        copy.wait()


def place(me, pieces, Z, widths, turned=0):
    n = len(pieces)
    R, rows = pieces[0].shape[0], pieces[0].shape[-2]
    cuts = cut_points(widths)
    if turned and rows % 8:
        outs = place(me, pieces, Z, widths)
        return outs + [outs[-1][:, :turned].T.astype(f32)]
    shapes = [(Z, R, 2, rows, w) for w in widths]
    total = 2 * Z * R * rows
    outs = run(
        functools.partial(place_body, n, cuts, 1 if turned else 0), "place", (1,), (me, *pieces), [SMEM] + [ANY] * n,
        [sds(s, bf16) for s in shapes] + ([sds((turned, total), f32)] if turned else []),
        [ANY] * len(cuts) + ([full_spec((turned, total))] if turned else []),
        scratch=[pltpu.VMEM(s, bf16) for s in shapes] + ([pltpu.VMEM(shapes[-1], f32)] if turned else [])
        + [pltpu.SemaphoreType.DMA((2 * Z * len(cuts),)), pltpu.SemaphoreType.DMA((Z * len(cuts),))],
        moved=4 * total * cuts[-1][1], vmem=60,
    )
    return [o.reshape(total, o.shape[-1]) for o in outs[: len(cuts)]] + list(outs[len(cuts) :])


def hand_out(me_ref, held, keep_ref, send_ref):
    Z, R = held.shape[:2]
    for r in range(R):
        for z in range(Z):
            keep_ref[r, z] = held[z, r, me_ref[2]].astype(bf16)
            send_ref[r, z] = held[z, r, 1 - me_ref[2]].astype(bf16)


def grads_body(counts, nvec, has_retr, me_ref, *refs):
    at_held = len(refs) - 1 - (2 if nvec else 0)
    held = refs[at_held]
    Z, R, _, rows, _ = held.shape
    D = Z * R * 2 * rows
    at, col = 0, 0
    for n in counts:
        y = refs[at + n][...]
        parts = [dot(r[...], y, 0, 0) for r in refs[at : at + n]]
        part = parts[0] if n == 1 else jnp.concatenate(parts, axis=0)
        w = part.shape[1]
        held[:, :, :, :, col : col + w] = part.reshape(Z, R, 2, rows, w)
        at += n + 1
        col += w
    if has_retr:
        w = refs[at].shape[1]
        held[:, :, :, :, col : col + w] = refs[at][...].reshape(Z, R, 2, rows, w)
        at += 1
        col += w
    if nvec:
        turn = refs[-1]
        turn[...] = jnp.zeros_like(turn)
        row, lane = 0, 0
        for r in refs[at : at + nvec]:
            w = r.shape[1]
            if w <= D:
                turn[row : row + 1, lane : lane + w] = r[...]
                lane += w
                if lane == D:
                    row, lane = row + 1, 0
        total = turn[...].T.reshape(Z, R, 2, rows, LANES)
        r = refs[at + nvec - 1]
        if r.shape[1] > D:
            Q = r.shape[1] // D
            wide = refs[-2]
            wide[...] = jnp.zeros_like(wide)
            place_of = lax.broadcasted_iota(jnp.int32, r.shape, 1) % (Q * rows) // rows
            for q in range(Q):
                wide[row + q : row + q + 1, :] = jnp.where(place_of == q, r[...], 0.0)
            spread = wide[...].T.reshape(Z * R * 2, Q, rows, LANES)
            for q in range(Q):
                total += spread[:, q].reshape(total.shape)
        held[:, :, :, :, col:] = total
    hand_out(me_ref, held, refs[at_held - 2], refs[at_held - 1])


def hand_out_plain(me, whole, Z, N, rows):
    whole = whole.astype(bf16).reshape(Z, N // 2, 2, rows, -1).swapaxes(0, 1)
    return [lax.dynamic_index_in_dim(whole, c, 2, keepdims=False) for c in (me[2], 1 - me[2])]


def grads(me, Z, N, name, products, retr=None, vectors=(), tile=None):
    counts = [len(xs) for xs, _ in products]
    D = sum(x.shape[1] for x in products[0][0])
    rows, R = D // (Z * N), N // 2
    width = sum(y.shape[1] for _, y in products) + (0 if retr is None else retr.shape[1]) + (LANES if vectors else 0)
    if rows % 8:
        cols = [jnp.concatenate([dot(x, y, 0, 0) for x in xs], axis=0) for xs, y in products]
        cols += [] if retr is None else [retr]
        if vectors:
            narrow = jnp.concatenate([v for v in vectors if v.shape[1] <= D], axis=1).reshape(-1, D)
            wide = [v.reshape(Z * N, -1, rows).swapaxes(0, 1).reshape(-1, D) for v in vectors if v.shape[1] > D]
            turned = jnp.concatenate([narrow] + wide, axis=0).T
            cols += [turned, jnp.zeros((D, LANES - turned.shape[1]), f32)]
        return hand_out_plain(me, jnp.concatenate(cols, axis=1), Z, N, rows)
    ins = [a for xs, y in products for a in (*xs, y)] + ([] if retr is None else [retr]) + list(vectors)
    T = products[0][1].shape[0]
    if tile is None:
        tile, specs, grid = width, [full_spec(a.shape) for a in ins], (1,)
    else:
        specs, grid = [full_spec(ins[0].shape), pl.BlockSpec((T, tile), lambda i: (0, i))], (width // tile,)
    return run(
        functools.partial(grads_body, counts, len(vectors), retr is not None), name, grid, (me, *ins), [SMEM] + specs,
        [sds((R, Z, rows, width), bf16)] * 2, [pl.BlockSpec((R, Z, rows, tile), lambda i: (0, 0, 0, i))] * 2,
        scratch=[pltpu.VMEM((Z, R, 2, rows, tile), f32)]
        + ([pltpu.VMEM((LANES, max(D, vectors[-1].shape[1])), f32), pltpu.VMEM((LANES, D), f32)] if vectors else []),
        flops=2 * T * D * width, moved=2 * T * (D + width) + 2 * D * width,
    )


def down_grad_body(me_ref, x_ref, y_ref, keep_ref, send_ref, held):
    held[...] = dot(x_ref[...], y_ref[...], 0, 0).reshape(held.shape)
    hand_out(me_ref, held, keep_ref, send_ref)


def down_grad(me, Z, N, act, feed):
    T, D = feed.shape
    F = act.shape[1]
    R, rows = N // 2, F // (Z * N)
    if rows % 8:
        return hand_out_plain(me, dot(act, feed, 0, 0), Z, N, rows)
    return run(
        down_grad_body, "down_grad", (Z,), (me, act, feed),
        [SMEM, pl.BlockSpec((T, N * rows), lambda i: (0, i)), full_spec(feed.shape)],
        [sds((R, Z, rows, D), bf16)] * 2, [pl.BlockSpec((R, 1, rows, D), lambda i: (0, i, 0, 0))] * 2,
        scratch=[pltpu.VMEM((1, R, 2, rows, D), f32)], flops=2 * T * F * D, moved=2 * (T * F + T * D + F * D),
    )


def pair_body(n, me_ref, *refs):
    out_ref = refs[-1]
    width = out_ref.shape[3]
    at = 0
    for keep_ref, got_ref in zip(refs[:n], refs[n : 2 * n]):
        rows = keep_ref.shape[2]
        for lo in range(0, keep_ref.shape[3], width):
            cols = slice(lo, lo + width)
            out_ref[:, :, at : at + rows, :] = (
                keep_ref[:, :, :, cols].astype(f32) + got_ref[:, :, :, cols].astype(f32)
            ).astype(bf16)
            at += rows
    if len(refs) > 2 * n + 1:
        mine, other = refs[2 * n][...].astype(f32), refs[2 * n + 1][...].astype(f32)
        first = me_ref[2] == 0
        both = [jnp.where(first, mine, other), jnp.where(first, other, mine)]
        n_rows, w = mine.shape
        line = jnp.concatenate(both + [jnp.zeros((n_rows, width - 2 * w), f32)], axis=1).astype(bf16)
        for z in range(out_ref.shape[1]):
            out_ref[0, z, at : at + n_rows, :] = line


def pair_sum(parts, N, tok, me=None, term=None):
    n = len(parts)
    keeps = [keep for keep, _ in parts]
    got = [other_core(send, N) for _, send in parts]
    R, Z, _, width = keeps[0].shape
    rows = sum(k.size for k in keeps) // (R * Z * width)
    keeps[0] = after(keeps[0], tok)
    ins = keeps + got
    specs = [pl.BlockSpec((1,) + a.shape[1:], lambda i: (i, 0, 0, 0)) for a in ins]
    if term is not None:
        ins += [term, other_core(term, N)]
        specs += [full_spec(term.shape)] * 2
        rows += term.shape[0]
    return run(
        functools.partial(pair_body, n), "pair_sum", (R,), [jnp.zeros((3,), jnp.int32) if me is None else me] + ins, [SMEM] + specs,
        sds((R, Z, rows, width), bf16), pl.BlockSpec((1, Z, rows, width), lambda i: (i, 0, 0, 0)), moved=6 * R * Z * rows * width, vmem=60,
    )


def spots(n, width, shape):
    each = width // shape[1]
    return [(t // each * shape[0], t % each * shape[1]) for t in range(n)], -(-n // each) * shape[0]


def chips_body(term, me_ref, in_ref, *outs):
    R, _, rows, width = in_ref.shape
    rows -= term[0]
    where, _ = spots(2 * R, width, term)
    for k, out in enumerate(outs):
        z = me_ref[0] ^ k
        total = in_ref[0, z, :rows].astype(f32)
        for r in range(1, R):
            total += in_ref[r, z, :rows].astype(f32)
        out[:rows, :] = total.astype(out.dtype)
        if term[0]:
            out[rows:, :] = jnp.zeros((out.shape[0] - rows, width), out.dtype)
            for t, (row, col) in enumerate(where):
                tile = in_ref[t // 2, z, rows : rows + term[0], t % 2 * term[1] : (t % 2 + 1) * term[1]]
                out[rows + row : rows + row + term[0], col : col + term[1]] = tile.astype(out.dtype)


def chips_sum(me, got, tok, term=(0, LANES)):
    R, Z, rows, width = got.shape
    rows += spots(2 * R, width, term)[1] - term[0]
    return once(
        functools.partial(chips_body, term), "chips_sum", (me, after(got, tok)), [SMEM, None],
        [sds((rows, width), f32)] + [sds((rows, width), bf16)] * (Z - 1), moved=2 * got.size + 2 * Z * rows * width,
    )


def total_of(parts, lo, hi, rows=None):
    total = parts[0][:rows, lo:hi].astype(f32)
    for p in parts[1:]:
        total += p[:rows, lo:hi].astype(f32)
    return total


def last_body(n, cuts, G, gc, *refs):
    parts, (in_ref, out_ref, retr_ref, small_ref, turn) = refs[:n], refs[n:]
    rows = parts[0].shape[0]
    out_ref[...] = total_of(parts, *cuts[0])
    for g in range(G):
        group = total_of(parts, *cuts[1 + g])
        for m in range(3):
            in_ref[:, (m * G + g) * gc : (m * G + g + 1) * gc] = group[:, m * gc : (m + 1) * gc]
    retr_ref[...] = total_of(parts, *cuts[1 + G])
    turn[...] = jnp.zeros_like(turn)
    turn[0:rows, :] = total_of(parts, *cuts[2 + G])
    small_ref[...] = turn[...].T[: small_ref.shape[0], :rows]


def last_sum(ins, widths, turned, G, gc):
    rows = ins[0].shape[0]
    cuts = cut_points(widths)
    shapes = [(rows, 3 * G * gc), (rows, widths[0]), (rows, widths[-2]), (turned, rows)]
    return once(
        functools.partial(last_body, len(ins), cuts, G, gc), "last_sum", ins, [None] * len(ins), [sds(s, f32) for s in shapes],
        scratch=[pltpu.VMEM((LANES, LANES), f32)], moved=12 * rows * cuts[-1][1],
    )


def last_feed_body(n, term, N, me_ref, *refs):
    parts, (down_ref, up_ref, table_ref, held) = refs[:n], refs[n:]
    drows, D = down_ref.shape
    rows = up_ref.shape[0]
    total = total_of(parts, 0, D, 2 * drows)
    down_ref[...] = total[:drows]
    for q in range(drows // rows):
        up_ref[:, q * D : (q + 1) * D] = total[drows + q * rows : drows + (q + 1) * rows]
    where, _ = spots(N, D, term)
    trows = table_ref.shape[0]
    count, half = N * n * term[0], term[0] // 2
    for i, p in enumerate(parts):
        for t, (row, col) in enumerate(where):
            at = (i * N + t) * term[0]
            tile = p[2 * drows + row : 2 * drows + row + term[0], col : col + term[1]]
            held[at : at + term[0], :] = tile.astype(f32)
    held[count:, :] = jnp.zeros((term[0], term[1]), f32)
    below = held[half : half + count, :]
    ids = (below[:, 0:1] * 256.0 + below[:, 1:2]).astype(jnp.int32) - (me_ref[0] * N + 2 * me_ref[1] + me_ref[2]) * trows
    line = lax.broadcasted_iota(jnp.int32, (count, trows), 0) % term[0]
    picker = (lax.broadcasted_iota(jnp.int32, (count, trows), 1) == ids) & (line < half)
    table_ref[...] = dot(picker.astype(bf16), held[0:count, :].astype(bf16), 0, 0)


def last_feed(me, ins, F, tok, trows, term, N):
    D = ins[0].shape[1]
    both = ins[0].shape[0] - spots(N, D, term)[1]
    return once(
        functools.partial(last_feed_body, len(ins), term, N), "last_feed", (me, after(ins[0], tok), *ins[1:]), [SMEM] + [None] * len(ins),
        [sds((both // 2, D), f32), sds((both // 2 * D // F, F), f32), sds((trows, term[1]), f32)], moved=12 * both * D,
        scratch=[pltpu.VMEM(((N * len(ins) + 1) * term[0], term[1]), f32)],
    )


def along_dp_sums(sums):
    return [sums[0]] + [lax.ppermute(sums[k], "dp", pairs(len(sums), k)) for k in range(1, len(sums))]


def lookup_body(F, trows, rows, index_ref, sg_ref, w_ref, r_ref, chosen_ref, back_ref, lead_ref, held, sem):
    seqs, _, width = held.shape
    copies = []
    for s in range(seqs):
        owner, within = index_ref[s] // trows, index_ref[s] % trows
        at = owner * rows + within % rows
        row = pl.multiple_of((at // 16) * 16, 16)
        col = pl.multiple_of(F + width * (within // rows), LANES)
        copies.append(
            (pltpu.make_async_copy(w_ref.at[pl.ds(row, 16), pl.ds(col, width)], held.at[s], sem.at[s]), at % 16)
        )
        copies[s][0].start()
    chosen_ref[...] = jnp.zeros_like(chosen_ref)
    line = lax.broadcasted_iota(jnp.int32, (16, width), 0)
    for s in range(seqs):
        copies[s][0].wait()
        block = jnp.where(line == copies[s][1], held[s].astype(f32), 0.0)
        chosen_ref[s : s + 1, :] = jnp.sum(block, axis=0, keepdims=True)
    back_ref[...] = jnp.zeros_like(back_ref)
    back_ref[0:seqs, :] = sg_ref[...] * chosen_ref[0:seqs, :]
    lead = dot(back_ref[...].astype(bf16), r_ref[...], 1, 1)
    for s in range(seqs):
        lead_ref[s] = lead[s : s + 1, :]


def lookup(index, sg, table, wr, F, trows, rows):
    seqs, width = sg.shape[0], wr.shape[1]
    return once(
        functools.partial(lookup_body, F, trows, rows), "lookup", (index, sg, table, wr), [SMEM, None, ANY, None],
        [sds((16, width), f32), sds((16, width), f32), sds((seqs, 1, wr.shape[0]), f32)],
        scratch=[pltpu.VMEM((seqs, 16, width), bf16), pltpu.SemaphoreType.DMA((seqs,))], moved=4 * wr.size,
    )


def score_body(top_ref, r_ref, chosen_ref, back_ref, sg_ref, id_ref, score_ref, retr_ref, term_ref, held):
    seqs = top_ref.shape[0]
    width = r_ref.shape[1]
    held[...] = jnp.zeros_like(held)
    for s in range(seqs):
        held[s : s + 1, :] = top_ref[s]
    leading = held[...].astype(bf16)
    projected = dot(leading, r_ref[...]).astype(bf16).astype(f32)[:seqs]
    score_ref[...] = jnp.sum(projected * chosen_ref[0:seqs, :], axis=-1, keepdims=True)
    retr_ref[...] = dot(leading, back_ref[...].astype(bf16), 0, 0)
    lane = lax.broadcasted_iota(jnp.int32, (seqs, width), 1)
    high, low = id_ref[...] // 256, id_ref[...] % 256
    ids = jnp.where(lane == 0, high, jnp.where(lane == 1, low, 0)).astype(f32)
    term_ref[...] = jnp.concatenate([sg_ref[...] * projected, ids], axis=0).astype(bf16)


def score(top, wr, chosen, back, sg, index):
    seqs, _, D = top.shape
    width = wr.shape[1]
    return once(
        score_body, "score", (top, wr, chosen, back, sg, index), [None] * 6,
        [sds((seqs, 1), f32), sds((D, width), f32), sds((2 * seqs, width), bf16)],
        scratch=[pltpu.VMEM((16, D), f32)], moved=8 * wr.size,
    )


def bias_row_body(Z, N, Q, s_ref, v_ref, out_ref):
    D = s_ref.shape[0]
    rows = D // (Z * N)
    lane = lax.broadcasted_iota(jnp.int32, (Z * N, rows, LANES), 2)
    whole = s_ref[...].astype(f32).reshape(Z * N, rows, LANES)
    parts = [jnp.where(lane == UB + q, whole, 0.0).reshape(Z * N, 1, rows, LANES) for q in range(Q)]
    turned = jnp.concatenate(parts, axis=1).reshape(Q * D, LANES).T
    out_ref[...] = jnp.sum(turned, axis=0, keepdims=True)


def bias_row(small, vec, Z, N, Q):
    D = small.shape[0]
    rows = D // (Z * N)
    if rows % 8:
        return vec[UB : UB + Q].reshape(Q, Z * N, rows).transpose(1, 0, 2).reshape(1, Q * D)
    return once(
        functools.partial(bias_row_body, Z, N, Q), "bias_row", (small, vec), [None] * 2, [sds((1, Q * D), f32)],
        moved=8 * Q * D * LANES,
    )[0]


def local(
    Z, N, tokens, input_weight, query_bias, value_bias, output_weight, output_bias, first_gain, first_shift,
    up_weight, up_bias, down_weight, down_bias, second_gain, second_shift, retriever_weight, document_table,
    document_index, output_grad, score_grad,
):
    both = ("dp", "fsdp")
    T, D = tokens.shape
    R = N // 2
    F = up_weight.shape[1]
    Rw = retriever_weight.shape[1]
    seqs = document_index.shape[0]
    L = T // seqs
    gc = 4 * HEAD_DIM
    G = D // gc
    Q = F // D
    trows, rows = document_table.shape[0], input_weight.shape[0]
    f = lax.axis_index("fsdp")
    me = jnp.stack([lax.axis_index("dp"), f // 2, f % 2]).astype(jnp.int32)

    vectors = [
        v.reshape(1, -1)
        for v in (query_bias, value_bias, output_bias, first_gain, first_shift, down_bias, second_gain, second_shift, up_bias)
    ]
    head, rest, wu = pack(input_weight, output_weight, retriever_weight, up_weight, document_table, vectors, gc)
    wu = lax.all_gather(wu, both, axis=0, tiled=True)
    head = repeat(along_dp(head, Z), R)
    rest = along_dp(after(rest, head), Z)
    head = between_chips(head, N)
    win = [None] * G
    win[0], small, vec = place(me, [head, other_core(head, N)], Z, [3 * gc, LANES], turned=16)
    rest = repeat([after(p, vec) for p in rest], R)
    wd = along_dp(after(down_weight, rest), Z)
    rest = between_chips(rest, N)

    qkv, soft, ctx = [None] * G, [None] * G, [None] * G

    def attend_group(g, tok):
        qkv[g], soft[g], ctx[g] = attend(after(tokens, tok), win[g], vec, g, seqs)

    ub = bias_row(small, vec, Z, N, Q)
    attend_group(0, ub)
    wd = repeat([after(w, ctx[0]) for w in wd], R)
    rest = after(rest, wd)
    *win[1:], wo, wr = place(me, [rest, other_core(rest, N)], Z, [3 * gc] * (G - 1) + [D, Rw])
    wd = between_chips(wd, N)
    for g in range(1, G):
        attend_group(g, ctx[g - 1])
    wd = after(wd, ctx[G - 1])
    n, inv, first, act, slope = up(ctx, tokens, wo, vec, wu, ub, L)
    (wd,) = place(me, [after(wd, first), other_core(wd, N)], Z, [D])
    chosen, back_projected, lead = lookup(document_index, score_grad.reshape(seqs, 1), after(wu, first), wr, F, trows, rows)
    final, top, two, feed, inner, gsg, gss, gdb, gub = down(first, act, slope, wd, vec, output_grad, lead, seqs)
    scores, retriever_back, term = score(top, wr, chosen, back_projected, score_grad.reshape(seqs, 1), document_index.reshape(seqs, 1))
    down_parts = down_grad(me, Z, N, act, feed)
    up_parts = grads(me, Z, N, "up_grad", [([after(first, *down_parts)], inner)], tile=D)
    feed_sums = pair_sum([down_parts, up_parts], N, up_parts[0], me, term)
    one, att, bctx, gfg, gfs, gob = mid(after(two, feed_sums), inner, wu, n, inv, vec, wo, L)
    mixed, gq, gv = [None] * G, [None] * G, [None] * G
    for g in range(G):
        mixed[g], gq[g], gv[g] = attend_back(
            qkv[g], soft[g], ctx[g], after(bctx, mixed[g - 1]) if g else bctx, g, seqs
        )
    parts = grads(
        me, Z, N, "mix_grad", [(ctx, att)] + [([tokens], m) for m in mixed],
        retr=retriever_back, vectors=gq + gv + [gob, gfg, gfs, gdb, gsg, gss, gub],
    )
    feed_sums = chips_sum(me, between_chips(feed_sums, N), parts[0], term.shape)
    mix_sums = pair_sum([parts], N, feed_sums[0])
    back_tokens = tokens_back(after(one, mix_sums), mixed, win, L)
    down_back, up_back, table_back = last_feed(me, along_dp_sums(feed_sums), F, back_tokens, trows, term.shape, N)
    mix_sums = chips_sum(me, between_chips(mix_sums, N), down_back)
    input_back, output_back, retriever_back, small = last_sum(
        along_dp_sums(mix_sums), [D] + [3 * gc] * G + [Rw, LANES], 16, G, gc
    )
    ub_back = small[8 : 8 + Q].reshape(-1)
    return (
        final, scores.reshape(seqs), back_tokens, input_back, small[0], small[1], output_back, small[2], small[3], small[4],
        up_back, ub_back, down_back, small[5], small[6], small[7], retriever_back, table_back,
    )


def solution(mesh):
    both = ("dp", "fsdp")
    mat, vec = P(both, None), P(both)
    in_specs = (mat, mat, vec, vec, mat, vec, vec, vec, mat, vec, mat, vec, vec, vec, mat, mat, vec, mat, vec)
    out_specs = (mat, vec, mat, mat, vec, vec, mat, vec, vec, vec, mat, vec, mat, vec, vec, vec, mat, mat)
    body = functools.partial(local, mesh.shape["dp"], mesh.shape["fsdp"])
    return jax.shard_map(body, mesh=mesh, in_specs=in_specs, out_specs=out_specs, check_vma=False)
```

time: 479 us -> 382 us (0.80)
  waiting for transfers between devices: 107 us -> 53.7 us
  local copies, waits for them, and re-layouts: 39 us -> 14 us
  between operations: 30.2 us -> 14.5 us
  blocking collectives: 0 us -> 12.7 us
  starting transfers between devices: 60.8 us -> 54.2 us
  other arithmetic: 7.78 us -> 1.21 us
    ppermute x60 -> x22, waiting for transfers between devices: 107 us -> 47.4 us  [the longest x6 24.2 us: along_dp_sums(): lax.ppermute(sums[k], 'dp', pairs(len(sums), k))]
    pallas_call x17 -> x29, Pallas kernels: 191 us -> 227 us  [run(): pl.pallas_call(body, name=name, grid=grid, in_specs=in_specs, out_specs=o...]
    pallas_call x13 -> x0, Pallas kernels: 35 us -> none  [plain(): pl.pallas_call(body, name=name, in_specs=in_specs, out_specs=out_specs, o...]
    ppermute x60 -> x22, starting transfers between devices: 60.7 us -> 36 us  [the longest x9 18.1 us: along_dp(): lax.ppermute(block, 'dp', pairs(Z, k))]
    all_to_all x0 -> x4, starting transfers between devices: none -> 18.2 us  [between_chips(): lax.all_to_all(blocks, 'fsdp', 0, 0, axis_index_groups=[list(range(c, N,...]
    all_to_all x0 -> x1, blocking collectives: none -> 12.7 us  [between_chips(): lax.all_to_all(blocks, 'fsdp', 0, 0, axis_index_groups=[list(range(c, N,...]
    unnamed x146 -> x56, local copies, waits for them, and re-layouts: 16.3 us -> 9.22 us
    all_to_all x0 -> x4, waiting for transfers between devices: none -> 6.22 us  [between_chips(): lax.all_to_all(blocks, 'fsdp', 0, 0, axis_index_groups=[list(range(c, N,...]
  transfers between devices with their start and end apart: 63 -> 27, of which waited for: 21 -> 14; matrix products, arithmetic and copies ran while one was open for 6% -> 1% of each run, Pallas kernels for 41% -> 41%
where the time goes in v2:
time: 382 us; the launch traced here: 377 us
  Pallas kernels  227 us (59%)
  starting transfers between devices  54.2 us (14%)
  waiting for transfers between devices  53.7 us (14%)
  between operations  14.5 us (4%)
  local copies, waits for them, and re-layouts  14 us (4%)
  blocking collectives  12.7 us (3%)
    pallas_call x29, Pallas kernels, run(): pl.pallas_call(body, name=name, grid=grid, in_specs=in_specs, out_specs=o...  227 us
    ppermute x6, waiting for transfers between devices, along_dp_sums(): lax.ppermute(sums[k], 'dp', pairs(len(sums), k))  24.2 us
    all_to_all x4, starting transfers between devices, between_chips(): lax.all_to_all(blocks, 'fsdp', 0, 0, axis_index_groups=[list(range(c, N,...  18.2 us
    ppermute x9, starting transfers between devices, along_dp(): lax.ppermute(block, 'dp', pairs(Z, k))  18.1 us
    ppermute x9, waiting for transfers between devices, along_dp(): lax.ppermute(block, 'dp', pairs(Z, k))  17.4 us
    ppermute x6, starting transfers between devices, along_dp_sums(): lax.ppermute(sums[k], 'dp', pairs(len(sums), k))  16.6 us
    all_to_all x1, blocking collectives, between_chips(): lax.all_to_all(blocks, 'fsdp', 0, 0, axis_index_groups=[list(range(c, N,...  12.7 us
    unnamed x56, local copies, waits for them, and re-layouts  9.22 us
  transfers between devices with their start and end apart: 27, of which 14 were waited for; matrix products, arithmetic and copies ran while one was open for 1% of the time, Pallas kernels for 41%

profile of v2, /device:TPU:0, one launch (start us, length us, event | category | flops | bytes accessed | tf_op | source)
XLA Modules:
  0.0 377.3 jit_solution(8913685172010453803)
XLA Ops:
  9.1 3.1 collective-permute-start
  12.2 2.6 collective-permute-start.1
  14.8 3.3 collective-permute-done.1.refs_2_
  18.2 2.7 collective-permute-done.2.refs_3_
  23.2 12.7 %all_to_all.25.refs_0_ = bf16[4,4,24,896]{3,2,1,0:T(8,128)(2,1)S(1)} all-to-all(bf16[4,4,24,896]{3,2,1,0:T(8,128)(2,1)} %repeat.3), channel_id=1, replica_groups={{0,2,4,6},{1,3,5,7},{8,10,12,14},{9,11,13,15},{16,18,20,22},{17,19,21,2..., dimensions={0} | all-to-all | bytes 1376256 | tf_op jit(solution)/shard_map/all_to_all | solution.py:370
  36.7 2.0 collective-permute-start.5
  41.8 3.7 place.3
  45.5 6.5 %collective-permute-done.5.refs_2_ = bf16[24,2432]{1,0:T(8,128)(2,1)S(1)} collective-permute-done((bf16[24,2432]{1,0:T(8,128)(2,1)S(1)}, bf16[24,2432]{1,0:T(8,128)(2,1)S(1)}, u32[]{:S(2)}, u32[]{:S(2)}) %collective-permute-start.5) | collective-permute-done | bytes 116768 | tf_op jit(solution)/shard_map/ppermute | solution.py:366
  53.2 2.5 repeat.4
  55.7 4.5 %all-to-all-start.1 = ((bf16[4,4,24,2432]{3,2,1,0:T(8,128)(2,1)}), bf16[4,4,24,2432]{3,2,1,0:T(8,128)(2,1)}, u32[]{:S(2)}, u32[]{:S(2)}) async-start(bf16[4,4,24,2432]{3,2,1,0:T(8,128)(2,1)} %repeat.4), calls=%async_computation.1 | async-start | bytes 3735552 | tf_op jit(solution)/shard_map/all_to_all | solution.py:370
  60.3 2.4 collective-permute-start.9
  62.7 5.2 %collective-permute-start.8 = (bf16[96,768]{1,0:T(8,128)(2,1)S(1)}, bf16[96,768]{1,0:T(8,128)(2,1)S(1)}, u32[]{:S(2)}, u32[]{:S(2)}) collective-permute-start(bf16[96,768]{1,0:T(8,128)(2,1)S(1)} %copy-done.12), channel_id=1, source_target_pairs={{0,16},{8,24},{16,0},{24,8},{1,17},{9,25},{17,1},{25,9},{2,18},{10... | collective-permute-start | bytes 442376 | tf_op jit(solution)/shard_map/ppermute | solution.py:366
  70.0 10.1 %attend.3 = (bf16[1152,768]{1,0:T(8,128)(2,1)}, bf16[4,1152,288]{2,1,0:T(8,128)(2,1)}, bf16[1152,256]{1,0:T(8,128)(2,1)}) custom-call(bf16[1152,768]{1,0:T(8,128)(2,1)} %refs_8_.1, bf16[768,768]{1,0:T(8,128)(2,1)} %bitcast.52, f32[16,768]{1,0:T(8,128)} %get-tuple-element.122.v_ref.refs_5_), custom_call_target="tpu_custom_call" | custom-call | flops 2717908992 | bytes 7962624 | tf_op jit(solution)/shard_map/attend/pallas_call | solution.py:36
  80.1 4.9 %collective-permute-done.8.refs_2_ = bf16[96,768]{1,0:T(8,128)(2,1)S(1)} collective-permute-done((bf16[96,768]{1,0:T(8,128)(2,1)S(1)}, bf16[96,768]{1,0:T(8,128)(2,1)S(1)}, u32[]{:S(2)}, u32[]{:S(2)}) %collective-permute-start.8) | collective-permute-done | bytes 147488 | tf_op jit(solution)/shard_map/ppermute | solution.py:366
  86.3 2.7 repeat.5
  89.0 2.3 all-to-all-done.1.refs_0_
  91.4 4.2 %all-to-all-start.2 = ((bf16[4,4,96,768]{3,2,1,0:T(8,128)(2,1)}), bf16[4,4,96,768]{3,2,1,0:T(8,128)(2,1)S(1)}, u32[]{:S(2)}, u32[]{:S(2)}) async-start(bf16[4,4,96,768]{3,2,1,0:T(8,128)(2,1)} %repeat.5), calls=%async_computation.2 | async-start | bytes 4718592 | tf_op jit(solution)/shard_map/all_to_all | solution.py:370
  95.7 4.2 %place.4 = (bf16[4,4,2,24,768]{4,3,2,1,0:T(8,128)(2,1)}, bf16[4,4,2,24,768]{4,3,2,1,0:T(8,128)(2,1)}, bf16[4,4,2,24,768]{4,3,2,1,0:T(8,128)(2,1)}, bf16[4,4,2,24,128]{4,3,2,1,0:T(8,128)(2,1)}) custom-call(s32[3]{0:T(128)} %pad_add_fusion.me_ref, bf16[4,4,24,2432]{3,2,1,0:T(8,128)(2,1)} %all-to-all-done.1.refs_0_, ...), custom_call_target="tpu_custom_call" | custom-call | bytes 7471104 | tf_op jit(solution)/shard_map/place/pallas_call | solution.py:36
  100.0 10.1 %attend.4 = (bf16[1152,768]{1,0:T(8,128)(2,1)}, bf16[4,1152,288]{2,1,0:T(8,128)(2,1)}, bf16[1152,256]{1,0:T(8,128)(2,1)}) custom-call(bf16[1152,768]{1,0:T(8,128)(2,1)} %refs_8_.1, bf16[768,768]{1,0:T(8,128)(2,1)} %bitcast.54, f32[16,768]{1,0:T(8,128)} %get-tuple-element.122.v_ref.refs_5_), custom_call_target="tpu_custom_call" | custom-call | flops 2717908992 | bytes 7962624 | tf_op jit(solution)/shard_map/attend/pallas_call | solution.py:36
  110.1 10.1 %attend.5 = (bf16[1152,768]{1,0:T(8,128)(2,1)}, bf16[4,1152,288]{2,1,0:T(8,128)(2,1)}, bf16[1152,256]{1,0:T(8,128)(2,1)}) custom-call(bf16[1152,768]{1,0:T(8,128)(2,1)} %refs_8_.1, bf16[768,768]{1,0:T(8,128)(2,1)} %bitcast.56, f32[16,768]{1,0:T(8,128)} %get-tuple-element.122.v_ref.refs_5_), custom_call_target="tpu_custom_call" | custom-call | flops 2717908992 | bytes 7962624 | tf_op jit(solution)/shard_map/attend/pallas_call | solution.py:36
  120.2 3.9 %all-to-all-done.2.refs_0_ = bf16[4,4,96,768]{3,2,1,0:T(8,128)(2,1)S(1)} async-done(((bf16[4,4,96,768]{3,2,1,0:T(8,128)(2,1)}), bf16[4,4,96,768]{3,2,1,0:T(8,128)(2,1)S(1)}, u32[]{:S(2)}, u32[]{:S(2)}) %all-to-all-start.2) | async-done | bytes 2359328 | tf_op jit(solution)/shard_map/all_to_all | solution.py:370
  124.9 27.7 %up.1 = (f32[1152,768]{1,0:T(8,128)}, f32[1152,1]{1,0:T(8,128)}, bf16[1152,768]{1,0:T(8,128)(2,1)}, bf16[1152,3072]{1,0:T(8,128)(2,1)}, bf16[1152,3072]{1,0:T(8,128)(2,1)}) custom-call(bf16[1152,256]{1,0:T(8,128)(2,1)} %get-tuple-element.125.refs_0_.ctx_ref, bf16[1152,256]{1,0:T(8,128)(2,1)} %get-tuple-element.140.refs_1_.ctx_ref, ...), custom_call_target="tpu_custom_call" | custom-call | flops 6794772480 | bytes 31064064 | tf_op jit(solution)/shard_map/up/pallas_call | solution.py:36
  152.6 2.6 lookup.1
  155.2 4.5 %place.5 = bf16[4,4,2,96,768]{4,3,2,1,0:T(8,128)(2,1)} custom-call(s32[3]{0:T(128)} %pad_add_fusion.me_ref, bf16[4,4,96,768]{3,2,1,0:T(8,128)(2,1)} %copy-done.1, bf16[4,4,96,768]{3,2,1,0:T(8,128)(2,1)} %collective-permute-done.11.refs_1_), custom_call_target="tpu_custom_call" | custom-call | bytes 9437184 | tf_op jit(solution)/shard_map/place/pallas_call | solution.py:36
  159.7 29.8 %down.1 = (bf16[1152,768]{1,0:T(8,128)(2,1)}, f32[4,1,768]{2,1,0:T(1,128)}, f32[1152,768]{1,0:T(8,128)}, bf16[1152,768]{1,0:T(8,128)(2,1)}, bf16[1152,3072]{1,0:...) custom-call(bf16[1152,768]{1,0:T(8,128)(2,1)} %get-tuple-element.163.first_ref.refs_0, ...), custom_call_target="tpu_custom_call" | custom-call | flops 10871635968 | bytes 36569088 | tf_op jit(solution)/shard_map/down/pallas_call | solution.py:36
  189.5 10.6 %down_grad.1 = (bf16[4,4,96,768]{3,2,1,0:T(8,128)(2,1)}, bf16[4,4,96,768]{3,2,1,0:T(8,128)(2,1)}) custom-call(s32[3]{0:T(128)} %pad_add_fusion.me_ref, bf16[1152,3072]{1,0:T(8,128)(2,1)} %get-tuple-element.147.act_ref.x_ref, bf16[1152,768]{1,0:T(8,128)(2,1)} %get-tuple-element.160.y_ref), custom_call_target="tpu_custom_call" | custom-call | flops 5435817984 | bytes 13565952 | tf_op jit(solution)/shard_map/down_grad/pallas_call | solution.py:36
  200.1 10.6 %up_grad.1 = (bf16[4,4,24,3072]{3,2,1,0:T(8,128)(2,1)}, bf16[4,4,24,3072]{3,2,1,0:T(8,128)(2,1)}) custom-call(s32[3]{0:T(128)} %pad_add_fusion.me_ref, bf16[1152,768]{1,0:T(8,128)(2,1)} %get-tuple-element.163.first_ref.refs_0_, bf16[1152,3072]{1,0:T(8,128)(2,1)} %get-tuple-element.164.refs_1_.inner_ref), custom_call_target="tpu_custom_call" | custom-call | flops 5435817984 | bytes 13565952 | tf_op jit(solution)/shard_map/up_grad/pallas_call | solution.py:36
  211.9 2.0 score.1
  214.3 3.9 %collective-permute-done.14.refs_5_ = bf16[8,128]{1,0:T(8,128)(2,1)S(1)} collective-permute-done((bf16[8,128]{1,0:T(8,128)(2,1)}, bf16[8,128]{1,0:T(8,128)(2,1)S(1)}, u32[]{:S(2)}, u32[]{:S(2)}) %collective-permute-start.14) | collective-permute-done | bytes 2080 | tf_op jit(solution)/shard_map/ppermute | solution.py:374
  219.5 6.5 %pair_sum.2 = bf16[4,4,200,768]{3,2,1,0:T(8,128)(2,1)} custom-call(s32[3]{0:T(128)} %pad_add_fusion.me_ref, bf16[4,4,96,768]{3,2,1,0:T(8,128)(2,1)} %get-tuple-element.166.refs_0_, bf16[4,4,24,3072]{3,2,1,0:T(8,128)(2,1)} %get-tuple-element.165.refs_1_, bf16[4,4,96,768]{3,2,1,0:T(8,128)(2,1)} %collective-permute-done.12.refs_2_, ...), custom_call_target="tpu_custom_call" | custom-call | bytes 14745600 | tf_op jit(solution)/shard_map/pair_sum/pallas_call | solution.py:36
  226.1 5.2 %all-to-all-start.3 = ((bf16[4,4,200,768]{3,2,1,0:T(8,128)(2,1)}), bf16[4,4,200,768]{3,2,1,0:T(8,128)(2,1)}, u32[]{:S(2)}, u32[]{:S(2)}) async-start(bf16[4,4,200,768]{3,2,1,0:T(8,128)(2,1)} %pair_sum.2), calls=%async_computation.3 | async-start | bytes 9830400 | tf_op jit(solution)/shard_map/all_to_all | solution.py:370
  231.2 18.7 %mid.1 = (f32[1152,768]{1,0:T(8,128)}, bf16[1152,768]{1,0:T(8,128)(2,1)}, bf16[1152,768]{1,0:T(8,128)(2,1)}, f32[1,768]{1,0:T(1,128)}, f32[1,768]{1,0:T(1,128)}, /*index=5*/f32[1,768]{1,0:T(1,128)}) custom-call(f32[1152,768]{1,0:T(8,128)} %get-tuple-element.169.two_ref, bf16[1152,3072]{1,0:T(8,128)(2,1)} %get-tuple-element.164.refs_1_.inner_ref, ...), custom_call_target="tpu_custom_call" | custom-call | flops 6794772480 | bytes 28114944 | tf_op jit(solution)/shard_map/mid/pallas_call | solution.py:36
  249.9 8.6 %attend_back.3 = (bf16[1152,768]{1,0:T(8,128)(2,1)}, f32[1,256]{1,0:T(1,128)}, f32[1,256]{1,0:T(1,128)}) custom-call(bf16[1152,768]{1,0:T(8,128)(2,1)} %get-tuple-element.174.qkv_ref, bf16[4,1152,288]{2,1,0:T(8,128)(2,1)} %get-tuple-element.175.soft_ref, bf16[1152,256]{1,0:T(8,128)(2,1)} %get-tuple-element.125.refs_0_.ctx_ref, ...), custom_call_target="tpu_custom_call" | custom-call | flops 2717908992 | bytes 7372800 | tf_op jit(solution)/shard_map/attend_back/pallas_call | solution.py:36
  258.5 8.6 %attend_back.4 = (bf16[1152,768]{1,0:T(8,128)(2,1)}, f32[1,256]{1,0:T(1,128)}, f32[1,256]{1,0:T(1,128)}) custom-call(bf16[1152,768]{1,0:T(8,128)(2,1)} %get-tuple-element.178.qkv_ref, bf16[4,1152,288]{2,1,0:T(8,128)(2,1)} %get-tuple-element.179.soft_ref, bf16[1152,256]{1,0:T(8,128)(2,1)} %get-tuple-element.140.refs_1_.ctx_ref, ...), custom_call_target="tpu_custom_call" | custom-call | flops 2717908992 | bytes 7372800 | tf_op jit(solution)/shard_map/attend_back/pallas_call | solution.py:36
  267.2 8.9 %attend_back.5 = (bf16[1152,768]{1,0:T(8,128)(2,1)}, f32[1,256]{1,0:T(1,128)}, f32[1,256]{1,0:T(1,128)}) custom-call(bf16[1152,768]{1,0:T(8,128)(2,1)} %get-tuple-element.182.qkv_ref, bf16[4,1152,288]{2,1,0:T(8,128)(2,1)} %get-tuple-element.183.soft_ref, bf16[1152,256]{1,0:T(8,128)(2,1)} %get-tuple-element.143.refs_2_.ctx_ref, ...), custom_call_target="tpu_custom_call" | custom-call | flops 2717908992 | bytes 7372800 | tf_op jit(solution)/shard_map/attend_back/pallas_call | solution.py:36
  276.0 14.3 %mix_grad.1 = (bf16[4,4,24,3328]{3,2,1,0:T(8,128)(2,1)}, bf16[4,4,24,3328]{3,2,1,0:T(8,128)(2,1)}) custom-call(s32[3]{0:T(128)} %pad_add_fusion.me_ref, bf16[1152,256]{1,0:T(8,128)(2,1)} %get-tuple-element.125.refs_0_.ctx_ref, bf16[1152,256]{1,0:T(8,128)(2,1)} %get-tuple-element.140.refs_1_.ctx_ref, bf16[1152,256]{1,0:T(8,128)(2,1)} %get-tuple-element.143.refs_2_.ctx_ref, ...), custom_call_target="tpu_custom_call" | custom-call | flops 5888802816 | bytes 14548992 | tf_op jit(solution)/shard_map/mix_grad/pallas_call | solution.py:36
  290.7 3.8 %chips_sum.2 = (f32[208,768]{1,0:T(8,128)}, bf16[208,768]{1,0:T(8,128)(2,1)}, bf16[208,768]{1,0:T(8,128)(2,1)}, bf16[208,768]{1,0:T(8,128)(2,1)}) custom-call(s32[3]{0:T(128)} %pad_add_fusion.me_ref, bf16[4,4,200,768]{3,2,1,0:T(8,128)(2,1)} %all-to-all-done.3.in_ref), custom_call_target="tpu_custom_call" | custom-call | bytes 6193152 | tf_op jit(solution)/shard_map/chips_sum/pallas_call | solution.py:36
  296.9 4.6 %pair_sum.3 = bf16[4,4,24,3328]{3,2,1,0:T(8,128)(2,1)} custom-call(s32[3]{0:T(128)} %broadcast_1_me_ref.2.me_ref, bf16[4,4,24,3328]{3,2,1,0:T(8,128)(2,1)} %get-tuple-element.203.refs_0_, bf16[4,4,24,3328]{3,2,1,0:T(8,128)(2,1)} %copy-done.3), custom_call_target="tpu_custom_call" | custom-call | bytes 7667712 | tf_op jit(solution)/shard_map/pair_sum/pallas_call | solution.py:36
  301.6 4.3 %all-to-all-start.4 = ((bf16[4,4,24,3328]{3,2,1,0:T(8,128)(2,1)}), bf16[4,4,24,3328]{3,2,1,0:T(8,128)(2,1)S(1)}, u32[]{:S(2)}, u32[]{:S(2)}) async-start(bf16[4,4,24,3328]{3,2,1,0:T(8,128)(2,1)} %pair_sum.3), calls=%async_computation.4 | async-start | bytes 5111808 | tf_op jit(solution)/shard_map/all_to_all | solution.py:370
  305.9 5.7 %collective-permute-start.16 = (bf16[208,768]{1,0:T(8,128)(2,1)}, bf16[208,768]{1,0:T(8,128)(2,1)S(1)}, u32[]{:S(2)}, u32[]{:S(2)}) collective-permute-start(bf16[208,768]{1,0:T(8,128)(2,1)} %get-tuple-element.207), channel_id=1, source_target_pairs={{0,8},{8,0},{16,24},{24,16},{1,9},{9,1},{17,25},{25,17},{2,10},{10... | collective-permute-start | bytes 958472 | tf_op jit(solution)/shard_map/ppermute | solution.py:694
  314.3 9.1 %tokens_back.1 = bf16[1152,768]{1,0:T(8,128)(2,1)} custom-call(f32[1152,768]{1,0:T(8,128)} %get-tuple-element.205.one_ref, bf16[1152,768]{1,0:T(8,128)(2,1)} %get-tuple-element.177.refs_5_.refs_0_, bf16[1152,768]{1,0:T(8,128)(2,1)} %get-tuple-element.181.refs_7_.refs_1_, bf16[1152,768]{1,0:T(8,128)(2,1)} %get-tuple-element.185.refs_9_.refs_2_, ...), custom_call_target="tpu_custom_call" | custom-call | flops 4076863488 | bytes 10616832 | tf_op jit(solution)/shard_map/tokens_back/pallas_call | solution.py:36
  323.5 2.2 collective-permute-done.16.refs_1_
  325.7 11.2 %collective-permute-done.17.refs_2_ = bf16[208,768]{1,0:T(8,128)(2,1)S(1)} collective-permute-done((bf16[208,768]{1,0:T(8,128)(2,1)}, bf16[208,768]{1,0:T(8,128)(2,1)S(1)}, u32[]{:S(2)}, u32[]{:S(2)}) %collective-permute-start.17) | collective-permute-done | bytes 319520 | tf_op jit(solution)/shard_map/ppermute | solution.py:694
  338.3 2.6 last_feed.1
  342.4 2.8 chips_sum.3
  345.2 5.4 %collective-permute-start.19 = (bf16[24,3328]{1,0:T(8,128)(2,1)}, bf16[24,3328]{1,0:T(8,128)(2,1)S(1)}, u32[]{:S(2)}, u32[]{:S(2)}) collective-permute-start(bf16[24,3328]{1,0:T(8,128)(2,1)} %get-tuple-element.213), channel_id=1, source_target_pairs={{0,8},{8,0},{16,24},{24,16},{1,9},{9,1},{17,25},{25,17},{2,10},{10... | collective-permute-start | bytes 479240 | tf_op jit(solution)/shard_map/ppermute | solution.py:694
  355.8 8.9 %collective-permute-done.20.refs_2_ = bf16[24,3328]{1,0:T(8,128)(2,1)S(1)} collective-permute-done((bf16[24,3328]{1,0:T(8,128)(2,1)}, bf16[24,3328]{1,0:T(8,128)(2,1)S(1)}, u32[]{:S(2)}, u32[]{:S(2)}) %collective-permute-start.20) | collective-permute-done | bytes 159776 | tf_op jit(solution)/shard_map/ppermute | solution.py:694
  365.5 1.9 last_sum.1
  (101 shorter events, 34.2 us)
Async XLA Ops:
  7.2 117.7 %all-gather.2.cloned.1.call-start = ((), (), s32[]{:S(2)}) async-start(), calls=%async_computation.5 | async-start | bytes 7096320 | tf_op jit(solution)/shard_map/all_gather | solution.py:802
  9.1 26.8 %copy-start.16 = (bf16[24,2432]{1,0:T(8,128)(2,1)S(1)}, bf16[24,2432]{1,0:T(8,128)(2,1)}, u32[]{:S(2)}) copy-start(bf16[24,2432]{1,0:T(8,128)(2,1)} %get-tuple-element.129.refs_0_) | copy-start | bytes 350212
  9.1 5.7 %collective-permute-start = (bf16[24,896]{1,0:T(8,128)(2,1)}, bf16[24,896]{1,0:T(8,128)(2,1)S(1)}, u32[]{:S(2)}, u32[]{:S(2)}) collective-permute-start(bf16[24,896]{1,0:T(8,128)(2,1)} %get-tuple-element.120.refs_0_), channel_id=1, source_target_pairs={{0,8},{8,0},{16,24},{24,16},{1,9},{9,1},{17,25},{25,17},{2,10},{10... | collective-permute-start | bytes 129032 | tf_op jit(solution)/shard_map/ppermute | solution.py:366
  12.2 5.9 %collective-permute-start.1 = (bf16[24,896]{1,0:T(8,128)(2,1)}, bf16[24,896]{1,0:T(8,128)(2,1)S(1)}, u32[]{:S(2)}, u32[]{:S(2)}) collective-permute-start(bf16[24,896]{1,0:T(8,128)(2,1)} %get-tuple-element.120.refs_0_), channel_id=1, source_target_pairs={{0,16},{8,24},{16,0},{24,8},{1,17},{9,25},{17,1},{25,9},{2,18},{10... | collective-permute-start | bytes 129032 | tf_op jit(solution)/shard_map/ppermute | solution.py:366
  14.8 6.0 %collective-permute-start.2 = (bf16[24,896]{1,0:T(8,128)(2,1)}, bf16[24,896]{1,0:T(8,128)(2,1)S(1)}, u32[]{:S(2)}, u32[]{:S(2)}) collective-permute-start(bf16[24,896]{1,0:T(8,128)(2,1)} %get-tuple-element.120.refs_0_), channel_id=1, source_target_pairs={{0,24},{8,16},{16,8},{24,0},{1,25},{9,17},{17,9},{25,1},{2,26},{10... | collective-permute-start | bytes 129032 | tf_op jit(solution)/shard_map/ppermute | solution.py:366
  14.8 6.0 %copy-start.20 = (bf16[24,896]{1,0:T(8,128)(2,1)}, bf16[24,896]{1,0:T(8,128)(2,1)S(1)}, u32[]{:S(2)}) copy-start(bf16[24,896]{1,0:T(8,128)(2,1)S(1)} %collective-permute-done.refs_1_) | copy-start | bytes 129028
  18.2 2.7 copy-start.21
  35.9 5.1 %copy-start.2 = (bf16[4,4,24,896]{3,2,1,0:T(8,128)(2,1)}, bf16[4,4,24,896]{3,2,1,0:T(8,128)(2,1)S(1)}, u32[]{:S(2)}) copy-start(bf16[4,4,24,896]{3,2,1,0:T(8,128)(2,1)S(1)} %all_to_all.25.refs_0_) | copy-start | bytes 2064388
  35.9 5.1 %collective-permute-start.3 = (bf16[4,4,24,896]{3,2,1,0:T(8,128)(2,1)S(1)}, bf16[4,4,24,896]{3,2,1,0:T(8,128)(2,1)S(1)}, u32[]{:S(2)}, u32[]{:S(2)}) collective-permute-start(bf16[4,4,24,896]{3,2,1,0:T(8,128)(2,1)S(1)} %all_to_all.25.refs_0_), channel_id=1, source_target_pairs={{0,1},{1,0},{2,3},{3,2},{4,5},{5,4},{6,7},{7,6},{8,9},{9,8},{10,11... | collective-permute-start | bytes 2064392 | tf_op jit(solution)/shard_map/ppermute | solution.py:374
  35.9 9.6 %collective-permute-start.4 = (bf16[24,2432]{1,0:T(8,128)(2,1)S(1)}, bf16[24,2432]{1,0:T(8,128)(2,1)S(1)}, u32[]{:S(2)}, u32[]{:S(2)}) collective-permute-start(bf16[24,2432]{1,0:T(8,128)(2,1)S(1)} %copy-done.16), channel_id=1, source_target_pairs={{0,8},{8,0},{16,24},{24,16},{1,9},{9,1},{17,25},{25,17},{2,10},{10... | collective-permute-start | bytes 350216 | tf_op jit(solution)/shard_map/ppermute | solution.py:366
  36.7 15.2 %collective-permute-start.5 = (bf16[24,2432]{1,0:T(8,128)(2,1)S(1)}, bf16[24,2432]{1,0:T(8,128)(2,1)S(1)}, u32[]{:S(2)}, u32[]{:S(2)}) collective-permute-start(bf16[24,2432]{1,0:T(8,128)(2,1)S(1)} %copy-done.16), channel_id=1, source_target_pairs={{0,16},{8,24},{16,0},{24,8},{1,17},{9,25},{17,1},{25,9},{2,18},{10... | collective-permute-start | bytes 350216 | tf_op jit(solution)/shard_map/ppermute | solution.py:366
  38.7 13.2 %collective-permute-start.6 = (bf16[24,2432]{1,0:T(8,128)(2,1)S(1)}, bf16[24,2432]{1,0:T(8,128)(2,1)S(1)}, u32[]{:S(2)}, u32[]{:S(2)}) collective-permute-start(bf16[24,2432]{1,0:T(8,128)(2,1)S(1)} %copy-done.16), channel_id=1, source_target_pairs={{0,24},{8,16},{16,8},{24,0},{1,25},{9,17},{17,9},{25,1},{2,26},{10... | collective-permute-start | bytes 350216 | tf_op jit(solution)/shard_map/ppermute | solution.py:366
  40.9 0.8 copy-start.5
  45.5 6.5 %copy-start.17 = (bf16[24,2432]{1,0:T(8,128)(2,1)}, bf16[24,2432]{1,0:T(8,128)(2,1)S(1)}, u32[]{:S(2)}) copy-start(bf16[24,2432]{1,0:T(8,128)(2,1)S(1)} %collective-permute-done.4.refs_1_) | copy-start | bytes 350212
  55.7 4.5 %copy-start.12 = (bf16[96,768]{1,0:T(8,128)(2,1)S(1)}, bf16[96,768]{1,0:T(8,128)(2,1)}, u32[]{:S(2)}) copy-start(bf16[96,768]{1,0:T(8,128)(2,1)} %refs_0_.2) | copy-start | bytes 442372
  55.7 35.7 %all-to-all-start.1 = ((bf16[4,4,24,2432]{3,2,1,0:T(8,128)(2,1)}), bf16[4,4,24,2432]{3,2,1,0:T(8,128)(2,1)}, u32[]{:S(2)}, u32[]{:S(2)}) async-start(bf16[4,4,24,2432]{3,2,1,0:T(8,128)(2,1)} %repeat.4), calls=%async_computation.1 | async-start | bytes 3735552 | tf_op jit(solution)/shard_map/all_to_all | solution.py:370
  60.3 19.9 %collective-permute-start.9 = (bf16[96,768]{1,0:T(8,128)(2,1)S(1)}, bf16[96,768]{1,0:T(8,128)(2,1)S(1)}, u32[]{:S(2)}, u32[]{:S(2)}) collective-permute-start(bf16[96,768]{1,0:T(8,128)(2,1)S(1)} %copy-done.12), channel_id=1, source_target_pairs={{0,24},{8,16},{16,8},{24,0},{1,25},{9,17},{17,9},{25,1},{2,26},{10... | collective-permute-start | bytes 442376 | tf_op jit(solution)/shard_map/ppermute | solution.py:366
  62.7 22.4 %collective-permute-start.8 = (bf16[96,768]{1,0:T(8,128)(2,1)S(1)}, bf16[96,768]{1,0:T(8,128)(2,1)S(1)}, u32[]{:S(2)}, u32[]{:S(2)}) collective-permute-start(bf16[96,768]{1,0:T(8,128)(2,1)S(1)} %copy-done.12), channel_id=1, source_target_pairs={{0,16},{8,24},{16,0},{24,8},{1,17},{9,25},{17,1},{25,9},{2,18},{10... | collective-permute-start | bytes 442376 | tf_op jit(solution)/shard_map/ppermute | solution.py:366
  67.8 17.2 %collective-permute-start.7 = (bf16[96,768]{1,0:T(8,128)(2,1)S(1)}, bf16[96,768]{1,0:T(8,128)(2,1)S(1)}, u32[]{:S(2)}, u32[]{:S(2)}) collective-permute-start(bf16[96,768]{1,0:T(8,128)(2,1)S(1)} %copy-done.12), channel_id=1, source_target_pairs={{0,8},{8,0},{16,24},{24,16},{1,9},{9,1},{17,25},{25,17},{2,10},{10... | collective-permute-start | bytes 442376 | tf_op jit(solution)/shard_map/ppermute | solution.py:366
  80.1 4.9 %copy-start.13 = (bf16[96,768]{1,0:T(8,128)(2,1)}, bf16[96,768]{1,0:T(8,128)(2,1)S(1)}, u32[]{:S(2)}) copy-start(bf16[96,768]{1,0:T(8,128)(2,1)S(1)} %collective-permute-done.9.refs_3_) | copy-start | bytes 442372
  91.4 4.4 %collective-permute-start.10 = (bf16[4,4,24,2432]{3,2,1,0:T(8,128)(2,1)}, bf16[4,4,24,2432]{3,2,1,0:T(8,128)(2,1)}, u32[]{:S(2)}, u32[]{:S(2)}) collective-permute-start(bf16[4,4,24,2432]{3,2,1,0:T(8,128)(2,1)} %all-to-all-done.1.refs_0_), channel_id=1, source_target_pairs={{0,1},{1,0},{2,3},{3,2},{4,5},{5,4},{6,7},{7,6},{8,9},{9,8},{10,11... | collective-permute-start | bytes 5603336 | tf_op jit(solution)/shard_map/ppermute | solution.py:374
  91.4 32.7 %all-to-all-start.2 = ((bf16[4,4,96,768]{3,2,1,0:T(8,128)(2,1)}), bf16[4,4,96,768]{3,2,1,0:T(8,128)(2,1)S(1)}, u32[]{:S(2)}, u32[]{:S(2)}) async-start(bf16[4,4,96,768]{3,2,1,0:T(8,128)(2,1)} %repeat.5), calls=%async_computation.2 | async-start | bytes 4718592 | tf_op jit(solution)/shard_map/all_to_all | solution.py:370
  110.1 14.0 %copy-start.26 = (f32[4]{0:T(128)S(1)}, f32[4]{0:T(128)}, u32[]{:S(2)}) copy-start(f32[4]{0:T(128)} %param.37) | copy-start | bytes 52
  124.1 28.5 %copy-start.1 = (bf16[4,4,96,768]{3,2,1,0:T(8,128)(2,1)}, bf16[4,4,96,768]{3,2,1,0:T(8,128)(2,1)S(1)}, u32[]{:S(2)}) copy-start(bf16[4,4,96,768]{3,2,1,0:T(8,128)(2,1)S(1)} %all-to-all-done.2.refs_0_) | copy-start | bytes 7077892
  124.1 31.1 %collective-permute-start.11 = (bf16[4,4,96,768]{3,2,1,0:T(8,128)(2,1)S(1)}, bf16[4,4,96,768]{3,2,1,0:T(8,128)(2,1)}, u32[]{:S(2)}, u32[]{:S(2)}) collective-permute-start(bf16[4,4,96,768]{3,2,1,0:T(8,128)(2,1)S(1)} %all-to-all-done.2.refs_0_), channel_id=1, source_target_pairs={{0,1},{1,0},{2,3},{3,2},{4,5},{5,4},{6,7},{7,6},{8,9},{9,8},{10,11... | collective-permute-start | bytes 7077896 | tf_op jit(solution)/shard_map/ppermute | solution.py:374
  200.1 11.1 %copy-start.24 = (s32[4]{0:T(128)S(1)}, s32[4]{0:T(128)}, u32[]{:S(2)}) copy-start(s32[4]{0:T(128)} %index_ref.1) | copy-start | bytes 52
  210.7 7.4 %collective-permute-start.13 = (bf16[4,4,24,3072]{3,2,1,0:T(8,128)(2,1)}, bf16[4,4,24,3072]{3,2,1,0:T(8,128)(2,1)S(1)}, u32[]{:S(2)}, u32[]{:S(2)}) collective-permute-start(bf16[4,4,24,3072]{3,2,1,0:T(8,128)(2,1)} %get-tuple-element.167), channel_id=1, source_target_pairs={{0,1},{1,0},{2,3},{3,2},{4,5},{5,4},{6,7},{7,6},{8,9},{9,8},{10,11... | collective-permute-start | bytes 7077896 | tf_op jit(solution)/shard_map/ppermute | solution.py:374
  211.1 7.9 %collective-permute-start.12 = (bf16[4,4,96,768]{3,2,1,0:T(8,128)(2,1)}, bf16[4,4,96,768]{3,2,1,0:T(8,128)(2,1)}, u32[]{:S(2)}, u32[]{:S(2)}) collective-permute-start(bf16[4,4,96,768]{3,2,1,0:T(8,128)(2,1)} %get-tuple-element.162), channel_id=1, source_target_pairs={{0,1},{1,0},{2,3},{3,2},{4,5},{5,4},{6,7},{7,6},{8,9},{9,8},{10,11... | collective-permute-start | bytes 7077896 | tf_op jit(solution)/shard_map/ppermute | solution.py:374
  213.8 4.3 %collective-permute-start.14 = (bf16[8,128]{1,0:T(8,128)(2,1)}, bf16[8,128]{1,0:T(8,128)(2,1)S(1)}, u32[]{:S(2)}, u32[]{:S(2)}) collective-permute-start(bf16[8,128]{1,0:T(8,128)(2,1)} %get-tuple-element.168.refs_4_), channel_id=1, source_target_pairs={{0,1},{1,0},{2,3},{3,2},{4,5},{5,4},{6,7},{7,6},{8,9},{9,8},{10,11... | collective-permute-start | bytes 6152 | tf_op jit(solution)/shard_map/ppermute | solution.py:374
  218.1 0.9 copy-start.23
  218.1 1.4 copy-start.4
  226.1 64.7 %all-to-all-start.3 = ((bf16[4,4,200,768]{3,2,1,0:T(8,128)(2,1)}), bf16[4,4,200,768]{3,2,1,0:T(8,128)(2,1)}, u32[]{:S(2)}, u32[]{:S(2)}) async-start(bf16[4,4,200,768]{3,2,1,0:T(8,128)(2,1)} %pair_sum.2), calls=%async_computation.3 | async-start | bytes 9830400 | tf_op jit(solution)/shard_map/all_to_all | solution.py:370
  290.3 5.1 %collective-permute-start.15 = (bf16[4,4,24,3328]{3,2,1,0:T(8,128)(2,1)}, bf16[4,4,24,3328]{3,2,1,0:T(8,128)(2,1)S(1)}, u32[]{:S(2)}, u32[]{:S(2)}) collective-permute-start(bf16[4,4,24,3328]{3,2,1,0:T(8,128)(2,1)} %get-tuple-element.204), channel_id=1, source_target_pairs={{0,1},{1,0},{2,3},{3,2},{4,5},{5,4},{6,7},{7,6},{8,9},{9,8},{10,11... | collective-permute-start | bytes 7667720 | tf_op jit(solution)/shard_map/ppermute | solution.py:374
  295.4 1.5 copy-start.3
  301.6 11.3 %copy-start.27 = (bf16[208,768]{1,0:T(8,128)(2,1)S(1)}, bf16[208,768]{1,0:T(8,128)(2,1)}, u32[]{:S(2)}) copy-start(bf16[208,768]{1,0:T(8,128)(2,1)} %get-tuple-element.209) | copy-start | bytes 958468
  301.6 39.3 %all-to-all-start.4 = ((bf16[4,4,24,3328]{3,2,1,0:T(8,128)(2,1)}), bf16[4,4,24,3328]{3,2,1,0:T(8,128)(2,1)S(1)}, u32[]{:S(2)}, u32[]{:S(2)}) async-start(bf16[4,4,24,3328]{3,2,1,0:T(8,128)(2,1)} %pair_sum.3), calls=%async_computation.4 | async-start | bytes 5111808 | tf_op jit(solution)/shard_map/all_to_all | solution.py:370
  305.9 19.8 %collective-permute-start.16 = (bf16[208,768]{1,0:T(8,128)(2,1)}, bf16[208,768]{1,0:T(8,128)(2,1)S(1)}, u32[]{:S(2)}, u32[]{:S(2)}) collective-permute-start(bf16[208,768]{1,0:T(8,128)(2,1)} %get-tuple-element.207), channel_id=1, source_target_pairs={{0,8},{8,0},{16,24},{24,16},{1,9},{9,1},{17,25},{25,17},{2,10},{10... | collective-permute-start | bytes 958472 | tf_op jit(solution)/shard_map/ppermute | solution.py:694
  311.6 25.3 %collective-permute-start.17 = (bf16[208,768]{1,0:T(8,128)(2,1)}, bf16[208,768]{1,0:T(8,128)(2,1)S(1)}, u32[]{:S(2)}, u32[]{:S(2)}) collective-permute-start(bf16[208,768]{1,0:T(8,128)(2,1)} %get-tuple-element.208), channel_id=1, source_target_pairs={{0,16},{8,24},{16,0},{24,8},{1,17},{9,25},{17,1},{25,9},{2,18},{10... | collective-permute-start | bytes 958472 | tf_op jit(solution)/shard_map/ppermute | solution.py:694
  312.9 24.0 %collective-permute-start.18 = (bf16[208,768]{1,0:T(8,128)(2,1)S(1)}, bf16[208,768]{1,0:T(8,128)(2,1)S(1)}, u32[]{:S(2)}, u32[]{:S(2)}) collective-permute-start(bf16[208,768]{1,0:T(8,128)(2,1)S(1)} %copy-done.27), channel_id=1, source_target_pairs={{0,24},{8,16},{16,8},{24,0},{1,25},{9,17},{17,9},{25,1},{2,26},{10... | collective-permute-start | bytes 958472 | tf_op jit(solution)/shard_map/ppermute | solution.py:694
  323.4 29.8 %copy-start.25 = (f32[4,1]{1,0:T(4,128)S(1)}, f32[4,1]{1,0:T(4,128)}, u32[]{:S(2)}) copy-start(f32[4,1]{1,0:T(4,128)} %get-tuple-element.158) | copy-start | bytes 52
  325.7 11.2 %copy-start.6 = (bf16[208,768]{1,0:T(8,128)(2,1)}, bf16[208,768]{1,0:T(8,128)(2,1)S(1)}, u32[]{:S(2)}) copy-start(bf16[208,768]{1,0:T(8,128)(2,1)S(1)} %collective-permute-done.16.refs_1_) | copy-start | bytes 958468
  337.6 0.7 copy-start.8
  340.9 1.5 copy-start
  345.2 10.6 %collective-permute-start.19 = (bf16[24,3328]{1,0:T(8,128)(2,1)}, bf16[24,3328]{1,0:T(8,128)(2,1)S(1)}, u32[]{:S(2)}, u32[]{:S(2)}) collective-permute-start(bf16[24,3328]{1,0:T(8,128)(2,1)} %get-tuple-element.213), channel_id=1, source_target_pairs={{0,8},{8,0},{16,24},{24,16},{1,9},{9,1},{17,25},{25,17},{2,10},{10... | collective-permute-start | bytes 479240 | tf_op jit(solution)/shard_map/ppermute | solution.py:694
  350.5 14.2 %collective-permute-start.20 = (bf16[24,3328]{1,0:T(8,128)(2,1)}, bf16[24,3328]{1,0:T(8,128)(2,1)S(1)}, u32[]{:S(2)}, u32[]{:S(2)}) collective-permute-start(bf16[24,3328]{1,0:T(8,128)(2,1)} %get-tuple-element.214), channel_id=1, source_target_pairs={{0,16},{8,24},{16,0},{24,8},{1,17},{9,25},{17,1},{25,9},{2,18},{10... | collective-permute-start | bytes 479240 | tf_op jit(solution)/shard_map/ppermute | solution.py:694
  351.8 12.9 %collective-permute-start.21 = (bf16[24,3328]{1,0:T(8,128)(2,1)}, bf16[24,3328]{1,0:T(8,128)(2,1)S(1)}, u32[]{:S(2)}, u32[]{:S(2)}) collective-permute-start(bf16[24,3328]{1,0:T(8,128)(2,1)} %get-tuple-element.215), channel_id=1, source_target_pairs={{0,24},{8,16},{16,8},{24,0},{1,25},{9,17},{17,9},{25,1},{2,26},{10... | collective-permute-start | bytes 479240 | tf_op jit(solution)/shard_map/ppermute | solution.py:694
  355.8 9.0 %copy-start.9 = (bf16[24,3328]{1,0:T(8,128)(2,1)}, bf16[24,3328]{1,0:T(8,128)(2,1)S(1)}, u32[]{:S(2)}) copy-start(bf16[24,3328]{1,0:T(8,128)(2,1)S(1)} %collective-permute-done.19.refs_1_) | copy-start | bytes 479236
  364.8 0.7 copy-start.11
  (7 other events, 4.6 us)
Sparse Core Ops, SparseCore 0:
  11.5 95.5 all-gather.1

commit v3 on v2

--- a/solution.py
+++ b/solution.py
@@ -11,8 +11,6 @@
 EPS = 1e-12
 QB, VB, OB, FG, FS, DB, SG, SS, UB = range(9)
 bf16, f32 = jnp.bfloat16, jnp.float32
-ERFC_P = 0.33
-ERFC_Q = (-0.1359291, 0.46268956, -0.35544136, 0.41254396, 0.04500932, 0.20192425, 0.18283717, 0.18636611)
 
 
 def dot(a, b, ca=1, cb=0):
@@ -55,7 +53,8 @@
     return jax.ShapeDtypeStruct(shape, dtype)
 
 
-def attend_body(x_ref, w_ref, v_ref, qkv_ref, soft_ref, ctx_ref):
+def attend_body(x_ref, w_ref, v_ref, *refs):
+    qkv_ref, soft_ref, ctx_ref = refs[-3:]
     length = x_ref.shape[0]
     gc = ctx_ref.shape[1]
     mixed = dot(x_ref[...], w_ref[...])
@@ -80,27 +79,28 @@
     ctx_ref[...] = total.astype(bf16)
 
 
-def attend(x, w, vec, g, seqs):
+def attend(x, w, vec, seqs, groups, at, into=()):
     T, D = x.shape
-    gc = w.shape[1] // 3
+    gc = D // groups
     hg = gc // HEAD_DIM
     L = T // seqs
+    count = w.shape[1] // (3 * gc)
+    ins = (x, w, vec, *into)
     return run(
-        attend_body, "attend", (seqs,), (x, w, vec),
-        [rows_spec(L, D), full_spec(w.shape), pl.BlockSpec((vec.shape[0], gc), lambda i: (0, g))],
-        [sds((T, 3 * gc), bf16), sds((hg, T, L), bf16), sds((T, gc), bf16)],
-        [rows_spec(L, 3 * gc), pl.BlockSpec((hg, L, L), lambda i: (0, i, 0)), rows_spec(L, gc)],
-        flops=2 * T * D * 3 * gc + 16 * T * L * gc, moved=2 * (T * D + w.size + 4 * T * gc + hg * T * L),
-    )
-
-
-def erfc_parts(u):
-    e = jnp.exp(u * u * -0.5)
-    t = 1.0 / (1.0 + (ERFC_P * math.sqrt(0.5)) * jnp.abs(u))
-    q = jnp.full_like(t, 0.5 * ERFC_Q[0])
-    for c in ERFC_Q[1:]:
-        q = q * t + 0.5 * c
-    return q * t * e, e
+        attend_body, "attend", (count, seqs), ins,
+        [
+            pl.BlockSpec((L, D), lambda g, s: (s, 0)), pl.BlockSpec((D, 3 * gc), lambda g, s: (0, g)),
+            pl.BlockSpec((vec.shape[0], gc), lambda g, s: (0, at + g)),
+        ] + [pl.BlockSpec(memory_space=pl.ANY)] * len(into),
+        [sds((groups, T, 3 * gc), bf16), sds((groups, hg, T, L), bf16), sds((groups, T, gc), bf16)],
+        [
+            pl.BlockSpec((None, L, 3 * gc), lambda g, s: (at + g, s, 0)),
+            pl.BlockSpec((None, hg, L, L), lambda g, s: (at + g, 0, s, 0)),
+            pl.BlockSpec((None, L, gc), lambda g, s: (at + g, s, 0)),
+        ],
+        flops=count * (2 * T * D * 3 * gc + 16 * T * L * gc), moved=2 * (T * D + w.size + count * (4 * T * gc + hg * T * L)),
+        alias={3 + i: i for i in range(len(into))},
+    )
 
 
 def norm_rows(h):
@@ -116,14 +116,11 @@
     return inv * (scaled - jnp.mean(scaled, axis=-1, keepdims=True) - n * jnp.mean(scaled * n, axis=-1, keepdims=True))
 
 
-def up_body(ngroups, step, *refs):
-    ctx_refs = refs[:ngroups]
-    x_ref, wo_ref, v_ref, wu_ref, ub_ref = refs[ngroups : ngroups + 5]
-    n_ref, inv_ref, first_ref, act_ref, slope_ref = refs[ngroups + 5 :]
-    gc = ctx_refs[0].shape[1]
+def up_body(step, ctx_ref, x_ref, wo_ref, v_ref, wu_ref, ub_ref, n_ref, inv_ref, first_ref, act_ref, slope_ref):
+    G, _, gc = ctx_ref.shape
     hidden = x_ref[...].astype(f32) + v_ref[OB : OB + 1, :]
-    for g, c in enumerate(ctx_refs):
-        hidden += dot(c[...], wo_ref[g * gc : (g + 1) * gc, :])
+    for g in range(G):
+        hidden += dot(ctx_ref[g], wo_ref[g * gc : (g + 1) * gc, :])
     n, inv = norm_rows(hidden)
     n_ref[...] = n
     inv_ref[...] = inv
@@ -133,29 +130,30 @@
     for at in range(0, ff, step):
         cols = slice(at, at + step)
         u = dot(first, wu_ref[:, cols]) + ub_ref[:, cols]
-        tail, e = erfc_parts(u)
-        phi = jnp.where(u < 0, tail, 1.0 - tail)
+        phi = 0.5 + 0.5 * lax.erf(u * math.sqrt(0.5))
         act_ref[:, cols] = (u * phi).astype(bf16)
-        slope_ref[:, cols] = (phi + u * e * (1.0 / math.sqrt(2 * math.pi))).astype(bf16)
-
-
-def up(ctxs, x, wo, vec, wu, ub, rows, step=512):
+        slope_ref[:, cols] = (phi + u * jnp.exp(u * u * -0.5) * (1.0 / math.sqrt(2 * math.pi))).astype(bf16)
+
+
+def out_spec(D, F):
+    return pl.BlockSpec((D, D), lambda i: (0, F // D))
+
+
+def up(ctx, x, vec, wide, ub, rows, step=512):
     T, D = x.shape
     F = ub.shape[1]
     return run(
-        functools.partial(up_body, len(ctxs), step), "up", (T // rows,), (*ctxs, x, wo, vec, wu, ub),
-        [rows_spec(rows, c.shape[1]) for c in ctxs] + [rows_spec(rows, D)] + [full_spec(wo.shape), full_spec(vec.shape), full_spec((D, F)), full_spec(ub.shape)],
+        functools.partial(up_body, step), "up", (T // rows,), (ctx, x, wide, vec, wide, ub),
+        [pl.BlockSpec((ctx.shape[0], rows, ctx.shape[2]), lambda i: (0, i, 0)), rows_spec(rows, D)] + [out_spec(D, F), full_spec(vec.shape), full_spec((D, F)), full_spec(ub.shape)],
         [sds((T, D), f32), sds((T, 1), f32), sds((T, D), bf16), sds((T, F), bf16), sds((T, F), bf16)],
         [rows_spec(rows, D), rows_spec(rows, 1), rows_spec(rows, D), rows_spec(rows, F), rows_spec(rows, F)],
-        flops=2 * T * D * (D + F), moved=T * D * 10 + 4 * T * F + 2 * (wo.size + wu.size),
-    )
-
-
-def add_rows(ref, value):
-    @pl.when(pl.program_id(0) == 0)
-    def _():
-        ref[...] = jnp.zeros_like(ref)
-    ref[...] += jnp.sum(value, axis=0, keepdims=True)
+        flops=2 * T * D * (D + F), moved=T * D * 10 + 4 * T * F + 2 * D * (D + F),
+    )
+
+
+def add_rows(ref, value, cols=slice(None), axis=0):
+    held = jnp.where(pl.program_id(axis) == 0, 0.0, ref[:, cols])
+    ref[:, cols] = held + jnp.sum(value, axis=0, keepdims=True)
 
 
 def down_body(step, first_ref, act_ref, slope_ref, w_ref, v_ref, og_ref, lead_ref,
@@ -181,10 +179,7 @@
         cols = slice(at, at + step)
         inner = (dot(feed, w_ref[cols, :], 1, 1) * slope_ref[:, cols].astype(f32)).astype(bf16)
         inner_ref[:, cols] = inner
-        @pl.when(pl.program_id(0) == 0)
-        def _():
-            gub_ref[:, cols] = jnp.zeros((1, step), f32)
-        gub_ref[:, cols] += jnp.sum(inner.astype(f32), axis=0, keepdims=True)
+        add_rows(gub_ref, inner.astype(f32), cols)
 
 
 def down(first, act, slope, w, vec, og, lead, seqs, step=512):
@@ -216,15 +211,15 @@
     bctx_ref[...] = dot(att, wo_ref[...], 1, 1).astype(bf16)
 
 
-def mid(two, inner, wu, n, inv, vec, wo, rows):
+def mid(two, inner, wide, n, inv, vec, rows):
     T, D = two.shape
     F = inner.shape[1]
     return run(
-        mid_body, "mid", (T // rows,), (two, inner, wu, n, inv, vec, wo),
-        [rows_spec(rows, D), rows_spec(rows, F), full_spec((D, F)), rows_spec(rows, D), rows_spec(rows, 1), full_spec(vec.shape), full_spec(wo.shape)],
+        mid_body, "mid", (T // rows,), (two, inner, wide, n, inv, vec, wide),
+        [rows_spec(rows, D), rows_spec(rows, F), full_spec((D, F)), rows_spec(rows, D), rows_spec(rows, 1), full_spec(vec.shape), out_spec(D, F)],
         [sds((T, D), f32), sds((T, D), bf16), sds((T, D), bf16)] + [sds((1, D), f32)] * 3,
         [rows_spec(rows, D)] * 3 + [full_spec((1, D))] * 3,
-        flops=2 * T * D * (F + D), moved=2 * T * F + 16 * T * D + 2 * wu.size,
+        flops=2 * T * D * (F + D), moved=2 * T * F + 16 * T * D + 2 * D * (D + F),
     )
 
 
@@ -255,38 +250,45 @@
     out_ref[:, :gc] = dq
     out_ref[:, gc : 2 * gc] = (dk * scale).astype(bf16)
     out_ref[:, 2 * gc :] = dv
-    add_rows(gq_ref, dq.astype(f32))
-    add_rows(gv_ref, dv.astype(f32))
-
-
-def attend_back(qkv, soft, ctx, bctx, g, seqs):
-    T, gc = ctx.shape
+    add_rows(gq_ref, dq.astype(f32), axis=1)
+    add_rows(gv_ref, dv.astype(f32), axis=1)
+
+
+def attend_back(qkv, soft, ctx, bctx, seqs):
+    G, T, gc = ctx.shape
     hg = gc // HEAD_DIM
     L = T // seqs
+    line = lambda w: pl.BlockSpec((None, L, w), lambda g, s: (g, s, 0))
+    row = pl.BlockSpec((1, gc), lambda g, s: (0, g))
     return run(
-        attend_back_body, "attend_back", (seqs,), (qkv, soft, ctx, bctx),
-        [rows_spec(L, 3 * gc), pl.BlockSpec((hg, L, L), lambda i: (0, i, 0)), rows_spec(L, gc), pl.BlockSpec((L, gc), lambda i: (i, g))],
-        [sds((T, 3 * gc), bf16), sds((1, gc), f32), sds((1, gc), f32)],
-        [rows_spec(L, 3 * gc), full_spec((1, gc)), full_spec((1, gc))],
-        flops=32 * T * L * gc, moved=2 * (8 * T * gc + hg * T * L),
-    )
-
-
-def tokens_back_body(ngroups, one_ref, *refs):
+        attend_back_body, "attend_back", (G, seqs), (qkv, soft, ctx, bctx),
+        [
+            line(3 * gc), pl.BlockSpec((None, hg, L, L), lambda g, s: (g, 0, s, 0)), line(gc),
+            pl.BlockSpec((L, gc), lambda g, s: (s, g)),
+        ],
+        [sds((G, T, 3 * gc), bf16), sds((1, G * gc), f32), sds((1, G * gc), f32)], [line(3 * gc), row, row],
+        flops=G * 32 * T * L * gc, moved=2 * G * (8 * T * gc + hg * T * L),
+    )
+
+
+def tokens_back_body(one_ref, mixed_ref, *refs):
     total = one_ref[...]
-    for g in range(ngroups):
-        total += dot(refs[g][...], refs[ngroups + g][...], 1, 1)
+    width = mixed_ref.shape[2]
+    g = 0
+    for w_ref in refs[:-1]:
+        for at in range(0, w_ref.shape[1], width):
+            total += dot(mixed_ref[g], w_ref[:, at : at + width], 1, 1)
+            g += 1
     refs[-1][...] = total.astype(bf16)
 
 
 def tokens_back(one, mixed, ws, rows):
     T, D = one.shape
-    n = len(mixed)
+    G, _, width = mixed.shape
     return run(
-        functools.partial(tokens_back_body, n), "tokens_back", (T // rows,), (one, *mixed, *ws),
-        [rows_spec(rows, D)] + [rows_spec(rows, m.shape[1]) for m in mixed] + [full_spec(w.shape) for w in ws],
-        sds((T, D), bf16), rows_spec(rows, D),
-        flops=2 * T * D * sum(m.shape[1] for m in mixed), moved=T * D * 12,
+        tokens_back_body, "tokens_back", (T // rows,), (one, mixed, *ws),
+        [rows_spec(rows, D), pl.BlockSpec((G, rows, width), lambda i: (0, i, 0))] + [full_spec(w.shape) for w in ws],
+        sds((T, D), bf16), rows_spec(rows, D), flops=2 * T * D * G * width, moved=T * D * 12,
     )
 
 
@@ -333,11 +335,12 @@
         for m in range(3):
             rest_ref[:, at : at + gc] = w_ref[:, m * D + g * gc : m * D + (g + 1) * gc]
             at += gc
-    rest_ref[:, at : at + D] = o_ref[...]
-    rest_ref[:, at + D :] = r_ref[...]
     trows, width = t_ref.shape
-    at = u_ref.shape[1]
-    up_ref[:, :at] = u_ref[...]
+    F = u_ref.shape[1]
+    at = F + D + r_ref.shape[1]
+    up_ref[:, :F] = u_ref[...]
+    up_ref[:, F : F + D] = o_ref[...]
+    up_ref[:, F + D : at] = r_ref[...]
     for lo in range(0, trows, rows):
         n = min(rows, trows - lo)
         up_ref[:n, at : at + width] = t_ref[lo : lo + n, :]
@@ -349,8 +352,8 @@
 def pack(w, o, r, u, t, vectors, gc):
     rows, D = o.shape
     head = 3 * gc + LANES
-    rest = 3 * D - 3 * gc + D + r.shape[1]
-    ups = u.shape[1] + -(-t.shape[0] // rows) * t.shape[1]
+    rest = 3 * D - 3 * gc
+    ups = u.shape[1] + D + r.shape[1] + -(-t.shape[0] // rows) * t.shape[1]
     return once(
         functools.partial(pack_body, D, gc, len(vectors)), "pack", (w, o, r, u, t, *vectors), [None] * (5 + len(vectors)),
         [sds((rows, head), bf16), sds((rows, rest), bf16), sds((rows, ups), bf16)],
@@ -446,46 +449,52 @@
     return [o.reshape(total, o.shape[-1]) for o in outs[: len(cuts)]] + list(outs[len(cuts) :])
 
 
-def hand_out(me_ref, held, keep_ref, send_ref):
-    Z, R = held.shape[:2]
-    for r in range(R):
-        for z in range(Z):
-            keep_ref[r, z] = held[z, r, me_ref[2]].astype(bf16)
-            send_ref[r, z] = held[z, r, 1 - me_ref[2]].astype(bf16)
-
-
-def grads_body(counts, nvec, has_retr, me_ref, *refs):
-    at_held = len(refs) - 1 - (2 if nvec else 0)
-    held = refs[at_held]
-    Z, R, _, rows, _ = held.shape
-    D = Z * R * 2 * rows
-    at, col = 0, 0
-    for n in counts:
-        y = refs[at + n][...]
-        parts = [dot(r[...], y, 0, 0) for r in refs[at : at + n]]
-        part = parts[0] if n == 1 else jnp.concatenate(parts, axis=0)
-        w = part.shape[1]
-        held[:, :, :, :, col : col + w] = part.reshape(Z, R, 2, rows, w)
-        at += n + 1
-        col += w
+def hand_out(me_ref, part, Z, R, keep_ref, send_ref, cols=slice(None)):
+    rows = part.shape[0] // (Z * R * 2)
+    part = part.reshape(Z, R, 2, rows, part.shape[1])
+    first = me_ref[2] == 0
+    for z in range(Z):
+        for r in range(R):
+            one, two = part[z, r, 0], part[z, r, 1]
+            keep_ref[r, z, :, cols] = jnp.where(first, one, two).astype(bf16)
+            send_ref[r, z, :, cols] = jnp.where(first, two, one).astype(bf16)
+
+
+def grads_body(plan, nvec, has_retr, Z, R, me_ref, *refs):
+    at_out = len(refs) - 2 - (2 if nvec else 0)
+    keep_ref, send_ref = refs[at_out : at_out + 2]
+    col = 0
+
+    def give(part):
+        nonlocal col
+        hand_out(me_ref, part, Z, R, keep_ref, send_ref, slice(col, col + part.shape[1]))
+        col += part.shape[1]
+
+    def read(spot):
+        return refs[spot[0]][...] if spot[1] is None else refs[spot[0]][spot[1]]
+
+    for lefts, right in plan:
+        y = read(right)
+        parts = [dot(read(left), y, 0, 0) for left in lefts]
+        give(parts[0] if len(parts) == 1 else jnp.concatenate(parts, axis=0))
+    at = at_out - nvec
     if has_retr:
-        w = refs[at].shape[1]
-        held[:, :, :, :, col : col + w] = refs[at][...].reshape(Z, R, 2, rows, w)
-        at += 1
-        col += w
+        give(refs[at - 1][...])
     if nvec:
         turn = refs[-1]
+        D = turn.shape[1]
+        rows = D // (Z * R * 2)
         turn[...] = jnp.zeros_like(turn)
         row, lane = 0, 0
-        for r in refs[at : at + nvec]:
+        for r in refs[at:at_out]:
             w = r.shape[1]
             if w <= D:
                 turn[row : row + 1, lane : lane + w] = r[...]
                 lane += w
                 if lane == D:
                     row, lane = row + 1, 0
-        total = turn[...].T.reshape(Z, R, 2, rows, LANES)
-        r = refs[at + nvec - 1]
+        total = turn[...].T
+        r = refs[at_out - 1]
         if r.shape[1] > D:
             Q = r.shape[1] // D
             wide = refs[-2]
@@ -496,8 +505,7 @@
             spread = wide[...].T.reshape(Z * R * 2, Q, rows, LANES)
             for q in range(Q):
                 total += spread[:, q].reshape(total.shape)
-        held[:, :, :, :, col:] = total
-    hand_out(me_ref, held, refs[at_held - 2], refs[at_held - 1])
+        give(total)
 
 
 def hand_out_plain(me, whole, Z, N, rows):
@@ -505,38 +513,37 @@
     return [lax.dynamic_index_in_dim(whole, c, 2, keepdims=False) for c in (me[2], 1 - me[2])]
 
 
-def grads(me, Z, N, name, products, retr=None, vectors=(), tile=None):
-    counts = [len(xs) for xs, _ in products]
-    D = sum(x.shape[1] for x in products[0][0])
+def grads(me, Z, N, name, arrays, plan, retr=None, vectors=(), tile=None):
+    read = lambda spot: arrays[spot[0]] if spot[1] is None else arrays[spot[0]][spot[1]]
+    shape = lambda spot: arrays[spot[0]].shape[-2:]
+    D = sum(shape(left)[1] for left in plan[0][0])
+    T = shape(plan[0][1])[0]
     rows, R = D // (Z * N), N // 2
-    width = sum(y.shape[1] for _, y in products) + (0 if retr is None else retr.shape[1]) + (LANES if vectors else 0)
+    width = sum(shape(right)[1] for _, right in plan) + (0 if retr is None else retr.shape[1]) + (LANES if vectors else 0)
     if rows % 8:
-        cols = [jnp.concatenate([dot(x, y, 0, 0) for x in xs], axis=0) for xs, y in products]
+        cols = [jnp.concatenate([dot(read(x), read(y), 0, 0) for x in xs], axis=0) for xs, y in plan]
         cols += [] if retr is None else [retr]
         if vectors:
-            narrow = jnp.concatenate([v for v in vectors if v.shape[1] <= D], axis=1).reshape(-1, D)
+            narrow = [jnp.concatenate([v for v in vectors if v.shape[1] <= D], axis=1).reshape(-1, D)]
             wide = [v.reshape(Z * N, -1, rows).swapaxes(0, 1).reshape(-1, D) for v in vectors if v.shape[1] > D]
-            turned = jnp.concatenate([narrow] + wide, axis=0).T
+            turned = jnp.concatenate(narrow + wide, axis=0).T
             cols += [turned, jnp.zeros((D, LANES - turned.shape[1]), f32)]
         return hand_out_plain(me, jnp.concatenate(cols, axis=1), Z, N, rows)
-    ins = [a for xs, y in products for a in (*xs, y)] + ([] if retr is None else [retr]) + list(vectors)
-    T = products[0][1].shape[0]
+    ins = [*arrays] + ([] if retr is None else [retr]) + list(vectors)
     if tile is None:
         tile, specs, grid = width, [full_spec(a.shape) for a in ins], (1,)
     else:
         specs, grid = [full_spec(ins[0].shape), pl.BlockSpec((T, tile), lambda i: (0, i))], (width // tile,)
     return run(
-        functools.partial(grads_body, counts, len(vectors), retr is not None), name, grid, (me, *ins), [SMEM] + specs,
+        functools.partial(grads_body, plan, len(vectors), retr is not None, Z, R), name, grid, (me, *ins), [SMEM] + specs,
         [sds((R, Z, rows, width), bf16)] * 2, [pl.BlockSpec((R, Z, rows, tile), lambda i: (0, 0, 0, i))] * 2,
-        scratch=[pltpu.VMEM((Z, R, 2, rows, tile), f32)]
-        + ([pltpu.VMEM((LANES, max(D, vectors[-1].shape[1])), f32), pltpu.VMEM((LANES, D), f32)] if vectors else []),
+        scratch=[pltpu.VMEM((LANES, max(D, vectors[-1].shape[1])), f32), pltpu.VMEM((LANES, D), f32)] if vectors else [],
         flops=2 * T * D * width, moved=2 * T * (D + width) + 2 * D * width,
     )
 
 
-def down_grad_body(me_ref, x_ref, y_ref, keep_ref, send_ref, held):
-    held[...] = dot(x_ref[...], y_ref[...], 0, 0).reshape(held.shape)
-    hand_out(me_ref, held, keep_ref, send_ref)
+def down_grad_body(me_ref, x_ref, y_ref, keep_ref, send_ref):
+    hand_out(me_ref, dot(x_ref[...], y_ref[...], 0, 0), 1, keep_ref.shape[0], keep_ref, send_ref)
 
 
 def down_grad(me, Z, N, act, feed):
@@ -549,7 +556,7 @@
         down_grad_body, "down_grad", (Z,), (me, act, feed),
         [SMEM, pl.BlockSpec((T, N * rows), lambda i: (0, i)), full_spec(feed.shape)],
         [sds((R, Z, rows, D), bf16)] * 2, [pl.BlockSpec((R, 1, rows, D), lambda i: (0, i, 0, 0))] * 2,
-        scratch=[pltpu.VMEM((1, R, 2, rows, D), f32)], flops=2 * T * F * D, moved=2 * (T * F + T * D + F * D),
+        flops=2 * T * F * D, moved=2 * (T * F + T * D + F * D),
     )
 
 
@@ -633,26 +640,26 @@
 
 
 def last_body(n, cuts, G, gc, *refs):
-    parts, (in_ref, out_ref, retr_ref, small_ref, turn) = refs[:n], refs[n:]
+    parts, (out_ref, in_ref, retr_ref, small_ref, turn) = refs[:n], refs[n:]
     rows = parts[0].shape[0]
     out_ref[...] = total_of(parts, *cuts[0])
     for g in range(G):
-        group = total_of(parts, *cuts[1 + g])
         for m in range(3):
-            in_ref[:, (m * G + g) * gc : (m * G + g + 1) * gc] = group[:, m * gc : (m + 1) * gc]
+            lo = cuts[1 + g][0] + m * gc
+            in_ref[:, (m * G + g) * gc : (m * G + g + 1) * gc] = total_of(parts, lo, lo + gc)
     retr_ref[...] = total_of(parts, *cuts[1 + G])
     turn[...] = jnp.zeros_like(turn)
     turn[0:rows, :] = total_of(parts, *cuts[2 + G])
     small_ref[...] = turn[...].T[: small_ref.shape[0], :rows]
 
 
-def last_sum(ins, widths, turned, G, gc):
+def last_sum(ins, widths, turned, G, gc, tok):
     rows = ins[0].shape[0]
     cuts = cut_points(widths)
-    shapes = [(rows, 3 * G * gc), (rows, widths[0]), (rows, widths[-2]), (turned, rows)]
+    shapes = [(rows, widths[0]), (rows, 3 * G * gc), (rows, widths[-2]), (turned, rows)]
     return once(
-        functools.partial(last_body, len(ins), cuts, G, gc), "last_sum", ins, [None] * len(ins), [sds(s, f32) for s in shapes],
-        scratch=[pltpu.VMEM((LANES, LANES), f32)], moved=12 * rows * cuts[-1][1],
+        functools.partial(last_body, len(ins), cuts, G, gc), "last_sum", (after(ins[0], tok), *ins[1:]), [None] * len(ins),
+        [sds(s, f32) for s in shapes], scratch=[pltpu.VMEM((LANES, LANES), f32)], moved=12 * rows * cuts[-1][1],
     )
 
 
@@ -694,14 +701,14 @@
     return [sums[0]] + [lax.ppermute(sums[k], "dp", pairs(len(sums), k)) for k in range(1, len(sums))]
 
 
-def lookup_body(F, trows, rows, index_ref, sg_ref, w_ref, r_ref, chosen_ref, back_ref, lead_ref, held, sem):
+def lookup_body(start, trows, rows, index_ref, sg_ref, w_ref, r_ref, chosen_ref, back_ref, lead_ref, held, sem):
     seqs, _, width = held.shape
     copies = []
     for s in range(seqs):
         owner, within = index_ref[s] // trows, index_ref[s] % trows
         at = owner * rows + within % rows
         row = pl.multiple_of((at // 16) * 16, 16)
-        col = pl.multiple_of(F + width * (within // rows), LANES)
+        col = pl.multiple_of(start + width * (within // rows), LANES)
         copies.append(
             (pltpu.make_async_copy(w_ref.at[pl.ds(row, 16), pl.ds(col, width)], held.at[s], sem.at[s]), at % 16)
         )
@@ -719,12 +726,13 @@
         lead_ref[s] = lead[s : s + 1, :]
 
 
-def lookup(index, sg, table, wr, F, trows, rows):
-    seqs, width = sg.shape[0], wr.shape[1]
+def lookup(index, sg, wide, F, D, width, trows, rows):
+    seqs = sg.shape[0]
     return once(
-        functools.partial(lookup_body, F, trows, rows), "lookup", (index, sg, table, wr), [SMEM, None, ANY, None],
-        [sds((16, width), f32), sds((16, width), f32), sds((seqs, 1, wr.shape[0]), f32)],
-        scratch=[pltpu.VMEM((seqs, 16, width), bf16), pltpu.SemaphoreType.DMA((seqs,))], moved=4 * wr.size,
+        functools.partial(lookup_body, F + D + width, trows, rows), "lookup", (index, sg, wide, wide),
+        [SMEM, None, ANY, pl.BlockSpec((D, width), lambda i: (0, (F + D) // width))],
+        [sds((16, width), f32), sds((16, width), f32), sds((seqs, 1, D), f32)],
+        scratch=[pltpu.VMEM((seqs, 16, width), bf16), pltpu.SemaphoreType.DMA((seqs,))], moved=4 * D * width,
     )
 
 
@@ -744,13 +752,14 @@
     term_ref[...] = jnp.concatenate([sg_ref[...] * projected, ids], axis=0).astype(bf16)
 
 
-def score(top, wr, chosen, back, sg, index):
+def score(top, wide, F, chosen, back, sg, index):
     seqs, _, D = top.shape
-    width = wr.shape[1]
+    width = chosen.shape[1]
     return once(
-        score_body, "score", (top, wr, chosen, back, sg, index), [None] * 6,
+        score_body, "score", (top, wide, chosen, back, sg, index),
+        [None, pl.BlockSpec((D, width), lambda i: (0, (F + D) // width))] + [None] * 4,
         [sds((seqs, 1), f32), sds((D, width), f32), sds((2 * seqs, width), bf16)],
-        scratch=[pltpu.VMEM((16, D), f32)], moved=8 * wr.size,
+        scratch=[pltpu.VMEM((16, D), f32)], moved=8 * D * width,
     )
 
 
@@ -798,56 +807,48 @@
         v.reshape(1, -1)
         for v in (query_bias, value_bias, output_bias, first_gain, first_shift, down_bias, second_gain, second_shift, up_bias)
     ]
-    head, rest, wu = pack(input_weight, output_weight, retriever_weight, up_weight, document_table, vectors, gc)
-    wu = lax.all_gather(wu, both, axis=0, tiled=True)
+    head, rest, wide = pack(input_weight, output_weight, retriever_weight, up_weight, document_table, vectors, gc)
+    wide = lax.all_gather(wide, both, axis=0, tiled=True)
     head = repeat(along_dp(head, Z), R)
     rest = along_dp(after(rest, head), Z)
     head = between_chips(head, N)
-    win = [None] * G
-    win[0], small, vec = place(me, [head, other_core(head, N)], Z, [3 * gc, LANES], turned=16)
+    win_one, small, vec = place(me, [head, other_core(head, N)], Z, [3 * gc, LANES], turned=16)
     rest = repeat([after(p, vec) for p in rest], R)
     wd = along_dp(after(down_weight, rest), Z)
     rest = between_chips(rest, N)
 
-    qkv, soft, ctx = [None] * G, [None] * G, [None] * G
-
-    def attend_group(g, tok):
-        qkv[g], soft[g], ctx[g] = attend(after(tokens, tok), win[g], vec, g, seqs)
-
     ub = bias_row(small, vec, Z, N, Q)
-    attend_group(0, ub)
-    wd = repeat([after(w, ctx[0]) for w in wd], R)
+    held = attend(after(tokens, ub), win_one, vec, seqs, G, 0)
+    wd = repeat([after(w, held[2]) for w in wd], R)
     rest = after(rest, wd)
-    *win[1:], wo, wr = place(me, [rest, other_core(rest, N)], Z, [3 * gc] * (G - 1) + [D, Rw])
+    (win_two,) = place(me, [rest, other_core(rest, N)], Z, [3 * gc * (G - 1)])
     wd = between_chips(wd, N)
-    for g in range(1, G):
-        attend_group(g, ctx[g - 1])
-    wd = after(wd, ctx[G - 1])
-    n, inv, first, act, slope = up(ctx, tokens, wo, vec, wu, ub, L)
+    qkv, soft, ctx = attend(tokens, win_two, vec, seqs, G, 1, held)
+    wd = after(wd, ctx)
+    n, inv, first, act, slope = up(ctx, tokens, vec, wide, ub, L)
     (wd,) = place(me, [after(wd, first), other_core(wd, N)], Z, [D])
-    chosen, back_projected, lead = lookup(document_index, score_grad.reshape(seqs, 1), after(wu, first), wr, F, trows, rows)
+    chosen, back_projected, lead = lookup(document_index, score_grad.reshape(seqs, 1), after(wide, first), F, D, Rw, trows, rows)
     final, top, two, feed, inner, gsg, gss, gdb, gub = down(first, act, slope, wd, vec, output_grad, lead, seqs)
-    scores, retriever_back, term = score(top, wr, chosen, back_projected, score_grad.reshape(seqs, 1), document_index.reshape(seqs, 1))
+    scores, retriever_back, term = score(top, wide, F, chosen, back_projected, score_grad.reshape(seqs, 1), document_index.reshape(seqs, 1))
     down_parts = down_grad(me, Z, N, act, feed)
-    up_parts = grads(me, Z, N, "up_grad", [([after(first, *down_parts)], inner)], tile=D)
+    up_parts = grads(me, Z, N, "up_grad", [after(first, *down_parts), inner], [([(0, None)], (1, None))], tile=D)
     feed_sums = pair_sum([down_parts, up_parts], N, up_parts[0], me, term)
-    one, att, bctx, gfg, gfs, gob = mid(after(two, feed_sums), inner, wu, n, inv, vec, wo, L)
-    mixed, gq, gv = [None] * G, [None] * G, [None] * G
-    for g in range(G):
-        mixed[g], gq[g], gv[g] = attend_back(
-            qkv[g], soft[g], ctx[g], after(bctx, mixed[g - 1]) if g else bctx, g, seqs
-        )
+    one, att, bctx, gfg, gfs, gob = mid(after(two, feed_sums), inner, wide, n, inv, vec, L)
+    mixed, gq, gv = attend_back(qkv, soft, ctx, after(bctx, feed_sums), seqs)
     parts = grads(
-        me, Z, N, "mix_grad", [(ctx, att)] + [([tokens], m) for m in mixed],
-        retr=retriever_back, vectors=gq + gv + [gob, gfg, gfs, gdb, gsg, gss, gub],
-    )
-    feed_sums = chips_sum(me, between_chips(feed_sums, N), parts[0], term.shape)
-    mix_sums = pair_sum([parts], N, feed_sums[0])
-    back_tokens = tokens_back(after(one, mix_sums), mixed, win, L)
-    down_back, up_back, table_back = last_feed(me, along_dp_sums(feed_sums), F, back_tokens, trows, term.shape, N)
-    mix_sums = chips_sum(me, between_chips(mix_sums, N), down_back)
-    input_back, output_back, retriever_back, small = last_sum(
-        along_dp_sums(mix_sums), [D] + [3 * gc] * G + [Rw, LANES], 16, G, gc
+        me, Z, N, "mix_grad", [ctx, att, tokens, mixed],
+        [([(0, g) for g in range(G)], (1, None))] + [([(2, None)], (3, g)) for g in range(G)],
+        retr=retriever_back, vectors=[gq, gv, gob, gfg, gfs, gdb, gsg, gss, gub],
+    )
+    mix_pair = pair_sum([parts], N, parts[0])
+    feed_sums = between_chips(feed_sums, N)
+    mix_sums = between_chips(after(mix_pair, feed_sums), N)
+    feed_sums = chips_sum(me, feed_sums, mix_pair, term.shape)
+    back_tokens = tokens_back(after(one, feed_sums[0]), mixed, [win_one, win_two], L)
+    mix_sums = chips_sum(me, mix_sums, back_tokens)
+    down_back, up_back, table_back = last_feed(me, along_dp_sums(feed_sums), F, mix_sums[0], trows, term.shape, N)
+    output_back, input_back, retriever_back, small = last_sum(
+        along_dp_sums(mix_sums), [D] + [3 * gc] * G + [Rw, LANES], 16, G, gc, down_back
     )
     ub_back = small[8 : 8 + Q].reshape(-1)
     return (

time: 382 us -> 341 us (0.89)
  Pallas kernels: 227 us -> 200 us
  starting transfers between devices: 54.2 us -> 41.9 us
    pallas_call x29 -> x26, Pallas kernels: 227 us -> 200 us  [run(): pl.pallas_call(body, name=name, grid=grid, in_specs=in_specs, out_specs=o...]
    ppermute x6, waiting for transfers between devices: 24.2 us -> 6.2 us  [along_dp_sums(): lax.ppermute(sums[k], 'dp', pairs(len(sums), k))]
    all_to_all x4, waiting for transfers between devices: 6.22 us -> 21.5 us  [between_chips(): lax.all_to_all(blocks, 'fsdp', 0, 0, axis_index_groups=[list(range(c, N,...]
    ppermute x9, waiting for transfers between devices: 17.4 us -> 8.49 us  [along_dp(): lax.ppermute(block, 'dp', pairs(Z, k))]
    ppermute x6, starting transfers between devices: 16.6 us -> 8.77 us  [along_dp_sums(): lax.ppermute(sums[k], 'dp', pairs(len(sums), k))]
    ppermute x7, waiting for transfers between devices: 5.79 us -> 12.7 us  [other_core(): return lax.ppermute(blocks, 'fsdp', pairs(N, 1))]
    all_gather x1, waiting for transfers between devices: 0.01 us -> 6.58 us  [local(): wide = lax.all_gather(wide, both, axis=0, tiled=True)]
  transfers between devices with their start and end apart: 27 -> 27, of which waited for: 14 -> 12; matrix products, arithmetic and copies ran while one was open for 1% -> 1% of each run, Pallas kernels for 41% -> 41%
where the time goes in v3:
time: 341 us; the launch traced here: 340 us
  Pallas kernels  200 us (59%)
  waiting for transfers between devices  55.5 us (16%)
  starting transfers between devices  41.9 us (12%)
  between operations  14.3 us (4%)
  local copies, waits for them, and re-layouts  14 us (4%)
  blocking collectives  12.7 us (4%)
    pallas_call x26, Pallas kernels, run(): pl.pallas_call(body, name=name, grid=grid, in_specs=in_specs, out_specs=o...  200 us
    all_to_all x4, waiting for transfers between devices, between_chips(): lax.all_to_all(blocks, 'fsdp', 0, 0, axis_index_groups=[list(range(c, N,...  21.5 us
    all_to_all x4, starting transfers between devices, between_chips(): lax.all_to_all(blocks, 'fsdp', 0, 0, axis_index_groups=[list(range(c, N,...  16.5 us
    ppermute x9, starting transfers between devices, along_dp(): lax.ppermute(block, 'dp', pairs(Z, k))  15.4 us
    ppermute x7, waiting for transfers between devices, other_core(): return lax.ppermute(blocks, 'fsdp', pairs(N, 1))  12.7 us
    all_to_all x1, blocking collectives, between_chips(): lax.all_to_all(blocks, 'fsdp', 0, 0, axis_index_groups=[list(range(c, N,...  12.7 us
    unnamed x56, local copies, waits for them, and re-layouts  9.22 us
    ppermute x6, starting transfers between devices, along_dp_sums(): lax.ppermute(sums[k], 'dp', pairs(len(sums), k))  8.77 us
  transfers between devices with their start and end apart: 27, of which 12 were waited for; matrix products, arithmetic and copies ran while one was open for 1% of the time, Pallas kernels for 41%

profile of v3, /device:TPU:0, one launch (start us, length us, event | category | flops | bytes accessed | tf_op | source)
XLA Modules:
  0.0 339.7 jit_solution(62527954306265180)
XLA Ops:
  7.2 1.9 pack.1
  9.1 3.1 collective-permute-start
  12.2 2.6 collective-permute-start.1
  14.8 3.3 collective-permute-done.1.refs_2_
  18.2 2.7 collective-permute-done.2.refs_3_
  23.2 12.7 %all_to_all.25.refs_0_ = bf16[4,4,24,896]{3,2,1,0:T(8,128)(2,1)S(1)} all-to-all(bf16[4,4,24,896]{3,2,1,0:T(8,128)(2,1)} %repeat.3), channel_id=1, replica_groups={{0,2,4,6},{1,3,5,7},{8,10,12,14},{9,11,13,15},{16,18,20,22},{17,19,21,2..., dimensions={0} | all-to-all | bytes 1376256 | tf_op jit(solution)/shard_map/all_to_all | solution.py:373
  35.9 2.6 collective-permute-start.6
  38.5 1.9 collective-permute-start.4
  41.8 3.7 %place.3 = (bf16[4,4,2,24,768]{4,3,2,1,0:T(8,128)(2,1)}, bf16[4,4,2,24,128]{4,3,2,1,0:T(8,128)(2,1)}, f32[16,768]{1,0:T(8,128)}) custom-call(s32[3]{0:T(128)} %pad_add_fusion.me_ref, bf16[4,4,24,896]{3,2,1,0:T(8,128)(2,1)} %copy-done.3, bf16[4,4,24,896]{3,2,1,0:T(8,128)(2,1)} %copy-done.6), custom_call_target="tpu_custom_call" | custom-call | bytes 2752512 | tf_op jit(solution)/shard_map/place/pallas_call | solution.py:34
  47.3 2.1 repeat.4
  49.4 3.5 %all-to-all-start.1 = ((bf16[4,4,24,1536]{3,2,1,0:T(8,128)(2,1)}), bf16[4,4,24,1536]{3,2,1,0:T(8,128)(2,1)S(1)}, u32[]{:S(2)}, u32[]{:S(2)}) async-start(bf16[4,4,24,1536]{3,2,1,0:T(8,128)(2,1)} %repeat.4), calls=%async_computation.1 | async-start | bytes 2359296 | tf_op jit(solution)/shard_map/all_to_all | solution.py:373
  52.9 4.7 %collective-permute-start.9 = (bf16[96,768]{1,0:T(8,128)(2,1)S(1)}, bf16[96,768]{1,0:T(8,128)(2,1)S(1)}, u32[]{:S(2)}, u32[]{:S(2)}) collective-permute-start(bf16[96,768]{1,0:T(8,128)(2,1)S(1)} %copy-done.13), channel_id=1, source_target_pairs={{0,24},{8,16},{16,8},{24,0},{1,25},{9,17},{17,9},{25,1},{2,26},{10... | collective-permute-start | bytes 442376 | tf_op jit(solution)/shard_map/ppermute | solution.py:369
  58.2 1.8 bias_row.1.ub_ref
  60.1 10.1 %attend.2 = (bf16[3,1152,768]{2,1,0:T(8,128)(2,1)}, bf16[3,4,1152,288]{3,2,1,0:T(8,128)(2,1)}, bf16[3,1152,256]{2,1,0:T(8,128)(2,1)}) custom-call(bf16[1152,768]{1,0:T(8,128)(2,1)} %refs_2_.3, bf16[768,768]{1,0:T(8,128)(2,1)} %bitcast.49, f32[16,768]{1,0:T(8,128)} %get-tuple-element.108.v_ref), custom_call_target="tpu_custom_call" | custom-call | flops 2717908992 | bytes 7962624 | tf_op jit(solution)/shard_map/attend/pallas_call | solution.py:34
  70.2 1.9 collective-permute-done.8.refs_2_
  73.4 2.7 repeat.5
  76.1 3.8 %all-to-all-start.2 = ((bf16[4,4,96,768]{3,2,1,0:T(8,128)(2,1)}), bf16[4,4,96,768]{3,2,1,0:T(8,128)(2,1)S(1)}, u32[]{:S(2)}, u32[]{:S(2)}) async-start(bf16[4,4,96,768]{3,2,1,0:T(8,128)(2,1)} %repeat.5), calls=%async_computation.2 | async-start | bytes 4718592 | tf_op jit(solution)/shard_map/all_to_all | solution.py:373
  80.1 3.1 collective-permute-done.10.refs_1_
  83.1 3.3 place.4
  86.4 18.0 %attend.3 = (bf16[3,1152,768]{2,1,0:T(8,128)(2,1)}, bf16[3,4,1152,288]{3,2,1,0:T(8,128)(2,1)}, bf16[3,1152,256]{2,1,0:T(8,128)(2,1)}) custom-call(bf16[1152,768]{1,0:T(8,128)(2,1)} %refs_2_.3, bf16[768,1536]{1,0:T(8,128)(2,1)} %bitcast.34, f32[16,768]{1,0:T(8,128)} %get-tuple-element.108.v_ref, ...), custom_call_target="tpu_custom_call", output_to_operand_aliasing={{0}: (3, {}), {1}: (4, {}), {2}: (5, {})} | custom-call | flops 5435817984 | bytes 14155776 | tf_op jit(solution)/shard_map/attend/pallas_call | solution.py:34
  104.4 8.4 %all-to-all-done.2.refs_0_ = bf16[4,4,96,768]{3,2,1,0:T(8,128)(2,1)S(1)} async-done(((bf16[4,4,96,768]{3,2,1,0:T(8,128)(2,1)}), bf16[4,4,96,768]{3,2,1,0:T(8,128)(2,1)S(1)}, u32[]{:S(2)}, u32[]{:S(2)}) %all-to-all-start.2) | async-done | bytes 2359328 | tf_op jit(solution)/shard_map/all_to_all | solution.py:373
  113.6 6.6 %all-gather.2.cloned.1.call-done.wo_ref.wu_ref.w_ref.r_ref = bf16[768,5376]{1,0:T(8,128)(2,1)} async-done(((bf16[24,5376]{1,0:T(8,128)(2,1)}), bf16[768,5376]{1,0:T(8,128)(2,1)}) %all-gather.2.cloned.1.call-update) | async-done | bytes 8257552 | tf_op jit(solution)/shard_map/all_gather | solution.py:811
  120.2 18.9 %up.1 = (f32[1152,768]{1,0:T(8,128)}, f32[1152,1]{1,0:T(8,128)}, bf16[1152,768]{1,0:T(8,128)(2,1)}, bf16[1152,3072]{1,0:T(8,128)(2,1)}, bf16[1152,3072]{1,0:T(8,128)(2,1)}) custom-call(bf16[3,1152,256]{2,1,0:T(8,128)(2,1)} %get-tuple-element.125.ctx_ref.refs_0_, bf16[1152,768]{1,0:T(8,128)(2,1)} %refs_2_.3, ...), custom_call_target="tpu_custom_call" | custom-call | flops 6794772480 | bytes 28901376 | tf_op jit(solution)/shard_map/up/pallas_call | solution.py:34
  139.1 2.6 lookup.1
  141.7 4.5 %place.5 = bf16[4,4,2,96,768]{4,3,2,1,0:T(8,128)(2,1)} custom-call(s32[3]{0:T(128)} %pad_add_fusion.me_ref, bf16[4,4,96,768]{3,2,1,0:T(8,128)(2,1)} %copy-done.1, bf16[4,4,96,768]{3,2,1,0:T(8,128)(2,1)} %collective-permute-done.11.refs_1_), custom_call_target="tpu_custom_call" | custom-call | bytes 9437184 | tf_op jit(solution)/shard_map/place/pallas_call | solution.py:34
  146.2 24.3 %down.1 = (bf16[1152,768]{1,0:T(8,128)(2,1)}, f32[4,1,768]{2,1,0:T(1,128)}, f32[1152,768]{1,0:T(8,128)}, bf16[1152,768]{1,0:T(8,128)(2,1)}, bf16[1152,3072]{1,0:...) custom-call(bf16[1152,768]{1,0:T(8,128)(2,1)} %get-tuple-element.143.first_ref.refs_0, ...), custom_call_target="tpu_custom_call" | custom-call | flops 10871635968 | bytes 36569088 | tf_op jit(solution)/shard_map/down/pallas_call | solution.py:34
  170.5 10.4 %down_grad.1 = (bf16[4,4,96,768]{3,2,1,0:T(8,128)(2,1)}, bf16[4,4,96,768]{3,2,1,0:T(8,128)(2,1)}) custom-call(s32[3]{0:T(128)} %pad_add_fusion.me_ref, bf16[1152,3072]{1,0:T(8,128)(2,1)} %get-tuple-element.128.act_ref.x_ref, bf16[1152,768]{1,0:T(8,128)(2,1)} %get-tuple-element.140.y_ref), custom_call_target="tpu_custom_call" | custom-call | flops 5435817984 | bytes 13565952 | tf_op jit(solution)/shard_map/down_grad/pallas_call | solution.py:34
  180.9 10.4 %up_grad.1 = (bf16[4,4,24,3072]{3,2,1,0:T(8,128)(2,1)}, bf16[4,4,24,3072]{3,2,1,0:T(8,128)(2,1)}) custom-call(s32[3]{0:T(128)} %pad_add_fusion.me_ref, bf16[1152,768]{1,0:T(8,128)(2,1)} %get-tuple-element.143.first_ref.refs_0_, bf16[1152,3072]{1,0:T(8,128)(2,1)} %get-tuple-element.144.refs_1_.inner_ref), custom_call_target="tpu_custom_call" | custom-call | flops 5435817984 | bytes 13565952 | tf_op jit(solution)/shard_map/up_grad/pallas_call | solution.py:34
  192.5 2.0 score.1
  194.7 2.2 collective-permute-done.14.refs_5_
  196.9 2.7 collective-permute-done.12.refs_2_
  199.6 6.8 %pair_sum.2 = bf16[4,4,200,768]{3,2,1,0:T(8,128)(2,1)} custom-call(s32[3]{0:T(128)} %pad_add_fusion.me_ref, bf16[4,4,96,768]{3,2,1,0:T(8,128)(2,1)} %get-tuple-element.146.refs_0_, bf16[4,4,24,3072]{3,2,1,0:T(8,128)(2,1)} %get-tuple-element.145.refs_1_, bf16[4,4,96,768]{3,2,1,0:T(8,128)(2,1)} %collective-permute-done.12.refs_2_, ...), custom_call_target="tpu_custom_call" | custom-call | bytes 14745600 | tf_op jit(solution)/shard_map/pair_sum/pallas_call | solution.py:34
  206.4 5.0 %all-to-all-start.3 = ((bf16[4,4,200,768]{3,2,1,0:T(8,128)(2,1)}), bf16[4,4,200,768]{3,2,1,0:T(8,128)(2,1)}, u32[]{:S(2)}, u32[]{:S(2)}) async-start(bf16[4,4,200,768]{3,2,1,0:T(8,128)(2,1)} %pair_sum.2), calls=%async_computation.3 | async-start | bytes 9830400 | tf_op jit(solution)/shard_map/all_to_all | solution.py:373
  211.4 16.7 %mid.1 = (f32[1152,768]{1,0:T(8,128)}, bf16[1152,768]{1,0:T(8,128)(2,1)}, bf16[1152,768]{1,0:T(8,128)(2,1)}, f32[1,768]{1,0:T(1,128)}, f32[1,768]{1,0:T(1,128)}, /*index=5*/f32[1,768]{1,0:T(1,128)}) custom-call(f32[1152,768]{1,0:T(8,128)} %get-tuple-element.149.two_ref, bf16[1152,3072]{1,0:T(8,128)(2,1)} %get-tuple-element.144.refs_1_.inner_ref, ...), custom_call_target="tpu_custom_call" | custom-call | flops 6794772480 | bytes 27131904 | tf_op jit(solution)/shard_map/mid/pallas_call | solution.py:34
  228.1 20.9 %attend_back.1 = (bf16[3,1152,768]{2,1,0:T(8,128)(2,1)}, f32[1,768]{1,0:T(1,128)}, f32[1,768]{1,0:T(1,128)}) custom-call(bf16[3,1152,768]{2,1,0:T(8,128)(2,1)} %get-tuple-element.154.qkv_ref, bf16[3,4,1152,288]{3,2,1,0:T(8,128)(2,1)} %get-tuple-element.155.soft_ref, bf16[3,1152,256]{2,1,0:T(8,128)(2,1)} %get-tuple-element.125.ctx_ref.refs_0_, ...), custom_call_target="tpu_custom_call" | custom-call | flops 8153726976 | bytes 22118400 | tf_op jit(solution)/shard_map/attend_back/pallas_call | solution.py:34
  249.0 12.7 %mix_grad.1 = (bf16[4,4,24,3328]{3,2,1,0:T(8,128)(2,1)}, bf16[4,4,24,3328]{3,2,1,0:T(8,128)(2,1)}) custom-call(s32[3]{0:T(128)} %pad_add_fusion.me_ref, bf16[3,1152,256]{2,1,0:T(8,128)(2,1)} %get-tuple-element.125.ctx_ref.refs_0_, bf16[1152,768]{1,0:T(8,128)(2,1)} %get-tuple-element.153.refs_1_, bf16[1152,768]{1,0:T(8,128)(2,1)} %refs_2_.3, ...), custom_call_target="tpu_custom_call" | custom-call | flops 5888802816 | bytes 14548992 | tf_op jit(solution)/shard_map/mix_grad/pallas_call | solution.py:34
  261.9 4.8 %collective-permute-done.15.refs_1_ = bf16[4,4,24,3328]{3,2,1,0:T(8,128)(2,1)S(1)} collective-permute-done((bf16[4,4,24,3328]{3,2,1,0:T(8,128)(2,1)}, bf16[4,4,24,3328]{3,2,1,0:T(8,128)(2,1)S(1)}, u32[]{:S(2)}, u32[]{:S(2)}) %collective-permute-start.15) | collective-permute-done | bytes 2555936 | tf_op jit(solution)/shard_map/ppermute | solution.py:377
  268.1 4.6 %pair_sum.3 = bf16[4,4,24,3328]{3,2,1,0:T(8,128)(2,1)} custom-call(s32[3]{0:T(128)} %broadcast_1_me_ref.2.me_ref, bf16[4,4,24,3328]{3,2,1,0:T(8,128)(2,1)} %get-tuple-element.169.refs_0_, bf16[4,4,24,3328]{3,2,1,0:T(8,128)(2,1)} %copy-done.4), custom_call_target="tpu_custom_call" | custom-call | bytes 7667712 | tf_op jit(solution)/shard_map/pair_sum/pallas_call | solution.py:34
  272.8 4.1 %all-to-all-start.4 = ((bf16[4,4,24,3328]{3,2,1,0:T(8,128)(2,1)}), bf16[4,4,24,3328]{3,2,1,0:T(8,128)(2,1)S(1)}, u32[]{:S(2)}, u32[]{:S(2)}) async-start(bf16[4,4,24,3328]{3,2,1,0:T(8,128)(2,1)} %pair_sum.3), calls=%async_computation.4 | async-start | bytes 5111808 | tf_op jit(solution)/shard_map/all_to_all | solution.py:373
  276.9 3.8 %chips_sum.2 = (f32[208,768]{1,0:T(8,128)}, bf16[208,768]{1,0:T(8,128)(2,1)}, bf16[208,768]{1,0:T(8,128)(2,1)}, bf16[208,768]{1,0:T(8,128)(2,1)}) custom-call(s32[3]{0:T(128)} %pad_add_fusion.me_ref, bf16[4,4,200,768]{3,2,1,0:T(8,128)(2,1)} %all-to-all-done.3.in_ref), custom_call_target="tpu_custom_call" | custom-call | bytes 6193152 | tf_op jit(solution)/shard_map/chips_sum/pallas_call | solution.py:34
  281.4 2.3 collective-permute-start.17
  285.1 9.1 %tokens_back.1 = bf16[1152,768]{1,0:T(8,128)(2,1)} custom-call(f32[1152,768]{1,0:T(8,128)} %get-tuple-element.173.one_ref, bf16[3,1152,768]{2,1,0:T(8,128)(2,1)} %get-tuple-element.158.refs_3_.mixed_ref, bf16[768,768]{1,0:T(8,128)(2,1)} %bitcast.50, bf16[768,1536]{1,0:T(8,128)(2,1)} %bitcast.35), custom_call_target="tpu_custom_call" | custom-call | flops 4076863488 | bytes 10616832 | tf_op jit(solution)/shard_map/tokens_back/pallas_call | solution.py:34
  294.2 13.1 %all-to-all-done.4.in_ref = bf16[4,4,24,3328]{3,2,1,0:T(8,128)(2,1)S(1)} async-done(((bf16[4,4,24,3328]{3,2,1,0:T(8,128)(2,1)}), bf16[4,4,24,3328]{3,2,1,0:T(8,128)(2,1)S(1)}, u32[]{:S(2)}, u32[]{:S(2)}) %all-to-all-start.4) | async-done | bytes 2555936 | tf_op jit(solution)/shard_map/all_to_all | solution.py:373
  308.7 2.8 chips_sum.3
  312.1 2.3 collective-permute-start.20
  318.0 2.6 last_feed.1
  320.6 6.2 %collective-permute-done.20.refs_2_ = bf16[24,3328]{1,0:T(8,128)(2,1)S(1)} collective-permute-done((bf16[24,3328]{1,0:T(8,128)(2,1)}, bf16[24,3328]{1,0:T(8,128)(2,1)S(1)}, u32[]{:S(2)}, u32[]{:S(2)}) %collective-permute-start.20) | collective-permute-done | bytes 159776 | tf_op jit(solution)/shard_map/ppermute | solution.py:701
  328.1 1.9 last_sum.1
  (98 shorter events, 23.6 us)
Async XLA Ops:
  7.2 113.0 %all-gather.2.cloned.1.call-start = ((), (), s32[]{:S(2)}) async-start(), calls=%async_computation.5 | async-start | bytes 8515584 | tf_op jit(solution)/shard_map/all_gather | solution.py:811
  9.1 26.8 %copy-start.17 = (bf16[24,1536]{1,0:T(8,128)(2,1)S(1)}, bf16[24,1536]{1,0:T(8,128)(2,1)}, u32[]{:S(2)}) copy-start(bf16[24,1536]{1,0:T(8,128)(2,1)} %get-tuple-element.109.refs_0_) | copy-start | bytes 221188
  9.1 5.7 %collective-permute-start = (bf16[24,896]{1,0:T(8,128)(2,1)}, bf16[24,896]{1,0:T(8,128)(2,1)S(1)}, u32[]{:S(2)}, u32[]{:S(2)}) collective-permute-start(bf16[24,896]{1,0:T(8,128)(2,1)} %get-tuple-element.106.refs_0_), channel_id=1, source_target_pairs={{0,8},{8,0},{16,24},{24,16},{1,9},{9,1},{17,25},{25,17},{2,10},{10... | collective-permute-start | bytes 129032 | tf_op jit(solution)/shard_map/ppermute | solution.py:369
  12.2 5.9 %collective-permute-start.1 = (bf16[24,896]{1,0:T(8,128)(2,1)}, bf16[24,896]{1,0:T(8,128)(2,1)S(1)}, u32[]{:S(2)}, u32[]{:S(2)}) collective-permute-start(bf16[24,896]{1,0:T(8,128)(2,1)} %get-tuple-element.106.refs_0_), channel_id=1, source_target_pairs={{0,16},{8,24},{16,0},{24,8},{1,17},{9,25},{17,1},{25,9},{2,18},{10... | collective-permute-start | bytes 129032 | tf_op jit(solution)/shard_map/ppermute | solution.py:369
  14.8 6.0 %collective-permute-start.2 = (bf16[24,896]{1,0:T(8,128)(2,1)}, bf16[24,896]{1,0:T(8,128)(2,1)S(1)}, u32[]{:S(2)}, u32[]{:S(2)}) collective-permute-start(bf16[24,896]{1,0:T(8,128)(2,1)} %get-tuple-element.106.refs_0_), channel_id=1, source_target_pairs={{0,24},{8,16},{16,8},{24,0},{1,25},{9,17},{17,9},{25,1},{2,26},{10... | collective-permute-start | bytes 129032 | tf_op jit(solution)/shard_map/ppermute | solution.py:369
  14.8 6.0 %copy-start.21 = (bf16[24,896]{1,0:T(8,128)(2,1)}, bf16[24,896]{1,0:T(8,128)(2,1)S(1)}, u32[]{:S(2)}) copy-start(bf16[24,896]{1,0:T(8,128)(2,1)S(1)} %collective-permute-done.refs_1_) | copy-start | bytes 129028
  18.2 2.7 copy-start.22
  35.9 5.1 %copy-start.3 = (bf16[4,4,24,896]{3,2,1,0:T(8,128)(2,1)}, bf16[4,4,24,896]{3,2,1,0:T(8,128)(2,1)S(1)}, u32[]{:S(2)}) copy-start(bf16[4,4,24,896]{3,2,1,0:T(8,128)(2,1)S(1)} %all_to_all.25.refs_0_) | copy-start | bytes 2064388
  35.9 5.1 %collective-permute-start.3 = (bf16[4,4,24,896]{3,2,1,0:T(8,128)(2,1)S(1)}, bf16[4,4,24,896]{3,2,1,0:T(8,128)(2,1)S(1)}, u32[]{:S(2)}, u32[]{:S(2)}) collective-permute-start(bf16[4,4,24,896]{3,2,1,0:T(8,128)(2,1)S(1)} %all_to_all.25.refs_0_), channel_id=1, source_target_pairs={{0,1},{1,0},{2,3},{3,2},{4,5},{5,4},{6,7},{7,6},{8,9},{9,8},{10,11... | collective-permute-start | bytes 2064392 | tf_op jit(solution)/shard_map/ppermute | solution.py:377
  35.9 9.6 %collective-permute-start.6 = (bf16[24,1536]{1,0:T(8,128)(2,1)S(1)}, bf16[24,1536]{1,0:T(8,128)(2,1)S(1)}, u32[]{:S(2)}, u32[]{:S(2)}) collective-permute-start(bf16[24,1536]{1,0:T(8,128)(2,1)S(1)} %copy-done.17), channel_id=1, source_target_pairs={{0,24},{8,16},{16,8},{24,0},{1,25},{9,17},{17,9},{25,1},{2,26},{10... | collective-permute-start | bytes 221192 | tf_op jit(solution)/shard_map/ppermute | solution.py:369
  38.5 7.5 %collective-permute-start.5 = (bf16[24,1536]{1,0:T(8,128)(2,1)S(1)}, bf16[24,1536]{1,0:T(8,128)(2,1)S(1)}, u32[]{:S(2)}, u32[]{:S(2)}) collective-permute-start(bf16[24,1536]{1,0:T(8,128)(2,1)S(1)} %copy-done.17), channel_id=1, source_target_pairs={{0,16},{8,24},{16,0},{24,8},{1,17},{9,25},{17,1},{25,9},{2,18},{10... | collective-permute-start | bytes 221192 | tf_op jit(solution)/shard_map/ppermute | solution.py:369
  38.5 7.5 %collective-permute-start.4 = (bf16[24,1536]{1,0:T(8,128)(2,1)S(1)}, bf16[24,1536]{1,0:T(8,128)(2,1)S(1)}, u32[]{:S(2)}, u32[]{:S(2)}) collective-permute-start(bf16[24,1536]{1,0:T(8,128)(2,1)S(1)} %copy-done.17), channel_id=1, source_target_pairs={{0,8},{8,0},{16,24},{24,16},{1,9},{9,1},{17,25},{25,17},{2,10},{10... | collective-permute-start | bytes 221192 | tf_op jit(solution)/shard_map/ppermute | solution.py:369
  41.0 12.0 %copy-start.13 = (bf16[96,768]{1,0:T(8,128)(2,1)S(1)}, bf16[96,768]{1,0:T(8,128)(2,1)}, u32[]{:S(2)}) copy-start(bf16[96,768]{1,0:T(8,128)(2,1)} %refs_0_.2) | copy-start | bytes 442372
  41.0 0.8 copy-start.6
  49.4 26.8 %all-to-all-start.1 = ((bf16[4,4,24,1536]{3,2,1,0:T(8,128)(2,1)}), bf16[4,4,24,1536]{3,2,1,0:T(8,128)(2,1)S(1)}, u32[]{:S(2)}, u32[]{:S(2)}) async-start(bf16[4,4,24,1536]{3,2,1,0:T(8,128)(2,1)} %repeat.4), calls=%async_computation.1 | async-start | bytes 2359296 | tf_op jit(solution)/shard_map/all_to_all | solution.py:373
  52.9 17.2 %collective-permute-start.9 = (bf16[96,768]{1,0:T(8,128)(2,1)S(1)}, bf16[96,768]{1,0:T(8,128)(2,1)S(1)}, u32[]{:S(2)}, u32[]{:S(2)}) collective-permute-start(bf16[96,768]{1,0:T(8,128)(2,1)S(1)} %copy-done.13), channel_id=1, source_target_pairs={{0,24},{8,16},{16,8},{24,0},{1,25},{9,17},{17,9},{25,1},{2,26},{10... | collective-permute-start | bytes 442376 | tf_op jit(solution)/shard_map/ppermute | solution.py:369
  57.6 14.5 %collective-permute-start.8 = (bf16[96,768]{1,0:T(8,128)(2,1)S(1)}, bf16[96,768]{1,0:T(8,128)(2,1)S(1)}, u32[]{:S(2)}, u32[]{:S(2)}) collective-permute-start(bf16[96,768]{1,0:T(8,128)(2,1)S(1)} %copy-done.13), channel_id=1, source_target_pairs={{0,16},{8,24},{16,0},{24,8},{1,17},{9,25},{17,1},{25,9},{2,18},{10... | collective-permute-start | bytes 442376 | tf_op jit(solution)/shard_map/ppermute | solution.py:369
  57.6 14.5 %collective-permute-start.7 = (bf16[96,768]{1,0:T(8,128)(2,1)S(1)}, bf16[96,768]{1,0:T(8,128)(2,1)S(1)}, u32[]{:S(2)}, u32[]{:S(2)}) collective-permute-start(bf16[96,768]{1,0:T(8,128)(2,1)S(1)} %copy-done.13), channel_id=1, source_target_pairs={{0,8},{8,0},{16,24},{24,16},{1,9},{9,1},{17,25},{25,17},{2,10},{10... | collective-permute-start | bytes 442376 | tf_op jit(solution)/shard_map/ppermute | solution.py:369
  70.1 1.9 copy-start.14
  76.1 7.0 %copy-start.2 = (bf16[4,4,24,1536]{3,2,1,0:T(8,128)(2,1)}, bf16[4,4,24,1536]{3,2,1,0:T(8,128)(2,1)S(1)}, u32[]{:S(2)}) copy-start(bf16[4,4,24,1536]{3,2,1,0:T(8,128)(2,1)S(1)} %all-to-all-done.1.refs_0_) | copy-start | bytes 3538948
  76.1 36.7 %all-to-all-start.2 = ((bf16[4,4,96,768]{3,2,1,0:T(8,128)(2,1)}), bf16[4,4,96,768]{3,2,1,0:T(8,128)(2,1)S(1)}, u32[]{:S(2)}, u32[]{:S(2)}) async-start(bf16[4,4,96,768]{3,2,1,0:T(8,128)(2,1)} %repeat.5), calls=%async_computation.2 | async-start | bytes 4718592 | tf_op jit(solution)/shard_map/all_to_all | solution.py:373
  80.0 3.2 collective-permute-start.10
  86.4 26.4 %copy-start.27 = (f32[4]{0:T(128)S(1)}, f32[4]{0:T(128)}, u32[]{:S(2)}) copy-start(f32[4]{0:T(128)} %param.37) | copy-start | bytes 52
  112.8 26.3 %copy-start.1 = (bf16[4,4,96,768]{3,2,1,0:T(8,128)(2,1)}, bf16[4,4,96,768]{3,2,1,0:T(8,128)(2,1)S(1)}, u32[]{:S(2)}) copy-start(bf16[4,4,96,768]{3,2,1,0:T(8,128)(2,1)S(1)} %all-to-all-done.2.refs_0_) | copy-start | bytes 7077892
  112.8 28.8 %collective-permute-start.11 = (bf16[4,4,96,768]{3,2,1,0:T(8,128)(2,1)S(1)}, bf16[4,4,96,768]{3,2,1,0:T(8,128)(2,1)}, u32[]{:S(2)}, u32[]{:S(2)}) collective-permute-start(bf16[4,4,96,768]{3,2,1,0:T(8,128)(2,1)S(1)} %all-to-all-done.2.refs_0_), channel_id=1, source_target_pairs={{0,1},{1,0},{2,3},{3,2},{4,5},{5,4},{6,7},{7,6},{8,9},{9,8},{10,11... | collective-permute-start | bytes 7077896 | tf_op jit(solution)/shard_map/ppermute | solution.py:377
  180.9 10.9 %copy-start.24 = (s32[4]{0:T(128)S(1)}, s32[4]{0:T(128)}, u32[]{:S(2)}) copy-start(s32[4]{0:T(128)} %index_ref.1) | copy-start | bytes 52
  191.3 5.6 %collective-permute-start.13 = (bf16[4,4,24,3072]{3,2,1,0:T(8,128)(2,1)}, bf16[4,4,24,3072]{3,2,1,0:T(8,128)(2,1)S(1)}, u32[]{:S(2)}, u32[]{:S(2)}) collective-permute-start(bf16[4,4,24,3072]{3,2,1,0:T(8,128)(2,1)} %get-tuple-element.147), channel_id=1, source_target_pairs={{0,1},{1,0},{2,3},{3,2},{4,5},{5,4},{6,7},{7,6},{8,9},{9,8},{10,11... | collective-permute-start | bytes 7077896 | tf_op jit(solution)/shard_map/ppermute | solution.py:377
  191.6 8.0 %collective-permute-start.12 = (bf16[4,4,96,768]{3,2,1,0:T(8,128)(2,1)}, bf16[4,4,96,768]{3,2,1,0:T(8,128)(2,1)}, u32[]{:S(2)}, u32[]{:S(2)}) collective-permute-start(bf16[4,4,96,768]{3,2,1,0:T(8,128)(2,1)} %get-tuple-element.142), channel_id=1, source_target_pairs={{0,1},{1,0},{2,3},{3,2},{4,5},{5,4},{6,7},{7,6},{8,9},{9,8},{10,11... | collective-permute-start | bytes 7077896 | tf_op jit(solution)/shard_map/ppermute | solution.py:377
  194.4 2.4 collective-permute-start.14
  196.9 2.7 copy-start.25
  196.9 2.7 copy-start.5
  206.4 66.4 %all-to-all-start.3 = ((bf16[4,4,200,768]{3,2,1,0:T(8,128)(2,1)}), bf16[4,4,200,768]{3,2,1,0:T(8,128)(2,1)}, u32[]{:S(2)}, u32[]{:S(2)}) async-start(bf16[4,4,200,768]{3,2,1,0:T(8,128)(2,1)} %pair_sum.2), calls=%async_computation.3 | async-start | bytes 9830400 | tf_op jit(solution)/shard_map/all_to_all | solution.py:373
  261.6 5.0 %collective-permute-start.15 = (bf16[4,4,24,3328]{3,2,1,0:T(8,128)(2,1)}, bf16[4,4,24,3328]{3,2,1,0:T(8,128)(2,1)S(1)}, u32[]{:S(2)}, u32[]{:S(2)}) collective-permute-start(bf16[4,4,24,3328]{3,2,1,0:T(8,128)(2,1)} %get-tuple-element.170), channel_id=1, source_target_pairs={{0,1},{1,0},{2,3},{3,2},{4,5},{5,4},{6,7},{7,6},{8,9},{9,8},{10,11... | collective-permute-start | bytes 7667720 | tf_op jit(solution)/shard_map/ppermute | solution.py:377
  266.7 1.5 copy-start.4
  272.8 34.5 %all-to-all-start.4 = ((bf16[4,4,24,3328]{3,2,1,0:T(8,128)(2,1)}), bf16[4,4,24,3328]{3,2,1,0:T(8,128)(2,1)S(1)}, u32[]{:S(2)}, u32[]{:S(2)}) async-start(bf16[4,4,24,3328]{3,2,1,0:T(8,128)(2,1)} %pair_sum.3), calls=%async_computation.4 | async-start | bytes 5111808 | tf_op jit(solution)/shard_map/all_to_all | solution.py:373
  280.7 33.7 %collective-permute-start.16 = (bf16[208,768]{1,0:T(8,128)(2,1)}, bf16[208,768]{1,0:T(8,128)(2,1)S(1)}, u32[]{:S(2)}, u32[]{:S(2)}) collective-permute-start(bf16[208,768]{1,0:T(8,128)(2,1)} %get-tuple-element.178), channel_id=1, source_target_pairs={{0,8},{8,0},{16,24},{24,16},{1,9},{9,1},{17,25},{25,17},{2,10},{10... | collective-permute-start | bytes 958472 | tf_op jit(solution)/shard_map/ppermute | solution.py:701
  281.4 35.1 %collective-permute-start.17 = (bf16[208,768]{1,0:T(8,128)(2,1)}, bf16[208,768]{1,0:T(8,128)(2,1)S(1)}, u32[]{:S(2)}, u32[]{:S(2)}) collective-permute-start(bf16[208,768]{1,0:T(8,128)(2,1)} %get-tuple-element.179), channel_id=1, source_target_pairs={{0,16},{8,24},{16,0},{24,8},{1,17},{9,25},{17,1},{25,9},{2,18},{10... | collective-permute-start | bytes 958472 | tf_op jit(solution)/shard_map/ppermute | solution.py:701
  283.6 32.9 %collective-permute-start.18 = (bf16[208,768]{1,0:T(8,128)(2,1)}, bf16[208,768]{1,0:T(8,128)(2,1)S(1)}, u32[]{:S(2)}, u32[]{:S(2)}) collective-permute-start(bf16[208,768]{1,0:T(8,128)(2,1)} %get-tuple-element.180), channel_id=1, source_target_pairs={{0,24},{8,16},{16,8},{24,0},{1,25},{9,17},{17,9},{25,1},{2,26},{10... | collective-permute-start | bytes 958472 | tf_op jit(solution)/shard_map/ppermute | solution.py:701
  294.2 21.7 %copy-start.26 = (f32[4,1]{1,0:T(4,128)S(1)}, f32[4,1]{1,0:T(4,128)}, u32[]{:S(2)}) copy-start(f32[4,1]{1,0:T(4,128)} %get-tuple-element.138) | copy-start | bytes 52
  307.2 1.4 copy-start
  311.5 9.1 %collective-permute-start.19 = (bf16[24,3328]{1,0:T(8,128)(2,1)}, bf16[24,3328]{1,0:T(8,128)(2,1)S(1)}, u32[]{:S(2)}, u32[]{:S(2)}) collective-permute-start(bf16[24,3328]{1,0:T(8,128)(2,1)} %get-tuple-element.183), channel_id=1, source_target_pairs={{0,8},{8,0},{16,24},{24,16},{1,9},{9,1},{17,25},{25,17},{2,10},{10... | collective-permute-start | bytes 479240 | tf_op jit(solution)/shard_map/ppermute | solution.py:701
  312.1 14.7 %collective-permute-start.20 = (bf16[24,3328]{1,0:T(8,128)(2,1)}, bf16[24,3328]{1,0:T(8,128)(2,1)S(1)}, u32[]{:S(2)}, u32[]{:S(2)}) collective-permute-start(bf16[24,3328]{1,0:T(8,128)(2,1)} %get-tuple-element.184), channel_id=1, source_target_pairs={{0,16},{8,24},{16,0},{24,8},{1,17},{9,25},{17,1},{25,9},{2,18},{10... | collective-permute-start | bytes 479240 | tf_op jit(solution)/shard_map/ppermute | solution.py:701
  314.4 2.1 copy-start.7
  314.4 12.4 %collective-permute-start.21 = (bf16[24,3328]{1,0:T(8,128)(2,1)}, bf16[24,3328]{1,0:T(8,128)(2,1)S(1)}, u32[]{:S(2)}, u32[]{:S(2)}) collective-permute-start(bf16[24,3328]{1,0:T(8,128)(2,1)} %get-tuple-element.185), channel_id=1, source_target_pairs={{0,24},{8,16},{16,8},{24,0},{1,25},{9,17},{17,9},{25,1},{2,26},{10... | collective-permute-start | bytes 479240 | tf_op jit(solution)/shard_map/ppermute | solution.py:701
  316.5 0.7 copy-start.8
  317.2 0.7 copy-start.9
  320.6 6.2 %copy-start.10 = (bf16[24,3328]{1,0:T(8,128)(2,1)}, bf16[24,3328]{1,0:T(8,128)(2,1)S(1)}, u32[]{:S(2)}) copy-start(bf16[24,3328]{1,0:T(8,128)(2,1)S(1)} %collective-permute-done.19.refs_1_) | copy-start | bytes 479236
  326.8 0.7 copy-start.11
  (7 other events, 4.5 us)
Sparse Core Ops, SparseCore 0:
  11.5 108.6 all-gather.1

commit v4 on v3

--- a/solution.py
+++ b/solution.py
@@ -116,34 +116,53 @@
     return inv * (scaled - jnp.mean(scaled, axis=-1, keepdims=True) - n * jnp.mean(scaled * n, axis=-1, keepdims=True))
 
 
-def up_body(step, ctx_ref, x_ref, wo_ref, v_ref, wu_ref, ub_ref, n_ref, inv_ref, first_ref, act_ref, slope_ref):
-    G, _, gc = ctx_ref.shape
-    hidden = x_ref[...].astype(f32) + v_ref[OB : OB + 1, :]
-    for g in range(G):
-        hidden += dot(ctx_ref[g], wo_ref[g * gc : (g + 1) * gc, :])
-    n, inv = norm_rows(hidden)
-    n_ref[...] = n
-    inv_ref[...] = inv
-    first = (n * v_ref[FG : FG + 1, :] + v_ref[FS : FS + 1, :]).astype(bf16)
-    first_ref[...] = first
-    ff = wu_ref.shape[1]
-    for at in range(0, ff, step):
-        cols = slice(at, at + step)
-        u = dot(first, wu_ref[:, cols]) + ub_ref[:, cols]
-        phi = 0.5 + 0.5 * lax.erf(u * math.sqrt(0.5))
-        act_ref[:, cols] = (u * phi).astype(bf16)
-        slope_ref[:, cols] = (phi + u * jnp.exp(u * u * -0.5) * (1.0 / math.sqrt(2 * math.pi))).astype(bf16)
+def in_turn(blocks, first, then):
+    held = first(blocks[0])
+    for i, block in enumerate(blocks):
+        ahead = first(blocks[i + 1]) if i + 1 < len(blocks) else None
+        then(i, block, held)
+        held = ahead
+
+
+def blocks_of(rows, size):
+    return [slice(at, at + size) for at in range(0, rows, size)]
+
+
+def up_body(size, step, ctx_ref, x_ref, wo_ref, v_ref, wu_ref, ub_ref, n_ref, inv_ref, first_ref, act_ref, slope_ref):
+    G, rows, gc = ctx_ref.shape
+
+    def attended(block):
+        hidden = x_ref[block].astype(f32) + v_ref[OB : OB + 1, :]
+        for g in range(G):
+            hidden += dot(ctx_ref[g, block], wo_ref[g * gc : (g + 1) * gc, :])
+        return hidden
+
+    def rest(_, block, hidden):
+        n, inv = norm_rows(hidden)
+        n_ref[block] = n
+        inv_ref[block] = inv
+        first = (n * v_ref[FG : FG + 1, :] + v_ref[FS : FS + 1, :]).astype(bf16)
+        first_ref[block] = first
+        ff = wu_ref.shape[1]
+        for at in range(0, ff, step):
+            cols = slice(at, at + step)
+            u = dot(first, wu_ref[:, cols]) + ub_ref[:, cols]
+            phi = 0.5 + 0.5 * lax.erf(u * math.sqrt(0.5))
+            act_ref[block, cols] = (u * phi).astype(bf16)
+            slope_ref[block, cols] = (phi + u * jnp.exp(u * u * -0.5) * (1.0 / math.sqrt(2 * math.pi))).astype(bf16)
+
+    in_turn(blocks_of(rows, size), attended, rest)
 
 
 def out_spec(D, F):
     return pl.BlockSpec((D, D), lambda i: (0, F // D))
 
 
-def up(ctx, x, vec, wide, ub, rows, step=512):
+def up(ctx, x, vec, wide, ub, rows, size, step=512):
     T, D = x.shape
     F = ub.shape[1]
     return run(
-        functools.partial(up_body, step), "up", (T // rows,), (ctx, x, wide, vec, wide, ub),
+        functools.partial(up_body, size, step), "up", (T // rows,), (ctx, x, wide, vec, wide, ub),
         [pl.BlockSpec((ctx.shape[0], rows, ctx.shape[2]), lambda i: (0, i, 0)), rows_spec(rows, D)] + [out_spec(D, F), full_spec(vec.shape), full_spec((D, F)), full_spec(ub.shape)],
         [sds((T, D), f32), sds((T, 1), f32), sds((T, D), bf16), sds((T, F), bf16), sds((T, F), bf16)],
         [rows_spec(rows, D), rows_spec(rows, 1), rows_spec(rows, D), rows_spec(rows, F), rows_spec(rows, F)],
@@ -156,66 +175,97 @@
     ref[:, cols] = held + jnp.sum(value, axis=0, keepdims=True)
 
 
-def down_body(step, first_ref, act_ref, slope_ref, w_ref, v_ref, og_ref, lead_ref,
+def down_body(size, step, first_ref, act_ref, slope_ref, w_ref, v_ref, og_ref, lead_ref,
               out_ref, top_ref, two_ref, feed_ref, inner_ref, gg_ref, gs_ref, gb_ref, gub_ref):
-    rows = first_ref.shape[0]
     gain = v_ref[SG : SG + 1, :]
-    hidden = first_ref[...].astype(f32) + v_ref[DB : DB + 1, :] + dot(act_ref[...], w_ref[...])
-    n, inv = norm_rows(hidden)
-    out = (n * gain + v_ref[SS : SS + 1, :]).astype(bf16)
-    out_ref[...] = out
-    top_ref[0] = out[0:16, :].astype(f32)[0:1, :]
-    row = lax.broadcasted_iota(jnp.int32, (rows, 1), 0)
-    cot = og_ref[...].astype(f32) + jnp.where(row == 0, lead_ref[0], 0.0)
-    add_rows(gg_ref, cot * n)
-    add_rows(gs_ref, cot)
-    two = norm_rows_back(cot, n, inv, gain)
-    two_ref[...] = two
-    feed = two.astype(bf16)
-    feed_ref[...] = feed
-    add_rows(gb_ref, feed.astype(f32))
     ff = w_ref.shape[0]
+    sums = {}
+
+    def count(name, value):
+        total = jnp.sum(value, axis=0, keepdims=True)
+        sums[name] = sums[name] + total if name in sums else total
+
+    def fed(block):
+        return first_ref[block].astype(f32) + v_ref[DB : DB + 1, :] + dot(act_ref[block], w_ref[...])
+
+    def rest(i, block, hidden):
+        n, inv = norm_rows(hidden)
+        out = (n * gain + v_ref[SS : SS + 1, :]).astype(bf16)
+        out_ref[block] = out
+        top_ref[i] = out[0:16, :].astype(f32)[0:1, :]
+        row = lax.broadcasted_iota(jnp.int32, (size, 1), 0)
+        cot = og_ref[block].astype(f32) + jnp.where(row == 0, lead_ref[i], 0.0)
+        count("gain", cot * n)
+        count("shift", cot)
+        two = norm_rows_back(cot, n, inv, gain)
+        two_ref[block] = two
+        feed = two.astype(bf16)
+        feed_ref[block] = feed
+        count("bias", feed.astype(f32))
+        for at in range(0, ff, step):
+            cols = slice(at, at + step)
+            inner = (dot(feed, w_ref[cols, :], 1, 1) * slope_ref[block, cols].astype(f32)).astype(bf16)
+            inner_ref[block, cols] = inner
+            count(at, inner.astype(f32))
+
+    in_turn(blocks_of(first_ref.shape[0], size), fed, rest)
+    add_rows(gg_ref, sums["gain"])
+    add_rows(gs_ref, sums["shift"])
+    add_rows(gb_ref, sums["bias"])
     for at in range(0, ff, step):
-        cols = slice(at, at + step)
-        inner = (dot(feed, w_ref[cols, :], 1, 1) * slope_ref[:, cols].astype(f32)).astype(bf16)
-        inner_ref[:, cols] = inner
-        add_rows(gub_ref, inner.astype(f32), cols)
-
-
-def down(first, act, slope, w, vec, og, lead, seqs, step=512):
+        add_rows(gub_ref, sums[at], slice(at, at + step))
+
+
+def down(first, act, slope, w, vec, og, lead, seqs, per, step=512):
     T, D = first.shape
     F = act.shape[1]
     L = T // seqs
+    rows = per * L
+    each = pl.BlockSpec((per, 1, D), lambda i: (i, 0, 0))
     return run(
-        functools.partial(down_body, step), "down", (seqs,), (first, act, slope, w, vec, og, lead),
-        [rows_spec(L, D), rows_spec(L, F), rows_spec(L, F)] + [full_spec((F, D)), full_spec(vec.shape)]
-        + [rows_spec(L, D), pl.BlockSpec((1, 1, D), lambda i: (i, 0, 0))],
+        functools.partial(down_body, L, step), "down", (seqs // per,), (first, act, slope, w, vec, og, lead),
+        [rows_spec(rows, D), rows_spec(rows, F), rows_spec(rows, F), full_spec((F, D)), full_spec(vec.shape), rows_spec(rows, D), each],
         [sds((T, D), bf16), sds((seqs, 1, D), f32), sds((T, D), f32), sds((T, D), bf16), sds((T, F), bf16),
          sds((1, D), f32), sds((1, D), f32), sds((1, D), f32), sds((1, F), f32)],
-        [rows_spec(L, D), pl.BlockSpec((1, 1, D), lambda i: (i, 0, 0)), rows_spec(L, D), rows_spec(L, D), rows_spec(L, F)] + [full_spec((1, D))] * 3 + [full_spec((1, F))],
-        flops=4 * T * D * F, moved=6 * T * F + 12 * T * D + 2 * w.size,
-    )
-
-
-def mid_body(two_ref, inner_ref, wu_ref, n_ref, inv_ref, v_ref, wo_ref,
+        [rows_spec(rows, D), each, rows_spec(rows, D), rows_spec(rows, D), rows_spec(rows, F)]
+        + [full_spec((1, D))] * 3 + [full_spec((1, F))],
+        flops=4 * T * D * F, moved=6 * T * F + 12 * T * D + 2 * F * D,
+    )
+
+
+def mid_body(size, two_ref, inner_ref, wu_ref, n_ref, inv_ref, v_ref, wo_ref,
              one_ref, att_ref, bctx_ref, gg_ref, gs_ref, gob_ref):
-    cot = two_ref[...] + dot(inner_ref[...], wu_ref[...], 1, 1)
-    n = n_ref[...]
-    add_rows(gg_ref, cot * n)
-    add_rows(gs_ref, cot)
-    one = norm_rows_back(cot, n, inv_ref[...], v_ref[FG : FG + 1, :])
-    one_ref[...] = one
-    att = one.astype(bf16)
-    att_ref[...] = att
-    add_rows(gob_ref, att.astype(f32))
-    bctx_ref[...] = dot(att, wo_ref[...], 1, 1).astype(bf16)
-
-
-def mid(two, inner, wide, n, inv, vec, rows):
+    sums = {}
+
+    def count(name, value):
+        total = jnp.sum(value, axis=0, keepdims=True)
+        sums[name] = sums[name] + total if name in sums else total
+
+    def back(block):
+        return two_ref[block] + dot(inner_ref[block], wu_ref[...], 1, 1)
+
+    def rest(_, block, cot):
+        n = n_ref[block]
+        count("gain", cot * n)
+        count("shift", cot)
+        one = norm_rows_back(cot, n, inv_ref[block], v_ref[FG : FG + 1, :])
+        one_ref[block] = one
+        att = one.astype(bf16)
+        att_ref[block] = att
+        count("bias", att.astype(f32))
+        bctx_ref[block] = dot(att, wo_ref[...], 1, 1).astype(bf16)
+
+    in_turn(blocks_of(two_ref.shape[0], size), back, rest)
+    add_rows(gg_ref, sums["gain"])
+    add_rows(gs_ref, sums["shift"])
+    add_rows(gob_ref, sums["bias"])
+
+
+def mid(two, inner, wide, n, inv, vec, rows, size):
     T, D = two.shape
     F = inner.shape[1]
     return run(
-        mid_body, "mid", (T // rows,), (two, inner, wide, n, inv, vec, wide),
+        functools.partial(mid_body, size), "mid", (T // rows,), (two, inner, wide, n, inv, vec, wide),
         [rows_spec(rows, D), rows_spec(rows, F), full_spec((D, F)), rows_spec(rows, D), rows_spec(rows, 1), full_spec(vec.shape), out_spec(D, F)],
         [sds((T, D), f32), sds((T, D), bf16), sds((T, D), bf16)] + [sds((1, D), f32)] * 3,
         [rows_spec(rows, D)] * 3 + [full_spec((1, D))] * 3,
@@ -315,7 +365,7 @@
 
 
 def pack_body(D, gc, nvec, *refs):
-    w_ref, o_ref, r_ref, u_ref, t_ref = refs[:5]
+    id_ref, w_ref, o_ref, r_ref, u_ref = refs[:5]
     head_ref, rest_ref, up_ref, held = refs[5 + nvec :]
     G = D // gc
     rows = w_ref.shape[0]
@@ -326,6 +376,12 @@
         for at in range(0, v.shape[1], rows):
             held[row : row + 1, 0:rows] = v[:, at : at + rows]
             row += 1
+    lane = lax.broadcasted_iota(jnp.int32, (1, LANES), 1)
+    ids = jnp.zeros((1, LANES), jnp.int32)
+    seqs = id_ref.shape[0]
+    for i in range(seqs):
+        ids = jnp.where(lane == i, id_ref[i] // 256, jnp.where(lane == seqs + i, id_ref[i] % 256, ids))
+    held[row : row + 1, :] = ids.astype(f32)
     turned = held[...].T
     for m in range(3):
         head_ref[:, m * gc : (m + 1) * gc] = w_ref[:, m * D : m * D + gc]
@@ -335,27 +391,19 @@
         for m in range(3):
             rest_ref[:, at : at + gc] = w_ref[:, m * D + g * gc : m * D + (g + 1) * gc]
             at += gc
-    trows, width = t_ref.shape
     F = u_ref.shape[1]
-    at = F + D + r_ref.shape[1]
     up_ref[:, :F] = u_ref[...]
     up_ref[:, F : F + D] = o_ref[...]
-    up_ref[:, F + D : at] = r_ref[...]
-    for lo in range(0, trows, rows):
-        n = min(rows, trows - lo)
-        up_ref[:n, at : at + width] = t_ref[lo : lo + n, :]
-        if n < rows:
-            up_ref[n:, at : at + width] = jnp.zeros((rows - n, width), bf16)
-        at += width
-
-
-def pack(w, o, r, u, t, vectors, gc):
+    up_ref[:, F + D :] = r_ref[...]
+
+
+def pack(ids, w, o, r, u, vectors, gc):
     rows, D = o.shape
     head = 3 * gc + LANES
     rest = 3 * D - 3 * gc
-    ups = u.shape[1] + D + r.shape[1] + -(-t.shape[0] // rows) * t.shape[1]
+    ups = u.shape[1] + D + r.shape[1]
     return once(
-        functools.partial(pack_body, D, gc, len(vectors)), "pack", (w, o, r, u, t, *vectors), [None] * (5 + len(vectors)),
+        functools.partial(pack_body, D, gc, len(vectors)), "pack", (ids, w, o, r, u, *vectors), [SMEM] + [None] * (4 + len(vectors)),
         [sds((rows, head), bf16), sds((rows, rest), bf16), sds((rows, ups), bf16)],
         scratch=[pltpu.VMEM((LANES, LANES), f32)], moved=4 * rows * (head + rest + ups),
     )
@@ -365,8 +413,8 @@
     return [(i, i ^ flip) for i in range(n)]
 
 
-def along_dp(block, Z):
-    return [block] + [lax.ppermute(block, "dp", pairs(Z, k)) for k in range(1, Z)]
+def along_dp(blocks):
+    return [blocks[0]] + [lax.ppermute(b, "dp", pairs(len(blocks), k)) for k, b in enumerate(blocks) if k]
 
 
 def between_chips(blocks, N):
@@ -377,18 +425,60 @@
     return lax.ppermute(blocks, "fsdp", pairs(N, 1))
 
 
-def repeat_body(*refs):
-    out = refs[-1]
+def repeat_body(n, *refs):
+    out, blocks, tiles = refs[-1], refs[:n], refs[n:-1]
+    rows, width = blocks[0].shape
     for r in range(out.shape[0]):
-        for k, ref in enumerate(refs[:-1]):
-            out[r, k] = ref[...]
-
-
-def repeat(blocks, R):
+        for k, ref in enumerate(blocks):
+            out[r, k, :rows] = ref[...]
+        if tiles:
+            w = tiles[0].shape[1] // out.shape[0]
+            total = tiles[0][:, r * w : (r + 1) * w].astype(f32)
+            for ref in tiles[1:]:
+                total += ref[:, r * w : (r + 1) * w].astype(f32)
+            blank = jnp.zeros((total.shape[0], width - w), f32)
+            out[r, 0, rows:] = jnp.concatenate([total, blank], axis=1).astype(bf16)
+            for k in range(1, n):
+                out[r, k, rows:] = jnp.zeros((total.shape[0], width), bf16)
+
+
+def repeat(blocks, R, tiles=()):
     n = len(blocks)
+    rows, width = blocks[0].shape
+    rows += tiles[0].shape[0] if tiles else 0
     return once(
-        repeat_body, "repeat", blocks, [None] * n, [sds((R, n) + blocks[0].shape, bf16)], moved=2 * (R + 1) * n * blocks[0].size
+        functools.partial(repeat_body, n), "repeat", [*blocks, *tiles], [None] * (n + len(tiles)),
+        [sds((R, n, rows, width), bf16)], moved=2 * (R + 1) * n * rows * width,
     )[0]
+
+
+def ask_body(seqs, Z, R, at, me_ref, s_ref, t_ref, *refs):
+    outs, below, held = refs[:Z], refs[Z], refs[Z + 1]
+    D, trows = s_ref.shape[0], t_ref.shape[0]
+    rows = D // (Z * R * 2)
+    flat = s_ref[...].astype(f32)
+    below[0:D, :] = flat
+    below[D:, :] = jnp.zeros((below.shape[0] - D, LANES), f32)
+    ids = flat[:, at : at + 1] * 256.0 + below[seqs : seqs + D, at : at + 1]
+    ids = ids.astype(jnp.int32) - ((me_ref[0] * R + me_ref[1]) * 2 + me_ref[2]) * trows
+    line = lax.broadcasted_iota(jnp.int32, (D, trows), 0) % rows
+    picker = (lax.broadcasted_iota(jnp.int32, (D, trows), 1) == ids) & (line < seqs)
+    held[...] = dot(picker.astype(bf16), t_ref[...]).reshape(held.shape)
+    for k, out in enumerate(outs):
+        z = me_ref[0] ^ k
+        tiles = [jnp.concatenate([held[z, r, 0, 0:seqs], held[z, r, 1, 0:seqs]], axis=0) for r in range(R)]
+        out[...] = jnp.concatenate(tiles, axis=1).astype(bf16)
+
+
+def ask(me, small, table, seqs, Z, N, at):
+    D = small.shape[0]
+    R, width = N // 2, table.shape[1]
+    return once(
+        functools.partial(ask_body, seqs, Z, R, at), "ask", (me, small, table), [SMEM, None, None],
+        [sds((2 * seqs, R * width), bf16)] * Z,
+        scratch=[pltpu.VMEM((D + 8, LANES), f32), pltpu.VMEM((Z, R, 2, D // (Z * N), width), f32)],
+        flops=2 * D * width * table.shape[0], moved=2 * table.size,
+    )
 
 
 def place_body(n, cuts, turned, me_ref, *refs):
@@ -402,10 +492,10 @@
     copies = []
     for k in range(Z):
         for other in range(2):
-            piece = pieces[other].at[:, k] if n == 2 else pieces[other * Z + k]
+            z = me_ref[0] ^ k
             for c, (lo, hi) in enumerate(cuts):
                 copy = pltpu.make_async_copy(
-                    piece.at[:, :, lo:hi], held[c].at[me_ref[0] ^ k, :, me_ref[2] ^ other], in_sem.at[len(copies)]
+                    pieces[other].at[:, k, 0 : held[c].shape[3], lo:hi], held[c].at[z, :, me_ref[2] ^ other], in_sem.at[len(copies)]
                 )
                 copies.append((copy, k))
     for copy, _ in copies:
@@ -429,9 +519,9 @@
         copy.wait()
 
 
-def place(me, pieces, Z, widths, turned=0):
+def place(me, pieces, Z, widths, turned=0, rows=None):
     n = len(pieces)
-    R, rows = pieces[0].shape[0], pieces[0].shape[-2]
+    R, rows = pieces[0].shape[0], rows or pieces[0].shape[-2]
     cuts = cut_points(widths)
     if turned and rows % 8:
         outs = place(me, pieces, Z, widths)
@@ -701,24 +791,18 @@
     return [sums[0]] + [lax.ppermute(sums[k], "dp", pairs(len(sums), k)) for k in range(1, len(sums))]
 
 
-def lookup_body(start, trows, rows, index_ref, sg_ref, w_ref, r_ref, chosen_ref, back_ref, lead_ref, held, sem):
-    seqs, _, width = held.shape
-    copies = []
-    for s in range(seqs):
-        owner, within = index_ref[s] // trows, index_ref[s] % trows
-        at = owner * rows + within % rows
-        row = pl.multiple_of((at // 16) * 16, 16)
-        col = pl.multiple_of(start + width * (within // rows), LANES)
-        copies.append(
-            (pltpu.make_async_copy(w_ref.at[pl.ds(row, 16), pl.ds(col, width)], held.at[s], sem.at[s]), at % 16)
-        )
-        copies[s][0].start()
+def lookup_body(found, me_ref, sg_ref, r_ref, *refs):
+    chosen_ref, back_ref, lead_ref = refs[found:]
+    seqs = sg_ref.shape[0]
     chosen_ref[...] = jnp.zeros_like(chosen_ref)
-    line = lax.broadcasted_iota(jnp.int32, (16, width), 0)
-    for s in range(seqs):
-        copies[s][0].wait()
-        block = jnp.where(line == copies[s][1], held[s].astype(f32), 0.0)
-        chosen_ref[s : s + 1, :] = jnp.sum(block, axis=0, keepdims=True)
+    if found == 2:
+        total = jnp.zeros((2 * seqs, r_ref.shape[1]), f32)
+        for ref in refs[:2]:
+            for r in range(ref.shape[0]):
+                total += ref[r, 0, ref.shape[2] - 2 * seqs :].astype(f32)
+        chosen_ref[0:seqs, :] = jnp.where(me_ref[2] == 0, total[:seqs], total[seqs:])
+    else:
+        chosen_ref[0:seqs, :] = refs[0][...].astype(f32)
     back_ref[...] = jnp.zeros_like(back_ref)
     back_ref[0:seqs, :] = sg_ref[...] * chosen_ref[0:seqs, :]
     lead = dot(back_ref[...].astype(bf16), r_ref[...], 1, 1)
@@ -726,13 +810,15 @@
         lead_ref[s] = lead[s : s + 1, :]
 
 
-def lookup(index, sg, wide, F, D, width, trows, rows):
+def lookup(me, sg, wide, F, D, width, found):
     seqs = sg.shape[0]
+    specs = [None]
+    if len(found) == 2:
+        specs = [pl.BlockSpec((a.shape[0], 1, a.shape[2], width), lambda i: (0, 0, 0, 0)) for a in found]
     return once(
-        functools.partial(lookup_body, F + D + width, trows, rows), "lookup", (index, sg, wide, wide),
-        [SMEM, None, ANY, pl.BlockSpec((D, width), lambda i: (0, (F + D) // width))],
-        [sds((16, width), f32), sds((16, width), f32), sds((seqs, 1, D), f32)],
-        scratch=[pltpu.VMEM((seqs, 16, width), bf16), pltpu.SemaphoreType.DMA((seqs,))], moved=4 * D * width,
+        functools.partial(lookup_body, len(found)), "lookup", (me, sg, wide, *found),
+        [SMEM, None, pl.BlockSpec((D, width), lambda i: (0, (F + D) // width))] + specs,
+        [sds((16, width), f32), sds((16, width), f32), sds((seqs, 1, D), f32)], moved=4 * D * width,
     )
 
 
@@ -796,6 +882,7 @@
     Rw = retriever_weight.shape[1]
     seqs = document_index.shape[0]
     L = T // seqs
+    per = 2 - seqs % 2
     gc = 4 * HEAD_DIM
     G = D // gc
     Q = F // D
@@ -807,33 +894,40 @@
         v.reshape(1, -1)
         for v in (query_bias, value_bias, output_bias, first_gain, first_shift, down_bias, second_gain, second_shift, up_bias)
     ]
-    head, rest, wide = pack(input_weight, output_weight, retriever_weight, up_weight, document_table, vectors, gc)
+    head, rest, wide = pack(document_index, input_weight, output_weight, retriever_weight, up_weight, vectors, gc)
     wide = lax.all_gather(wide, both, axis=0, tiled=True)
-    head = repeat(along_dp(head, Z), R)
-    rest = along_dp(after(rest, head), Z)
+    head = repeat(along_dp([head] * Z), R)
+    rest = along_dp([after(rest, head)] * Z)
     head = between_chips(head, N)
     win_one, small, vec = place(me, [head, other_core(head, N)], Z, [3 * gc, LANES], turned=16)
-    rest = repeat([after(p, vec) for p in rest], R)
-    wd = along_dp(after(down_weight, rest), Z)
+    ub = bias_row(small, vec, Z, N, Q)
+    rest = repeat([after(p, ub) for p in rest], R)
+    if rows % 8:
+        found, asked = [lax.all_gather(document_table, both, axis=0, tiled=True)[document_index]], ()
+    else:
+        asked = along_dp(ask(me, small, after(document_table, rest), seqs, Z, N, UB + Q))
+    wd = along_dp([after(down_weight, rest)] * Z)
     rest = between_chips(rest, N)
 
-    ub = bias_row(small, vec, Z, N, Q)
     held = attend(after(tokens, ub), win_one, vec, seqs, G, 0)
-    wd = repeat([after(w, held[2]) for w in wd], R)
+    wd = repeat([after(w, held[2]) for w in wd], R, asked)
     rest = after(rest, wd)
     (win_two,) = place(me, [rest, other_core(rest, N)], Z, [3 * gc * (G - 1)])
     wd = between_chips(wd, N)
     qkv, soft, ctx = attend(tokens, win_two, vec, seqs, G, 1, held)
     wd = after(wd, ctx)
-    n, inv, first, act, slope = up(ctx, tokens, vec, wide, ub, L)
-    (wd,) = place(me, [after(wd, first), other_core(wd, N)], Z, [D])
-    chosen, back_projected, lead = lookup(document_index, score_grad.reshape(seqs, 1), after(wide, first), F, D, Rw, trows, rows)
-    final, top, two, feed, inner, gsg, gss, gdb, gub = down(first, act, slope, wd, vec, output_grad, lead, seqs)
+    n, inv, first, act, slope = up(ctx, tokens, vec, wide, ub, L, L // 2)
+    wd = [wd, other_core(wd, N)]
+    if rows % 8 == 0:
+        found = wd
+    (wd,) = place(me, [after(wd[0], first), wd[1]], Z, [D], rows=down_weight.shape[0])
+    chosen, back_projected, lead = lookup(me, score_grad.reshape(seqs, 1), after(wide, first), F, D, Rw, found)
+    final, top, two, feed, inner, gsg, gss, gdb, gub = down(first, act, slope, wd, vec, output_grad, lead, seqs, per)
     scores, retriever_back, term = score(top, wide, F, chosen, back_projected, score_grad.reshape(seqs, 1), document_index.reshape(seqs, 1))
     down_parts = down_grad(me, Z, N, act, feed)
     up_parts = grads(me, Z, N, "up_grad", [after(first, *down_parts), inner], [([(0, None)], (1, None))], tile=D)
     feed_sums = pair_sum([down_parts, up_parts], N, up_parts[0], me, term)
-    one, att, bctx, gfg, gfs, gob = mid(after(two, feed_sums), inner, wide, n, inv, vec, L)
+    one, att, bctx, gfg, gfs, gob = mid(after(two, feed_sums), inner, wide, n, inv, vec, per * L, L)
     mixed, gq, gv = attend_back(qkv, soft, ctx, after(bctx, feed_sums), seqs)
     parts = grads(
         me, Z, N, "mix_grad", [ctx, att, tokens, mixed],

time: 341 us -> 332 us (0.974)
  waiting for transfers between devices: 55.5 us -> 43.6 us
  starting transfers between devices: 41.9 us -> 47.7 us
    all_gather x1, waiting for transfers between devices: 6.58 us -> 0.01 us  [local(): wide = lax.all_gather(wide, both, axis=0, tiled=True)]
    all_to_all x4, waiting for transfers between devices: 21.5 us -> 16.1 us  [between_chips(): lax.all_to_all(blocks, 'fsdp', 0, 0, axis_index_groups=[list(range(c, N,...]
    ppermute x9 -> x12, starting transfers between devices: 15.4 us -> 20.7 us  [along_dp(): lax.ppermute(b, 'dp', pairs(len(blocks), k))]
    pallas_call x26 -> x27, Pallas kernels: 200 us -> 197 us  [run(): pl.pallas_call(body, name=name, grid=grid, in_specs=in_specs, out_specs=o...]
    ppermute x9 -> x12, waiting for transfers between devices: 8.49 us -> 7.57 us  [along_dp(): lax.ppermute(b, 'dp', pairs(len(blocks), k))]
    unnamed x56 -> x60, local copies, waits for them, and re-layouts: 9.22 us -> 9.65 us
  transfers between devices with their start and end apart: 27 -> 30, of which waited for: 12 -> 10; matrix products, arithmetic and copies ran while one was open for 1% -> 1% of each run, Pallas kernels for 41% -> 42%
where the time goes in v4:
time: 332 us; the launch traced here: 331 us
  Pallas kernels  197 us (59%)
  starting transfers between devices  47.7 us (14%)
  waiting for transfers between devices  43.6 us (13%)
  local copies, waits for them, and re-layouts  14.4 us (4%)
  between operations  14.3 us (4%)
  blocking collectives  12.7 us (4%)
    pallas_call x27, Pallas kernels, run(): pl.pallas_call(body, name=name, grid=grid, in_specs=in_specs, out_specs=o...  197 us
    ppermute x12, starting transfers between devices, along_dp(): lax.ppermute(b, 'dp', pairs(len(blocks), k))  20.7 us
    all_to_all x4, starting transfers between devices, between_chips(): lax.all_to_all(blocks, 'fsdp', 0, 0, axis_index_groups=[list(range(c, N,...  17.1 us
    all_to_all x4, waiting for transfers between devices, between_chips(): lax.all_to_all(blocks, 'fsdp', 0, 0, axis_index_groups=[list(range(c, N,...  16.1 us
    ppermute x7, waiting for transfers between devices, other_core(): return lax.ppermute(blocks, 'fsdp', pairs(N, 1))  13.2 us
    all_to_all x1, blocking collectives, between_chips(): lax.all_to_all(blocks, 'fsdp', 0, 0, axis_index_groups=[list(range(c, N,...  12.7 us
    unnamed x60, local copies, waits for them, and re-layouts  9.65 us
    ppermute x6, starting transfers between devices, along_dp_sums(): lax.ppermute(sums[k], 'dp', pairs(len(sums), k))  8.77 us
  transfers between devices with their start and end apart: 30, of which 10 were waited for; matrix products, arithmetic and copies ran while one was open for 1% of the time, Pallas kernels for 42%

profile of v4, /device:TPU:0, one launch (start us, length us, event | category | flops | bytes accessed | tf_op | source)
XLA Modules:
  0.0 330.8 jit_solution(9561519627201418234)
XLA Ops:
  7.2 1.9 pack.1
  9.1 3.1 collective-permute-start
  12.2 2.6 collective-permute-start.1
  14.8 3.3 %collective-permute-done.1.refs_2_ = bf16[24,896]{1,0:T(8,128)(2,1)S(1)} collective-permute-done((bf16[24,896]{1,0:T(8,128)(2,1)}, bf16[24,896]{1,0:T(8,128)(2,1)S(1)}, u32[]{:S(2)}, u32[]{:S(2)}) %collective-permute-start.1) | collective-permute-done | bytes 43040 | tf_op jit(solution)/shard_map/ppermute | solution.py:417
  18.1 2.7 collective-permute-done.2.refs_3_
  23.2 12.7 %all_to_all.25.refs_0_ = bf16[4,4,24,896]{3,2,1,0:T(8,128)(2,1)S(1)} all-to-all(bf16[4,4,24,896]{3,2,1,0:T(8,128)(2,1)} %repeat.3), channel_id=1, replica_groups={{0,2,4,6},{1,3,5,7},{8,10,12,14},{9,11,13,15},{16,18,20,22},{17,19,21,2..., dimensions={0} | all-to-all | bytes 1376256 | tf_op jit(solution)/shard_map/all_to_all | solution.py:421
  35.9 2.0 collective-permute-start.6
  37.9 2.3 collective-permute-start.4
  41.7 3.7 %place.3 = (bf16[4,4,2,24,768]{4,3,2,1,0:T(8,128)(2,1)}, bf16[4,4,2,24,128]{4,3,2,1,0:T(8,128)(2,1)}, f32[16,768]{1,0:T(8,128)}) custom-call(s32[3]{0:T(128)} %pad_add_fusion.me_ref, bf16[4,4,24,896]{3,2,1,0:T(8,128)(2,1)} %copy-done.3, bf16[4,4,24,896]{3,2,1,0:T(8,128)(2,1)} %copy-done.6), custom_call_target="tpu_custom_call" | custom-call | bytes 2752512 | tf_op jit(solution)/shard_map/place/pallas_call | solution.py:34
  45.4 1.8 bias_row.1.ub_ref
  50.0 2.1 repeat.4
  52.1 3.5 %all-to-all-start.1 = ((bf16[4,4,24,1536]{3,2,1,0:T(8,128)(2,1)}), bf16[4,4,24,1536]{3,2,1,0:T(8,128)(2,1)S(1)}, u32[]{:S(2)}, u32[]{:S(2)}) async-start(bf16[4,4,24,1536]{3,2,1,0:T(8,128)(2,1)} %repeat.4), calls=%async_computation.1 | async-start | bytes 2359296 | tf_op jit(solution)/shard_map/all_to_all | solution.py:421
  55.6 2.3 collective-permute-start.9
  58.0 2.1 collective-permute-start.7
  60.1 2.1 ask.1
  62.2 2.7 collective-permute-start.11
  64.9 3.5 %collective-permute-start.12 = (bf16[8,512]{1,0:T(8,128)(2,1)}, bf16[8,512]{1,0:T(8,128)(2,1)S(1)}, u32[]{:S(2)}, u32[]{:S(2)}) collective-permute-start(bf16[8,512]{1,0:T(8,128)(2,1)} %get-tuple-element.131), channel_id=1, source_target_pairs={{0,24},{8,16},{16,8},{24,0},{1,25},{9,17},{17,9},{25,1},{2,26},{10... | collective-permute-start | bytes 24584 | tf_op jit(solution)/shard_map/ppermute | solution.py:417
  68.4 10.1 %attend.2 = (bf16[3,1152,768]{2,1,0:T(8,128)(2,1)}, bf16[3,4,1152,288]{3,2,1,0:T(8,128)(2,1)}, bf16[3,1152,256]{2,1,0:T(8,128)(2,1)}) custom-call(bf16[1152,768]{1,0:T(8,128)(2,1)} %refs_2_.3, bf16[768,768]{1,0:T(8,128)(2,1)} %bitcast.50, f32[16,768]{1,0:T(8,128)} %get-tuple-element.114.v_ref), custom_call_target="tpu_custom_call" | custom-call | flops 2717908992 | bytes 7962624 | tf_op jit(solution)/shard_map/attend/pallas_call | solution.py:34
  79.2 2.9 repeat.5
  83.1 4.4 %all-to-all-start.2 = ((bf16[4,4,104,768]{3,2,1,0:T(8,128)(2,1)}), bf16[4,4,104,768]{3,2,1,0:T(8,128)(2,1)S(1)}, u32[]{:S(2)}, u32[]{:S(2)}) async-start(bf16[4,4,104,768]{3,2,1,0:T(8,128)(2,1)} %repeat.5), calls=%async_computation.2 | async-start | bytes 5111808 | tf_op jit(solution)/shard_map/all_to_all | solution.py:421
  87.5 3.7 %collective-permute-done.13.refs_1_ = bf16[4,4,24,1536]{3,2,1,0:T(8,128)(2,1)} collective-permute-done((bf16[4,4,24,1536]{3,2,1,0:T(8,128)(2,1)}, bf16[4,4,24,1536]{3,2,1,0:T(8,128)(2,1)}, u32[]{:S(2)}, u32[]{:S(2)}) %collective-permute-start.13) | collective-permute-done | bytes 1179680 | tf_op jit(solution)/shard_map/ppermute | solution.py:425
  91.2 3.2 place.4
  94.4 17.9 %attend.3 = (bf16[3,1152,768]{2,1,0:T(8,128)(2,1)}, bf16[3,4,1152,288]{3,2,1,0:T(8,128)(2,1)}, bf16[3,1152,256]{2,1,0:T(8,128)(2,1)}) custom-call(bf16[1152,768]{1,0:T(8,128)(2,1)} %refs_2_.3, bf16[768,1536]{1,0:T(8,128)(2,1)} %bitcast.34, f32[16,768]{1,0:T(8,128)} %get-tuple-element.114.v_ref, ...), custom_call_target="tpu_custom_call", output_to_operand_aliasing={{0}: (3, {}), {1}: (4, {}), {2}: (5, {})} | custom-call | flops 5435817984 | bytes 14155776 | tf_op jit(solution)/shard_map/attend/pallas_call | solution.py:34
  112.4 3.0 all-to-all-done.2.refs_0_
  116.2 18.4 %up.1 = (f32[1152,768]{1,0:T(8,128)}, f32[1152,1]{1,0:T(8,128)}, bf16[1152,768]{1,0:T(8,128)(2,1)}, bf16[1152,3072]{1,0:T(8,128)(2,1)}, bf16[1152,3072]{1,0:T(8,128)(2,1)}) custom-call(bf16[3,1152,256]{2,1,0:T(8,128)(2,1)} %get-tuple-element.135.ctx_ref.refs_0_, bf16[1152,768]{1,0:T(8,128)(2,1)} %refs_2_.3, ...), custom_call_target="tpu_custom_call" | custom-call | flops 6794772480 | bytes 28901376 | tf_op jit(solution)/shard_map/up/pallas_call | solution.py:34
  134.6 4.6 %place.5 = bf16[4,4,2,96,768]{4,3,2,1,0:T(8,128)(2,1)} custom-call(s32[3]{0:T(128)} %pad_add_fusion.me_ref, bf16[4,4,104,768]{3,2,1,0:T(8,128)(2,1)} %copy-done, bf16[4,4,104,768]{3,2,1,0:T(8,128)(2,1)} %collective-permute-done.14.refs_1_), custom_call_target="tpu_custom_call" | custom-call | bytes 9437184 | tf_op jit(solution)/shard_map/place/pallas_call | solution.py:34
  139.2 1.9 lookup.1
  141.1 21.4 %down.1 = (bf16[1152,768]{1,0:T(8,128)(2,1)}, f32[4,1,768]{2,1,0:T(1,128)}, f32[1152,768]{1,0:T(8,128)}, bf16[1152,768]{1,0:T(8,128)(2,1)}, bf16[1152,3072]{1,0:...) custom-call(bf16[1152,768]{1,0:T(8,128)(2,1)} %get-tuple-element.153.first_ref.refs_0, ...), custom_call_target="tpu_custom_call" | custom-call | flops 10871635968 | bytes 36569088 | tf_op jit(solution)/shard_map/down/pallas_call | solution.py:34
  162.5 10.5 %down_grad.1 = (bf16[4,4,96,768]{3,2,1,0:T(8,128)(2,1)}, bf16[4,4,96,768]{3,2,1,0:T(8,128)(2,1)}) custom-call(s32[3]{0:T(128)} %pad_add_fusion.me_ref, bf16[1152,3072]{1,0:T(8,128)(2,1)} %get-tuple-element.138.act_ref.x_ref, bf16[1152,768]{1,0:T(8,128)(2,1)} %get-tuple-element.150.y_ref), custom_call_target="tpu_custom_call" | custom-call | flops 5435817984 | bytes 13565952 | tf_op jit(solution)/shard_map/down_grad/pallas_call | solution.py:34
  173.1 10.3 %up_grad.1 = (bf16[4,4,24,3072]{3,2,1,0:T(8,128)(2,1)}, bf16[4,4,24,3072]{3,2,1,0:T(8,128)(2,1)}) custom-call(s32[3]{0:T(128)} %pad_add_fusion.me_ref, bf16[1152,768]{1,0:T(8,128)(2,1)} %get-tuple-element.153.first_ref.refs_0_, bf16[1152,3072]{1,0:T(8,128)(2,1)} %get-tuple-element.154.refs_1_.inner_ref), custom_call_target="tpu_custom_call" | custom-call | flops 5435817984 | bytes 13565952 | tf_op jit(solution)/shard_map/up_grad/pallas_call | solution.py:34
  184.6 2.0 score.1
  186.9 2.7 collective-permute-done.17.refs_5_
  189.6 2.0 collective-permute-done.15.refs_2_
  191.7 6.5 %pair_sum.2 = bf16[4,4,200,768]{3,2,1,0:T(8,128)(2,1)} custom-call(s32[3]{0:T(128)} %pad_add_fusion.me_ref, bf16[4,4,96,768]{3,2,1,0:T(8,128)(2,1)} %get-tuple-element.156.refs_0_, bf16[4,4,24,3072]{3,2,1,0:T(8,128)(2,1)} %get-tuple-element.155.refs_1_, bf16[4,4,96,768]{3,2,1,0:T(8,128)(2,1)} %collective-permute-done.15.refs_2_, ...), custom_call_target="tpu_custom_call" | custom-call | bytes 14745600 | tf_op jit(solution)/shard_map/pair_sum/pallas_call | solution.py:34
  198.2 5.0 %all-to-all-start.3 = ((bf16[4,4,200,768]{3,2,1,0:T(8,128)(2,1)}), bf16[4,4,200,768]{3,2,1,0:T(8,128)(2,1)}, u32[]{:S(2)}, u32[]{:S(2)}) async-start(bf16[4,4,200,768]{3,2,1,0:T(8,128)(2,1)} %pair_sum.2), calls=%async_computation.3 | async-start | bytes 9830400 | tf_op jit(solution)/shard_map/all_to_all | solution.py:421
  203.2 15.2 %mid.1 = (f32[1152,768]{1,0:T(8,128)}, bf16[1152,768]{1,0:T(8,128)(2,1)}, bf16[1152,768]{1,0:T(8,128)(2,1)}, f32[1,768]{1,0:T(1,128)}, f32[1,768]{1,0:T(1,128)}, /*index=5*/f32[1,768]{1,0:T(1,128)}) custom-call(f32[1152,768]{1,0:T(8,128)} %get-tuple-element.159.two_ref, bf16[1152,3072]{1,0:T(8,128)(2,1)} %get-tuple-element.154.refs_1_.inner_ref, ...), custom_call_target="tpu_custom_call" | custom-call | flops 6794772480 | bytes 27131904 | tf_op jit(solution)/shard_map/mid/pallas_call | solution.py:34
  218.4 20.9 %attend_back.1 = (bf16[3,1152,768]{2,1,0:T(8,128)(2,1)}, f32[1,768]{1,0:T(1,128)}, f32[1,768]{1,0:T(1,128)}) custom-call(bf16[3,1152,768]{2,1,0:T(8,128)(2,1)} %get-tuple-element.164.qkv_ref, bf16[3,4,1152,288]{3,2,1,0:T(8,128)(2,1)} %get-tuple-element.165.soft_ref, bf16[3,1152,256]{2,1,0:T(8,128)(2,1)} %get-tuple-element.135.ctx_ref.refs_0_, ...), custom_call_target="tpu_custom_call" | custom-call | flops 8153726976 | bytes 22118400 | tf_op jit(solution)/shard_map/attend_back/pallas_call | solution.py:34
  239.3 12.7 %mix_grad.1 = (bf16[4,4,24,3328]{3,2,1,0:T(8,128)(2,1)}, bf16[4,4,24,3328]{3,2,1,0:T(8,128)(2,1)}) custom-call(s32[3]{0:T(128)} %pad_add_fusion.me_ref, bf16[3,1152,256]{2,1,0:T(8,128)(2,1)} %get-tuple-element.135.ctx_ref.refs_0_, bf16[1152,768]{1,0:T(8,128)(2,1)} %get-tuple-element.163.refs_1_, bf16[1152,768]{1,0:T(8,128)(2,1)} %refs_2_.3, ...), custom_call_target="tpu_custom_call" | custom-call | flops 5888802816 | bytes 14548992 | tf_op jit(solution)/shard_map/mix_grad/pallas_call | solution.py:34
  252.4 4.7 %collective-permute-done.18.refs_1_ = bf16[4,4,24,3328]{3,2,1,0:T(8,128)(2,1)S(1)} collective-permute-done((bf16[4,4,24,3328]{3,2,1,0:T(8,128)(2,1)}, bf16[4,4,24,3328]{3,2,1,0:T(8,128)(2,1)S(1)}, u32[]{:S(2)}, u32[]{:S(2)}) %collective-permute-start.18) | collective-permute-done | bytes 2555936 | tf_op jit(solution)/shard_map/ppermute | solution.py:425
  258.6 4.7 %pair_sum.3 = bf16[4,4,24,3328]{3,2,1,0:T(8,128)(2,1)} custom-call(s32[3]{0:T(128)} %broadcast_1_me_ref.2.me_ref, bf16[4,4,24,3328]{3,2,1,0:T(8,128)(2,1)} %get-tuple-element.179.refs_0_, bf16[4,4,24,3328]{3,2,1,0:T(8,128)(2,1)} %copy-done.4), custom_call_target="tpu_custom_call" | custom-call | bytes 7667712 | tf_op jit(solution)/shard_map/pair_sum/pallas_call | solution.py:34
  263.3 4.1 %all-to-all-start.4 = ((bf16[4,4,24,3328]{3,2,1,0:T(8,128)(2,1)}), bf16[4,4,24,3328]{3,2,1,0:T(8,128)(2,1)S(1)}, u32[]{:S(2)}, u32[]{:S(2)}) async-start(bf16[4,4,24,3328]{3,2,1,0:T(8,128)(2,1)} %pair_sum.3), calls=%async_computation.4 | async-start | bytes 5111808 | tf_op jit(solution)/shard_map/all_to_all | solution.py:421
  267.4 3.8 %chips_sum.2 = (f32[208,768]{1,0:T(8,128)}, bf16[208,768]{1,0:T(8,128)(2,1)}, bf16[208,768]{1,0:T(8,128)(2,1)}, bf16[208,768]{1,0:T(8,128)(2,1)}) custom-call(s32[3]{0:T(128)} %pad_add_fusion.me_ref, bf16[4,4,200,768]{3,2,1,0:T(8,128)(2,1)} %all-to-all-done.3.in_ref), custom_call_target="tpu_custom_call" | custom-call | bytes 6193152 | tf_op jit(solution)/shard_map/chips_sum/pallas_call | solution.py:34
  275.6 9.1 %tokens_back.1 = bf16[1152,768]{1,0:T(8,128)(2,1)} custom-call(f32[1152,768]{1,0:T(8,128)} %get-tuple-element.183.one_ref, bf16[3,1152,768]{2,1,0:T(8,128)(2,1)} %get-tuple-element.168.refs_3_.mixed_ref, bf16[768,768]{1,0:T(8,128)(2,1)} %bitcast.51, bf16[768,1536]{1,0:T(8,128)(2,1)} %bitcast.35), custom_call_target="tpu_custom_call" | custom-call | flops 4076863488 | bytes 10616832 | tf_op jit(solution)/shard_map/tokens_back/pallas_call | solution.py:34
  284.7 13.0 %all-to-all-done.4.in_ref = bf16[4,4,24,3328]{3,2,1,0:T(8,128)(2,1)S(1)} async-done(((bf16[4,4,24,3328]{3,2,1,0:T(8,128)(2,1)}), bf16[4,4,24,3328]{3,2,1,0:T(8,128)(2,1)S(1)}, u32[]{:S(2)}, u32[]{:S(2)}) %all-to-all-start.4) | async-done | bytes 2555936 | tf_op jit(solution)/shard_map/all_to_all | solution.py:421
  299.2 2.8 chips_sum.3
  308.5 2.6 last_feed.1
  311.1 6.8 %collective-permute-done.23.refs_2_ = bf16[24,3328]{1,0:T(8,128)(2,1)S(1)} collective-permute-done((bf16[24,3328]{1,0:T(8,128)(2,1)}, bf16[24,3328]{1,0:T(8,128)(2,1)S(1)}, u32[]{:S(2)}, u32[]{:S(2)}) %collective-permute-start.23) | collective-permute-done | bytes 159776 | tf_op jit(solution)/shard_map/ppermute | solution.py:791
  319.2 1.9 last_sum.1
  (109 shorter events, 28.9 us)
Async XLA Ops:
  7.2 109.0 %all-gather.2.cloned.1.call-start = ((), (), s32[]{:S(2)}) async-start(), calls=%async_computation.5 | async-start | bytes 6285312 | tf_op jit(solution)/shard_map/all_gather | solution.py:898
  9.1 5.7 %collective-permute-start = (bf16[24,896]{1,0:T(8,128)(2,1)}, bf16[24,896]{1,0:T(8,128)(2,1)S(1)}, u32[]{:S(2)}, u32[]{:S(2)}) collective-permute-start(bf16[24,896]{1,0:T(8,128)(2,1)} %get-tuple-element.111.refs_0_), channel_id=1, source_target_pairs={{0,8},{8,0},{16,24},{24,16},{1,9},{9,1},{17,25},{25,17},{2,10},{10... | collective-permute-start | bytes 129032 | tf_op jit(solution)/shard_map/ppermute | solution.py:417
  12.2 5.9 %collective-permute-start.1 = (bf16[24,896]{1,0:T(8,128)(2,1)}, bf16[24,896]{1,0:T(8,128)(2,1)S(1)}, u32[]{:S(2)}, u32[]{:S(2)}) collective-permute-start(bf16[24,896]{1,0:T(8,128)(2,1)} %get-tuple-element.111.refs_0_), channel_id=1, source_target_pairs={{0,16},{8,24},{16,0},{24,8},{1,17},{9,25},{17,1},{25,9},{2,18},{10... | collective-permute-start | bytes 129032 | tf_op jit(solution)/shard_map/ppermute | solution.py:417
  14.8 6.0 %collective-permute-start.2 = (bf16[24,896]{1,0:T(8,128)(2,1)}, bf16[24,896]{1,0:T(8,128)(2,1)S(1)}, u32[]{:S(2)}, u32[]{:S(2)}) collective-permute-start(bf16[24,896]{1,0:T(8,128)(2,1)} %get-tuple-element.111.refs_0_), channel_id=1, source_target_pairs={{0,24},{8,16},{16,8},{24,0},{1,25},{9,17},{17,9},{25,1},{2,26},{10... | collective-permute-start | bytes 129032 | tf_op jit(solution)/shard_map/ppermute | solution.py:417
  14.8 6.0 %copy-start.20 = (bf16[24,896]{1,0:T(8,128)(2,1)}, bf16[24,896]{1,0:T(8,128)(2,1)S(1)}, u32[]{:S(2)}) copy-start(bf16[24,896]{1,0:T(8,128)(2,1)S(1)} %collective-permute-done.refs_1_) | copy-start | bytes 129028
  18.1 2.7 copy-start.21
  35.9 5.0 %copy-start.3 = (bf16[4,4,24,896]{3,2,1,0:T(8,128)(2,1)}, bf16[4,4,24,896]{3,2,1,0:T(8,128)(2,1)S(1)}, u32[]{:S(2)}) copy-start(bf16[4,4,24,896]{3,2,1,0:T(8,128)(2,1)S(1)} %all_to_all.25.refs_0_) | copy-start | bytes 2064388
  35.9 5.0 %collective-permute-start.3 = (bf16[4,4,24,896]{3,2,1,0:T(8,128)(2,1)S(1)}, bf16[4,4,24,896]{3,2,1,0:T(8,128)(2,1)S(1)}, u32[]{:S(2)}, u32[]{:S(2)}) collective-permute-start(bf16[4,4,24,896]{3,2,1,0:T(8,128)(2,1)S(1)} %all_to_all.25.refs_0_), channel_id=1, source_target_pairs={{0,1},{1,0},{2,3},{3,2},{4,5},{5,4},{6,7},{7,6},{8,9},{9,8},{10,11... | collective-permute-start | bytes 2064392 | tf_op jit(solution)/shard_map/ppermute | solution.py:425
  35.9 11.3 %collective-permute-start.6 = (bf16[24,1536]{1,0:T(8,128)(2,1)}, bf16[24,1536]{1,0:T(8,128)(2,1)S(1)}, u32[]{:S(2)}, u32[]{:S(2)}) collective-permute-start(bf16[24,1536]{1,0:T(8,128)(2,1)} %get-tuple-element.115.refs_0_), channel_id=1, source_target_pairs={{0,24},{8,16},{16,8},{24,0},{1,25},{9,17},{17,9},{25,1},{2,26},{10... | collective-permute-start | bytes 221192 | tf_op jit(solution)/shard_map/ppermute | solution.py:417
  37.9 10.8 %collective-permute-start.5 = (bf16[24,1536]{1,0:T(8,128)(2,1)}, bf16[24,1536]{1,0:T(8,128)(2,1)S(1)}, u32[]{:S(2)}, u32[]{:S(2)}) collective-permute-start(bf16[24,1536]{1,0:T(8,128)(2,1)} %get-tuple-element.115.refs_0_), channel_id=1, source_target_pairs={{0,16},{8,24},{16,0},{24,8},{1,17},{9,25},{17,1},{25,9},{2,18},{10... | collective-permute-start | bytes 221192 | tf_op jit(solution)/shard_map/ppermute | solution.py:417
  37.9 10.8 %collective-permute-start.4 = (bf16[24,1536]{1,0:T(8,128)(2,1)}, bf16[24,1536]{1,0:T(8,128)(2,1)S(1)}, u32[]{:S(2)}, u32[]{:S(2)}) collective-permute-start(bf16[24,1536]{1,0:T(8,128)(2,1)} %get-tuple-element.115.refs_0_), channel_id=1, source_target_pairs={{0,8},{8,0},{16,24},{24,16},{1,9},{9,1},{17,25},{25,17},{2,10},{10... | collective-permute-start | bytes 221192 | tf_op jit(solution)/shard_map/ppermute | solution.py:417
  40.9 14.8 %copy-start.13 = (bf16[96,768]{1,0:T(8,128)(2,1)S(1)}, bf16[96,768]{1,0:T(8,128)(2,1)}, u32[]{:S(2)}) copy-start(bf16[96,768]{1,0:T(8,128)(2,1)} %refs_0_.2) | copy-start | bytes 442372
  40.9 0.8 copy-start.6
  47.2 1.5 copy-start.17
  52.1 30.0 %all-to-all-start.1 = ((bf16[4,4,24,1536]{3,2,1,0:T(8,128)(2,1)}), bf16[4,4,24,1536]{3,2,1,0:T(8,128)(2,1)S(1)}, u32[]{:S(2)}, u32[]{:S(2)}) async-start(bf16[4,4,24,1536]{3,2,1,0:T(8,128)(2,1)} %repeat.4), calls=%async_computation.1 | async-start | bytes 2359296 | tf_op jit(solution)/shard_map/all_to_all | solution.py:421
  55.6 9.3 %collective-permute-start.9 = (bf16[96,768]{1,0:T(8,128)(2,1)S(1)}, bf16[96,768]{1,0:T(8,128)(2,1)S(1)}, u32[]{:S(2)}, u32[]{:S(2)}) collective-permute-start(bf16[96,768]{1,0:T(8,128)(2,1)S(1)} %copy-done.13), channel_id=1, source_target_pairs={{0,24},{8,16},{16,8},{24,0},{1,25},{9,17},{17,9},{25,1},{2,26},{10... | collective-permute-start | bytes 442376 | tf_op jit(solution)/shard_map/ppermute | solution.py:417
  58.0 20.5 %collective-permute-start.8 = (bf16[96,768]{1,0:T(8,128)(2,1)S(1)}, bf16[96,768]{1,0:T(8,128)(2,1)S(1)}, u32[]{:S(2)}, u32[]{:S(2)}) collective-permute-start(bf16[96,768]{1,0:T(8,128)(2,1)S(1)} %copy-done.13), channel_id=1, source_target_pairs={{0,16},{8,24},{16,0},{24,8},{1,17},{9,25},{17,1},{25,9},{2,18},{10... | collective-permute-start | bytes 442376 | tf_op jit(solution)/shard_map/ppermute | solution.py:417
  58.0 20.5 %collective-permute-start.7 = (bf16[96,768]{1,0:T(8,128)(2,1)S(1)}, bf16[96,768]{1,0:T(8,128)(2,1)S(1)}, u32[]{:S(2)}, u32[]{:S(2)}) collective-permute-start(bf16[96,768]{1,0:T(8,128)(2,1)S(1)} %copy-done.13), channel_id=1, source_target_pairs={{0,8},{8,0},{16,24},{24,16},{1,9},{9,1},{17,25},{25,17},{2,10},{10... | collective-permute-start | bytes 442376 | tf_op jit(solution)/shard_map/ppermute | solution.py:417
  62.2 16.3 %collective-permute-start.10 = (bf16[8,512]{1,0:T(8,128)(2,1)}, bf16[8,512]{1,0:T(8,128)(2,1)S(1)}, u32[]{:S(2)}, u32[]{:S(2)}) collective-permute-start(bf16[8,512]{1,0:T(8,128)(2,1)} %get-tuple-element.129), channel_id=1, source_target_pairs={{0,8},{8,0},{16,24},{24,16},{1,9},{9,1},{17,25},{25,17},{2,10},{10... | collective-permute-start | bytes 24584 | tf_op jit(solution)/shard_map/ppermute | solution.py:417
  62.2 16.3 %collective-permute-start.11 = (bf16[8,512]{1,0:T(8,128)(2,1)}, bf16[8,512]{1,0:T(8,128)(2,1)S(1)}, u32[]{:S(2)}, u32[]{:S(2)}) collective-permute-start(bf16[8,512]{1,0:T(8,128)(2,1)} %get-tuple-element.130), channel_id=1, source_target_pairs={{0,16},{8,24},{16,0},{24,8},{1,17},{9,25},{17,1},{25,9},{2,18},{10... | collective-permute-start | bytes 24584 | tf_op jit(solution)/shard_map/ppermute | solution.py:417
  64.9 13.5 %copy-start.14 = (bf16[96,768]{1,0:T(8,128)(2,1)}, bf16[96,768]{1,0:T(8,128)(2,1)S(1)}, u32[]{:S(2)}) copy-start(bf16[96,768]{1,0:T(8,128)(2,1)S(1)} %collective-permute-done.9.refs_3_) | copy-start | bytes 442372
  64.9 13.6 %collective-permute-start.12 = (bf16[8,512]{1,0:T(8,128)(2,1)}, bf16[8,512]{1,0:T(8,128)(2,1)S(1)}, u32[]{:S(2)}, u32[]{:S(2)}) collective-permute-start(bf16[8,512]{1,0:T(8,128)(2,1)} %get-tuple-element.131), channel_id=1, source_target_pairs={{0,24},{8,16},{16,8},{24,0},{1,25},{9,17},{17,9},{25,1},{2,26},{10... | collective-permute-start | bytes 24584 | tf_op jit(solution)/shard_map/ppermute | solution.py:417
  82.1 1.0 copy-start.2
  83.1 32.3 %all-to-all-start.2 = ((bf16[4,4,104,768]{3,2,1,0:T(8,128)(2,1)}), bf16[4,4,104,768]{3,2,1,0:T(8,128)(2,1)S(1)}, u32[]{:S(2)}, u32[]{:S(2)}) async-start(bf16[4,4,104,768]{3,2,1,0:T(8,128)(2,1)} %repeat.5), calls=%async_computation.2 | async-start | bytes 5111808 | tf_op jit(solution)/shard_map/all_to_all | solution.py:421
  87.5 3.7 %collective-permute-start.13 = (bf16[4,4,24,1536]{3,2,1,0:T(8,128)(2,1)}, bf16[4,4,24,1536]{3,2,1,0:T(8,128)(2,1)}, u32[]{:S(2)}, u32[]{:S(2)}) collective-permute-start(bf16[4,4,24,1536]{3,2,1,0:T(8,128)(2,1)} %copy-done.2), channel_id=1, source_target_pairs={{0,1},{1,0},{2,3},{3,2},{4,5},{5,4},{6,7},{7,6},{8,9},{9,8},{10,11... | collective-permute-start | bytes 3538952 | tf_op jit(solution)/shard_map/ppermute | solution.py:425
  94.4 21.0 %copy-start.29 = (f32[4]{0:T(128)S(1)}, f32[4]{0:T(128)}, u32[]{:S(2)}) copy-start(f32[4]{0:T(128)} %param.37) | copy-start | bytes 52
  115.4 19.2 %copy-start = (bf16[4,4,104,768]{3,2,1,0:T(8,128)(2,1)}, bf16[4,4,104,768]{3,2,1,0:T(8,128)(2,1)S(1)}, u32[]{:S(2)}) copy-start(bf16[4,4,104,768]{3,2,1,0:T(8,128)(2,1)S(1)} %all-to-all-done.2.refs_0_) | copy-start | bytes 7667716
  115.4 19.2 %collective-permute-start.14 = (bf16[4,4,104,768]{3,2,1,0:T(8,128)(2,1)S(1)}, bf16[4,4,104,768]{3,2,1,0:T(8,128)(2,1)}, u32[]{:S(2)}, u32[]{:S(2)}) collective-permute-start(bf16[4,4,104,768]{3,2,1,0:T(8,128)(2,1)S(1)} %all-to-all-done.2.refs_0_), channel_id=1, source_target_pairs={{0,1},{1,0},{2,3},{3,2},{4,5},{5,4},{6,7},{7,6},{8,9},{9,8},{10,11... | collective-permute-start | bytes 7667720 | tf_op jit(solution)/shard_map/ppermute | solution.py:425
  173.1 10.8 %copy-start.27 = (s32[4]{0:T(128)S(1)}, s32[4]{0:T(128)}, u32[]{:S(2)}) copy-start(s32[4]{0:T(128)} %refs_0_.1) | copy-start | bytes 52
  183.4 6.2 %collective-permute-start.16 = (bf16[4,4,24,3072]{3,2,1,0:T(8,128)(2,1)}, bf16[4,4,24,3072]{3,2,1,0:T(8,128)(2,1)S(1)}, u32[]{:S(2)}, u32[]{:S(2)}) collective-permute-start(bf16[4,4,24,3072]{3,2,1,0:T(8,128)(2,1)} %get-tuple-element.157), channel_id=1, source_target_pairs={{0,1},{1,0},{2,3},{3,2},{4,5},{5,4},{6,7},{7,6},{8,9},{9,8},{10,11... | collective-permute-start | bytes 7077896 | tf_op jit(solution)/shard_map/ppermute | solution.py:425
  183.7 7.9 %collective-permute-start.15 = (bf16[4,4,96,768]{3,2,1,0:T(8,128)(2,1)}, bf16[4,4,96,768]{3,2,1,0:T(8,128)(2,1)}, u32[]{:S(2)}, u32[]{:S(2)}) collective-permute-start(bf16[4,4,96,768]{3,2,1,0:T(8,128)(2,1)} %get-tuple-element.152), channel_id=1, source_target_pairs={{0,1},{1,0},{2,3},{3,2},{4,5},{5,4},{6,7},{7,6},{8,9},{9,8},{10,11... | collective-permute-start | bytes 7077896 | tf_op jit(solution)/shard_map/ppermute | solution.py:425
  186.6 3.1 collective-permute-start.17
  189.6 2.0 copy-start.26
  189.6 2.0 copy-start.5
  198.2 65.1 %all-to-all-start.3 = ((bf16[4,4,200,768]{3,2,1,0:T(8,128)(2,1)}), bf16[4,4,200,768]{3,2,1,0:T(8,128)(2,1)}, u32[]{:S(2)}, u32[]{:S(2)}) async-start(bf16[4,4,200,768]{3,2,1,0:T(8,128)(2,1)} %pair_sum.2), calls=%async_computation.3 | async-start | bytes 9830400 | tf_op jit(solution)/shard_map/all_to_all | solution.py:421
  252.1 5.0 %collective-permute-start.18 = (bf16[4,4,24,3328]{3,2,1,0:T(8,128)(2,1)}, bf16[4,4,24,3328]{3,2,1,0:T(8,128)(2,1)S(1)}, u32[]{:S(2)}, u32[]{:S(2)}) collective-permute-start(bf16[4,4,24,3328]{3,2,1,0:T(8,128)(2,1)} %get-tuple-element.180), channel_id=1, source_target_pairs={{0,1},{1,0},{2,3},{3,2},{4,5},{5,4},{6,7},{7,6},{8,9},{9,8},{10,11... | collective-permute-start | bytes 7667720 | tf_op jit(solution)/shard_map/ppermute | solution.py:425
  257.1 1.5 copy-start.4
  263.3 34.5 %all-to-all-start.4 = ((bf16[4,4,24,3328]{3,2,1,0:T(8,128)(2,1)}), bf16[4,4,24,3328]{3,2,1,0:T(8,128)(2,1)S(1)}, u32[]{:S(2)}, u32[]{:S(2)}) async-start(bf16[4,4,24,3328]{3,2,1,0:T(8,128)(2,1)} %pair_sum.3), calls=%async_computation.4 | async-start | bytes 5111808 | tf_op jit(solution)/shard_map/all_to_all | solution.py:421
  271.2 33.6 %collective-permute-start.19 = (bf16[208,768]{1,0:T(8,128)(2,1)}, bf16[208,768]{1,0:T(8,128)(2,1)S(1)}, u32[]{:S(2)}, u32[]{:S(2)}) collective-permute-start(bf16[208,768]{1,0:T(8,128)(2,1)} %get-tuple-element.188), channel_id=1, source_target_pairs={{0,8},{8,0},{16,24},{24,16},{1,9},{9,1},{17,25},{25,17},{2,10},{10... | collective-permute-start | bytes 958472 | tf_op jit(solution)/shard_map/ppermute | solution.py:791
  272.9 34.1 %collective-permute-start.20 = (bf16[208,768]{1,0:T(8,128)(2,1)}, bf16[208,768]{1,0:T(8,128)(2,1)S(1)}, u32[]{:S(2)}, u32[]{:S(2)}) collective-permute-start(bf16[208,768]{1,0:T(8,128)(2,1)} %get-tuple-element.189), channel_id=1, source_target_pairs={{0,16},{8,24},{16,0},{24,8},{1,17},{9,25},{17,1},{25,9},{2,18},{10... | collective-permute-start | bytes 958472 | tf_op jit(solution)/shard_map/ppermute | solution.py:791
  274.1 33.0 %collective-permute-start.21 = (bf16[208,768]{1,0:T(8,128)(2,1)}, bf16[208,768]{1,0:T(8,128)(2,1)S(1)}, u32[]{:S(2)}, u32[]{:S(2)}) collective-permute-start(bf16[208,768]{1,0:T(8,128)(2,1)} %get-tuple-element.190), channel_id=1, source_target_pairs={{0,24},{8,16},{16,8},{24,0},{1,25},{9,17},{17,9},{25,1},{2,26},{10... | collective-permute-start | bytes 958472 | tf_op jit(solution)/shard_map/ppermute | solution.py:791
  284.7 21.7 %copy-start.28 = (f32[4,1]{1,0:T(4,128)S(1)}, f32[4,1]{1,0:T(4,128)}, u32[]{:S(2)}) copy-start(f32[4,1]{1,0:T(4,128)} %get-tuple-element.148) | copy-start | bytes 52
  297.7 1.5 copy-start.1
  302.0 9.1 %collective-permute-start.22 = (bf16[24,3328]{1,0:T(8,128)(2,1)}, bf16[24,3328]{1,0:T(8,128)(2,1)S(1)}, u32[]{:S(2)}, u32[]{:S(2)}) collective-permute-start(bf16[24,3328]{1,0:T(8,128)(2,1)} %get-tuple-element.193), channel_id=1, source_target_pairs={{0,8},{8,0},{16,24},{24,16},{1,9},{9,1},{17,25},{25,17},{2,10},{10... | collective-permute-start | bytes 479240 | tf_op jit(solution)/shard_map/ppermute | solution.py:791
  303.6 14.2 %collective-permute-start.23 = (bf16[24,3328]{1,0:T(8,128)(2,1)}, bf16[24,3328]{1,0:T(8,128)(2,1)S(1)}, u32[]{:S(2)}, u32[]{:S(2)}) collective-permute-start(bf16[24,3328]{1,0:T(8,128)(2,1)} %get-tuple-element.194), channel_id=1, source_target_pairs={{0,16},{8,24},{16,0},{24,8},{1,17},{9,25},{17,1},{25,9},{2,18},{10... | collective-permute-start | bytes 479240 | tf_op jit(solution)/shard_map/ppermute | solution.py:791
  304.8 2.2 copy-start.7
  304.8 13.1 %collective-permute-start.24 = (bf16[24,3328]{1,0:T(8,128)(2,1)}, bf16[24,3328]{1,0:T(8,128)(2,1)S(1)}, u32[]{:S(2)}, u32[]{:S(2)}) collective-permute-start(bf16[24,3328]{1,0:T(8,128)(2,1)} %get-tuple-element.195), channel_id=1, source_target_pairs={{0,24},{8,16},{16,8},{24,0},{1,25},{9,17},{17,9},{25,1},{2,26},{10... | collective-permute-start | bytes 479240 | tf_op jit(solution)/shard_map/ppermute | solution.py:791
  311.1 6.8 %copy-start.10 = (bf16[24,3328]{1,0:T(8,128)(2,1)}, bf16[24,3328]{1,0:T(8,128)(2,1)S(1)}, u32[]{:S(2)}) copy-start(bf16[24,3328]{1,0:T(8,128)(2,1)S(1)} %collective-permute-done.22.refs_1_) | copy-start | bytes 479236
  (12 other events, 8.0 us)
Sparse Core Ops, SparseCore 0:
  11.5 79.5 all-gather.1

commit v5 on v4

--- a/solution.py
+++ b/solution.py
@@ -9,6 +9,7 @@
 
 HEAD_DIM = 64
 EPS = 1e-12
+ROOM = {"tokens_back": 28, "chips_sum": 28, "last_sum": 28, "last_feed": 28, "pair_sum": 28, "lookup": 28, "score": 28, "place": 28, "repeat": 28, "ask": 28, "bias_row": 28}
 QB, VB, OB, FG, FS, DB, SG, SS, UB = range(9)
 bf16, f32 = jnp.bfloat16, jnp.float32
 
@@ -30,7 +31,7 @@
     return (lane >= h * HEAD_DIM) & (lane < (h + 1) * HEAD_DIM)
 
 
-def run(body, name, grid, ins, in_specs, outs, out_specs, scratch=(), flops=0, moved=0, vmem=60, alias=None):
+def run(body, name, grid, ins, in_specs, outs, out_specs, scratch=(), flops=0, moved=0, alias=None):
     return pl.pallas_call(
         body,
         name=name,
@@ -41,7 +42,7 @@
         scratch_shapes=list(scratch),
         cost_estimate=estimate(flops, moved),
         input_output_aliases=alias or {},
-        compiler_params=pltpu.CompilerParams(vmem_limit_bytes=vmem * 2**20),
+        compiler_params=pltpu.CompilerParams(vmem_limit_bytes=ROOM.get(name, 60) * 2**20),
     )(*ins)
 
 
@@ -351,9 +352,9 @@
 LANES = 128
 
 
-def once(body, name, ins, in_specs, outs, scratch=(), moved=0, flops=0, vmem=60):
+def once(body, name, ins, in_specs, outs, scratch=(), moved=0, flops=0):
     specs = [full_spec(a.shape) if spec is None else spec for a, spec in zip(ins, in_specs)]
-    return run(body, name, (1,), ins, specs, outs, [full_spec(o.shape) for o in outs], scratch, flops, moved, vmem)
+    return run(body, name, (1,), ins, specs, outs, [full_spec(o.shape) for o in outs], scratch, flops, moved)
 
 
 def cut_points(widths):
@@ -534,7 +535,7 @@
         [ANY] * len(cuts) + ([full_spec((turned, total))] if turned else []),
         scratch=[pltpu.VMEM(s, bf16) for s in shapes] + ([pltpu.VMEM(shapes[-1], f32)] if turned else [])
         + [pltpu.SemaphoreType.DMA((2 * Z * len(cuts),)), pltpu.SemaphoreType.DMA((Z * len(cuts),))],
-        moved=4 * total * cuts[-1][1], vmem=60,
+        moved=4 * total * cuts[-1][1],
     )
     return [o.reshape(total, o.shape[-1]) for o in outs[: len(cuts)]] + list(outs[len(cuts) :])
 
@@ -687,7 +688,7 @@
         rows += term.shape[0]
     return run(
         functools.partial(pair_body, n), "pair_sum", (R,), [jnp.zeros((3,), jnp.int32) if me is None else me] + ins, [SMEM] + specs,
-        sds((R, Z, rows, width), bf16), pl.BlockSpec((1, Z, rows, width), lambda i: (i, 0, 0, 0)), moved=6 * R * Z * rows * width, vmem=60,
+        sds((R, Z, rows, width), bf16), pl.BlockSpec((1, Z, rows, width), lambda i: (i, 0, 0, 0)), moved=6 * R * Z * rows * width,
     )
 
 
@@ -791,6 +792,14 @@
     return [sums[0]] + [lax.ppermute(sums[k], "dp", pairs(len(sums), k)) for k in range(1, len(sums))]
 
 
+def column(ref, n):
+    line = lax.broadcasted_iota(jnp.int32, (n, 1), 0)
+    total = jnp.zeros((n, 1), ref.dtype)
+    for i in range(n):
+        total = jnp.where(line == i, ref[i], total)
+    return total
+
+
 def lookup_body(found, me_ref, sg_ref, r_ref, *refs):
     chosen_ref, back_ref, lead_ref = refs[found:]
     seqs = sg_ref.shape[0]
@@ -804,7 +813,7 @@
     else:
         chosen_ref[0:seqs, :] = refs[0][...].astype(f32)
     back_ref[...] = jnp.zeros_like(back_ref)
-    back_ref[0:seqs, :] = sg_ref[...] * chosen_ref[0:seqs, :]
+    back_ref[0:seqs, :] = column(sg_ref, seqs) * chosen_ref[0:seqs, :]
     lead = dot(back_ref[...].astype(bf16), r_ref[...], 1, 1)
     for s in range(seqs):
         lead_ref[s] = lead[s : s + 1, :]
@@ -817,7 +826,7 @@
         specs = [pl.BlockSpec((a.shape[0], 1, a.shape[2], width), lambda i: (0, 0, 0, 0)) for a in found]
     return once(
         functools.partial(lookup_body, len(found)), "lookup", (me, sg, wide, *found),
-        [SMEM, None, pl.BlockSpec((D, width), lambda i: (0, (F + D) // width))] + specs,
+        [SMEM, SMEM, pl.BlockSpec((D, width), lambda i: (0, (F + D) // width))] + specs,
         [sds((16, width), f32), sds((16, width), f32), sds((seqs, 1, D), f32)], moved=4 * D * width,
     )
 
@@ -833,9 +842,10 @@
     score_ref[...] = jnp.sum(projected * chosen_ref[0:seqs, :], axis=-1, keepdims=True)
     retr_ref[...] = dot(leading, back_ref[...].astype(bf16), 0, 0)
     lane = lax.broadcasted_iota(jnp.int32, (seqs, width), 1)
-    high, low = id_ref[...] // 256, id_ref[...] % 256
+    index = column(id_ref, seqs)
+    high, low = index // 256, index % 256
     ids = jnp.where(lane == 0, high, jnp.where(lane == 1, low, 0)).astype(f32)
-    term_ref[...] = jnp.concatenate([sg_ref[...] * projected, ids], axis=0).astype(bf16)
+    term_ref[...] = jnp.concatenate([column(sg_ref, seqs) * projected, ids], axis=0).astype(bf16)
 
 
 def score(top, wide, F, chosen, back, sg, index):
@@ -843,7 +853,7 @@
     width = chosen.shape[1]
     return once(
         score_body, "score", (top, wide, chosen, back, sg, index),
-        [None, pl.BlockSpec((D, width), lambda i: (0, (F + D) // width))] + [None] * 4,
+        [None, pl.BlockSpec((D, width), lambda i: (0, (F + D) // width))] + [None] * 2 + [SMEM] * 2,
         [sds((seqs, 1), f32), sds((D, width), f32), sds((2 * seqs, width), bf16)],
         scratch=[pltpu.VMEM((16, D), f32)], moved=8 * D * width,
     )
@@ -921,9 +931,9 @@
     if rows % 8 == 0:
         found = wd
     (wd,) = place(me, [after(wd[0], first), wd[1]], Z, [D], rows=down_weight.shape[0])
-    chosen, back_projected, lead = lookup(me, score_grad.reshape(seqs, 1), after(wide, first), F, D, Rw, found)
+    chosen, back_projected, lead = lookup(me, score_grad, after(wide, first), F, D, Rw, found)
     final, top, two, feed, inner, gsg, gss, gdb, gub = down(first, act, slope, wd, vec, output_grad, lead, seqs, per)
-    scores, retriever_back, term = score(top, wide, F, chosen, back_projected, score_grad.reshape(seqs, 1), document_index.reshape(seqs, 1))
+    scores, retriever_back, term = score(top, wide, F, chosen, back_projected, score_grad, document_index)
     down_parts = down_grad(me, Z, N, act, feed)
     up_parts = grads(me, Z, N, "up_grad", [after(first, *down_parts), inner], [([(0, None)], (1, None))], tile=D)
     feed_sums = pair_sum([down_parts, up_parts], N, up_parts[0], me, term)

time: 332 us -> 316 us (0.952)
  Pallas kernels: 197 us -> 168 us
  local copies, waits for them, and re-layouts: 14.4 us -> 24.4 us
  waiting for transfers between devices: 43.6 us -> 47.6 us
    pallas_call x27, Pallas kernels: 197 us -> 168 us  [run(): pl.pallas_call(body, name=name, grid=grid, in_specs=in_specs, out_specs=o...]
    unnamed x60 -> x64, local copies, waits for them, and re-layouts: 9.65 us -> 23.2 us
    ppermute x12, waiting for transfers between devices: 7.57 us -> 12 us  [along_dp(): lax.ppermute(b, 'dp', pairs(len(blocks), k))]
    ppermute x12, starting transfers between devices: 20.7 us -> 17 us  [along_dp(): lax.ppermute(b, 'dp', pairs(len(blocks), k))]
  transfers between devices with their start and end apart: 30 -> 30, of which waited for: 10 -> 10; matrix products, arithmetic and copies ran while one was open for 1% -> 0% of each run, Pallas kernels for 42% -> 37%
where the time goes in v5:
time: 316 us; the launch traced here: 315 us
  Pallas kernels  168 us (53%)
  waiting for transfers between devices  47.6 us (15%)
  starting transfers between devices  46.5 us (15%)
  local copies, waits for them, and re-layouts  24.4 us (8%)
  between operations  14.4 us (5%)
  blocking collectives  13.4 us (4%)
    pallas_call x27, Pallas kernels, run(): pl.pallas_call(body, name=name, grid=grid, in_specs=in_specs, out_specs=o...  168 us
    unnamed x64, local copies, waits for them, and re-layouts  23.2 us
    ppermute x12, starting transfers between devices, along_dp(): lax.ppermute(b, 'dp', pairs(len(blocks), k))  17 us
    all_to_all x4, starting transfers between devices, between_chips(): lax.all_to_all(blocks, 'fsdp', 0, 0, axis_index_groups=[list(range(c, N,...  16.6 us
    all_to_all x4, waiting for transfers between devices, between_chips(): lax.all_to_all(blocks, 'fsdp', 0, 0, axis_index_groups=[list(range(c, N,...  16.1 us
    all_to_all x1, blocking collectives, between_chips(): lax.all_to_all(blocks, 'fsdp', 0, 0, axis_index_groups=[list(range(c, N,...  13.4 us
    ppermute x12, waiting for transfers between devices, along_dp(): lax.ppermute(b, 'dp', pairs(len(blocks), k))  12 us
    ppermute x6, starting transfers between devices, along_dp_sums(): lax.ppermute(sums[k], 'dp', pairs(len(sums), k))  11.4 us
  transfers between devices with their start and end apart: 30, of which 10 were waited for; matrix products, arithmetic and copies ran while one was open for 0% of the time, Pallas kernels for 37%

profile of v5, /device:TPU:0, one launch (start us, length us, event | category | flops | bytes accessed | tf_op | source)
XLA Modules:
  0.0 315.0 jit_solution(9704300456536305285)
XLA Ops:
  7.2 1.9 pack.1
  9.1 3.1 collective-permute-start
  12.2 2.6 collective-permute-start.1
  14.8 3.3 %collective-permute-done.1.refs_2_ = bf16[24,896]{1,0:T(8,128)(2,1)S(1)} collective-permute-done((bf16[24,896]{1,0:T(8,128)(2,1)}, bf16[24,896]{1,0:T(8,128)(2,1)S(1)}, u32[]{:S(2)}, u32[]{:S(2)}) %collective-permute-start.1) | collective-permute-done | bytes 43040 | tf_op jit(solution)/shard_map/ppermute | solution.py:418
  18.1 2.7 collective-permute-done.2.refs_3_
  21.7 13.4 %all_to_all.25.refs_0_ = bf16[4,4,24,896]{3,2,1,0:T(8,128)(2,1)S(1)} all-to-all(bf16[4,4,24,896]{3,2,1,0:T(8,128)(2,1)S(1)} %repeat.3), channel_id=1, replica_groups={{0,2,4,6},{1,3,5,7},{8,10,12,14},{9,11,13,15},{16,18,20,22},{17,19,21,2..., dimensions={0} | all-to-all | bytes 1376256 | tf_op jit(solution)/shard_map/all_to_all | solution.py:422
  36.3 3.2 %collective-permute-start.4 = (bf16[24,1536]{1,0:T(8,128)(2,1)}, bf16[24,1536]{1,0:T(8,128)(2,1)S(1)}, u32[]{:S(2)}, u32[]{:S(2)}) collective-permute-start(bf16[24,1536]{1,0:T(8,128)(2,1)} %get-tuple-element.115.refs_0_), channel_id=1, source_target_pairs={{0,8},{8,0},{16,24},{24,16},{1,9},{9,1},{17,25},{25,17},{2,10},{10... | collective-permute-start | bytes 221192 | tf_op jit(solution)/shard_map/ppermute | solution.py:418
  39.6 1.6 place.3
  42.5 2.4 collective-permute-done.5.refs_2_
  46.0 3.5 %all-to-all-start.1 = ((bf16[4,4,24,1536]{3,2,1,0:T(8,128)(2,1)}), bf16[4,4,24,1536]{3,2,1,0:T(8,128)(2,1)S(1)}, u32[]{:S(2)}, u32[]{:S(2)}) async-start(bf16[4,4,24,1536]{3,2,1,0:T(8,128)(2,1)} %repeat.4), calls=%async_computation.1 | async-start | bytes 2359296 | tf_op jit(solution)/shard_map/all_to_all | solution.py:422
  50.7 3.2 %collective-permute-start.7 = (bf16[96,768]{1,0:T(8,128)(2,1)S(1)}, bf16[96,768]{1,0:T(8,128)(2,1)S(1)}, u32[]{:S(2)}, u32[]{:S(2)}) collective-permute-start(bf16[96,768]{1,0:T(8,128)(2,1)S(1)} %copy-done.14), channel_id=1, source_target_pairs={{0,8},{8,0},{16,24},{24,16},{1,9},{9,1},{17,25},{25,17},{2,10},{10... | collective-permute-start | bytes 442376 | tf_op jit(solution)/shard_map/ppermute | solution.py:418
  55.1 1.7 collective-permute-start.11
  56.8 3.6 %collective-permute-done.9.refs_3_ = bf16[96,768]{1,0:T(8,128)(2,1)S(1)} collective-permute-done((bf16[96,768]{1,0:T(8,128)(2,1)S(1)}, bf16[96,768]{1,0:T(8,128)(2,1)S(1)}, u32[]{:S(2)}, u32[]{:S(2)}) %collective-permute-start.9) | collective-permute-done | bytes 147488 | tf_op jit(solution)/shard_map/ppermute | solution.py:418
  61.1 10.1 %attend.2 = (bf16[3,1152,768]{2,1,0:T(8,128)(2,1)}, bf16[3,4,1152,288]{3,2,1,0:T(8,128)(2,1)}, bf16[3,1152,256]{2,1,0:T(8,128)(2,1)}) custom-call(bf16[1152,768]{1,0:T(8,128)(2,1)} %refs_2_.3, bf16[768,768]{1,0:T(8,128)(2,1)} %bitcast.37, f32[16,768]{1,0:T(8,128)} %copy-done.13), custom_call_target="tpu_custom_call" | custom-call | flops 2717908992 | bytes 7962624 | tf_op jit(solution)/shard_map/attend/pallas_call | solution.py:35
  71.4 1.5 copy-done.4
  73.9 3.8 %all-to-all-start.2 = ((bf16[4,4,104,768]{3,2,1,0:T(8,128)(2,1)}), bf16[4,4,104,768]{3,2,1,0:T(8,128)(2,1)S(1)}, u32[]{:S(2)}, u32[]{:S(2)}) async-start(bf16[4,4,104,768]{3,2,1,0:T(8,128)(2,1)} %copy-done.4), calls=%async_computation.2 | async-start | bytes 5111808 | tf_op jit(solution)/shard_map/all_to_all | solution.py:422
  77.8 3.0 collective-permute-done.13.refs_1_
  85.0 17.9 %attend.3 = (bf16[3,1152,768]{2,1,0:T(8,128)(2,1)}, bf16[3,4,1152,288]{3,2,1,0:T(8,128)(2,1)}, bf16[3,1152,256]{2,1,0:T(8,128)(2,1)}) custom-call(bf16[1152,768]{1,0:T(8,128)(2,1)} %refs_2_.3, bf16[768,1536]{1,0:T(8,128)(2,1)} %bitcast.32, f32[16,768]{1,0:T(8,128)} %copy-done.13, ...), custom_call_target="tpu_custom_call", output_to_operand_aliasing={{0}: (3, {}), {1}: (4, {}), {2}: (5, {})} | custom-call | flops 5435817984 | bytes 14155776 | tf_op jit(solution)/shard_map/attend/pallas_call | solution.py:35
  102.9 6.0 %all-to-all-done.2.refs_0_ = bf16[4,4,104,768]{3,2,1,0:T(8,128)(2,1)S(1)} async-done(((bf16[4,4,104,768]{3,2,1,0:T(8,128)(2,1)}), bf16[4,4,104,768]{3,2,1,0:T(8,128)(2,1)S(1)}, u32[]{:S(2)}, u32[]{:S(2)}) %all-to-all-start.2) | async-done | bytes 2555936 | tf_op jit(solution)/shard_map/all_to_all | solution.py:422
  108.9 18.4 %up.1 = (f32[1152,768]{1,0:T(8,128)}, f32[1152,1]{1,0:T(8,128)}, bf16[1152,768]{1,0:T(8,128)(2,1)}, bf16[1152,3072]{1,0:T(8,128)(2,1)}, bf16[1152,3072]{1,0:T(8,128)(2,1)}) custom-call(bf16[3,1152,256]{2,1,0:T(8,128)(2,1)} %get-tuple-element.135.ctx_ref.refs_0_, bf16[1152,768]{1,0:T(8,128)(2,1)} %refs_2_.3, ...), custom_call_target="tpu_custom_call" | custom-call | flops 6794772480 | bytes 28901376 | tf_op jit(solution)/shard_map/up/pallas_call | solution.py:35
  127.3 3.0 place.5
  130.3 2.2 copy-done.7
  134.3 21.4 %down.1 = (bf16[1152,768]{1,0:T(8,128)(2,1)}, f32[4,1,768]{2,1,0:T(1,128)}, f32[1152,768]{1,0:T(8,128)}, bf16[1152,768]{1,0:T(8,128)(2,1)}, bf16[1152,3072]{1,0:...) custom-call(bf16[1152,768]{1,0:T(8,128)(2,1)} %get-tuple-element.153.first_ref.refs_0, ...), custom_call_target="tpu_custom_call" | custom-call | flops 10871635968 | bytes 36569088 | tf_op jit(solution)/shard_map/down/pallas_call | solution.py:35
  155.7 10.6 %down_grad.1 = (bf16[4,4,96,768]{3,2,1,0:T(8,128)(2,1)}, bf16[4,4,96,768]{3,2,1,0:T(8,128)(2,1)}) custom-call(s32[3]{0:T(128)} %copy-done.17, bf16[1152,3072]{1,0:T(8,128)(2,1)} %get-tuple-element.138.act_ref.x_ref, bf16[1152,768]{1,0:T(8,128)(2,1)} %get-tuple-element.150.y_ref), custom_call_target="tpu_custom_call" | custom-call | flops 5435817984 | bytes 13565952 | tf_op jit(solution)/shard_map/down_grad/pallas_call | solution.py:35
  166.3 10.5 %up_grad.1 = (bf16[4,4,24,3072]{3,2,1,0:T(8,128)(2,1)}, bf16[4,4,24,3072]{3,2,1,0:T(8,128)(2,1)}) custom-call(s32[3]{0:T(128)} %copy-done.17, bf16[1152,768]{1,0:T(8,128)(2,1)} %get-tuple-element.153.first_ref.refs_0_, bf16[1152,3072]{1,0:T(8,128)(2,1)} %get-tuple-element.154.refs_1_.inner_ref), custom_call_target="tpu_custom_call" | custom-call | flops 5435817984 | bytes 13565952 | tf_op jit(solution)/shard_map/up_grad/pallas_call | solution.py:35
  177.3 2.7 copy-done.1
  182.1 2.7 collective-permute-done.17.refs_5_
  184.8 1.8 pair_sum.2
  186.6 2.2 copy-done.2
  188.8 5.0 %all-to-all-start.3 = ((bf16[4,4,200,768]{3,2,1,0:T(8,128)(2,1)}), bf16[4,4,200,768]{3,2,1,0:T(8,128)(2,1)}, u32[]{:S(2)}, u32[]{:S(2)}) async-start(bf16[4,4,200,768]{3,2,1,0:T(8,128)(2,1)} %copy-done.2), calls=%async_computation.3 | async-start | bytes 9830400 | tf_op jit(solution)/shard_map/all_to_all | solution.py:422
  193.8 15.3 %mid.1 = (f32[1152,768]{1,0:T(8,128)}, bf16[1152,768]{1,0:T(8,128)(2,1)}, bf16[1152,768]{1,0:T(8,128)(2,1)}, f32[1,768]{1,0:T(1,128)}, f32[1,768]{1,0:T(1,128)}, /*index=5*/f32[1,768]{1,0:T(1,128)}) custom-call(f32[1152,768]{1,0:T(8,128)} %get-tuple-element.159.two_ref, bf16[1152,3072]{1,0:T(8,128)(2,1)} %get-tuple-element.154.refs_1_.inner_ref, ...), custom_call_target="tpu_custom_call" | custom-call | flops 6794772480 | bytes 27131904 | tf_op jit(solution)/shard_map/mid/pallas_call | solution.py:35
  209.1 20.9 %attend_back.1 = (bf16[3,1152,768]{2,1,0:T(8,128)(2,1)}, f32[1,768]{1,0:T(1,128)}, f32[1,768]{1,0:T(1,128)}) custom-call(bf16[3,1152,768]{2,1,0:T(8,128)(2,1)} %get-tuple-element.164.qkv_ref, bf16[3,4,1152,288]{3,2,1,0:T(8,128)(2,1)} %get-tuple-element.165.soft_ref, bf16[3,1152,256]{2,1,0:T(8,128)(2,1)} %get-tuple-element.135.ctx_ref.refs_0_, ...), custom_call_target="tpu_custom_call" | custom-call | flops 8153726976 | bytes 22118400 | tf_op jit(solution)/shard_map/attend_back/pallas_call | solution.py:35
  230.0 12.8 %mix_grad.1 = (bf16[4,4,24,3328]{3,2,1,0:T(8,128)(2,1)}, bf16[4,4,24,3328]{3,2,1,0:T(8,128)(2,1)}) custom-call(s32[3]{0:T(128)} %copy-done.17, bf16[3,1152,256]{2,1,0:T(8,128)(2,1)} %get-tuple-element.135.ctx_ref.refs_0_, bf16[1152,768]{1,0:T(8,128)(2,1)} %get-tuple-element.163.refs_1_, bf16[1152,768]{1,0:T(8,128)(2,1)} %refs_2_.3, ...), custom_call_target="tpu_custom_call" | custom-call | flops 5888802816 | bytes 14548992 | tf_op jit(solution)/shard_map/mix_grad/pallas_call | solution.py:35
  243.2 4.7 %collective-permute-done.18.refs_1_ = bf16[4,4,24,3328]{3,2,1,0:T(8,128)(2,1)S(1)} collective-permute-done((bf16[4,4,24,3328]{3,2,1,0:T(8,128)(2,1)}, bf16[4,4,24,3328]{3,2,1,0:T(8,128)(2,1)S(1)}, u32[]{:S(2)}, u32[]{:S(2)}) %collective-permute-start.18) | collective-permute-done | bytes 2555936 | tf_op jit(solution)/shard_map/ppermute | solution.py:426
  247.9 1.7 copy-done.10
  252.3 4.3 %all-to-all-start.4 = ((bf16[4,4,24,3328]{3,2,1,0:T(8,128)(2,1)}), bf16[4,4,24,3328]{3,2,1,0:T(8,128)(2,1)S(1)}, u32[]{:S(2)}, u32[]{:S(2)}) async-start(bf16[4,4,24,3328]{3,2,1,0:T(8,128)(2,1)} %copy-done.3), calls=%async_computation.4 | async-start | bytes 5111808 | tf_op jit(solution)/shard_map/all_to_all | solution.py:422
  256.6 3.9 %chips_sum.2 = (f32[208,768]{1,0:T(8,128)S(1)}, bf16[208,768]{1,0:T(8,128)(2,1)}, bf16[208,768]{1,0:T(8,128)(2,1)}, bf16[208,768]{1,0:T(8,128)(2,1)}) custom-call(s32[3]{0:T(128)S(1)} %copy-done.19, bf16[4,4,200,768]{3,2,1,0:T(8,128)(2,1)} %all-to-all-done.3.in_ref), custom_call_target="tpu_custom_call" | custom-call | bytes 6193152 | tf_op jit(solution)/shard_map/chips_sum/pallas_call | solution.py:35
  260.5 3.3 %collective-permute-start.19 = (bf16[208,768]{1,0:T(8,128)(2,1)}, bf16[208,768]{1,0:T(8,128)(2,1)}, u32[]{:S(2)}, u32[]{:S(2)}) collective-permute-start(bf16[208,768]{1,0:T(8,128)(2,1)} %get-tuple-element.188), channel_id=1, source_target_pairs={{0,8},{8,0},{16,24},{24,16},{1,9},{9,1},{17,25},{25,17},{2,10},{10... | collective-permute-start | bytes 958472 | tf_op jit(solution)/shard_map/ppermute | solution.py:792
  264.4 1.8 collective-permute-start.21
  266.2 2.0 copy-done.25
  268.2 2.5 copy-done.30
  270.7 6.1 %tokens_back.1 = bf16[1152,768]{1,0:T(8,128)(2,1)} custom-call(f32[1152,768]{1,0:T(8,128)S(1)} %copy-done.25, bf16[3,1152,768]{2,1,0:T(8,128)(2,1)S(1)} %copy-done.30, bf16[768,768]{1,0:T(8,128)(2,1)S(1)} %bitcast.38, bf16[768,1536]{1,0:T(8,128)(2,1)S(1)} %bitcast.33), custom_call_target="tpu_custom_call" | custom-call | flops 4076863488 | bytes 10616832 | tf_op jit(solution)/shard_map/tokens_back/pallas_call | solution.py:35
  276.8 10.1 %all-to-all-done.4.in_ref = bf16[4,4,24,3328]{3,2,1,0:T(8,128)(2,1)S(1)} async-done(((bf16[4,4,24,3328]{3,2,1,0:T(8,128)(2,1)}), bf16[4,4,24,3328]{3,2,1,0:T(8,128)(2,1)S(1)}, u32[]{:S(2)}, u32[]{:S(2)}) %all-to-all-start.4) | async-done | bytes 2555936 | tf_op jit(solution)/shard_map/all_to_all | solution.py:422
  286.9 1.5 chips_sum.3
  288.4 3.3 %collective-permute-start.22 = (bf16[24,3328]{1,0:T(8,128)(2,1)}, bf16[24,3328]{1,0:T(8,128)(2,1)S(1)}, u32[]{:S(2)}, u32[]{:S(2)}) collective-permute-start(bf16[24,3328]{1,0:T(8,128)(2,1)} %get-tuple-element.193), channel_id=1, source_target_pairs={{0,8},{8,0},{16,24},{24,16},{1,9},{9,1},{17,25},{25,17},{2,10},{10... | collective-permute-start | bytes 479240 | tf_op jit(solution)/shard_map/ppermute | solution.py:792
  292.3 1.8 collective-permute-start.24
  294.8 2.4 last_feed.1
  297.2 9.0 %collective-permute-done.23.refs_2_ = bf16[24,3328]{1,0:T(8,128)(2,1)S(1)} collective-permute-done((bf16[24,3328]{1,0:T(8,128)(2,1)}, bf16[24,3328]{1,0:T(8,128)(2,1)S(1)}, u32[]{:S(2)}, u32[]{:S(2)}) %collective-permute-start.23) | collective-permute-done | bytes 159776 | tf_op jit(solution)/shard_map/ppermute | solution.py:792
  (111 shorter events, 24.0 us)
Async XLA Ops:
  7.2 101.7 %all-gather.2.cloned.1.call-start = ((), (), s32[]{:S(2)}) async-start(), calls=%async_computation.5 | async-start | bytes 6285312 | tf_op jit(solution)/shard_map/all_gather | solution.py:908
  9.1 35.8 %copy-start.15 = (bf16[24,1536]{1,0:T(8,128)(2,1)S(1)}, bf16[24,1536]{1,0:T(8,128)(2,1)}, u32[]{:S(2)}) copy-start(bf16[24,1536]{1,0:T(8,128)(2,1)} %get-tuple-element.115.refs_0_) | copy-start | bytes 221188
  9.1 5.7 %collective-permute-start = (bf16[24,896]{1,0:T(8,128)(2,1)}, bf16[24,896]{1,0:T(8,128)(2,1)S(1)}, u32[]{:S(2)}, u32[]{:S(2)}) collective-permute-start(bf16[24,896]{1,0:T(8,128)(2,1)} %get-tuple-element.111.refs_0_), channel_id=1, source_target_pairs={{0,8},{8,0},{16,24},{24,16},{1,9},{9,1},{17,25},{25,17},{2,10},{10... | collective-permute-start | bytes 129032 | tf_op jit(solution)/shard_map/ppermute | solution.py:418
  12.2 5.9 %collective-permute-start.1 = (bf16[24,896]{1,0:T(8,128)(2,1)}, bf16[24,896]{1,0:T(8,128)(2,1)S(1)}, u32[]{:S(2)}, u32[]{:S(2)}) collective-permute-start(bf16[24,896]{1,0:T(8,128)(2,1)} %get-tuple-element.111.refs_0_), channel_id=1, source_target_pairs={{0,16},{8,24},{16,0},{24,8},{1,17},{9,25},{17,1},{25,9},{2,18},{10... | collective-permute-start | bytes 129032 | tf_op jit(solution)/shard_map/ppermute | solution.py:418
  14.8 6.0 %collective-permute-start.2 = (bf16[24,896]{1,0:T(8,128)(2,1)}, bf16[24,896]{1,0:T(8,128)(2,1)S(1)}, u32[]{:S(2)}, u32[]{:S(2)}) collective-permute-start(bf16[24,896]{1,0:T(8,128)(2,1)} %get-tuple-element.111.refs_0_), channel_id=1, source_target_pairs={{0,24},{8,16},{16,8},{24,0},{1,25},{9,17},{17,9},{25,1},{2,26},{10... | collective-permute-start | bytes 129032 | tf_op jit(solution)/shard_map/ppermute | solution.py:418
  35.1 4.5 %collective-permute-start.3 = (bf16[4,4,24,896]{3,2,1,0:T(8,128)(2,1)S(1)}, bf16[4,4,24,896]{3,2,1,0:T(8,128)(2,1)S(1)}, u32[]{:S(2)}, u32[]{:S(2)}) collective-permute-start(bf16[4,4,24,896]{3,2,1,0:T(8,128)(2,1)S(1)} %all_to_all.25.refs_0_), channel_id=1, source_target_pairs={{0,1},{1,0},{2,3},{3,2},{4,5},{5,4},{6,7},{7,6},{8,9},{9,8},{10,11... | collective-permute-start | bytes 2064392 | tf_op jit(solution)/shard_map/ppermute | solution.py:426
  35.1 7.4 %collective-permute-start.6 = (bf16[24,1536]{1,0:T(8,128)(2,1)}, bf16[24,1536]{1,0:T(8,128)(2,1)S(1)}, u32[]{:S(2)}, u32[]{:S(2)}) collective-permute-start(bf16[24,1536]{1,0:T(8,128)(2,1)} %get-tuple-element.115.refs_0_), channel_id=1, source_target_pairs={{0,24},{8,16},{16,8},{24,0},{1,25},{9,17},{17,9},{25,1},{2,26},{10... | collective-permute-start | bytes 221192 | tf_op jit(solution)/shard_map/ppermute | solution.py:418
  36.2 8.7 %collective-permute-start.5 = (bf16[24,1536]{1,0:T(8,128)(2,1)}, bf16[24,1536]{1,0:T(8,128)(2,1)S(1)}, u32[]{:S(2)}, u32[]{:S(2)}) collective-permute-start(bf16[24,1536]{1,0:T(8,128)(2,1)} %get-tuple-element.115.refs_0_), channel_id=1, source_target_pairs={{0,16},{8,24},{16,0},{24,8},{1,17},{9,25},{17,1},{25,9},{2,18},{10... | collective-permute-start | bytes 221192 | tf_op jit(solution)/shard_map/ppermute | solution.py:418
  36.3 8.6 %collective-permute-start.4 = (bf16[24,1536]{1,0:T(8,128)(2,1)}, bf16[24,1536]{1,0:T(8,128)(2,1)S(1)}, u32[]{:S(2)}, u32[]{:S(2)}) collective-permute-start(bf16[24,1536]{1,0:T(8,128)(2,1)} %get-tuple-element.115.refs_0_), channel_id=1, source_target_pairs={{0,8},{8,0},{16,24},{24,16},{1,9},{9,1},{17,25},{25,17},{2,10},{10... | collective-permute-start | bytes 221192 | tf_op jit(solution)/shard_map/ppermute | solution.py:418
  39.5 90.8 %copy-start.17 = (s32[3]{0:T(128)}, s32[3]{0:T(128)S(1)}, u32[]{:S(2)}) copy-start(s32[3]{0:T(128)S(1)} %pad_add_fusion.me_ref) | copy-start | bytes 40
  39.5 10.0 %copy-start.14 = (bf16[96,768]{1,0:T(8,128)(2,1)S(1)}, bf16[96,768]{1,0:T(8,128)(2,1)}, u32[]{:S(2)}) copy-start(bf16[96,768]{1,0:T(8,128)(2,1)} %refs_0_.2) | copy-start | bytes 442372
  39.5 14.4 %copy-start.16 = (bf16[256,128]{1,0:T(8,128)(2,1)S(1)}, bf16[256,128]{1,0:T(8,128)(2,1)}, u32[]{:S(2)}) copy-start(bf16[256,128]{1,0:T(8,128)(2,1)} %t_ref) | copy-start | bytes 196612
  42.2 18.9 %copy-start.13 = (f32[16,768]{1,0:T(8,128)}, f32[16,768]{1,0:T(8,128)S(1)}, u32[]{:S(2)}) copy-start(f32[16,768]{1,0:T(8,128)S(1)} %get-tuple-element.114.v_ref) | copy-start | bytes 147460
  42.5 7.0 %copy-start.21 = (f32[1,3072]{1,0:T(1,128)}, f32[1,3072]{1,0:T(1,128)S(1)}, u32[]{:S(2)}) copy-start(f32[1,3072]{1,0:T(1,128)S(1)} %bias_row.1.ub_ref) | copy-start | bytes 36868
  46.0 27.0 %all-to-all-start.1 = ((bf16[4,4,24,1536]{3,2,1,0:T(8,128)(2,1)}), bf16[4,4,24,1536]{3,2,1,0:T(8,128)(2,1)S(1)}, u32[]{:S(2)}, u32[]{:S(2)}) async-start(bf16[4,4,24,1536]{3,2,1,0:T(8,128)(2,1)} %repeat.4), calls=%async_computation.1 | async-start | bytes 2359296 | tf_op jit(solution)/shard_map/all_to_all | solution.py:422
  49.5 10.9 %collective-permute-start.9 = (bf16[96,768]{1,0:T(8,128)(2,1)S(1)}, bf16[96,768]{1,0:T(8,128)(2,1)S(1)}, u32[]{:S(2)}, u32[]{:S(2)}) collective-permute-start(bf16[96,768]{1,0:T(8,128)(2,1)S(1)} %copy-done.14), channel_id=1, source_target_pairs={{0,24},{8,16},{16,8},{24,0},{1,25},{9,17},{17,9},{25,1},{2,26},{10... | collective-permute-start | bytes 442376 | tf_op jit(solution)/shard_map/ppermute | solution.py:418
  50.7 20.4 %collective-permute-start.8 = (bf16[96,768]{1,0:T(8,128)(2,1)S(1)}, bf16[96,768]{1,0:T(8,128)(2,1)S(1)}, u32[]{:S(2)}, u32[]{:S(2)}) collective-permute-start(bf16[96,768]{1,0:T(8,128)(2,1)S(1)} %copy-done.14), channel_id=1, source_target_pairs={{0,16},{8,24},{16,0},{24,8},{1,17},{9,25},{17,1},{25,9},{2,18},{10... | collective-permute-start | bytes 442376 | tf_op jit(solution)/shard_map/ppermute | solution.py:418
  50.7 20.4 %collective-permute-start.7 = (bf16[96,768]{1,0:T(8,128)(2,1)S(1)}, bf16[96,768]{1,0:T(8,128)(2,1)S(1)}, u32[]{:S(2)}, u32[]{:S(2)}) collective-permute-start(bf16[96,768]{1,0:T(8,128)(2,1)S(1)} %copy-done.14), channel_id=1, source_target_pairs={{0,8},{8,0},{16,24},{24,16},{1,9},{9,1},{17,25},{25,17},{2,10},{10... | collective-permute-start | bytes 442376 | tf_op jit(solution)/shard_map/ppermute | solution.py:418
  55.0 16.2 %collective-permute-start.10 = (bf16[8,512]{1,0:T(8,128)(2,1)S(1)}, bf16[8,512]{1,0:T(8,128)(2,1)S(1)}, u32[]{:S(2)}, u32[]{:S(2)}) collective-permute-start(bf16[8,512]{1,0:T(8,128)(2,1)S(1)} %get-tuple-element.129), channel_id=1, source_target_pairs={{0,8},{8,0},{16,24},{24,16},{1,9},{9,1},{17,25},{25,17},{2,10},{10... | collective-permute-start | bytes 24584 | tf_op jit(solution)/shard_map/ppermute | solution.py:418
  55.1 16.1 %collective-permute-start.11 = (bf16[8,512]{1,0:T(8,128)(2,1)S(1)}, bf16[8,512]{1,0:T(8,128)(2,1)S(1)}, u32[]{:S(2)}, u32[]{:S(2)}) collective-permute-start(bf16[8,512]{1,0:T(8,128)(2,1)S(1)} %get-tuple-element.130), channel_id=1, source_target_pairs={{0,16},{8,24},{16,0},{24,8},{1,17},{9,25},{17,1},{25,9},{2,18},{10... | collective-permute-start | bytes 24584 | tf_op jit(solution)/shard_map/ppermute | solution.py:418
  60.4 10.8 %collective-permute-start.12 = (bf16[8,512]{1,0:T(8,128)(2,1)S(1)}, bf16[8,512]{1,0:T(8,128)(2,1)S(1)}, u32[]{:S(2)}, u32[]{:S(2)}) collective-permute-start(bf16[8,512]{1,0:T(8,128)(2,1)S(1)} %get-tuple-element.131), channel_id=1, source_target_pairs={{0,24},{8,16},{16,8},{24,0},{1,25},{9,17},{17,9},{25,1},{2,26},{10... | collective-permute-start | bytes 24584 | tf_op jit(solution)/shard_map/ppermute | solution.py:418
  73.9 34.9 %all-to-all-start.2 = ((bf16[4,4,104,768]{3,2,1,0:T(8,128)(2,1)}), bf16[4,4,104,768]{3,2,1,0:T(8,128)(2,1)S(1)}, u32[]{:S(2)}, u32[]{:S(2)}) async-start(bf16[4,4,104,768]{3,2,1,0:T(8,128)(2,1)} %copy-done.4), calls=%async_computation.2 | async-start | bytes 5111808 | tf_op jit(solution)/shard_map/all_to_all | solution.py:422
  77.8 3.1 collective-permute-start.13
  108.9 18.4 %collective-permute-start.14 = (bf16[4,4,104,768]{3,2,1,0:T(8,128)(2,1)S(1)}, bf16[4,4,104,768]{3,2,1,0:T(8,128)(2,1)}, u32[]{:S(2)}, u32[]{:S(2)}) collective-permute-start(bf16[4,4,104,768]{3,2,1,0:T(8,128)(2,1)S(1)} %all-to-all-done.2.refs_0_), channel_id=1, source_target_pairs={{0,1},{1,0},{2,3},{3,2},{4,5},{5,4},{6,7},{7,6},{8,9},{9,8},{10,11... | collective-permute-start | bytes 7667720 | tf_op jit(solution)/shard_map/ppermute | solution.py:426
  127.2 5.3 %copy-start = (bf16[768,3968]{1,0:T(8,128)(2,1)S(1)}, bf16[768,3968]{1,0:T(8,128)(2,1)}, u32[]{:S(2)}) copy-start(bf16[768,3968]{1,0:T(8,128)(2,1)} %all-gather.2.cloned.1.call-done.wo_ref.wu_ref.r_ref) | copy-start | bytes 18284548
  127.2 5.3 %copy-start.24 = (f32[4]{0:T(128)S(1)}, f32[4]{0:T(128)}, u32[]{:S(2)}) copy-start(f32[4]{0:T(128)} %sg_ref.3) | copy-start | bytes 52
  166.3 11.0 %copy-start.31 = (bf16[4,4,96,768]{3,2,1,0:T(8,128)(2,1)S(1)}, bf16[4,4,96,768]{3,2,1,0:T(8,128)(2,1)}, u32[]{:S(2)}) copy-start(bf16[4,4,96,768]{3,2,1,0:T(8,128)(2,1)} %get-tuple-element.152) | copy-start | bytes 7077892
  166.3 11.1 %copy-start.22 = (f32[4,1,768]{2,1,0:T(1,128)S(1)}, f32[4,1,768]{2,1,0:T(1,128)}, u32[]{:S(2)}) copy-start(f32[4,1,768]{2,1,0:T(1,128)} %get-tuple-element.145.top_ref) | copy-start | bytes 36868
  166.3 11.1 %copy-start.23 = (s32[4]{0:T(128)S(1)}, s32[4]{0:T(128)}, u32[]{:S(2)}) copy-start(s32[4]{0:T(128)} %id_ref.1) | copy-start | bytes 52
  176.7 8.0 %collective-permute-start.16 = (bf16[4,4,24,3072]{3,2,1,0:T(8,128)(2,1)}, bf16[4,4,24,3072]{3,2,1,0:T(8,128)(2,1)S(1)}, u32[]{:S(2)}, u32[]{:S(2)}) collective-permute-start(bf16[4,4,24,3072]{3,2,1,0:T(8,128)(2,1)} %get-tuple-element.157), channel_id=1, source_target_pairs={{0,1},{1,0},{2,3},{3,2},{4,5},{5,4},{6,7},{7,6},{8,9},{9,8},{10,11... | collective-permute-start | bytes 7077896 | tf_op jit(solution)/shard_map/ppermute | solution.py:426
  177.2 7.5 %collective-permute-start.15 = (bf16[4,4,96,768]{3,2,1,0:T(8,128)(2,1)S(1)}, bf16[4,4,96,768]{3,2,1,0:T(8,128)(2,1)S(1)}, u32[]{:S(2)}, u32[]{:S(2)}) collective-permute-start(bf16[4,4,96,768]{3,2,1,0:T(8,128)(2,1)S(1)} %copy-done.31), channel_id=1, source_target_pairs={{0,1},{1,0},{2,3},{3,2},{4,5},{5,4},{6,7},{7,6},{8,9},{9,8},{10,11... | collective-permute-start | bytes 7077896 | tf_op jit(solution)/shard_map/ppermute | solution.py:426
  177.3 2.7 copy-start.1
  180.1 4.7 %copy-start.11 = (bf16[4,4,96,768]{3,2,1,0:T(8,128)(2,1)S(1)}, bf16[4,4,96,768]{3,2,1,0:T(8,128)(2,1)}, u32[]{:S(2)}) copy-start(bf16[4,4,96,768]{3,2,1,0:T(8,128)(2,1)} %get-tuple-element.156.refs_0_) | copy-start | bytes 7077892
  180.1 4.7 %copy-start.12 = (bf16[4,4,24,3072]{3,2,1,0:T(8,128)(2,1)S(1)}, bf16[4,4,24,3072]{3,2,1,0:T(8,128)(2,1)}, u32[]{:S(2)}) copy-start(bf16[4,4,24,3072]{3,2,1,0:T(8,128)(2,1)} %get-tuple-element.155.refs_1_) | copy-start | bytes 7077892
  180.1 4.7 %copy-start.18 = (s32[3]{0:T(128)S(1)}, s32[3]{0:T(128)}, u32[]{:S(2)}) copy-start(s32[3]{0:T(128)} %copy-done.17) | copy-start | bytes 40
  181.7 3.1 collective-permute-start.17
  188.8 63.5 %all-to-all-start.3 = ((bf16[4,4,200,768]{3,2,1,0:T(8,128)(2,1)}), bf16[4,4,200,768]{3,2,1,0:T(8,128)(2,1)}, u32[]{:S(2)}, u32[]{:S(2)}) async-start(bf16[4,4,200,768]{3,2,1,0:T(8,128)(2,1)} %copy-done.2), calls=%async_computation.3 | async-start | bytes 9830400 | tf_op jit(solution)/shard_map/all_to_all | solution.py:422
  242.8 5.0 %collective-permute-start.18 = (bf16[4,4,24,3328]{3,2,1,0:T(8,128)(2,1)}, bf16[4,4,24,3328]{3,2,1,0:T(8,128)(2,1)S(1)}, u32[]{:S(2)}, u32[]{:S(2)}) collective-permute-start(bf16[4,4,24,3328]{3,2,1,0:T(8,128)(2,1)} %get-tuple-element.180), channel_id=1, source_target_pairs={{0,1},{1,0},{2,3},{3,2},{4,5},{5,4},{6,7},{7,6},{8,9},{9,8},{10,11... | collective-permute-start | bytes 7667720 | tf_op jit(solution)/shard_map/ppermute | solution.py:426
  252.3 4.3 %copy-start.19 = (s32[3]{0:T(128)S(1)}, s32[3]{0:T(128)}, u32[]{:S(2)}) copy-start(s32[3]{0:T(128)} %copy-done.17) | copy-start | bytes 40
  252.3 34.6 %all-to-all-start.4 = ((bf16[4,4,24,3328]{3,2,1,0:T(8,128)(2,1)}), bf16[4,4,24,3328]{3,2,1,0:T(8,128)(2,1)S(1)}, u32[]{:S(2)}, u32[]{:S(2)}) async-start(bf16[4,4,24,3328]{3,2,1,0:T(8,128)(2,1)} %copy-done.3), calls=%async_computation.4 | async-start | bytes 5111808 | tf_op jit(solution)/shard_map/all_to_all | solution.py:422
  256.6 9.6 %copy-start.6 = (bf16[4,4,2,24,1536]{4,3,2,1,0:T(8,128)(2,1)S(1)}, bf16[4,4,2,24,1536]{4,3,2,1,0:T(8,128)(2,1)}, u32[]{:S(2)}) copy-start(bf16[4,4,2,24,1536]{4,3,2,1,0:T(8,128)(2,1)} %copy-done.5) | copy-start | bytes 7077892
  256.6 9.6 %copy-start.27 = (bf16[4,4,2,24,768]{4,3,2,1,0:T(8,128)(2,1)S(1)}, bf16[4,4,2,24,768]{4,3,2,1,0:T(8,128)(2,1)}, u32[]{:S(2)}) copy-start(bf16[4,4,2,24,768]{4,3,2,1,0:T(8,128)(2,1)} %copy-done.26) | copy-start | bytes 3538948
  260.5 31.8 %collective-permute-start.19 = (bf16[208,768]{1,0:T(8,128)(2,1)}, bf16[208,768]{1,0:T(8,128)(2,1)}, u32[]{:S(2)}, u32[]{:S(2)}) collective-permute-start(bf16[208,768]{1,0:T(8,128)(2,1)} %get-tuple-element.188), channel_id=1, source_target_pairs={{0,8},{8,0},{16,24},{24,16},{1,9},{9,1},{17,25},{25,17},{2,10},{10... | collective-permute-start | bytes 958472 | tf_op jit(solution)/shard_map/ppermute | solution.py:792
  263.8 30.9 %collective-permute-start.20 = (bf16[208,768]{1,0:T(8,128)(2,1)}, bf16[208,768]{1,0:T(8,128)(2,1)}, u32[]{:S(2)}, u32[]{:S(2)}) collective-permute-start(bf16[208,768]{1,0:T(8,128)(2,1)} %get-tuple-element.189), channel_id=1, source_target_pairs={{0,16},{8,24},{16,0},{24,8},{1,17},{9,25},{17,1},{25,9},{2,18},{10... | collective-permute-start | bytes 958472 | tf_op jit(solution)/shard_map/ppermute | solution.py:792
  264.4 30.4 %collective-permute-start.21 = (bf16[208,768]{1,0:T(8,128)(2,1)}, bf16[208,768]{1,0:T(8,128)(2,1)}, u32[]{:S(2)}, u32[]{:S(2)}) collective-permute-start(bf16[208,768]{1,0:T(8,128)(2,1)} %get-tuple-element.190), channel_id=1, source_target_pairs={{0,24},{8,16},{16,8},{24,0},{1,25},{9,17},{17,9},{25,1},{2,26},{10... | collective-permute-start | bytes 958472 | tf_op jit(solution)/shard_map/ppermute | solution.py:792
  288.4 8.8 %collective-permute-start.22 = (bf16[24,3328]{1,0:T(8,128)(2,1)}, bf16[24,3328]{1,0:T(8,128)(2,1)S(1)}, u32[]{:S(2)}, u32[]{:S(2)}) collective-permute-start(bf16[24,3328]{1,0:T(8,128)(2,1)} %get-tuple-element.193), channel_id=1, source_target_pairs={{0,8},{8,0},{16,24},{24,16},{1,9},{9,1},{17,25},{25,17},{2,10},{10... | collective-permute-start | bytes 479240 | tf_op jit(solution)/shard_map/ppermute | solution.py:792
  291.8 14.5 %collective-permute-start.23 = (bf16[24,3328]{1,0:T(8,128)(2,1)}, bf16[24,3328]{1,0:T(8,128)(2,1)S(1)}, u32[]{:S(2)}, u32[]{:S(2)}) collective-permute-start(bf16[24,3328]{1,0:T(8,128)(2,1)} %get-tuple-element.194), channel_id=1, source_target_pairs={{0,16},{8,24},{16,0},{24,8},{1,17},{9,25},{17,1},{25,9},{2,18},{10... | collective-permute-start | bytes 479240 | tf_op jit(solution)/shard_map/ppermute | solution.py:792
  292.3 13.9 %collective-permute-start.24 = (bf16[24,3328]{1,0:T(8,128)(2,1)}, bf16[24,3328]{1,0:T(8,128)(2,1)S(1)}, u32[]{:S(2)}, u32[]{:S(2)}) collective-permute-start(bf16[24,3328]{1,0:T(8,128)(2,1)} %get-tuple-element.195), channel_id=1, source_target_pairs={{0,24},{8,16},{16,8},{24,0},{1,25},{9,17},{17,9},{25,1},{2,26},{10... | collective-permute-start | bytes 479240 | tf_op jit(solution)/shard_map/ppermute | solution.py:792
  (14 other events, 20.5 us)
Sparse Core Ops, SparseCore 0:
  11.5 89.5 all-gather.1

commit v6 on v5

--- a/solution.py
+++ b/solution.py
@@ -9,7 +9,7 @@
 
 HEAD_DIM = 64
 EPS = 1e-12
-ROOM = {"tokens_back": 28, "chips_sum": 28, "last_sum": 28, "last_feed": 28, "pair_sum": 28, "lookup": 28, "score": 28, "place": 28, "repeat": 28, "ask": 28, "bias_row": 28}
+ROOM = {"tokens_back": 28, "chips_sum": 28, "last_sum": 28, "last_feed": 28, "pair_sum": 28, "lookup": 28, "score": 28, "place": 40, "repeat": 40, "ask": 28, "bias_row": 28}
 QB, VB, OB, FG, FS, DB, SG, SS, UB = range(9)
 bf16, f32 = jnp.bfloat16, jnp.float32
 
@@ -150,7 +150,8 @@
             u = dot(first, wu_ref[:, cols]) + ub_ref[:, cols]
             phi = 0.5 + 0.5 * lax.erf(u * math.sqrt(0.5))
             act_ref[block, cols] = (u * phi).astype(bf16)
-            slope_ref[block, cols] = (phi + u * jnp.exp(u * u * -0.5) * (1.0 / math.sqrt(2 * math.pi))).astype(bf16)
+            bell = jnp.exp2(u * u * (-0.5 / math.log(2)) - 0.5 * math.log2(2 * math.pi))
+            slope_ref[block, cols] = (phi + u * bell).astype(bf16)
 
     in_turn(blocks_of(rows, size), attended, rest)
 

time: 316 us -> 315 us (level)
  no operation moved by 1% of the time
where the time goes in v6:
time: 315 us; the launch traced here: 314 us
  Pallas kernels  168 us (53%)
  waiting for transfers between devices  47.6 us (15%)
  starting transfers between devices  46.5 us (15%)
  local copies, waits for them, and re-layouts  23.5 us (7%)
  between operations  14.4 us (5%)
  blocking collectives  13.4 us (4%)
    pallas_call x27, Pallas kernels, run(): pl.pallas_call(body, name=name, grid=grid, in_specs=in_specs, out_specs=o...  168 us
    unnamed x64, local copies, waits for them, and re-layouts  22.3 us
    ppermute x12, starting transfers between devices, along_dp(): lax.ppermute(b, 'dp', pairs(len(blocks), k))  17 us
    all_to_all x4, starting transfers between devices, between_chips(): lax.all_to_all(blocks, 'fsdp', 0, 0, axis_index_groups=[list(range(c, N,...  16.6 us
    all_to_all x4, waiting for transfers between devices, between_chips(): lax.all_to_all(blocks, 'fsdp', 0, 0, axis_index_groups=[list(range(c, N,...  16.1 us
    all_to_all x1, blocking collectives, between_chips(): lax.all_to_all(blocks, 'fsdp', 0, 0, axis_index_groups=[list(range(c, N,...  13.4 us
    ppermute x12, waiting for transfers between devices, along_dp(): lax.ppermute(b, 'dp', pairs(len(blocks), k))  12 us
    ppermute x6, starting transfers between devices, along_dp_sums(): lax.ppermute(sums[k], 'dp', pairs(len(sums), k))  11.4 us
  transfers between devices with their start and end apart: 30, of which 10 were waited for; matrix products, arithmetic and copies ran while one was open for 0% of the time, Pallas kernels for 37%

profile of v6, /device:TPU:0, one launch (start us, length us, event | category | flops | bytes accessed | tf_op | source)
XLA Modules:
  0.0 314.0 jit_solution(11107774159524788954)
XLA Ops:
  7.2 1.9 pack.1
  9.1 3.1 collective-permute-start
  12.2 2.6 collective-permute-start.1
  14.8 3.3 %collective-permute-done.1.refs_2_ = bf16[24,896]{1,0:T(8,128)(2,1)S(1)} collective-permute-done((bf16[24,896]{1,0:T(8,128)(2,1)}, bf16[24,896]{1,0:T(8,128)(2,1)S(1)}, u32[]{:S(2)}, u32[]{:S(2)}) %collective-permute-start.1) | collective-permute-done | bytes 43040 | tf_op jit(solution)/shard_map/ppermute | solution.py:419
  18.1 2.7 collective-permute-done.2.refs_3_
  21.7 13.4 %all_to_all.25.refs_0_ = bf16[4,4,24,896]{3,2,1,0:T(8,128)(2,1)S(1)} all-to-all(bf16[4,4,24,896]{3,2,1,0:T(8,128)(2,1)S(1)} %repeat.3), channel_id=1, replica_groups={{0,2,4,6},{1,3,5,7},{8,10,12,14},{9,11,13,15},{16,18,20,22},{17,19,21,2..., dimensions={0} | all-to-all | bytes 1376256 | tf_op jit(solution)/shard_map/all_to_all | solution.py:423
  36.3 3.2 %collective-permute-start.4 = (bf16[24,1536]{1,0:T(8,128)(2,1)}, bf16[24,1536]{1,0:T(8,128)(2,1)S(1)}, u32[]{:S(2)}, u32[]{:S(2)}) collective-permute-start(bf16[24,1536]{1,0:T(8,128)(2,1)} %get-tuple-element.115.refs_0_), channel_id=1, source_target_pairs={{0,8},{8,0},{16,24},{24,16},{1,9},{9,1},{17,25},{25,17},{2,10},{10... | collective-permute-start | bytes 221192 | tf_op jit(solution)/shard_map/ppermute | solution.py:419
  39.6 1.6 place.3
  42.5 2.4 collective-permute-done.5.refs_2_
  46.0 3.5 %all-to-all-start.1 = ((bf16[4,4,24,1536]{3,2,1,0:T(8,128)(2,1)}), bf16[4,4,24,1536]{3,2,1,0:T(8,128)(2,1)S(1)}, u32[]{:S(2)}, u32[]{:S(2)}) async-start(bf16[4,4,24,1536]{3,2,1,0:T(8,128)(2,1)} %repeat.4), calls=%async_computation.1 | async-start | bytes 2359296 | tf_op jit(solution)/shard_map/all_to_all | solution.py:423
  50.7 3.2 %collective-permute-start.7 = (bf16[96,768]{1,0:T(8,128)(2,1)S(1)}, bf16[96,768]{1,0:T(8,128)(2,1)S(1)}, u32[]{:S(2)}, u32[]{:S(2)}) collective-permute-start(bf16[96,768]{1,0:T(8,128)(2,1)S(1)} %copy-done.14), channel_id=1, source_target_pairs={{0,8},{8,0},{16,24},{24,16},{1,9},{9,1},{17,25},{25,17},{2,10},{10... | collective-permute-start | bytes 442376 | tf_op jit(solution)/shard_map/ppermute | solution.py:419
  55.1 1.7 collective-permute-start.11
  56.8 3.6 %collective-permute-done.9.refs_3_ = bf16[96,768]{1,0:T(8,128)(2,1)S(1)} collective-permute-done((bf16[96,768]{1,0:T(8,128)(2,1)S(1)}, bf16[96,768]{1,0:T(8,128)(2,1)S(1)}, u32[]{:S(2)}, u32[]{:S(2)}) %collective-permute-start.9) | collective-permute-done | bytes 147488 | tf_op jit(solution)/shard_map/ppermute | solution.py:419
  61.1 10.1 %attend.2 = (bf16[3,1152,768]{2,1,0:T(8,128)(2,1)}, bf16[3,4,1152,288]{3,2,1,0:T(8,128)(2,1)}, bf16[3,1152,256]{2,1,0:T(8,128)(2,1)}) custom-call(bf16[1152,768]{1,0:T(8,128)(2,1)} %refs_2_.3, bf16[768,768]{1,0:T(8,128)(2,1)} %bitcast.37, f32[16,768]{1,0:T(8,128)} %copy-done.13), custom_call_target="tpu_custom_call" | custom-call | flops 2717908992 | bytes 7962624 | tf_op jit(solution)/shard_map/attend/pallas_call | solution.py:35
  71.4 1.5 copy-done.4
  73.9 3.8 %all-to-all-start.2 = ((bf16[4,4,104,768]{3,2,1,0:T(8,128)(2,1)}), bf16[4,4,104,768]{3,2,1,0:T(8,128)(2,1)S(1)}, u32[]{:S(2)}, u32[]{:S(2)}) async-start(bf16[4,4,104,768]{3,2,1,0:T(8,128)(2,1)} %copy-done.4), calls=%async_computation.2 | async-start | bytes 5111808 | tf_op jit(solution)/shard_map/all_to_all | solution.py:423
  77.8 3.0 collective-permute-done.13.refs_1_
  85.0 17.9 %attend.3 = (bf16[3,1152,768]{2,1,0:T(8,128)(2,1)}, bf16[3,4,1152,288]{3,2,1,0:T(8,128)(2,1)}, bf16[3,1152,256]{2,1,0:T(8,128)(2,1)}) custom-call(bf16[1152,768]{1,0:T(8,128)(2,1)} %refs_2_.3, bf16[768,1536]{1,0:T(8,128)(2,1)} %bitcast.32, f32[16,768]{1,0:T(8,128)} %copy-done.13, ...), custom_call_target="tpu_custom_call", output_to_operand_aliasing={{0}: (3, {}), {1}: (4, {}), {2}: (5, {})} | custom-call | flops 5435817984 | bytes 14155776 | tf_op jit(solution)/shard_map/attend/pallas_call | solution.py:35
  102.9 6.0 %all-to-all-done.2.refs_0_ = bf16[4,4,104,768]{3,2,1,0:T(8,128)(2,1)S(1)} async-done(((bf16[4,4,104,768]{3,2,1,0:T(8,128)(2,1)}), bf16[4,4,104,768]{3,2,1,0:T(8,128)(2,1)S(1)}, u32[]{:S(2)}, u32[]{:S(2)}) %all-to-all-start.2) | async-done | bytes 2555936 | tf_op jit(solution)/shard_map/all_to_all | solution.py:423
  108.9 18.1 %up.1 = (f32[1152,768]{1,0:T(8,128)}, f32[1152,1]{1,0:T(8,128)}, bf16[1152,768]{1,0:T(8,128)(2,1)}, bf16[1152,3072]{1,0:T(8,128)(2,1)}, bf16[1152,3072]{1,0:T(8,128)(2,1)}) custom-call(bf16[3,1152,256]{2,1,0:T(8,128)(2,1)} %get-tuple-element.135.ctx_ref.refs_0_, bf16[1152,768]{1,0:T(8,128)(2,1)} %refs_2_.3, ...), custom_call_target="tpu_custom_call" | custom-call | flops 6794772480 | bytes 28901376 | tf_op jit(solution)/shard_map/up/pallas_call | solution.py:35
  127.0 3.0 place.5
  133.2 21.4 %down.1 = (bf16[1152,768]{1,0:T(8,128)(2,1)}, f32[4,1,768]{2,1,0:T(1,128)}, f32[1152,768]{1,0:T(8,128)}, bf16[1152,768]{1,0:T(8,128)(2,1)}, bf16[1152,3072]{1,0:...) custom-call(bf16[1152,768]{1,0:T(8,128)(2,1)} %get-tuple-element.153.first_ref.refs_0, ...), custom_call_target="tpu_custom_call" | custom-call | flops 10871635968 | bytes 36569088 | tf_op jit(solution)/shard_map/down/pallas_call | solution.py:35
  154.7 10.6 %down_grad.1 = (bf16[4,4,96,768]{3,2,1,0:T(8,128)(2,1)}, bf16[4,4,96,768]{3,2,1,0:T(8,128)(2,1)}) custom-call(s32[3]{0:T(128)} %copy-done.17, bf16[1152,3072]{1,0:T(8,128)(2,1)} %get-tuple-element.138.act_ref.x_ref, bf16[1152,768]{1,0:T(8,128)(2,1)} %get-tuple-element.150.y_ref), custom_call_target="tpu_custom_call" | custom-call | flops 5435817984 | bytes 13565952 | tf_op jit(solution)/shard_map/down_grad/pallas_call | solution.py:35
  165.2 10.5 %up_grad.1 = (bf16[4,4,24,3072]{3,2,1,0:T(8,128)(2,1)}, bf16[4,4,24,3072]{3,2,1,0:T(8,128)(2,1)}) custom-call(s32[3]{0:T(128)} %copy-done.17, bf16[1152,768]{1,0:T(8,128)(2,1)} %get-tuple-element.153.first_ref.refs_0_, bf16[1152,3072]{1,0:T(8,128)(2,1)} %get-tuple-element.154.refs_1_.inner_ref), custom_call_target="tpu_custom_call" | custom-call | flops 5435817984 | bytes 13565952 | tf_op jit(solution)/shard_map/up_grad/pallas_call | solution.py:35
  176.3 2.7 copy-done.1
  181.1 2.7 collective-permute-done.17.refs_5_
  183.8 1.8 pair_sum.2
  185.6 2.2 copy-done.2
  187.8 5.0 %all-to-all-start.3 = ((bf16[4,4,200,768]{3,2,1,0:T(8,128)(2,1)}), bf16[4,4,200,768]{3,2,1,0:T(8,128)(2,1)}, u32[]{:S(2)}, u32[]{:S(2)}) async-start(bf16[4,4,200,768]{3,2,1,0:T(8,128)(2,1)} %copy-done.2), calls=%async_computation.3 | async-start | bytes 9830400 | tf_op jit(solution)/shard_map/all_to_all | solution.py:423
  192.8 15.3 %mid.1 = (f32[1152,768]{1,0:T(8,128)}, bf16[1152,768]{1,0:T(8,128)(2,1)}, bf16[1152,768]{1,0:T(8,128)(2,1)}, f32[1,768]{1,0:T(1,128)}, f32[1,768]{1,0:T(1,128)}, /*index=5*/f32[1,768]{1,0:T(1,128)}) custom-call(f32[1152,768]{1,0:T(8,128)} %get-tuple-element.159.two_ref, bf16[1152,3072]{1,0:T(8,128)(2,1)} %get-tuple-element.154.refs_1_.inner_ref, ...), custom_call_target="tpu_custom_call" | custom-call | flops 6794772480 | bytes 27131904 | tf_op jit(solution)/shard_map/mid/pallas_call | solution.py:35
  208.1 20.9 %attend_back.1 = (bf16[3,1152,768]{2,1,0:T(8,128)(2,1)}, f32[1,768]{1,0:T(1,128)}, f32[1,768]{1,0:T(1,128)}) custom-call(bf16[3,1152,768]{2,1,0:T(8,128)(2,1)} %get-tuple-element.164.qkv_ref, bf16[3,4,1152,288]{3,2,1,0:T(8,128)(2,1)} %get-tuple-element.165.soft_ref, bf16[3,1152,256]{2,1,0:T(8,128)(2,1)} %get-tuple-element.135.ctx_ref.refs_0_, ...), custom_call_target="tpu_custom_call" | custom-call | flops 8153726976 | bytes 22118400 | tf_op jit(solution)/shard_map/attend_back/pallas_call | solution.py:35
  229.0 12.8 %mix_grad.1 = (bf16[4,4,24,3328]{3,2,1,0:T(8,128)(2,1)}, bf16[4,4,24,3328]{3,2,1,0:T(8,128)(2,1)}) custom-call(s32[3]{0:T(128)} %copy-done.17, bf16[3,1152,256]{2,1,0:T(8,128)(2,1)} %get-tuple-element.135.ctx_ref.refs_0_, bf16[1152,768]{1,0:T(8,128)(2,1)} %get-tuple-element.163.refs_1_, bf16[1152,768]{1,0:T(8,128)(2,1)} %refs_2_.3, ...), custom_call_target="tpu_custom_call" | custom-call | flops 5888802816 | bytes 14548992 | tf_op jit(solution)/shard_map/mix_grad/pallas_call | solution.py:35
  242.2 4.7 %collective-permute-done.18.refs_1_ = bf16[4,4,24,3328]{3,2,1,0:T(8,128)(2,1)S(1)} collective-permute-done((bf16[4,4,24,3328]{3,2,1,0:T(8,128)(2,1)}, bf16[4,4,24,3328]{3,2,1,0:T(8,128)(2,1)S(1)}, u32[]{:S(2)}, u32[]{:S(2)}) %collective-permute-start.18) | collective-permute-done | bytes 2555936 | tf_op jit(solution)/shard_map/ppermute | solution.py:427
  246.8 1.7 copy-done.10
  249.8 1.4 copy-done.3
  251.3 4.3 %all-to-all-start.4 = ((bf16[4,4,24,3328]{3,2,1,0:T(8,128)(2,1)}), bf16[4,4,24,3328]{3,2,1,0:T(8,128)(2,1)S(1)}, u32[]{:S(2)}, u32[]{:S(2)}) async-start(bf16[4,4,24,3328]{3,2,1,0:T(8,128)(2,1)} %copy-done.3), calls=%async_computation.4 | async-start | bytes 5111808 | tf_op jit(solution)/shard_map/all_to_all | solution.py:423
  255.6 3.9 %chips_sum.2 = (f32[208,768]{1,0:T(8,128)S(1)}, bf16[208,768]{1,0:T(8,128)(2,1)}, bf16[208,768]{1,0:T(8,128)(2,1)}, bf16[208,768]{1,0:T(8,128)(2,1)}) custom-call(s32[3]{0:T(128)S(1)} %copy-done.19, bf16[4,4,200,768]{3,2,1,0:T(8,128)(2,1)} %all-to-all-done.3.in_ref), custom_call_target="tpu_custom_call" | custom-call | bytes 6193152 | tf_op jit(solution)/shard_map/chips_sum/pallas_call | solution.py:35
  259.5 3.3 %collective-permute-start.19 = (bf16[208,768]{1,0:T(8,128)(2,1)}, bf16[208,768]{1,0:T(8,128)(2,1)}, u32[]{:S(2)}, u32[]{:S(2)}) collective-permute-start(bf16[208,768]{1,0:T(8,128)(2,1)} %get-tuple-element.188), channel_id=1, source_target_pairs={{0,8},{8,0},{16,24},{24,16},{1,9},{9,1},{17,25},{25,17},{2,10},{10... | collective-permute-start | bytes 958472 | tf_op jit(solution)/shard_map/ppermute | solution.py:793
  263.4 1.8 collective-permute-start.21
  265.2 2.0 copy-done.25
  267.2 2.5 copy-done.30
  269.7 6.1 %tokens_back.1 = bf16[1152,768]{1,0:T(8,128)(2,1)} custom-call(f32[1152,768]{1,0:T(8,128)S(1)} %copy-done.25, bf16[3,1152,768]{2,1,0:T(8,128)(2,1)S(1)} %copy-done.30, bf16[768,768]{1,0:T(8,128)(2,1)S(1)} %bitcast.38, bf16[768,1536]{1,0:T(8,128)(2,1)S(1)} %bitcast.33), custom_call_target="tpu_custom_call" | custom-call | flops 4076863488 | bytes 10616832 | tf_op jit(solution)/shard_map/tokens_back/pallas_call | solution.py:35
  275.8 10.1 %all-to-all-done.4.in_ref = bf16[4,4,24,3328]{3,2,1,0:T(8,128)(2,1)S(1)} async-done(((bf16[4,4,24,3328]{3,2,1,0:T(8,128)(2,1)}), bf16[4,4,24,3328]{3,2,1,0:T(8,128)(2,1)S(1)}, u32[]{:S(2)}, u32[]{:S(2)}) %all-to-all-start.4) | async-done | bytes 2555936 | tf_op jit(solution)/shard_map/all_to_all | solution.py:423
  285.9 1.5 chips_sum.3
  287.4 3.3 %collective-permute-start.22 = (bf16[24,3328]{1,0:T(8,128)(2,1)}, bf16[24,3328]{1,0:T(8,128)(2,1)S(1)}, u32[]{:S(2)}, u32[]{:S(2)}) collective-permute-start(bf16[24,3328]{1,0:T(8,128)(2,1)} %get-tuple-element.193), channel_id=1, source_target_pairs={{0,8},{8,0},{16,24},{24,16},{1,9},{9,1},{17,25},{25,17},{2,10},{10... | collective-permute-start | bytes 479240 | tf_op jit(solution)/shard_map/ppermute | solution.py:793
  291.3 1.8 collective-permute-start.24
  293.7 2.4 last_feed.1
  296.2 9.0 %collective-permute-done.23.refs_2_ = bf16[24,3328]{1,0:T(8,128)(2,1)S(1)} collective-permute-done((bf16[24,3328]{1,0:T(8,128)(2,1)}, bf16[24,3328]{1,0:T(8,128)(2,1)S(1)}, u32[]{:S(2)}, u32[]{:S(2)}) %collective-permute-start.23) | collective-permute-done | bytes 159776 | tf_op jit(solution)/shard_map/ppermute | solution.py:793
  (111 shorter events, 24.0 us)
Async XLA Ops:
  7.2 101.7 %all-gather.2.cloned.1.call-start = ((), (), s32[]{:S(2)}) async-start(), calls=%async_computation.5 | async-start | bytes 6285312 | tf_op jit(solution)/shard_map/all_gather | solution.py:909
  9.1 35.8 %copy-start.15 = (bf16[24,1536]{1,0:T(8,128)(2,1)S(1)}, bf16[24,1536]{1,0:T(8,128)(2,1)}, u32[]{:S(2)}) copy-start(bf16[24,1536]{1,0:T(8,128)(2,1)} %get-tuple-element.115.refs_0_) | copy-start | bytes 221188
  9.1 5.7 %collective-permute-start = (bf16[24,896]{1,0:T(8,128)(2,1)}, bf16[24,896]{1,0:T(8,128)(2,1)S(1)}, u32[]{:S(2)}, u32[]{:S(2)}) collective-permute-start(bf16[24,896]{1,0:T(8,128)(2,1)} %get-tuple-element.111.refs_0_), channel_id=1, source_target_pairs={{0,8},{8,0},{16,24},{24,16},{1,9},{9,1},{17,25},{25,17},{2,10},{10... | collective-permute-start | bytes 129032 | tf_op jit(solution)/shard_map/ppermute | solution.py:419
  12.2 5.9 %collective-permute-start.1 = (bf16[24,896]{1,0:T(8,128)(2,1)}, bf16[24,896]{1,0:T(8,128)(2,1)S(1)}, u32[]{:S(2)}, u32[]{:S(2)}) collective-permute-start(bf16[24,896]{1,0:T(8,128)(2,1)} %get-tuple-element.111.refs_0_), channel_id=1, source_target_pairs={{0,16},{8,24},{16,0},{24,8},{1,17},{9,25},{17,1},{25,9},{2,18},{10... | collective-permute-start | bytes 129032 | tf_op jit(solution)/shard_map/ppermute | solution.py:419
  14.8 6.0 %collective-permute-start.2 = (bf16[24,896]{1,0:T(8,128)(2,1)}, bf16[24,896]{1,0:T(8,128)(2,1)S(1)}, u32[]{:S(2)}, u32[]{:S(2)}) collective-permute-start(bf16[24,896]{1,0:T(8,128)(2,1)} %get-tuple-element.111.refs_0_), channel_id=1, source_target_pairs={{0,24},{8,16},{16,8},{24,0},{1,25},{9,17},{17,9},{25,1},{2,26},{10... | collective-permute-start | bytes 129032 | tf_op jit(solution)/shard_map/ppermute | solution.py:419
  35.1 4.5 %collective-permute-start.3 = (bf16[4,4,24,896]{3,2,1,0:T(8,128)(2,1)S(1)}, bf16[4,4,24,896]{3,2,1,0:T(8,128)(2,1)S(1)}, u32[]{:S(2)}, u32[]{:S(2)}) collective-permute-start(bf16[4,4,24,896]{3,2,1,0:T(8,128)(2,1)S(1)} %all_to_all.25.refs_0_), channel_id=1, source_target_pairs={{0,1},{1,0},{2,3},{3,2},{4,5},{5,4},{6,7},{7,6},{8,9},{9,8},{10,11... | collective-permute-start | bytes 2064392 | tf_op jit(solution)/shard_map/ppermute | solution.py:427
  35.1 7.4 %collective-permute-start.6 = (bf16[24,1536]{1,0:T(8,128)(2,1)}, bf16[24,1536]{1,0:T(8,128)(2,1)S(1)}, u32[]{:S(2)}, u32[]{:S(2)}) collective-permute-start(bf16[24,1536]{1,0:T(8,128)(2,1)} %get-tuple-element.115.refs_0_), channel_id=1, source_target_pairs={{0,24},{8,16},{16,8},{24,0},{1,25},{9,17},{17,9},{25,1},{2,26},{10... | collective-permute-start | bytes 221192 | tf_op jit(solution)/shard_map/ppermute | solution.py:419
  36.2 8.7 %collective-permute-start.5 = (bf16[24,1536]{1,0:T(8,128)(2,1)}, bf16[24,1536]{1,0:T(8,128)(2,1)S(1)}, u32[]{:S(2)}, u32[]{:S(2)}) collective-permute-start(bf16[24,1536]{1,0:T(8,128)(2,1)} %get-tuple-element.115.refs_0_), channel_id=1, source_target_pairs={{0,16},{8,24},{16,0},{24,8},{1,17},{9,25},{17,1},{25,9},{2,18},{10... | collective-permute-start | bytes 221192 | tf_op jit(solution)/shard_map/ppermute | solution.py:419
  36.3 8.6 %collective-permute-start.4 = (bf16[24,1536]{1,0:T(8,128)(2,1)}, bf16[24,1536]{1,0:T(8,128)(2,1)S(1)}, u32[]{:S(2)}, u32[]{:S(2)}) collective-permute-start(bf16[24,1536]{1,0:T(8,128)(2,1)} %get-tuple-element.115.refs_0_), channel_id=1, source_target_pairs={{0,8},{8,0},{16,24},{24,16},{1,9},{9,1},{17,25},{25,17},{2,10},{10... | collective-permute-start | bytes 221192 | tf_op jit(solution)/shard_map/ppermute | solution.py:419
  39.5 90.5 %copy-start.17 = (s32[3]{0:T(128)}, s32[3]{0:T(128)S(1)}, u32[]{:S(2)}) copy-start(s32[3]{0:T(128)S(1)} %pad_add_fusion.me_ref) | copy-start | bytes 40
  39.5 10.0 %copy-start.14 = (bf16[96,768]{1,0:T(8,128)(2,1)S(1)}, bf16[96,768]{1,0:T(8,128)(2,1)}, u32[]{:S(2)}) copy-start(bf16[96,768]{1,0:T(8,128)(2,1)} %refs_0_.2) | copy-start | bytes 442372
  39.5 14.4 %copy-start.16 = (bf16[256,128]{1,0:T(8,128)(2,1)S(1)}, bf16[256,128]{1,0:T(8,128)(2,1)}, u32[]{:S(2)}) copy-start(bf16[256,128]{1,0:T(8,128)(2,1)} %t_ref) | copy-start | bytes 196612
  42.2 18.9 %copy-start.13 = (f32[16,768]{1,0:T(8,128)}, f32[16,768]{1,0:T(8,128)S(1)}, u32[]{:S(2)}) copy-start(f32[16,768]{1,0:T(8,128)S(1)} %get-tuple-element.114.v_ref) | copy-start | bytes 147460
  42.5 7.0 %copy-start.21 = (f32[1,3072]{1,0:T(1,128)}, f32[1,3072]{1,0:T(1,128)S(1)}, u32[]{:S(2)}) copy-start(f32[1,3072]{1,0:T(1,128)S(1)} %bias_row.1.ub_ref) | copy-start | bytes 36868
  46.0 27.0 %all-to-all-start.1 = ((bf16[4,4,24,1536]{3,2,1,0:T(8,128)(2,1)}), bf16[4,4,24,1536]{3,2,1,0:T(8,128)(2,1)S(1)}, u32[]{:S(2)}, u32[]{:S(2)}) async-start(bf16[4,4,24,1536]{3,2,1,0:T(8,128)(2,1)} %repeat.4), calls=%async_computation.1 | async-start | bytes 2359296 | tf_op jit(solution)/shard_map/all_to_all | solution.py:423
  49.5 10.9 %collective-permute-start.9 = (bf16[96,768]{1,0:T(8,128)(2,1)S(1)}, bf16[96,768]{1,0:T(8,128)(2,1)S(1)}, u32[]{:S(2)}, u32[]{:S(2)}) collective-permute-start(bf16[96,768]{1,0:T(8,128)(2,1)S(1)} %copy-done.14), channel_id=1, source_target_pairs={{0,24},{8,16},{16,8},{24,0},{1,25},{9,17},{17,9},{25,1},{2,26},{10... | collective-permute-start | bytes 442376 | tf_op jit(solution)/shard_map/ppermute | solution.py:419
  50.7 20.4 %collective-permute-start.8 = (bf16[96,768]{1,0:T(8,128)(2,1)S(1)}, bf16[96,768]{1,0:T(8,128)(2,1)S(1)}, u32[]{:S(2)}, u32[]{:S(2)}) collective-permute-start(bf16[96,768]{1,0:T(8,128)(2,1)S(1)} %copy-done.14), channel_id=1, source_target_pairs={{0,16},{8,24},{16,0},{24,8},{1,17},{9,25},{17,1},{25,9},{2,18},{10... | collective-permute-start | bytes 442376 | tf_op jit(solution)/shard_map/ppermute | solution.py:419
  50.7 20.4 %collective-permute-start.7 = (bf16[96,768]{1,0:T(8,128)(2,1)S(1)}, bf16[96,768]{1,0:T(8,128)(2,1)S(1)}, u32[]{:S(2)}, u32[]{:S(2)}) collective-permute-start(bf16[96,768]{1,0:T(8,128)(2,1)S(1)} %copy-done.14), channel_id=1, source_target_pairs={{0,8},{8,0},{16,24},{24,16},{1,9},{9,1},{17,25},{25,17},{2,10},{10... | collective-permute-start | bytes 442376 | tf_op jit(solution)/shard_map/ppermute | solution.py:419
  55.0 16.2 %collective-permute-start.10 = (bf16[8,512]{1,0:T(8,128)(2,1)S(1)}, bf16[8,512]{1,0:T(8,128)(2,1)S(1)}, u32[]{:S(2)}, u32[]{:S(2)}) collective-permute-start(bf16[8,512]{1,0:T(8,128)(2,1)S(1)} %get-tuple-element.129), channel_id=1, source_target_pairs={{0,8},{8,0},{16,24},{24,16},{1,9},{9,1},{17,25},{25,17},{2,10},{10... | collective-permute-start | bytes 24584 | tf_op jit(solution)/shard_map/ppermute | solution.py:419
  55.1 16.1 %collective-permute-start.11 = (bf16[8,512]{1,0:T(8,128)(2,1)S(1)}, bf16[8,512]{1,0:T(8,128)(2,1)S(1)}, u32[]{:S(2)}, u32[]{:S(2)}) collective-permute-start(bf16[8,512]{1,0:T(8,128)(2,1)S(1)} %get-tuple-element.130), channel_id=1, source_target_pairs={{0,16},{8,24},{16,0},{24,8},{1,17},{9,25},{17,1},{25,9},{2,18},{10... | collective-permute-start | bytes 24584 | tf_op jit(solution)/shard_map/ppermute | solution.py:419
  60.4 10.8 %collective-permute-start.12 = (bf16[8,512]{1,0:T(8,128)(2,1)S(1)}, bf16[8,512]{1,0:T(8,128)(2,1)S(1)}, u32[]{:S(2)}, u32[]{:S(2)}) collective-permute-start(bf16[8,512]{1,0:T(8,128)(2,1)S(1)} %get-tuple-element.131), channel_id=1, source_target_pairs={{0,24},{8,16},{16,8},{24,0},{1,25},{9,17},{17,9},{25,1},{2,26},{10... | collective-permute-start | bytes 24584 | tf_op jit(solution)/shard_map/ppermute | solution.py:419
  73.9 34.9 %all-to-all-start.2 = ((bf16[4,4,104,768]{3,2,1,0:T(8,128)(2,1)}), bf16[4,4,104,768]{3,2,1,0:T(8,128)(2,1)S(1)}, u32[]{:S(2)}, u32[]{:S(2)}) async-start(bf16[4,4,104,768]{3,2,1,0:T(8,128)(2,1)} %copy-done.4), calls=%async_computation.2 | async-start | bytes 5111808 | tf_op jit(solution)/shard_map/all_to_all | solution.py:423
  77.8 3.1 collective-permute-start.13
  108.9 18.1 %collective-permute-start.14 = (bf16[4,4,104,768]{3,2,1,0:T(8,128)(2,1)S(1)}, bf16[4,4,104,768]{3,2,1,0:T(8,128)(2,1)}, u32[]{:S(2)}, u32[]{:S(2)}) collective-permute-start(bf16[4,4,104,768]{3,2,1,0:T(8,128)(2,1)S(1)} %all-to-all-done.2.refs_0_), channel_id=1, source_target_pairs={{0,1},{1,0},{2,3},{3,2},{4,5},{5,4},{6,7},{7,6},{8,9},{9,8},{10,11... | collective-permute-start | bytes 7667720 | tf_op jit(solution)/shard_map/ppermute | solution.py:427
  127.0 3.4 %copy-start = (bf16[768,3968]{1,0:T(8,128)(2,1)S(1)}, bf16[768,3968]{1,0:T(8,128)(2,1)}, u32[]{:S(2)}) copy-start(bf16[768,3968]{1,0:T(8,128)(2,1)} %all-gather.2.cloned.1.call-done.wo_ref.wu_ref.r_ref) | copy-start | bytes 18284548
  127.0 3.4 %copy-start.24 = (f32[4]{0:T(128)S(1)}, f32[4]{0:T(128)}, u32[]{:S(2)}) copy-start(f32[4]{0:T(128)} %sg_ref.3) | copy-start | bytes 52
  165.2 11.0 %copy-start.31 = (bf16[4,4,96,768]{3,2,1,0:T(8,128)(2,1)S(1)}, bf16[4,4,96,768]{3,2,1,0:T(8,128)(2,1)}, u32[]{:S(2)}) copy-start(bf16[4,4,96,768]{3,2,1,0:T(8,128)(2,1)} %get-tuple-element.152) | copy-start | bytes 7077892
  165.2 11.1 %copy-start.22 = (f32[4,1,768]{2,1,0:T(1,128)S(1)}, f32[4,1,768]{2,1,0:T(1,128)}, u32[]{:S(2)}) copy-start(f32[4,1,768]{2,1,0:T(1,128)} %get-tuple-element.145.top_ref) | copy-start | bytes 36868
  165.2 11.1 %copy-start.23 = (s32[4]{0:T(128)S(1)}, s32[4]{0:T(128)}, u32[]{:S(2)}) copy-start(s32[4]{0:T(128)} %id_ref.1) | copy-start | bytes 52
  175.7 8.0 %collective-permute-start.16 = (bf16[4,4,24,3072]{3,2,1,0:T(8,128)(2,1)}, bf16[4,4,24,3072]{3,2,1,0:T(8,128)(2,1)S(1)}, u32[]{:S(2)}, u32[]{:S(2)}) collective-permute-start(bf16[4,4,24,3072]{3,2,1,0:T(8,128)(2,1)} %get-tuple-element.157), channel_id=1, source_target_pairs={{0,1},{1,0},{2,3},{3,2},{4,5},{5,4},{6,7},{7,6},{8,9},{9,8},{10,11... | collective-permute-start | bytes 7077896 | tf_op jit(solution)/shard_map/ppermute | solution.py:427
  176.2 7.5 %collective-permute-start.15 = (bf16[4,4,96,768]{3,2,1,0:T(8,128)(2,1)S(1)}, bf16[4,4,96,768]{3,2,1,0:T(8,128)(2,1)S(1)}, u32[]{:S(2)}, u32[]{:S(2)}) collective-permute-start(bf16[4,4,96,768]{3,2,1,0:T(8,128)(2,1)S(1)} %copy-done.31), channel_id=1, source_target_pairs={{0,1},{1,0},{2,3},{3,2},{4,5},{5,4},{6,7},{7,6},{8,9},{9,8},{10,11... | collective-permute-start | bytes 7077896 | tf_op jit(solution)/shard_map/ppermute | solution.py:427
  176.3 2.7 copy-start.1
  179.0 4.7 %copy-start.11 = (bf16[4,4,96,768]{3,2,1,0:T(8,128)(2,1)S(1)}, bf16[4,4,96,768]{3,2,1,0:T(8,128)(2,1)}, u32[]{:S(2)}) copy-start(bf16[4,4,96,768]{3,2,1,0:T(8,128)(2,1)} %get-tuple-element.156.refs_0_) | copy-start | bytes 7077892
  179.0 4.7 %copy-start.12 = (bf16[4,4,24,3072]{3,2,1,0:T(8,128)(2,1)S(1)}, bf16[4,4,24,3072]{3,2,1,0:T(8,128)(2,1)}, u32[]{:S(2)}) copy-start(bf16[4,4,24,3072]{3,2,1,0:T(8,128)(2,1)} %get-tuple-element.155.refs_1_) | copy-start | bytes 7077892
  179.0 4.7 %copy-start.18 = (s32[3]{0:T(128)S(1)}, s32[3]{0:T(128)}, u32[]{:S(2)}) copy-start(s32[3]{0:T(128)} %copy-done.17) | copy-start | bytes 40
  180.6 3.1 collective-permute-start.17
  187.8 63.5 %all-to-all-start.3 = ((bf16[4,4,200,768]{3,2,1,0:T(8,128)(2,1)}), bf16[4,4,200,768]{3,2,1,0:T(8,128)(2,1)}, u32[]{:S(2)}, u32[]{:S(2)}) async-start(bf16[4,4,200,768]{3,2,1,0:T(8,128)(2,1)} %copy-done.2), calls=%async_computation.3 | async-start | bytes 9830400 | tf_op jit(solution)/shard_map/all_to_all | solution.py:423
  241.8 5.0 %collective-permute-start.18 = (bf16[4,4,24,3328]{3,2,1,0:T(8,128)(2,1)}, bf16[4,4,24,3328]{3,2,1,0:T(8,128)(2,1)S(1)}, u32[]{:S(2)}, u32[]{:S(2)}) collective-permute-start(bf16[4,4,24,3328]{3,2,1,0:T(8,128)(2,1)} %get-tuple-element.180), channel_id=1, source_target_pairs={{0,1},{1,0},{2,3},{3,2},{4,5},{5,4},{6,7},{7,6},{8,9},{9,8},{10,11... | collective-permute-start | bytes 7667720 | tf_op jit(solution)/shard_map/ppermute | solution.py:427
  251.3 4.3 %copy-start.19 = (s32[3]{0:T(128)S(1)}, s32[3]{0:T(128)}, u32[]{:S(2)}) copy-start(s32[3]{0:T(128)} %copy-done.17) | copy-start | bytes 40
  251.3 34.6 %all-to-all-start.4 = ((bf16[4,4,24,3328]{3,2,1,0:T(8,128)(2,1)}), bf16[4,4,24,3328]{3,2,1,0:T(8,128)(2,1)S(1)}, u32[]{:S(2)}, u32[]{:S(2)}) async-start(bf16[4,4,24,3328]{3,2,1,0:T(8,128)(2,1)} %copy-done.3), calls=%async_computation.4 | async-start | bytes 5111808 | tf_op jit(solution)/shard_map/all_to_all | solution.py:423
  255.6 9.6 %copy-start.6 = (bf16[4,4,2,24,1536]{4,3,2,1,0:T(8,128)(2,1)S(1)}, bf16[4,4,2,24,1536]{4,3,2,1,0:T(8,128)(2,1)}, u32[]{:S(2)}) copy-start(bf16[4,4,2,24,1536]{4,3,2,1,0:T(8,128)(2,1)} %copy-done.5) | copy-start | bytes 7077892
  255.6 9.6 %copy-start.27 = (bf16[4,4,2,24,768]{4,3,2,1,0:T(8,128)(2,1)S(1)}, bf16[4,4,2,24,768]{4,3,2,1,0:T(8,128)(2,1)}, u32[]{:S(2)}) copy-start(bf16[4,4,2,24,768]{4,3,2,1,0:T(8,128)(2,1)} %copy-done.26) | copy-start | bytes 3538948
  259.5 31.8 %collective-permute-start.19 = (bf16[208,768]{1,0:T(8,128)(2,1)}, bf16[208,768]{1,0:T(8,128)(2,1)}, u32[]{:S(2)}, u32[]{:S(2)}) collective-permute-start(bf16[208,768]{1,0:T(8,128)(2,1)} %get-tuple-element.188), channel_id=1, source_target_pairs={{0,8},{8,0},{16,24},{24,16},{1,9},{9,1},{17,25},{25,17},{2,10},{10... | collective-permute-start | bytes 958472 | tf_op jit(solution)/shard_map/ppermute | solution.py:793
  262.8 30.9 %collective-permute-start.20 = (bf16[208,768]{1,0:T(8,128)(2,1)}, bf16[208,768]{1,0:T(8,128)(2,1)}, u32[]{:S(2)}, u32[]{:S(2)}) collective-permute-start(bf16[208,768]{1,0:T(8,128)(2,1)} %get-tuple-element.189), channel_id=1, source_target_pairs={{0,16},{8,24},{16,0},{24,8},{1,17},{9,25},{17,1},{25,9},{2,18},{10... | collective-permute-start | bytes 958472 | tf_op jit(solution)/shard_map/ppermute | solution.py:793
  263.4 30.4 %collective-permute-start.21 = (bf16[208,768]{1,0:T(8,128)(2,1)}, bf16[208,768]{1,0:T(8,128)(2,1)}, u32[]{:S(2)}, u32[]{:S(2)}) collective-permute-start(bf16[208,768]{1,0:T(8,128)(2,1)} %get-tuple-element.190), channel_id=1, source_target_pairs={{0,24},{8,16},{16,8},{24,0},{1,25},{9,17},{17,9},{25,1},{2,26},{10... | collective-permute-start | bytes 958472 | tf_op jit(solution)/shard_map/ppermute | solution.py:793
  287.4 8.8 %collective-permute-start.22 = (bf16[24,3328]{1,0:T(8,128)(2,1)}, bf16[24,3328]{1,0:T(8,128)(2,1)S(1)}, u32[]{:S(2)}, u32[]{:S(2)}) collective-permute-start(bf16[24,3328]{1,0:T(8,128)(2,1)} %get-tuple-element.193), channel_id=1, source_target_pairs={{0,8},{8,0},{16,24},{24,16},{1,9},{9,1},{17,25},{25,17},{2,10},{10... | collective-permute-start | bytes 479240 | tf_op jit(solution)/shard_map/ppermute | solution.py:793
  290.7 14.5 %collective-permute-start.23 = (bf16[24,3328]{1,0:T(8,128)(2,1)}, bf16[24,3328]{1,0:T(8,128)(2,1)S(1)}, u32[]{:S(2)}, u32[]{:S(2)}) collective-permute-start(bf16[24,3328]{1,0:T(8,128)(2,1)} %get-tuple-element.194), channel_id=1, source_target_pairs={{0,16},{8,24},{16,0},{24,8},{1,17},{9,25},{17,1},{25,9},{2,18},{10... | collective-permute-start | bytes 479240 | tf_op jit(solution)/shard_map/ppermute | solution.py:793
  291.3 13.9 %collective-permute-start.24 = (bf16[24,3328]{1,0:T(8,128)(2,1)}, bf16[24,3328]{1,0:T(8,128)(2,1)S(1)}, u32[]{:S(2)}, u32[]{:S(2)}) collective-permute-start(bf16[24,3328]{1,0:T(8,128)(2,1)} %get-tuple-element.195), channel_id=1, source_target_pairs={{0,24},{8,16},{16,8},{24,0},{1,25},{9,17},{17,9},{25,1},{2,26},{10... | collective-permute-start | bytes 479240 | tf_op jit(solution)/shard_map/ppermute | solution.py:793
  (14 other events, 20.5 us)
Sparse Core Ops, SparseCore 0:
  11.5 89.5 all-gather.1
